TPU v7x, 32 devices: a whole 2x2x4 slice. The times are simulated.
32 devices in a mesh: ens: 2 (over y), sub: 4 (over x, core), hor: 4 (over z).
Axes of the slice: x: 2, y: 2, z: 4, core: 2. Of those that a mesh axis runs over, the one named last changes fastest.
Arguments:
- adjoint_state: float32 [8, 2, 48, 16, 768], P(('ens', 'sub'), None, 'hor'), parts along dimension 0, may hold values from -6 to 6
- courant_east: float32 [8, 48, 16, 768], P(('ens', 'sub'), 'hor'), parts along dimension 0, may hold values from -0.47 to 0.47
- courant_north: float32 [8, 48, 16, 768], P(('ens', 'sub'), 'hor'), parts along dimension 0, may hold values from -0.47 to 0.47
- parent_cell: int32 [2, 2, 48], P(None, None, 'hor'), may hold values from 1 to 29, as said below
- stencil_offset: int32 [4, 2, 2, 48], P(None, None, None, 'hor'), may hold values from -1 to 2
- stencil_weight: float32 [4, 2, 2, 48], P(None, None, None, 'hor'), may hold values from 0.05 to 0.35
- owner_slot: int32 [32], replicated, may hold values from 0 to 31, each once
Outputs:
- adjoint_result: float32 [8, 2, 48, 16, 768], P(('ens', 'sub'), None, 'hor'), parts along dimension 0
- boundary_gradient: float32 [4, 16, 32], P('ens', 'sub', 'hor'), parts along dimension 0
There are 2 independent parts, one for each index of `ens`. A program takes and returns all parts, laid end to end along the dimension named above; an argument that names none is the same for every part. Nothing has to cross between parts.
Inputs may be any that keep to these rules, and one draw needn't show every extreme that they name: `parent_cell`: on side s the parent cell lies between s * 16 + 1 and s * 16 + 13, so every interpolation point stays on its own side.
All inputs are finite; a program needn't handle non-finite values.
Results may differ from a plain program's by a relative error of at most 0.000084.
Values sent between devices are 32-bit elements; how exact they have to be, the bound alone decides.
No kernel may reach another device: no remote copies, remote signals or barrier semaphores. Data moves between devices by JAX's collectives and lax.ppermute only.
A program may use at most 384 MiB of HBM per device.

v0:
```python
import jax
import jax.numpy as jnp
from jax import lax
from jax.sharding import PartitionSpec as P

STEPS = 4


def from_behind(value, axis, by):
    peers = lax.axis_size(axis)
    pairs = [(i, i + by) for i in range(peers) if 0 <= i + by < peers]
    return lax.ppermute(value, axis, pairs)


def coefficients(east_rate, north_rate):
    return (
        jnp.maximum(east_rate, 0.0),
        jnp.maximum(-east_rate, 0.0),
        jnp.maximum(north_rate, 0.0),
        jnp.maximum(-north_rate, 0.0),
        1.0 - jnp.abs(east_rate) - jnp.abs(north_rate),
    )


def northward(adjoint, north_plus, north_minus):
    upper = jnp.pad((north_plus * adjoint)[..., 1:], ((0, 0), (0, 0), (0, 0), (0, 1)))
    lower = jnp.pad((north_minus * adjoint)[..., :-1], ((0, 0), (0, 0), (0, 0), (1, 0)))
    return upper + lower


def local(
    adjoint_state,
    courant_east,
    courant_north,
    parent_cell,
    stencil_offset,
    stencil_weight,
    owner_slot,
):
    incoming = adjoint_state[0]
    east_rate = courant_east[0]
    north_rate = courant_north[0]
    tile_rows = incoming.shape[1]
    levels = incoming.shape[2]
    south_grad = jnp.zeros((2, tile_rows, levels), jnp.float32)
    north_grad = jnp.zeros((2, tile_rows, levels), jnp.float32)
    east_plus, east_minus, north_plus, north_minus, centre = coefficients(east_rate, north_rate)
    adjoint = incoming
    for substep in range(STEPS):
        south_grad = south_grad + north_plus[:, :, 0] * adjoint[..., 0]
        north_grad = north_grad + north_minus[:, :, -1] * adjoint[..., -1]
        flux_east = east_plus * adjoint
        flux_west = east_minus * adjoint
        east_edge = from_behind(flux_east[:, :1], "hor", -1)
        west_edge = from_behind(flux_west[:, -1:], "hor", 1)
        from_east = jnp.concatenate([flux_east[:, 1:], east_edge], 1)
        from_west = jnp.concatenate([west_edge, flux_west[:, :-1]], 1)
        adjoint = (
            centre * adjoint + from_east + from_west + northward(adjoint, north_plus, north_minus)
        )
    received = from_behind(adjoint, "sub", -1)
    adjoint_result = (incoming - received)[None]
    ghost = jnp.stack([south_grad, north_grad], 1)
    parent_count = owner_slot.shape[0]
    slot_ids = lax.broadcasted_iota(jnp.int32, (parent_count,), 0)
    target = parent_cell[None] + stencil_offset
    onehot = (target[..., None] == slot_ids).astype(jnp.float32)
    mixing = jnp.sum(stencil_weight[..., None] * onehot, 0)
    placing = (owner_slot[:, None] == slot_ids[None, :]).astype(jnp.float32)
    spread = jnp.einsum("csip,pq->csiq", mixing, placing, precision=lax.Precision.HIGHEST)
    summed = lax.psum_scatter(ghost, "sub", scatter_dimension=3, tiled=True)
    partial_grad = jnp.einsum("csil,csiq->clq", summed, spread, precision=lax.Precision.HIGHEST)
    boundary_gradient = lax.psum_scatter(partial_grad, "hor", scatter_dimension=2, tiled=True)
    return (adjoint_result, boundary_gradient)


def solution(mesh):
    in_specs = (
        P(("ens", "sub"), None, "hor", None, None),
        P(("ens", "sub"), "hor", None, None),
        P(("ens", "sub"), "hor", None, None),
        P(None, None, "hor"),
        P(None, None, None, "hor"),
        P(None, None, None, "hor"),
        P(),
    )
    out_specs = (P(("ens", "sub"), None, "hor", None, None), P("ens", "sub", "hor"))
    return jax.shard_map(local, mesh=mesh, in_specs=in_specs, out_specs=out_specs, check_vma=False)
```

profile of v0, /device:TPU:0, one launch (start us, length us, event | category | flops | bytes accessed | tf_op | source)
XLA Modules:
  0.0 88.4 jit_solution(6411980164305266429)
XLA Ops:
  0.6 2.6 %subtract_bitcast_fusion.1 = (f32[12,16,768]{2,1,0:T(8,128)}, f32[12,16,768]{2,1,0:T(8,128)S(1)}, f32[12,16,768]{2,1,0:T(8,128)S(1)}, f32[12,16,768]{2,1,0:T(8,128)S(1)}, f32[12,16,768]{2,1,0:T(8,128)S(1)}) fusion(f32[1,12,16,768]{3,2,1,0:T(8,128)} %param.9, f32[1,12,16,768]{3,2,1,0:T(8,128)} %param.8), kind=kLoop, calls=%fused_computation.34 | loop fusion | flops 1474560 | bytes 4128768 | tf_op jit(solution)/shard_map/mul | solution.py:59
  5.1 4.9 %collective-permute-start.1 = (f32[2,1,16,768]{3,2,1,0:T(8,128)S(1)}, f32[2,1,16,768]{3,2,1,0:T(8,128)S(1)}, u32[]{:S(2)}, u32[]{:S(2)}) collective-permute-start(f32[2,1,16,768]{3,2,1,0:T(8,128)S(1)} %slice.144), channel_id=1, source_target_pairs={{0,1},{1,2},{2,3},{4,5},{5,6},{6,7},{8,9},{9,10},{10,11},{12,13},{... | collective-permute-start | bytes 294920 | tf_op jit(solution)/shard_map/ppermute | solution.py:12
  10.0 1.3 %collective-permute-start = (f32[2,1,16,768]{3,2,1,0:T(8,128)S(1)}, f32[2,1,16,768]{3,2,1,0:T(8,128)S(1)}, u32[]{:S(2)}, u32[]{:S(2)}) collective-permute-start(f32[2,1,16,768]{3,2,1,0:T(8,128)S(1)} %slice.143), channel_id=1, source_target_pairs={{1,0},{2,1},{3,2},{5,4},{6,5},{7,6},{9,8},{10,9},{11,10},{13,12},{... | collective-permute-start | bytes 294920 | tf_op jit(solution)/shard_map/ppermute | solution.py:12
  14.2 2.4 %collective-permute-done = f32[2,1,16,768]{3,2,1,0:T(8,128)S(1)} collective-permute-done((f32[2,1,16,768]{3,2,1,0:T(8,128)S(1)}, f32[2,1,16,768]{3,2,1,0:T(8,128)S(1)}, u32[]{:S(2)}, u32[]{:S(2)}) %collective-permute-start) | collective-permute-done | bytes 98336 | tf_op jit(solution)/shard_map/ppermute | solution.py:12
  17.2 1.8 %broadcast_multiply_fusion.2 = (f32[2,12,16,768]{3,2,1,0:T(8,128)S(1)}, f32[2,12,16,768]{3,2,1,0:T(8,128)S(1)}) fusion(f32[12,16,768]{2,1,0:T(8,128)S(1)} %get-tuple-element.27, f32[2,12,16,767]{3,2,1,0:T(8,128)S(1)} %get-tuple-element.25, f32[2,12,16,767]{3,2,1,0:T(8,128)S(1)} %get-tuple-element.24, f32[2,11,16,768]{3,2,1,0:T(8,128)S(1)} %slice.145, ...), kind=kLoop, calls=%fused_computation.26 | loop fusion | flops 2359296 | bytes 9434112 | tf_op jit(solution)/shard_map/mul | solution.py:53
  19.0 3.5 %collective-permute-start.3 = (f32[2,1,16,768]{3,2,1,0:T(8,128)S(1)}, f32[2,1,16,768]{3,2,1,0:T(8,128)S(1)}, u32[]{:S(2)}, u32[]{:S(2)}) collective-permute-start(f32[2,1,16,768]{3,2,1,0:T(8,128)S(1)} %slice.152), channel_id=1, source_target_pairs={{0,1},{1,2},{2,3},{4,5},{5,6},{6,7},{8,9},{9,10},{10,11},{12,13},{... | collective-permute-start | bytes 294920 | tf_op jit(solution)/shard_map/ppermute | solution.py:12
  22.6 1.3 %collective-permute-start.2 = (f32[2,1,16,768]{3,2,1,0:T(8,128)S(1)}, f32[2,1,16,768]{3,2,1,0:T(8,128)S(1)}, u32[]{:S(2)}, u32[]{:S(2)}) collective-permute-start(f32[2,1,16,768]{3,2,1,0:T(8,128)S(1)} %slice.151), channel_id=1, source_target_pairs={{1,0},{2,1},{3,2},{5,4},{6,5},{7,6},{9,8},{10,9},{11,10},{13,12},{... | collective-permute-start | bytes 294920 | tf_op jit(solution)/shard_map/ppermute | solution.py:12
  24.7 4.5 %collective-permute-done.2 = f32[2,1,16,768]{3,2,1,0:T(8,128)S(1)} collective-permute-done((f32[2,1,16,768]{3,2,1,0:T(8,128)S(1)}, f32[2,1,16,768]{3,2,1,0:T(8,128)S(1)}, u32[]{:S(2)}, u32[]{:S(2)}) %collective-permute-start.2) | collective-permute-done | bytes 98336 | tf_op jit(solution)/shard_map/ppermute | solution.py:12
  29.8 3.5 %collective-permute-start.5 = (f32[2,1,16,768]{3,2,1,0:T(8,128)S(1)}, f32[2,1,16,768]{3,2,1,0:T(8,128)S(1)}, u32[]{:S(2)}, u32[]{:S(2)}) collective-permute-start(f32[2,1,16,768]{3,2,1,0:T(8,128)S(1)} %slice.160), channel_id=1, source_target_pairs={{0,1},{1,2},{2,3},{4,5},{5,6},{6,7},{8,9},{9,10},{10,11},{12,13},{... | collective-permute-start | bytes 294920 | tf_op jit(solution)/shard_map/ppermute | solution.py:12
  33.5 1.4 %collective-permute-start.4 = (f32[2,1,16,768]{3,2,1,0:T(8,128)S(1)}, f32[2,1,16,768]{3,2,1,0:T(8,128)S(1)}, u32[]{:S(2)}, u32[]{:S(2)}) collective-permute-start(f32[2,1,16,768]{3,2,1,0:T(8,128)S(1)} %slice.159), channel_id=1, source_target_pairs={{1,0},{2,1},{3,2},{5,4},{6,5},{7,6},{9,8},{10,9},{11,10},{13,12},{... | collective-permute-start | bytes 294920 | tf_op jit(solution)/shard_map/ppermute | solution.py:12
  35.5 4.6 %collective-permute-done.4 = f32[2,1,16,768]{3,2,1,0:T(8,128)S(1)} collective-permute-done((f32[2,1,16,768]{3,2,1,0:T(8,128)S(1)}, f32[2,1,16,768]{3,2,1,0:T(8,128)S(1)}, u32[]{:S(2)}, u32[]{:S(2)}) %collective-permute-start.4) | collective-permute-done | bytes 98336 | tf_op jit(solution)/shard_map/ppermute | solution.py:12
  40.8 2.5 %collective-permute-start.7 = (f32[2,1,16,768]{3,2,1,0:T(8,128)S(1)}, f32[2,1,16,768]{3,2,1,0:T(8,128)S(1)}, u32[]{:S(2)}, u32[]{:S(2)}) collective-permute-start(f32[2,1,16,768]{3,2,1,0:T(8,128)S(1)} %slice.168), channel_id=1, source_target_pairs={{0,1},{1,2},{2,3},{4,5},{5,6},{6,7},{8,9},{9,10},{10,11},{12,13},{... | collective-permute-start | bytes 294920 | tf_op jit(solution)/shard_map/ppermute | solution.py:12
  43.5 1.3 %collective-permute-start.6 = (f32[2,1,16,768]{3,2,1,0:T(8,128)S(1)}, f32[2,1,16,768]{3,2,1,0:T(8,128)S(1)}, u32[]{:S(2)}, u32[]{:S(2)}) collective-permute-start(f32[2,1,16,768]{3,2,1,0:T(8,128)S(1)} %slice.167), channel_id=1, source_target_pairs={{1,0},{2,1},{3,2},{5,4},{6,5},{7,6},{9,8},{10,9},{11,10},{13,12},{... | collective-permute-start | bytes 294920 | tf_op jit(solution)/shard_map/ppermute | solution.py:12
  45.5 4.4 %collective-permute-done.6 = f32[2,1,16,768]{3,2,1,0:T(8,128)S(1)} collective-permute-done((f32[2,1,16,768]{3,2,1,0:T(8,128)S(1)}, f32[2,1,16,768]{3,2,1,0:T(8,128)S(1)}, u32[]{:S(2)}, u32[]{:S(2)}) %collective-permute-start.6) | collective-permute-done | bytes 98336 | tf_op jit(solution)/shard_map/ppermute | solution.py:12
  50.0 1.7 %fusion.7 = f32[2,12,16,768]{3,2,1,0:T(8,128)} fusion(f32[2,1,16,768]{3,2,1,0:T(8,128)S(1)} %collective-permute-done.6, f32[2,11,16,768]{3,2,1,0:T(8,128)S(1)} %slice.166, f32[2,11,16,768]{3,2,1,0:T(8,128)S(1)} %slice.169, f32[2,1,16,768]{3,2,1,0:T(8,128)S(1)} %collective-permute-done.7, f32[2,12,16,767]{3,2,1,0:T(8,128)S(1)} %get-tuple-element.17, ...), kind=kLoop, calls=%fused_computation.19 | loop fusion | flops 2064384 | bytes 7664640 | tf_op jit(solution)/shard_map/add | solution.py:59
  51.7 1.3 %collective-permute-start.8 = (f32[2,12,16,768]{3,2,1,0:T(8,128)}, f32[2,12,16,768]{3,2,1,0:T(8,128)}, u32[]{:S(2)}, u32[]{:S(2)}) collective-permute-start(f32[2,12,16,768]{3,2,1,0:T(8,128)} %fusion.7), channel_id=1, source_target_pairs={{4,0},{8,4},{12,8},{5,1},{9,5},{13,9},{6,2},{10,6},{14,10},{7,3},{... | collective-permute-start | bytes 3538952 | tf_op jit(solution)/shard_map/ppermute | solution.py:12
  54.1 1.3 %dynamic-slice.2 = u32[1]{0:T(128)} dynamic-slice(u32[32]{0:T(128)} %constant.33, u32[]{:T(128)S(6)} %add.173), dynamic_slice_sizes={1} | dynamic-slice | bytes 12
  55.4 1.2 %dynamic-slice = u32[1]{0:T(128)} dynamic-slice(u32[32]{0:T(128)} %constant.29, u32[]{:T(128)S(6)} %add.173), dynamic_slice_sizes={1} | dynamic-slice | bytes 12
  58.0 2.0 %slice_add_fusion.3 = (f32[2,12,16,1]{3,2,1,0:T(8,128)}, f32[2,12,16,1]{3,2,1,0:T(8,128)}) fusion(f32[2,12,16,768]{3,2,1,0:T(8,128)} %copy-done.1, f32[2,12,16,768]{3,2,1,0:T(8,128)S(1)} %get-tuple-element.11, f32[2,12,16,768]{3,2,1,0:T(8,128)S(1)} %get-tuple-element.13, f32[2,12,16,768]{3,2,1,0:T(8,128)S(1)} %bitcast.38), kind=kLoop, calls=%fused_computation.38 | loop fusion | flops 2304 | bytes 15360 | tf_op jit(solution)/shard_map/add | solution.py:50
  60.0 1.1 %copy.117 = f32[2,12,16,1]{2,0,1,3:T(2,128)S(1)} copy(f32[2,12,16,1]{3,2,1,0:T(8,128)} %get-tuple-element.14) | data formatting | bytes 3072 | tf_op jit(solution)/shard_map/add | solution.py:50
  61.2 1.1 %copy.118 = f32[2,12,16,1]{2,0,1,3:T(2,128)S(1)} copy(f32[2,12,16,1]{3,2,1,0:T(8,128)} %get-tuple-element.15) | data formatting | bytes 3072 | tf_op jit(solution)/shard_map/add | solution.py:51
  62.5 13.4 %all-reduce.8 = f32[2,2,12,16]{2,1,0,3:T(2,128)S(1)} all-reduce(f32[2,2,12,16]{2,1,0,3:T(2,128)S(1)} %copy.119), channel_id=2, replica_groups=mesh['ens'=2,'sub'=4,'hor'=4] {'sub'}, use_global_device_ids=true, to_apply=%region_0.1.clone | all-reduce | flops 768 | bytes 6144
  76.9 8.4 %all-reduce.9 = f32[2,4,32]{2,1,0:T(4,128)S(1)} all-reduce(f32[2,4,32]{2,1,0:T(4,128)S(1)} %convolution_bitcast_fusion), channel_id=3, replica_groups=mesh['ens'=2,'sub'=4,'hor'=4] {'hor'}, use_global_device_ids=true, to_apply=%region_2.3.clone | all-reduce | flops 256 | bytes 2048
  85.9 2.4 %subtract_bitcast_fusion = f32[1,2,12,16,768]{4,3,2,1,0:T(8,128)} fusion(f32[2,12,16,768]{3,2,1,0:T(8,128)} %collective-permute-done.8, f32[1,2,12,16,768]{4,3,2,1,0:T(8,128)S(1)} %copy-done), kind=kLoop, calls=%fused_computation.20 | loop fusion | flops 294912 | bytes 3538944 | tf_op jit(solution)/shard_map/broadcast_in_dim | solution.py:62
  (85 shorter events, 11.8 us)
Async XLA Ops:
  0.6 2.6 %copy-start = (f32[1,2,12,16,768]{4,3,2,1,0:T(8,128)S(1)}, f32[1,2,12,16,768]{4,3,2,1,0:T(8,128)}, u32[]{:S(2)}) copy-start(f32[1,2,12,16,768]{4,3,2,1,0:T(8,128)} %param.7) | copy-start | bytes 3538948
  3.2 8.4 %copy-start.13 = (f32[12,16,768]{2,1,0:T(8,128)}, f32[12,16,768]{2,1,0:T(8,128)S(1)}, u32[]{:S(2)}) copy-start(f32[12,16,768]{2,1,0:T(8,128)S(1)} %get-tuple-element.30) | copy-start | bytes 1769476
  3.2 13.9 %copy-start.4 = (f32[12,16,768]{2,1,0:T(8,128)}, f32[12,16,768]{2,1,0:T(8,128)S(1)}, u32[]{:S(2)}) copy-start(f32[12,16,768]{2,1,0:T(8,128)S(1)} %get-tuple-element.27) | copy-start | bytes 1769476
  3.2 20.7 %copy-start.2 = (f32[12,16,768]{2,1,0:T(8,128)}, f32[12,16,768]{2,1,0:T(8,128)S(1)}, u32[]{:S(2)}) copy-start(f32[12,16,768]{2,1,0:T(8,128)S(1)} %get-tuple-element.29) | copy-start | bytes 1769476
  3.3 8.1 %copy-start.17 = (s32[4,2,2,12]{3,2,1,0:T(2,128)S(1)}, s32[4,2,2,12]{3,2,1,0:T(2,128)}, u32[]{:S(2)}) copy-start(s32[4,2,2,12]{3,2,1,0:T(2,128)} %param.11) | copy-start | bytes 2308
  3.3 8.1 %copy-start.18 = (s32[2,2,12]{2,1,0:T(2,128)S(1)}, s32[2,2,12]{2,1,0:T(2,128)}, u32[]{:S(2)}) copy-start(s32[2,2,12]{2,1,0:T(2,128)} %param.10) | copy-start | bytes 580
  3.3 8.2 %copy-start.16 = (f32[4,2,2,12]{3,2,1,0:T(2,128)S(1)}, f32[4,2,2,12]{3,2,1,0:T(2,128)}, u32[]{:S(2)}) copy-start(f32[4,2,2,12]{3,2,1,0:T(2,128)} %param.12) | copy-start | bytes 2308
  4.1 6.0 %copy-start.11 = (f32[2,12,16,768]{3,2,1,0:T(8,128)}, f32[2,12,16,768]{3,2,1,0:T(8,128)S(1)}, u32[]{:S(2)}) copy-start(f32[2,12,16,768]{3,2,1,0:T(8,128)S(1)} %get-tuple-element.22) | copy-start | bytes 3538948
  5.1 9.1 %collective-permute-start.1 = (f32[2,1,16,768]{3,2,1,0:T(8,128)S(1)}, f32[2,1,16,768]{3,2,1,0:T(8,128)S(1)}, u32[]{:S(2)}, u32[]{:S(2)}) collective-permute-start(f32[2,1,16,768]{3,2,1,0:T(8,128)S(1)} %slice.144), channel_id=1, source_target_pairs={{0,1},{1,2},{2,3},{4,5},{5,6},{6,7},{8,9},{9,10},{10,11},{12,13},{... | collective-permute-start | bytes 294920 | tf_op jit(solution)/shard_map/ppermute | solution.py:12
  10.0 6.5 %collective-permute-start = (f32[2,1,16,768]{3,2,1,0:T(8,128)S(1)}, f32[2,1,16,768]{3,2,1,0:T(8,128)S(1)}, u32[]{:S(2)}, u32[]{:S(2)}) collective-permute-start(f32[2,1,16,768]{3,2,1,0:T(8,128)S(1)} %slice.143), channel_id=1, source_target_pairs={{1,0},{2,1},{3,2},{5,4},{6,5},{7,6},{9,8},{10,9},{11,10},{13,12},{... | collective-permute-start | bytes 294920 | tf_op jit(solution)/shard_map/ppermute | solution.py:12
  12.0 1.5 %copy-start.12 = (f32[2,12,16,768]{3,2,1,0:T(8,128)S(1)}, f32[2,12,16,768]{3,2,1,0:T(8,128)}, u32[]{:S(2)}) copy-start(f32[2,12,16,768]{3,2,1,0:T(8,128)} %copy-done.11) | copy-start | bytes 3538948
  14.1 3.1 %copy-start.6 = (f32[12,16,768]{2,1,0:T(8,128)S(1)}, f32[12,16,768]{2,1,0:T(8,128)}, u32[]{:S(2)}) copy-start(f32[12,16,768]{2,1,0:T(8,128)} %get-tuple-element.26) | copy-start | bytes 1769476
  14.1 2.4 %copy-start.14 = (f32[2,1,16,768]{3,2,1,0:T(8,128)}, f32[2,1,16,768]{3,2,1,0:T(8,128)S(1)}, u32[]{:S(2)}) copy-start(f32[2,1,16,768]{3,2,1,0:T(8,128)S(1)} %collective-permute-done.1) | copy-start | bytes 294916
  17.2 5.3 %copy-start.8 = (f32[12,16,768]{2,1,0:T(8,128)S(1)}, f32[12,16,768]{2,1,0:T(8,128)}, u32[]{:S(2)}) copy-start(f32[12,16,768]{2,1,0:T(8,128)} %copy-done.7) | copy-start | bytes 1769476
  19.0 5.7 %collective-permute-start.3 = (f32[2,1,16,768]{3,2,1,0:T(8,128)S(1)}, f32[2,1,16,768]{3,2,1,0:T(8,128)S(1)}, u32[]{:S(2)}, u32[]{:S(2)}) collective-permute-start(f32[2,1,16,768]{3,2,1,0:T(8,128)S(1)} %slice.152), channel_id=1, source_target_pairs={{0,1},{1,2},{2,3},{4,5},{5,6},{6,7},{8,9},{9,10},{10,11},{12,13},{... | collective-permute-start | bytes 294920 | tf_op jit(solution)/shard_map/ppermute | solution.py:12
  22.6 6.5 %collective-permute-start.2 = (f32[2,1,16,768]{3,2,1,0:T(8,128)S(1)}, f32[2,1,16,768]{3,2,1,0:T(8,128)S(1)}, u32[]{:S(2)}, u32[]{:S(2)}) collective-permute-start(f32[2,1,16,768]{3,2,1,0:T(8,128)S(1)} %slice.151), channel_id=1, source_target_pairs={{1,0},{2,1},{3,2},{5,4},{6,5},{7,6},{9,8},{10,9},{11,10},{13,12},{... | collective-permute-start | bytes 294920 | tf_op jit(solution)/shard_map/ppermute | solution.py:12
  24.5 4.7 %copy-start.5 = (f32[12,16,768]{2,1,0:T(8,128)S(1)}, f32[12,16,768]{2,1,0:T(8,128)}, u32[]{:S(2)}) copy-start(f32[12,16,768]{2,1,0:T(8,128)} %copy-done.4) | copy-start | bytes 1769476
  29.8 5.7 %collective-permute-start.5 = (f32[2,1,16,768]{3,2,1,0:T(8,128)S(1)}, f32[2,1,16,768]{3,2,1,0:T(8,128)S(1)}, u32[]{:S(2)}, u32[]{:S(2)}) collective-permute-start(f32[2,1,16,768]{3,2,1,0:T(8,128)S(1)} %slice.160), channel_id=1, source_target_pairs={{0,1},{1,2},{2,3},{4,5},{5,6},{6,7},{8,9},{9,10},{10,11},{12,13},{... | collective-permute-start | bytes 294920 | tf_op jit(solution)/shard_map/ppermute | solution.py:12
  33.3 1.6 %copy-start.3 = (f32[12,16,768]{2,1,0:T(8,128)S(1)}, f32[12,16,768]{2,1,0:T(8,128)}, u32[]{:S(2)}) copy-start(f32[12,16,768]{2,1,0:T(8,128)} %copy-done.2) | copy-start | bytes 1769476
  33.5 6.6 %collective-permute-start.4 = (f32[2,1,16,768]{3,2,1,0:T(8,128)S(1)}, f32[2,1,16,768]{3,2,1,0:T(8,128)S(1)}, u32[]{:S(2)}, u32[]{:S(2)}) collective-permute-start(f32[2,1,16,768]{3,2,1,0:T(8,128)S(1)} %slice.159), channel_id=1, source_target_pairs={{1,0},{2,1},{3,2},{5,4},{6,5},{7,6},{9,8},{10,9},{11,10},{13,12},{... | collective-permute-start | bytes 294920 | tf_op jit(solution)/shard_map/ppermute | solution.py:12
  40.8 9.2 %copy-start.1 = (f32[2,12,16,768]{3,2,1,0:T(8,128)}, f32[2,12,16,768]{3,2,1,0:T(8,128)S(1)}, u32[]{:S(2)}) copy-start(f32[2,12,16,768]{3,2,1,0:T(8,128)S(1)} %get-tuple-element.9) | copy-start | bytes 3538948
  40.8 4.7 %collective-permute-start.7 = (f32[2,1,16,768]{3,2,1,0:T(8,128)S(1)}, f32[2,1,16,768]{3,2,1,0:T(8,128)S(1)}, u32[]{:S(2)}, u32[]{:S(2)}) collective-permute-start(f32[2,1,16,768]{3,2,1,0:T(8,128)S(1)} %slice.168), channel_id=1, source_target_pairs={{0,1},{1,2},{2,3},{4,5},{5,6},{6,7},{8,9},{9,10},{10,11},{12,13},{... | collective-permute-start | bytes 294920 | tf_op jit(solution)/shard_map/ppermute | solution.py:12
  43.5 6.5 %collective-permute-start.6 = (f32[2,1,16,768]{3,2,1,0:T(8,128)S(1)}, f32[2,1,16,768]{3,2,1,0:T(8,128)S(1)}, u32[]{:S(2)}, u32[]{:S(2)}) collective-permute-start(f32[2,1,16,768]{3,2,1,0:T(8,128)S(1)} %slice.167), channel_id=1, source_target_pairs={{1,0},{2,1},{3,2},{5,4},{6,5},{7,6},{9,8},{10,9},{11,10},{13,12},{... | collective-permute-start | bytes 294920 | tf_op jit(solution)/shard_map/ppermute | solution.py:12
  51.7 34.2 %collective-permute-start.8 = (f32[2,12,16,768]{3,2,1,0:T(8,128)}, f32[2,12,16,768]{3,2,1,0:T(8,128)}, u32[]{:S(2)}, u32[]{:S(2)}) collective-permute-start(f32[2,12,16,768]{3,2,1,0:T(8,128)} %fusion.7), channel_id=1, source_target_pairs={{4,0},{8,4},{12,8},{5,1},{9,5},{13,9},{6,2},{10,6},{14,10},{7,3},{... | collective-permute-start | bytes 3538952 | tf_op jit(solution)/shard_map/ppermute | solution.py:12
  (5 other events, 4.5 us)
where the time goes:
time: 89.1 us; the launch traced here: 88.4 us
  blocking collectives  21.8 us (24%)
  starting transfers between devices  21 us (24%)
  waiting for transfers between devices  16.2 us (18%)
  other arithmetic  14.4 us (16%)
  local copies, waits for them, and re-layouts  10.7 us (12%)
  between operations  2.48 us (3%)
  matrix products  1.79 us (2%)
    unnamed x2, blocking collectives  21.8 us
    ppermute x9, starting transfers between devices, from_behind(): return lax.ppermute(value, axis, pairs)  21 us
    ppermute x9, waiting for transfers between devices, from_behind(): return lax.ppermute(value, axis, pairs)  16.2 us
    unnamed x45, local copies, waits for them, and re-layouts  6.28 us
    mul x3, other arithmetic, local(): flux_west = east_minus * adjoint  3.04 us
    mul x1, other arithmetic, local(): centre * adjoint + from_east + from_west  2.6 us
    broadcast_in_dim x1, other arithmetic, local(): adjoint_result = (incoming - received)[None]  2.42 us
    add x2, other arithmetic, local(): south_grad = south_grad + north_plus[:, :, 0] * adjoint[..., 0]  2.06 us
  transfers between devices with their start and end apart: 9, of which 6 were waited for; matrix products, arithmetic and copies ran while one was open for 16% of the time, Pallas kernels for 0%

commit v1 on v0

v1 whole, which is shorter than its diff:
```python
import functools

import jax
import jax.numpy as jnp
from jax import lax
from jax.experimental import pallas as pl
from jax.experimental.pallas import tpu as pltpu
from jax.sharding import PartitionSpec as P

STEPS = 4
HALF = 8
FLUX_ROWS = 2 * STEPS
PACK_ROWS = FLUX_ROWS + 3


def from_behind(value, axis, by):
    peers = lax.axis_size(axis)
    pairs = [(i, i + by) for i in range(peers) if 0 <= i + by < peers]
    return lax.ppermute(value, axis, pairs)


def north_rates(north_rate):
    width = north_rate.shape[-1]
    column = lax.broadcasted_iota(jnp.int32, north_rate.shape, len(north_rate.shape) - 1)
    plus = jnp.where(column == 0, 0.0, jnp.maximum(north_rate, 0.0))
    minus = jnp.where(column == width - 1, 0.0, jnp.maximum(-north_rate, 0.0))
    return plus, minus


def shifted(flux_plus, flux_minus):
    width = flux_plus.shape[-1]
    axis = len(flux_plus.shape) - 1
    return pltpu.roll(flux_plus, width - 1, axis) + pltpu.roll(flux_minus, 1, axis)


class Row:
    def __init__(self, east_rate, north_rate=None, flip=False):
        self.outward = jnp.maximum(-east_rate if flip else east_rate, 0.0)
        self.inward = jnp.maximum(east_rate if flip else -east_rate, 0.0)
        if north_rate is not None:
            self.centre = 1.0 - jnp.abs(east_rate) - jnp.abs(north_rate)
            self.plus, self.minus = north_rates(north_rate)

    def stay(self, value):
        return self.centre * value + shifted(self.plus * value, self.minus * value)


def edge_kernel(state_ref, east_ref, north_ref, low_ref, high_ref):
    def one_side(flip, pack_ref):
        def half(h, carry):
            levels = pl.ds(pl.multiple_of(h * HALF, HALF), HALF)
            place = (lambda r: STEPS - 1 - r) if flip else (lambda r: r)
            rows = [
                Row(east_ref[0, place(r), levels, :], north_ref[0, place(r), levels, :], flip)
                for r in range(STEPS)
            ]
            pack_ref[FLUX_ROWS, levels, :] = east_ref[0, place(0), levels, :]
            pack_ref[FLUX_ROWS + 1, levels, :] = north_ref[0, place(0), levels, :]
            pack_ref[FLUX_ROWS + 2, levels, :] = east_ref[0, place(1), levels, :]
            for c in range(2):
                field = [state_ref[0, c, place(r), levels, :] for r in range(STEPS)]
                for k in range(STEPS):
                    pack_ref[2 * k + c, levels, :] = rows[0].outward * field[0]
                    after = []
                    for r in range(STEPS - 1 - k):
                        value = rows[r].stay(field[r]) + rows[r + 1].outward * field[r + 1]
                        if r > 0:
                            value = value + rows[r - 1].inward * field[r - 1]
                        after.append(value)
                    field = after
            return carry

        lax.fori_loop(0, pack_ref.shape[1] // HALF, half, 0)

    @pl.when(pl.program_id(0) == 0)
    def _():
        one_side(False, low_ref)

    @pl.when(pl.program_id(0) == 1)
    def _():
        one_side(True, high_ref)


def main_kernel(
    cell_ref, offset_ref, weight_ref, owner_ref,
    state_ref, east_ref, north_ref,
    middle_ref, ends_ref, spread_ref, partial_ref,
    field, plus_ref, minus_ref, centre_ref, ghost_ref,
):
    rows = east_ref.shape[1]
    slots = spread_ref.shape[-1]

    @pl.when(pl.program_id(0) == 0)
    def _():
        slot_ids = lax.broadcasted_iota(jnp.int32, (1, slots), 1)

        def one_row(i, carry):
            for c in range(2):
                for s in range(2):
                    total = jnp.zeros((1, slots), jnp.float32)
                    for point in range(offset_ref.shape[0]):
                        slot = owner_ref[cell_ref[c, s, i] + offset_ref[point, c, s, i]]
                        total = total + jnp.where(slot_ids == slot, weight_ref[point, c, s, i], 0.0)
                    spread_ref[c, s, pl.ds(i, 1), :] = total
            return carry

        lax.fori_loop(0, rows, one_row, 0)

    for i in range(rows):
        east_rate = east_ref[0, i]
        north_rate = north_ref[0, i]
        centre_ref[i] = 1.0 - jnp.abs(east_rate) - jnp.abs(north_rate)
        plus_ref[i] = jnp.maximum(north_rate, 0.0)
        minus_ref[i] = jnp.maximum(-north_rate, 0.0)

    width = east_ref.shape[-1]
    column = lax.broadcasted_iota(jnp.int32, (HALF, width), 1)
    first = column == 0
    last = column == width - 1

    for k in range(STEPS):
        read = (lambda c, i: state_ref[0, c, i]) if k == 0 else (lambda c, i, s=(k - 1) % 2: field[s, c, i])
        prior = [read(c, 0) for c in range(2)]
        here_flux = None
        west = [None, None]
        here = prior
        for i in range(rows):
            east_here = east_ref[0, i]
            after = [read(c, i + 1) for c in range(2)] if i + 1 < rows else None
            east_after = jnp.maximum(east_ref[0, i + 1], 0.0) if i + 1 < rows else None
            leave_west = jnp.maximum(-east_here, 0.0)
            centre = centre_ref[i]
            plus = plus_ref[i]
            minus = minus_ref[i]
            for c in range(2):
                value = here[c]
                up = plus * value
                down = minus * value
                if k == 0:
                    ghost_ref[c, 0, i] = up[:, :128]
                    ghost_ref[c, 1, i] = down[:, width - 128:]
                else:
                    ghost_ref[c, 0, i] += up[:, :128]
                    ghost_ref[c, 1, i] += down[:, width - 128:]
                up = jnp.where(first, 0.0, up)
                down = jnp.where(last, 0.0, down)
                total = centre * value + shifted(up, down)
                if after is not None:
                    total = total + east_after * after[c]
                if west[c] is not None:
                    total = total + west[c]
                west[c] = leave_west * value
                if k < STEPS - 1:
                    field[k % 2, c, i] = total
                elif i < STEPS:
                    ends_ref[c, i] = total
                elif i >= rows - STEPS:
                    ends_ref[c, i - rows + 2 * STEPS] = total
                else:
                    middle_ref[c, i - STEPS] = total
            here = after

    for c in range(2):
        total = jnp.zeros((HALF, slots), jnp.float32)
        for s in range(2):
            lane = 0 if s == 0 else 127
            for i in range(rows):
                total = total + ghost_ref[c, s, i, :, lane:lane + 1] * spread_ref[c, s, i:i + 1, :]
        partial_ref[c] = total


def mend_kernel(
    east_ref, north_ref, low_ref, high_ref, below_ref, above_ref, ends_ref, spread_ref, partial_ref,
    out_ref, sum_ref,
):
    levels_all = sum_ref.shape[1]
    rows = spread_ref.shape[2]
    width = east_ref.shape[-1]

    def one_side(flip, mine_ref, other_ref):
        place = (lambda r: STEPS - 1 - r) if flip else (lambda r: r)

        def half(h, carry):
            levels = pl.ds(pl.multiple_of(h * HALF, HALF), HALF)
            own = [
                Row(east_ref[0, place(r), levels, :], north_ref[0, place(r), levels, :], flip)
                for r in range(STEPS - 1)
            ]
            near = Row(other_ref[FLUX_ROWS, levels, :], other_ref[FLUX_ROWS + 1, levels, :], flip)
            far = Row(other_ref[FLUX_ROWS + 2, levels, :], None, flip)
            for c in range(2):
                mine = lambda k: mine_ref[2 * k + c, levels, :]
                theirs = lambda k: other_ref[2 * k + c, levels, :]
                a0 = theirs(0)
                n1 = mine(0)
                b0 = own[0].stay(a0) + near.inward * n1 + theirs(1)
                b1 = own[0].inward * a0
                bn1 = near.stay(n1) + own[0].outward * a0 + mine(1)
                bn2 = near.outward * n1
                c0 = own[0].stay(b0) + near.inward * bn1 + own[1].outward * b1 + theirs(2)
                c1 = own[1].stay(b1) + own[0].inward * b0
                c2 = own[1].inward * b1
                cn1 = near.stay(bn1) + own[0].outward * b0 + far.inward * bn2 + mine(2)
                d0 = own[0].stay(c0) + near.inward * cn1 + own[1].outward * c1 + theirs(3)
                d1 = own[1].stay(c1) + own[0].inward * c0 + own[2].outward * c2
                d2 = own[2].stay(c2) + own[1].inward * c1
                d3 = own[2].inward * c2
                for r, value in enumerate((d0, d1, d2, d3)):
                    out_ref[c, place(r), levels, :] = ends_ref[c, place(r), levels, :] + value
                total = sum_ref[c, levels, :]
                for r, value in enumerate((a0 + b0 + c0, b1 + c1, c2)):
                    i = rows - 1 - r if flip else r
                    rate = north_ref[0, place(r), levels, :]
                    south = jnp.maximum(rate[:, :1], 0.0) * value[:, :1]
                    north = jnp.maximum(-rate[:, width - 1:], 0.0) * value[:, width - 1:]
                    total = total + south * spread_ref[c, 0, i:i + 1, :]
                    total = total + north * spread_ref[c, 1, i:i + 1, :]
                sum_ref[c, levels, :] = total
            return carry

        lax.fori_loop(0, levels_all // HALF, half, 0)

    @pl.when(pl.program_id(0) == 0)
    def _():
        sum_ref[...] = partial_ref[...]
        one_side(False, low_ref, below_ref)

    @pl.when(pl.program_id(0) == 1)
    def _():
        one_side(True, high_ref, above_ref)


def subtract_middle(state_ref, other_ref, out_ref):
    out_ref[0] = state_ref[0] - other_ref[...]


def subtract_ends(begun_ref, state_ref, other_ref, out_ref):
    out_ref[0] = state_ref[0] - other_ref[...]


def cost(flops, moved):
    return pl.CostEstimate(flops=flops, bytes_accessed=moved, transcendentals=0)


PARAMS = pltpu.CompilerParams(vmem_limit_bytes=40 * 1024 * 1024)


def local(
    adjoint_state,
    courant_east,
    courant_north,
    parent_cell,
    stencil_offset,
    stencil_weight,
    owner_slot,
):
    _, parts, rows, levels, width = adjoint_state.shape
    slots = owner_slot.shape[0]
    blocks = rows // STEPS
    inner = rows - 2 * STEPS
    row_bytes = levels * width * 4
    f32 = functools.partial(jax.ShapeDtypeStruct, dtype=jnp.float32)
    at_end = lambda s: (0, 0, s * (blocks - 1), 0, 0)
    at_end4 = lambda s: (0, s * (blocks - 1), 0, 0)
    whole = lambda *dims: pl.BlockSpec(dims, lambda s: (0,) * len(dims))
    state_end = pl.BlockSpec((1, parts, STEPS, levels, width), at_end)
    rate_end = pl.BlockSpec((1, STEPS, levels, width), at_end4)
    pack_spec = whole(PACK_ROWS, levels, width)

    low, high = pl.pallas_call(
        edge_kernel,
        grid=(2,),
        in_specs=[state_end, rate_end, rate_end],
        out_specs=[pack_spec, pack_spec],
        out_shape=[f32((PACK_ROWS, levels, width))] * 2,
        compiler_params=PARAMS,
        cost_estimate=cost(24 * levels * width * 13, 54 * row_bytes),
        name="edge_fluxes",
    )(adjoint_state, courant_east, courant_north)
    below = from_behind(high, "hor", 1)
    above = from_behind(low, "hor", -1)

    smem = pl.BlockSpec(memory_space=pltpu.SMEM)
    by_half = pl.BlockSpec((1, rows, HALF, width), lambda h: (0, 0, h, 0))
    middle, ends, spread, partial = pl.pallas_call(
        main_kernel,
        grid=(levels // HALF,),
        in_specs=[
            smem, smem, smem, smem,
            pl.BlockSpec((1, parts, rows, HALF, width), lambda h: (0, 0, 0, h, 0)),
            by_half, by_half,
        ],
        out_specs=[
            pl.BlockSpec((parts, inner, HALF, width), lambda h: (0, 0, h, 0)),
            pl.BlockSpec((parts, 2 * STEPS, HALF, width), lambda h: (0, 0, h, 0)),
            whole(parts, 2, rows, slots),
            pl.BlockSpec((parts, HALF, slots), lambda h: (0, h, 0)),
        ],
        out_shape=[
            f32((parts, inner, levels, width)),
            f32((parts, 2 * STEPS, levels, width)),
            f32((parts, 2, rows, slots)),
            f32((parts, levels, slots)),
        ],
        scratch_shapes=[
            pltpu.VMEM((2, parts, rows, HALF, width), jnp.float32),
            pltpu.VMEM((rows, HALF, width), jnp.float32),
            pltpu.VMEM((rows, HALF, width), jnp.float32),
            pltpu.VMEM((rows, HALF, width), jnp.float32),
            pltpu.VMEM((parts, 2, rows, HALF, 128), jnp.float32),
        ],
        compiler_params=PARAMS,
        cost_estimate=cost(8 * rows * levels * width * 13, 6 * rows * row_bytes),
        name="inner_sweep",
    )(parent_cell, stencil_offset, stencil_weight, owner_slot, adjoint_state, courant_east, courant_north)
    middle_next = from_behind(middle, "sub", -1)

    ends, partial = pl.pallas_call(
        mend_kernel,
        grid=(2,),
        in_specs=[
            rate_end, rate_end, pack_spec, pack_spec, pack_spec, pack_spec,
            pl.BlockSpec((parts, STEPS, levels, width), lambda s: (0, s, 0, 0)),
            whole(parts, 2, rows, slots),
            whole(parts, levels, slots),
        ],
        out_specs=[
            pl.BlockSpec((parts, STEPS, levels, width), lambda s: (0, s, 0, 0)),
            whole(parts, levels, slots),
        ],
        out_shape=[f32((parts, 2 * STEPS, levels, width)), f32((parts, levels, slots))],
        compiler_params=PARAMS,
        cost_estimate=cost(32 * levels * width * 13, 92 * row_bytes),
        name="mend_ends",
    )(courant_east, courant_north, low, high, below, above, ends, spread, partial)
    ends_next = from_behind(ends, "sub", -1)

    subs, hors = lax.axis_size("sub"), lax.axis_size("hor")
    pieces = partial.reshape(parts, subs, levels // subs, hors, slots // hors)
    pieces = pieces.transpose(1, 3, 0, 2, 4).reshape(subs * hors, parts, levels // subs, slots // hors)
    boundary_gradient = jnp.sum(lax.all_to_all(pieces, ("sub", "hor"), 0, 0, tiled=True), 0)

    state_block = lambda pick: pl.BlockSpec((1, parts, STEPS, levels, width), lambda s: (0, 0, pick(s), 0, 0))
    other_block = pl.BlockSpec((parts, STEPS, levels, width), lambda s: (0, s, 0, 0))
    begun = pl.pallas_call(
        subtract_middle,
        grid=(inner // STEPS,),
        in_specs=[state_block(lambda s: s + 1), other_block],
        out_specs=state_block(lambda s: s + 1),
        out_shape=f32(adjoint_state.shape),
        compiler_params=PARAMS,
        cost_estimate=cost(parts * inner * levels * width, 3 * parts * inner * row_bytes),
        name="subtract_middle",
    )(adjoint_state, middle_next)
    adjoint_result = pl.pallas_call(
        subtract_ends,
        grid=(2,),
        in_specs=[
            pl.BlockSpec(memory_space=pl.ANY),
            state_block(lambda s: s * (blocks - 1)),
            other_block,
        ],
        out_specs=state_block(lambda s: s * (blocks - 1)),
        out_shape=f32(adjoint_state.shape),
        input_output_aliases={0: 0},
        compiler_params=PARAMS,
        cost_estimate=cost(parts * 2 * STEPS * levels * width, 6 * parts * STEPS * row_bytes),
        name="subtract_ends",
    )(begun, adjoint_state, ends_next)
    return (adjoint_result, boundary_gradient)


def solution(mesh):
    in_specs = (
        P(("ens", "sub"), None, "hor", None, None),
        P(("ens", "sub"), "hor", None, None),
        P(("ens", "sub"), "hor", None, None),
        P(None, None, "hor"),
        P(None, None, None, "hor"),
        P(None, None, None, "hor"),
        P(),
    )
    out_specs = (P(("ens", "sub"), None, "hor", None, None), P("ens", "sub", "hor"))
    return jax.shard_map(local, mesh=mesh, in_specs=in_specs, out_specs=out_specs, check_vma=False)
```

time: 89.1 us -> 49.3 us (0.55)
  blocking collectives: 21.8 us -> 0 us
  other arithmetic: 14.4 us -> 1.46 us
  Pallas kernels: 0 us -> 9.57 us
  local copies, waits for them, and re-layouts: 10.7 us -> 5.63 us
  waiting for transfers between devices: 16.2 us -> 12.8 us
  starting transfers between devices: 21 us -> 18.5 us
  matrix products: 1.79 us -> 0 us
  between operations: 2.48 us -> 0.79 us
    unnamed x2 -> x0, blocking collectives: 21.8 us -> none
    ppermute x9 -> x4, starting transfers between devices: 21 us -> 9.6 us  [from_behind(): return lax.ppermute(value, axis, pairs)]
    pallas_call x0 -> x5, Pallas kernels: none -> 9.57 us  [the longest x1 4.5 us: local(): pl.pallas_call(main_kernel, grid=(levels // HALF,), in_specs=[smem, smem,...]
    ppermute x9 -> x4, waiting for transfers between devices: 16.2 us -> 6.93 us  [from_behind(): return lax.ppermute(value, axis, pairs)]
    all_to_all x0 -> x1, starting transfers between devices: none -> 8.93 us  [local(): lax.all_to_all(pieces, ('sub', 'hor'), 0, 0, tiled=True)]
    mul x12 -> x0, other arithmetic: 7.95 us -> none  [the longest x3 3.04 us: local(): flux_west = east_minus * adjoint]
    all_to_all x0 -> x1, waiting for transfers between devices: none -> 5.88 us  [local(): lax.all_to_all(pieces, ('sub', 'hor'), 0, 0, tiled=True)]
    add x5 -> x0, other arithmetic: 3.81 us -> none  [the longest x2 2.06 us: local(): south_grad = south_grad + north_plus[:, :, 0] * adjoint[..., 0]]
  transfers between devices with their start and end apart: 9 -> 5, of which waited for: 6 -> 3; matrix products, arithmetic and copies ran while one was open for 16% -> 8% of each run, Pallas kernels for 0% -> 11%
where the time goes in v1:
time: 49.3 us; the launch traced here: 48.8 us
  starting transfers between devices  18.5 us (38%)
  waiting for transfers between devices  12.8 us (26%)
  Pallas kernels  9.57 us (19%)
  local copies, waits for them, and re-layouts  5.63 us (11%)
  other arithmetic  1.46 us (3%)
  between operations  0.79 us (2%)
    ppermute x4, starting transfers between devices, from_behind(): return lax.ppermute(value, axis, pairs)  9.6 us
    all_to_all x1, starting transfers between devices, local(): lax.all_to_all(pieces, ('sub', 'hor'), 0, 0, tiled=True)  8.93 us
    ppermute x4, waiting for transfers between devices, from_behind(): return lax.ppermute(value, axis, pairs)  6.93 us
    all_to_all x1, waiting for transfers between devices, local(): lax.all_to_all(pieces, ('sub', 'hor'), 0, 0, tiled=True)  5.88 us
    pallas_call x1, Pallas kernels, local(): pl.pallas_call(main_kernel, grid=(levels // HALF,), in_specs=[smem, smem,...  4.5 us
    unnamed x20, local copies, waits for them, and re-layouts  3.42 us
    pallas_call x1, Pallas kernels, local(): pl.pallas_call(mend_kernel, grid=(2,), in_specs=[rate_end, rate_end, pack...  1.89 us
    reshape x2, local copies, waits for them, and re-layouts, local(): pieces = partial.reshape(parts, subs, levels // subs, hors, slots // hors)  1.57 us
  transfers between devices with their start and end apart: 5, of which 3 were waited for; matrix products, arithmetic and copies ran while one was open for 8% of the time, Pallas kernels for 11%

profile of v1, /device:TPU:0, one launch (start us, length us, event | category | flops | bytes accessed | tf_op | source)
XLA Modules:
  0.0 48.8 jit_solution(13810755204092628048)
XLA Ops:
  0.6 1.3 %copy-done = f32[1,2,12,16,768]{4,3,2,1,0:T(8,128)S(1)} copy-done((f32[1,2,12,16,768]{4,3,2,1,0:T(8,128)S(1)}, f32[1,2,12,16,768]{4,3,2,1,0:T(8,128)}, u32[]{:S(2)}) %copy-start) | copy-done | bytes 1179672
  1.9 1.1 %copy-done.2 = f32[1,12,16,768]{3,2,1,0:T(8,128)S(1)} copy-done((f32[1,12,16,768]{3,2,1,0:T(8,128)S(1)}, f32[1,12,16,768]{3,2,1,0:T(8,128)}, u32[]{:S(2)}) %copy-start.2) | copy-done | bytes 589848
  3.0 1.1 %copy-done.4 = f32[1,12,16,768]{3,2,1,0:T(8,128)S(1)} copy-done((f32[1,12,16,768]{3,2,1,0:T(8,128)S(1)}, f32[1,12,16,768]{3,2,1,0:T(8,128)}, u32[]{:S(2)}) %copy-start.4) | copy-done | bytes 589848
  4.1 1.3 %edge_fluxes.1 = (f32[11,16,768]{2,1,0:T(8,128)S(1)}, f32[11,16,768]{2,1,0:T(8,128)S(1)}) custom-call(f32[1,2,12,16,768]{4,3,2,1,0:T(8,128)S(1)} %copy-done, f32[1,12,16,768]{3,2,1,0:T(8,128)S(1)} %copy-done.2, f32[1,12,16,768]{3,2,1,0:T(8,128)S(1)} %copy-done.4), custom_call_target="tpu_custom_call" | custom-call | flops 3833856 | bytes 2654208 | tf_op jit(solution)/shard_map/edge_fluxes/pallas_call | solution.py:270
  5.4 1.3 %collective-permute-start.2 = (f32[11,16,768]{2,1,0:T(8,128)S(1)}, f32[11,16,768]{2,1,0:T(8,128)S(1)}, u32[]{:S(2)}, u32[]{:S(2)}) collective-permute-start(f32[11,16,768]{2,1,0:T(8,128)S(1)} %get-tuple-element.11.low_ref), channel_id=1, source_target_pairs={{1,0},{2,1},{3,2},{5,4},{6,5},{7,6},{9,8},{10,9},{11,10},{13,12},{... | collective-permute-start | bytes 1622024 | tf_op jit(solution)/shard_map/ppermute | solution.py:19
  6.7 0.0 copy-start.3
  6.7 0.0 copy-start.5
  6.7 5.7 %collective-permute-start.1 = (f32[11,16,768]{2,1,0:T(8,128)S(1)}, f32[11,16,768]{2,1,0:T(8,128)S(1)}, u32[]{:S(2)}, u32[]{:S(2)}) collective-permute-start(f32[11,16,768]{2,1,0:T(8,128)S(1)} %get-tuple-element.12.high_ref), channel_id=1, source_target_pairs={{0,1},{1,2},{2,3},{4,5},{5,6},{6,7},{8,9},{9,10},{10,11},{12,13},{... | collective-permute-start | bytes 1622024 | tf_op jit(solution)/shard_map/ppermute | solution.py:19
  12.5 4.5 %inner_sweep.1 = (f32[2,4,16,768]{3,2,1,0:T(8,128)S(1)}, f32[2,8,16,768]{3,2,1,0:T(8,128)S(1)}, f32[2,2,12,32]{3,2,1,0:T(8,128)S(1)}, f32[2,16,32]{2,1,0:T(8,128)S(1)}) custom-call(s32[2,2,12]{2,1,0:T(2,128)S(1)} %copy-done.8, s32[4,2,2,12]{3,2,1,0:T(2,128)S(1)} %copy-done.6, f32[4,2,2,12]{3,2,1,0:T(2,128)S(1)} %copy-done.7, s32[32]{0:T(128)S(1)} %copy-done.9, ...), custom_call_target="tpu_custom_call" | custom-call | flops 15335424 | bytes 3538944 | tf_op jit(solution)/shard_map/inner_sweep/pallas_call | solution.py:285
  17.0 5.6 %collective-permute-done.2.above_ref = f32[11,16,768]{2,1,0:T(8,128)S(1)} collective-permute-done((f32[11,16,768]{2,1,0:T(8,128)S(1)}, f32[11,16,768]{2,1,0:T(8,128)S(1)}, u32[]{:S(2)}, u32[]{:S(2)}) %collective-permute-start.2) | collective-permute-done | bytes 540704 | tf_op jit(solution)/shard_map/ppermute | solution.py:19
  22.6 1.3 %collective-permute-done.1.below_ref = f32[11,16,768]{2,1,0:T(8,128)S(1)} collective-permute-done((f32[11,16,768]{2,1,0:T(8,128)S(1)}, f32[11,16,768]{2,1,0:T(8,128)S(1)}, u32[]{:S(2)}, u32[]{:S(2)}) %collective-permute-start.1) | collective-permute-done | bytes 540704 | tf_op jit(solution)/shard_map/ppermute | solution.py:19
  23.9 1.9 %mend_ends.1 = (f32[2,8,16,768]{3,2,1,0:T(8,128)S(1)}, f32[2,16,32]{2,1,0:T(8,128)S(1)}) custom-call(f32[1,12,16,768]{3,2,1,0:T(8,128)S(1)} %copy-done.3, f32[1,12,16,768]{3,2,1,0:T(8,128)S(1)} %copy-done.5, f32[11,16,768]{2,1,0:T(8,128)S(1)} %get-tuple-element.11.low_ref, f32[11,16,768]{2,1,0:T(8,128)S(1)} %get-tuple-element.12.high_ref, ...), custom_call_target="tpu_custom_call" | custom-call | flops 5111808 | bytes 4521984 | tf_op jit(solution)/shard_map/mend_ends/pallas_call | solution.py:318
  25.8 1.3 %collective-permute-start.3 = (f32[2,8,16,768]{3,2,1,0:T(8,128)S(1)}, f32[2,8,16,768]{3,2,1,0:T(8,128)S(1)}, u32[]{:S(2)}, u32[]{:S(2)}) collective-permute-start(f32[2,8,16,768]{3,2,1,0:T(8,128)S(1)} %get-tuple-element.16), channel_id=1, source_target_pairs={{4,0},{8,4},{12,8},{5,1},{9,5},{13,9},{6,2},{10,6},{14,10},{7,3},{... | collective-permute-start | bytes 2359304 | tf_op jit(solution)/shard_map/ppermute | solution.py:19
  27.1 1.3 %collective-permute-start = (f32[2,4,16,768]{3,2,1,0:T(8,128)S(1)}, f32[2,4,16,768]{3,2,1,0:T(8,128)S(1)}, u32[]{:S(2)}, u32[]{:S(2)}) collective-permute-start(f32[2,4,16,768]{3,2,1,0:T(8,128)S(1)} %get-tuple-element.10), channel_id=1, source_target_pairs={{4,0},{8,4},{12,8},{5,1},{9,5},{13,9},{6,2},{10,6},{14,10},{7,3},{... | collective-permute-start | bytes 1179656 | tf_op jit(solution)/shard_map/ppermute | solution.py:19
  28.4 0.7 %reshape.10 = f32[2,4,4,4,8]{4,3,2,1,0:T(4,128)} reshape(f32[2,16,32]{2,1,0:T(8,128)S(1)} %get-tuple-element.17) | data formatting | bytes 8192 | tf_op jit(solution)/shard_map/reshape | solution.py:339
  29.2 0.8 %copy.11 = f32[2,4,4,4,8]{4,3,1,2,0:T(4,128)S(1)} copy(f32[2,4,4,4,8]{4,3,2,1,0:T(4,128)} %reshape.10) | data formatting | bytes 8192 | tf_op jit(solution)/shard_map/reshape | solution.py:339
  30.0 0.6 %copy.12 = f32[16,2,4,8]{3,2,1,0:T(4,128)} copy(f32[16,2,4,8]{3,0,2,1:T(8,128)S(1)} %bitcast.3) | data formatting | bytes 8192 | tf_op jit(solution)/shard_map/reshape | solution.py:340
  30.7 8.9 %all-to-all-start = ((f32[16,2,4,8]{3,2,1,0:T(4,128)}), f32[16,2,4,8]{3,2,1,0:T(4,128)}, u32[]{:S(2)}, u32[]{:S(2)}) async-start(f32[16,2,4,8]{3,2,1,0:T(4,128)} %copy.12), calls=%async_computation | async-start | bytes 131072 | tf_op jit(solution)/shard_map/all_to_all | solution.py:341
  39.6 0.0 collective-permute-done.other_ref
  39.6 0.8 %subtract_middle.1.begun_ref = f32[1,2,12,16,768]{4,3,2,1,0:T(8,128)} custom-call(f32[1,2,12,16,768]{4,3,2,1,0:T(8,128)S(1)} %copy-done.1, f32[2,4,16,768]{3,2,1,0:T(8,128)S(1)} %collective-permute-done.other_ref), custom_call_target="tpu_custom_call" | custom-call | flops 98304 | bytes 1179648 | tf_op jit(solution)/shard_map/subtract_middle/pallas_call | solution.py:345
  40.4 5.9 %all-to-all-done = f32[16,2,4,8]{3,2,1,0:T(4,128)} async-done(((f32[16,2,4,8]{3,2,1,0:T(4,128)}), f32[16,2,4,8]{3,2,1,0:T(4,128)}, u32[]{:S(2)}, u32[]{:S(2)}) %all-to-all-start) | async-done | bytes 4128 | tf_op jit(solution)/shard_map/all_to_all | solution.py:341
  46.3 1.5 %reduce_sum.9 = f32[2,4,8]{2,1,0:T(4,128)} reduce(f32[16,2,4,8]{3,2,1,0:T(4,128)} %all-to-all-done, f32[]{:T(128)} %constant.0.clone.1), dimensions={0}, to_apply=%region_0.0 | reduce | flops 960 | bytes 4356 | tf_op jit(solution)/shard_map/reduce_sum | solution.py:341
  47.7 0.0 collective-permute-done.3.other_ref
  47.7 1.1 %subtract_ends.1 = f32[1,2,12,16,768]{4,3,2,1,0:T(8,128)} custom-call(f32[1,2,12,16,768]{4,3,2,1,0:T(8,128)} %subtract_middle.1.begun_ref, f32[1,2,12,16,768]{4,3,2,1,0:T(8,128)S(1)} %copy-done.1, f32[2,8,16,768]{3,2,1,0:T(8,128)S(1)} %collective-permute-done.3.other_ref), custom_call_target="tpu_custom_call", output_to_operand_aliasing={{}: (0, {})} | custom-call | flops 196608 | bytes 2359296 | tf_op jit(solution)/shard_map/subtract_ends/pallas_call | solution.py:355
  (15 shorter events, 0.0 us)
Async XLA Ops:
  0.6 1.3 %copy-start = (f32[1,2,12,16,768]{4,3,2,1,0:T(8,128)S(1)}, f32[1,2,12,16,768]{4,3,2,1,0:T(8,128)}, u32[]{:S(2)}) copy-start(f32[1,2,12,16,768]{4,3,2,1,0:T(8,128)} %state_ref.7) | copy-start | bytes 3538948
  1.9 1.1 %copy-start.2 = (f32[1,12,16,768]{3,2,1,0:T(8,128)S(1)}, f32[1,12,16,768]{3,2,1,0:T(8,128)}, u32[]{:S(2)}) copy-start(f32[1,12,16,768]{3,2,1,0:T(8,128)} %east_ref.5) | copy-start | bytes 1769476
  3.0 1.1 %copy-start.4 = (f32[1,12,16,768]{3,2,1,0:T(8,128)S(1)}, f32[1,12,16,768]{3,2,1,0:T(8,128)}, u32[]{:S(2)}) copy-start(f32[1,12,16,768]{3,2,1,0:T(8,128)} %north_ref.5) | copy-start | bytes 1769476
  4.0 8.4 %copy-start.1 = (f32[1,2,12,16,768]{4,3,2,1,0:T(8,128)S(1)}, f32[1,2,12,16,768]{4,3,2,1,0:T(8,128)}, u32[]{:S(2)}) copy-start(f32[1,2,12,16,768]{4,3,2,1,0:T(8,128)} %state_ref.7) | copy-start | bytes 3538948
  4.0 8.4 %copy-start.6 = (s32[4,2,2,12]{3,2,1,0:T(2,128)S(1)}, s32[4,2,2,12]{3,2,1,0:T(2,128)}, u32[]{:S(2)}) copy-start(s32[4,2,2,12]{3,2,1,0:T(2,128)} %offset_ref.1) | copy-start | bytes 2308
  4.0 8.4 %copy-start.7 = (f32[4,2,2,12]{3,2,1,0:T(2,128)S(1)}, f32[4,2,2,12]{3,2,1,0:T(2,128)}, u32[]{:S(2)}) copy-start(f32[4,2,2,12]{3,2,1,0:T(2,128)} %weight_ref.1) | copy-start | bytes 2308
  4.0 8.4 %copy-start.8 = (s32[2,2,12]{2,1,0:T(2,128)S(1)}, s32[2,2,12]{2,1,0:T(2,128)}, u32[]{:S(2)}) copy-start(s32[2,2,12]{2,1,0:T(2,128)} %cell_ref.1) | copy-start | bytes 580
  4.0 8.4 %copy-start.9 = (s32[32]{0:T(128)S(1)}, s32[32]{0:T(128)}, u32[]{:S(2)}) copy-start(s32[32]{0:T(128)} %owner_ref.1) | copy-start | bytes 388
  5.4 17.2 %collective-permute-start.2 = (f32[11,16,768]{2,1,0:T(8,128)S(1)}, f32[11,16,768]{2,1,0:T(8,128)S(1)}, u32[]{:S(2)}, u32[]{:S(2)}) collective-permute-start(f32[11,16,768]{2,1,0:T(8,128)S(1)} %get-tuple-element.11.low_ref), channel_id=1, source_target_pairs={{1,0},{2,1},{3,2},{5,4},{6,5},{7,6},{9,8},{10,9},{11,10},{13,12},{... | collective-permute-start | bytes 1622024 | tf_op jit(solution)/shard_map/ppermute | solution.py:19
  6.7 17.2 %copy-start.3 = (f32[1,12,16,768]{3,2,1,0:T(8,128)S(1)}, f32[1,12,16,768]{3,2,1,0:T(8,128)}, u32[]{:S(2)}) copy-start(f32[1,12,16,768]{3,2,1,0:T(8,128)} %east_ref.5) | copy-start | bytes 1769476
  6.7 17.2 %copy-start.5 = (f32[1,12,16,768]{3,2,1,0:T(8,128)S(1)}, f32[1,12,16,768]{3,2,1,0:T(8,128)}, u32[]{:S(2)}) copy-start(f32[1,12,16,768]{3,2,1,0:T(8,128)} %north_ref.5) | copy-start | bytes 1769476
  6.7 17.2 %collective-permute-start.1 = (f32[11,16,768]{2,1,0:T(8,128)S(1)}, f32[11,16,768]{2,1,0:T(8,128)S(1)}, u32[]{:S(2)}, u32[]{:S(2)}) collective-permute-start(f32[11,16,768]{2,1,0:T(8,128)S(1)} %get-tuple-element.12.high_ref), channel_id=1, source_target_pairs={{0,1},{1,2},{2,3},{4,5},{5,6},{6,7},{8,9},{9,10},{10,11},{12,13},{... | collective-permute-start | bytes 1622024 | tf_op jit(solution)/shard_map/ppermute | solution.py:19
  25.8 21.9 %collective-permute-start.3 = (f32[2,8,16,768]{3,2,1,0:T(8,128)S(1)}, f32[2,8,16,768]{3,2,1,0:T(8,128)S(1)}, u32[]{:S(2)}, u32[]{:S(2)}) collective-permute-start(f32[2,8,16,768]{3,2,1,0:T(8,128)S(1)} %get-tuple-element.16), channel_id=1, source_target_pairs={{4,0},{8,4},{12,8},{5,1},{9,5},{13,9},{6,2},{10,6},{14,10},{7,3},{... | collective-permute-start | bytes 2359304 | tf_op jit(solution)/shard_map/ppermute | solution.py:19
  27.1 12.5 %collective-permute-start = (f32[2,4,16,768]{3,2,1,0:T(8,128)S(1)}, f32[2,4,16,768]{3,2,1,0:T(8,128)S(1)}, u32[]{:S(2)}, u32[]{:S(2)}) collective-permute-start(f32[2,4,16,768]{3,2,1,0:T(8,128)S(1)} %get-tuple-element.10), channel_id=1, source_target_pairs={{4,0},{8,4},{12,8},{5,1},{9,5},{13,9},{6,2},{10,6},{14,10},{7,3},{... | collective-permute-start | bytes 1179656 | tf_op jit(solution)/shard_map/ppermute | solution.py:19
  30.7 15.6 %all-to-all-start = ((f32[16,2,4,8]{3,2,1,0:T(4,128)}), f32[16,2,4,8]{3,2,1,0:T(4,128)}, u32[]{:S(2)}, u32[]{:S(2)}) async-start(f32[16,2,4,8]{3,2,1,0:T(4,128)} %copy.12), calls=%async_computation | async-start | bytes 131072 | tf_op jit(solution)/shard_map/all_to_all | solution.py:341

commit v2 on v0

v2 whole, which is shorter than its diff:
```python
import functools

import jax
import jax.numpy as jnp
from jax import lax
from jax.experimental import pallas as pl
from jax.experimental.pallas import tpu as pltpu
from jax.sharding import PartitionSpec as P

STEPS = 4
HALF = 8
FLUX_ROWS = 2 * STEPS
PACK_ROWS = FLUX_ROWS + 3
LANES = 128


def along(value, axis, step_of):
    peers = lax.axis_size(axis)
    pairs = [(i, i + step_of) for i in range(peers) if 0 <= i + step_of < peers]
    return lax.ppermute(value, axis, pairs)


def alternating(value, sign):
    subs, hors = lax.axis_size("sub"), lax.axis_size("hor")
    pairs = []
    for s in range(subs):
        step = sign if s % 2 == 0 else -sign
        pairs += [(s * hors + h, s * hors + h + step) for h in range(hors) if 0 <= h + step < hors]
    return lax.ppermute(value, ("sub", "hor"), pairs)


def parity():
    return lax.rem(lax.axis_index("sub"), 2)


def sign_of(flip):
    return jnp.where(flip == 1, jnp.float32(-1.0), jnp.float32(1.0))


def north_rates(north_rate):
    width = north_rate.shape[-1]
    column = lax.broadcasted_iota(jnp.int32, north_rate.shape, len(north_rate.shape) - 1)
    plus = jnp.where(column == 0, 0.0, jnp.maximum(north_rate, 0.0))
    minus = jnp.where(column == width - 1, 0.0, jnp.maximum(-north_rate, 0.0))
    return plus, minus


def shifted(flux_plus, flux_minus):
    width = flux_plus.shape[-1]
    axis = len(flux_plus.shape) - 1
    return pltpu.roll(flux_plus, width - 1, axis) + pltpu.roll(flux_minus, 1, axis)


class Row:
    def __init__(self, east_rate, north_rate=None):
        self.outward = jnp.maximum(east_rate, 0.0)
        self.inward = jnp.maximum(-east_rate, 0.0)
        if north_rate is not None:
            self.centre = 1.0 - jnp.abs(east_rate) - jnp.abs(north_rate)
            self.plus, self.minus = north_rates(north_rate)

    def stay(self, value):
        return self.centre * value + shifted(self.plus * value, self.minus * value)


def level_halves(levels, body):
    def step(h, carry):
        body(pl.ds(pl.multiple_of(h * HALF, HALF), HALF))
        return carry

    lax.fori_loop(0, levels // HALF, step, 0)


def first_kernel(
    state_hbm, east_hbm, north_hbm, pack_ref, state_ref, east_ref, north_ref, early_sems, late_sems
):
    parts, rows, levels = state_ref.shape[1:4]
    flip = parity()
    sign = sign_of(flip)
    start = flip * (rows - STEPS)
    place = lambda r: start + r + flip * (STEPS - 1 - 2 * r)

    def copies(first_row, count, sems):
        at = pl.ds(first_row, count)
        made = [
            pltpu.make_async_copy(state_hbm.at[0, c, at], state_ref.at[0, c, at], sems.at[c])
            for c in range(parts)
        ]
        made.append(pltpu.make_async_copy(east_hbm.at[0, at], east_ref.at[0, at], sems.at[parts]))
        made.append(pltpu.make_async_copy(north_hbm.at[0, at], north_ref.at[0, at], sems.at[parts + 1]))
        return made

    early = copies(start, STEPS, early_sems)
    late = copies(STEPS * (1 - flip), rows - STEPS, late_sems)
    for copy in early + late:
        copy.start()
    for copy in early:
        copy.wait()

    def half(at):
        row = [
            Row(east_ref[0, place(r), at, :] * sign, north_ref[0, place(r), at, :])
            for r in range(STEPS)
        ]
        pack_ref[FLUX_ROWS, at, :] = east_ref[0, place(0), at, :]
        pack_ref[FLUX_ROWS + 1, at, :] = north_ref[0, place(0), at, :]
        pack_ref[FLUX_ROWS + 2, at, :] = east_ref[0, place(1), at, :]
        for c in range(parts):
            field = [state_ref[0, c, place(r), at, :] for r in range(STEPS)]
            for k in range(STEPS):
                pack_ref[2 * k + c, at, :] = row[0].outward * field[0]
                after = []
                for r in range(STEPS - 1 - k):
                    value = row[r].stay(field[r]) + row[r + 1].outward * field[r + 1]
                    if r > 0:
                        value = value + row[r - 1].inward * field[r - 1]
                    after.append(value)
                field = after

    level_halves(levels, half)
    for copy in late:
        copy.wait()


def sweep_kernel(
    cell_ref, offset_ref, weight_ref, owner_ref, state_ref, east_ref, north_ref,
    pack_ref, middle_ref, ends_ref, spread_ref, partial_ref,
    field, plus_ref, minus_ref, centre_ref, ghost_ref,
):
    parts, rows, levels, width = state_ref.shape[1:]
    slots = spread_ref.shape[-1]
    slot_ids = lax.broadcasted_iota(jnp.int32, (1, slots), 1)
    flip = 1 - parity()
    sign = sign_of(flip)
    end_row = flip * (rows - 1)
    next_row = end_row + 1 - 2 * flip

    def one_row(i, carry):
        for c in range(2):
            for s in range(2):
                total = jnp.zeros((1, slots), jnp.float32)
                for point in range(offset_ref.shape[0]):
                    slot = owner_ref[cell_ref[c, s, i] + offset_ref[point, c, s, i]]
                    total = total + jnp.where(slot_ids == slot, weight_ref[point, c, s, i], 0.0)
                spread_ref[c, s, pl.ds(i, 1), :] = total
        return carry

    lax.fori_loop(0, rows, one_row, 0)

    def half(at):
        pack_ref[FLUX_ROWS, at, :] = east_ref[0, end_row, at, :]
        pack_ref[FLUX_ROWS + 1, at, :] = north_ref[0, end_row, at, :]
        pack_ref[FLUX_ROWS + 2, at, :] = east_ref[0, next_row, at, :]
        leaving = jnp.maximum(east_ref[0, end_row, at, :] * sign, 0.0)

        def coefficients(i, carry):
            east_rate = east_ref[0, i, at, :]
            north_rate = north_ref[0, i, at, :]
            centre_ref[i] = 1.0 - jnp.abs(east_rate) - jnp.abs(north_rate)
            plus_ref[i], minus_ref[i] = north_rates(north_rate)
            return carry

        lax.fori_loop(0, rows, coefficients, 0)

        for k in range(STEPS):
            if k == 0:
                read = lambda c, i: state_ref[0, c, i, at, :]
            else:
                read = lambda c, i, slot=(k - 1) % 2: field[slot, c, i]
            for c in range(parts):
                pack_ref[2 * k + c, at, :] = leaving * read(c, end_row)
            west = [None] * parts
            here = [read(c, 0) for c in range(parts)]
            for i in range(rows):
                east_here = east_ref[0, i, at, :]
                leave_west = jnp.maximum(-east_here, 0.0)
                if i + 1 < rows:
                    after = [read(c, i + 1) for c in range(parts)]
                    east_after = jnp.maximum(east_ref[0, i + 1, at, :], 0.0)
                centre, plus, minus = centre_ref[i], plus_ref[i], minus_ref[i]
                south_rate = jnp.maximum(north_ref[0, i, at, :LANES], 0.0)
                north_rate = jnp.maximum(-north_ref[0, i, at, width - LANES:], 0.0)
                for c in range(parts):
                    value = here[c]
                    south = south_rate * value[:, :LANES]
                    north = north_rate * value[:, width - LANES:]
                    if k == 0:
                        ghost_ref[c, 0, i] = south
                        ghost_ref[c, 1, i] = north
                    else:
                        ghost_ref[c, 0, i] += south
                        ghost_ref[c, 1, i] += north
                    total = centre * value + shifted(plus * value, minus * value)
                    if i + 1 < rows:
                        total = total + east_after * after[c]
                    if i > 0:
                        total = total + west[c]
                    west[c] = leave_west * value
                    if k < STEPS - 1:
                        field[k % 2, c, i] = total
                    elif i < STEPS:
                        ends_ref[c, i, at, :] = total
                    elif i >= rows - STEPS:
                        ends_ref[c, i - rows + 2 * STEPS, at, :] = total
                    else:
                        middle_ref[c, i - STEPS, at, :] = total
                here = after

        for c in range(parts):
            total = jnp.zeros((HALF, slots), jnp.float32)
            for s in range(2):
                lane = 0 if s == 0 else LANES - 1
                for i in range(rows):
                    total = total + ghost_ref[c, s, i, :, lane:lane + 1] * spread_ref[c, s, i:i + 1, :]
            partial_ref[c, at, :] = total

    level_halves(levels, half)


def mend_kernel(
    which, east_ref, north_ref, mine_ref, other_ref, ends_ref, spread_ref, partial_ref, out_ref, sum_ref
):
    parts, levels = sum_ref.shape[:2]
    rows = spread_ref.shape[2]
    width = east_ref.shape[-1]
    flip = 1 - parity() if which == 0 else parity()
    sign = sign_of(flip)
    turn = lambda r: r + flip * (STEPS - 1 - 2 * r)
    place = lambda r: flip * (rows - STEPS) + turn(r)

    def half(at):
        own = [Row(east_ref[0, place(r), at, :] * sign, north_ref[0, place(r), at, :]) for r in range(STEPS - 1)]
        near = Row(other_ref[FLUX_ROWS, at, :] * sign, other_ref[FLUX_ROWS + 1, at, :])
        far = Row(other_ref[FLUX_ROWS + 2, at, :] * sign)
        for c in range(parts):
            mine = lambda k: mine_ref[2 * k + c, at, :]
            theirs = lambda k: other_ref[2 * k + c, at, :]
            a0 = theirs(0)
            n1 = mine(0)
            b0 = own[0].stay(a0) + near.inward * n1 + theirs(1)
            b1 = own[0].inward * a0
            bn1 = near.stay(n1) + own[0].outward * a0 + mine(1)
            bn2 = near.outward * n1
            c0 = own[0].stay(b0) + near.inward * bn1 + own[1].outward * b1 + theirs(2)
            c1 = own[1].stay(b1) + own[0].inward * b0
            c2 = own[1].inward * b1
            cn1 = near.stay(bn1) + own[0].outward * b0 + far.inward * bn2 + mine(2)
            d0 = own[0].stay(c0) + near.inward * cn1 + own[1].outward * c1 + theirs(3)
            d1 = own[1].stay(c1) + own[0].inward * c0 + own[2].outward * c2
            d2 = own[2].stay(c2) + own[1].inward * c1
            d3 = own[2].inward * c2
            for r, value in enumerate((d0, d1, d2, d3)):
                out_ref[c, turn(r), at, :] = ends_ref[c, flip * STEPS + turn(r), at, :] + value
            total = partial_ref[c, at, :]
            for r, value in enumerate((a0 + b0 + c0, b1 + c1, c2)):
                i = place(r)
                rate = north_ref[0, i, at, :]
                south = jnp.maximum(rate[:, :1], 0.0) * value[:, :1]
                north = jnp.maximum(-rate[:, width - 1:], 0.0) * value[:, width - 1:]
                total = total + south * spread_ref[c, 0, pl.ds(i, 1), :]
                total = total + north * spread_ref[c, 1, pl.ds(i, 1), :]
            sum_ref[c, at, :] = total

    level_halves(levels, half)


def subtract_most(state_ref, middle_ref, side_ref, out_hbm, buffer, sems):
    parts, inner = middle_ref.shape[:2]
    rows = state_ref.shape[2]
    flip = parity()
    start = flip * (rows - STEPS)
    copies = []
    for c in range(parts):
        buffer[c, :inner] = state_ref[0, c, STEPS:STEPS + inner] - middle_ref[c]
        copies.append(
            pltpu.make_async_copy(buffer.at[c, pl.ds(0, inner)], out_hbm.at[0, c, pl.ds(STEPS, inner)], sems.at[2 * c])
        )
        copies[-1].start()
        for r in range(STEPS):
            buffer[c, inner + r] = state_ref[0, c, start + r] - side_ref[c, r]
        copies.append(
            pltpu.make_async_copy(
                buffer.at[c, pl.ds(inner, STEPS)], out_hbm.at[0, c, pl.ds(start, STEPS)], sems.at[2 * c + 1]
            )
        )
        copies[-1].start()
    for copy in copies:
        copy.wait()


def subtract_last(begun_hbm, state_ref, side_ref, out_hbm, buffer, sems):
    parts = side_ref.shape[0]
    rows = state_ref.shape[2]
    start = (1 - parity()) * (rows - STEPS)
    copies = []
    for c in range(parts):
        for r in range(STEPS):
            buffer[c, r] = state_ref[0, c, start + r] - side_ref[c, r]
        copies.append(pltpu.make_async_copy(buffer.at[c], out_hbm.at[0, c, pl.ds(start, STEPS)], sems.at[c]))
        copies[-1].start()
    for copy in copies:
        copy.wait()


def cost(flops, moved):
    return pl.CostEstimate(flops=flops, bytes_accessed=moved, transcendentals=0)


PARAMS = pltpu.CompilerParams(vmem_limit_bytes=24 * 1024 * 1024)


def local(
    adjoint_state,
    courant_east,
    courant_north,
    parent_cell,
    stencil_offset,
    stencil_weight,
    owner_slot,
):
    _, parts, rows, levels, width = adjoint_state.shape
    slots = owner_slot.shape[0]
    inner = rows - 2 * STEPS
    row_bytes = levels * width * 4
    f32 = lambda *shape: jax.ShapeDtypeStruct(shape, jnp.float32)
    vmem = pl.BlockSpec(memory_space=pltpu.VMEM)
    smem = pl.BlockSpec(memory_space=pltpu.SMEM)
    hbm = pl.BlockSpec(memory_space=pltpu.HBM)
    in_hbm = lambda value: pltpu.with_memory_space_constraint(value, pltpu.HBM)

    first_pack, state, east, north = pl.pallas_call(
        first_kernel,
        in_specs=[hbm] * 3,
        out_specs=[vmem] * 4,
        out_shape=[
            f32(PACK_ROWS, levels, width),
            f32(*adjoint_state.shape), f32(*courant_east.shape), f32(*courant_north.shape),
        ],
        scratch_shapes=[pltpu.SemaphoreType.DMA((parts + 2,)), pltpu.SemaphoreType.DMA((parts + 2,))],
        compiler_params=PARAMS,
        cost_estimate=cost(12 * levels * width * 13, 48 * row_bytes),
        name="first_pack",
    )(in_hbm(adjoint_state), in_hbm(courant_east), in_hbm(courant_north))
    first_came = alternating(first_pack, -1)

    second_pack, middle, ends, spread, partial = pl.pallas_call(
        sweep_kernel,
        in_specs=[smem] * 4 + [vmem] * 3,
        out_specs=[vmem] * 5,
        out_shape=[
            f32(PACK_ROWS, levels, width),
            f32(parts, inner, levels, width),
            f32(parts, 2 * STEPS, levels, width),
            f32(parts, 2, rows, slots),
            f32(parts, levels, slots),
        ],
        scratch_shapes=[
            pltpu.VMEM((2, parts, rows, HALF, width), jnp.float32),
            pltpu.VMEM((rows, HALF, width), jnp.float32),
            pltpu.VMEM((rows, HALF, width), jnp.float32),
            pltpu.VMEM((rows, HALF, width), jnp.float32),
            pltpu.VMEM((parts, 2, rows, HALF, LANES), jnp.float32),
        ],
        compiler_params=PARAMS,
        cost_estimate=cost(8 * rows * levels * width * 13, 6 * rows * row_bytes),
        name="sweep",
    )(parent_cell, stencil_offset, stencil_weight, owner_slot, state, east, north)
    middle_came = along(middle, "sub", -1)
    second_came = alternating(second_pack, 1)

    def mend(which, mine, other, so_far):
        return pl.pallas_call(
            functools.partial(mend_kernel, which),
            in_specs=[vmem] * 7,
            out_specs=[vmem] * 2,
            out_shape=[f32(parts, STEPS, levels, width), f32(parts, levels, slots)],
            compiler_params=PARAMS,
            cost_estimate=cost(16 * levels * width * 13, 46 * row_bytes),
            name="mend_" + "ab"[which],
        )(east, north, mine, other, ends, spread, so_far)

    side_a, partial = mend(0, second_pack, first_came, partial)
    a_came = along(side_a, "sub", -1)
    side_b, partial = mend(1, first_pack, second_came, partial)
    b_came = along(side_b, "sub", -1)

    subs, hors = lax.axis_size("sub"), lax.axis_size("hor")
    gathered = lax.all_gather(partial, ("sub", "hor"))
    mine_part = lax.dynamic_slice(
        gathered,
        (0, 0, lax.axis_index("sub") * (levels // subs), lax.axis_index("hor") * (slots // hors)),
        (subs * hors, parts, levels // subs, slots // hors),
    )
    boundary_gradient = jnp.sum(mine_part, 0)

    begun = pl.pallas_call(
        subtract_most,
        in_specs=[vmem] * 3,
        out_specs=hbm,
        out_shape=f32(*adjoint_state.shape),
        scratch_shapes=[
            pltpu.VMEM((parts, inner + STEPS, levels, width), jnp.float32),
            pltpu.SemaphoreType.DMA((2 * parts,)),
        ],
        compiler_params=PARAMS,
        cost_estimate=cost(parts * 8 * levels * width, 48 * row_bytes),
        name="subtract_most",
    )(state, middle_came, a_came)
    adjoint_result = pl.pallas_call(
        subtract_last,
        in_specs=[hbm, vmem, vmem],
        out_specs=hbm,
        out_shape=f32(*adjoint_state.shape),
        input_output_aliases={0: 0},
        scratch_shapes=[
            pltpu.VMEM((parts, STEPS, levels, width), jnp.float32),
            pltpu.SemaphoreType.DMA((parts,)),
        ],
        compiler_params=PARAMS,
        cost_estimate=cost(parts * 4 * levels * width, 24 * row_bytes),
        name="subtract_last",
    )(begun, state, b_came)
    return (adjoint_result, boundary_gradient)


def solution(mesh):
    in_specs = (
        P(("ens", "sub"), None, "hor", None, None),
        P(("ens", "sub"), "hor", None, None),
        P(("ens", "sub"), "hor", None, None),
        P(None, None, "hor"),
        P(None, None, None, "hor"),
        P(None, None, None, "hor"),
        P(),
    )
    out_specs = (P(("ens", "sub"), None, "hor", None, None), P("ens", "sub", "hor"))
    return jax.shard_map(local, mesh=mesh, in_specs=in_specs, out_specs=out_specs, check_vma=False)
```

time: 89.1 us -> 63.1 us (0.71)
  blocking collectives: 21.8 us -> 37.1 us
  other arithmetic: 14.4 us -> 0.71 us
  waiting for transfers between devices: 16.2 us -> 3.3 us
  local copies, waits for them, and re-layouts: 10.7 us -> 0.02 us
  Pallas kernels: 0 us -> 10.2 us
  starting transfers between devices: 21 us -> 10.8 us
  matrix products: 1.79 us -> 0 us
  between operations: 2.48 us -> 0.8 us
    all_gather x0 -> x1, blocking collectives: none -> 37.1 us  [local(): gathered = lax.all_gather(partial, ('sub', 'hor'))]
    unnamed x2 -> x0, blocking collectives: 21.8 us -> none
    ppermute x9 -> x5, waiting for transfers between devices: 16.2 us -> 3.3 us  [the longest x2 3.3 us: alternating(): return lax.ppermute(value, ('sub', 'hor'), pairs)]
    ppermute x9 -> x5, starting transfers between devices: 21 us -> 10.8 us  [the longest x2 6.88 us: alternating(): return lax.ppermute(value, ('sub', 'hor'), pairs)]
    pallas_call x0 -> x6, Pallas kernels: none -> 10.2 us  [the longest x1 4.49 us: local(): pl.pallas_call(sweep_kernel, in_specs=[smem] * 4 + [vmem] * 3, out_specs=...]
    mul x12 -> x0, other arithmetic: 7.95 us -> none  [the longest x3 3.04 us: local(): flux_west = east_minus * adjoint]
    unnamed x45 -> x8, local copies, waits for them, and re-layouts: 6.28 us -> 0.02 us
    add x5 -> x0, other arithmetic: 3.81 us -> none  [the longest x2 2.06 us: local(): south_grad = south_grad + north_plus[:, :, 0] * adjoint[..., 0]]
  transfers between devices with their start and end apart: 9 -> 5, of which waited for: 6 -> 1; matrix products, arithmetic and copies ran while one was open for 16% -> 1% of each run, Pallas kernels for 0% -> 11%
where the time goes in v2:
time: 63.1 us; the launch traced here: 62.8 us
  blocking collectives  37.1 us (59%)
  starting transfers between devices  10.8 us (17%)
  Pallas kernels  10.2 us (16%)
  waiting for transfers between devices  3.3 us (5%)
  between operations  0.8 us (1%)
  other arithmetic  0.71 us (1%)
    all_gather x1, blocking collectives, local(): gathered = lax.all_gather(partial, ('sub', 'hor'))  37.1 us
    ppermute x2, starting transfers between devices, alternating(): return lax.ppermute(value, ('sub', 'hor'), pairs)  6.88 us
    pallas_call x1, Pallas kernels, local(): pl.pallas_call(sweep_kernel, in_specs=[smem] * 4 + [vmem] * 3, out_specs=...  4.49 us
    ppermute x3, starting transfers between devices, along(): return lax.ppermute(value, axis, pairs)  3.88 us
    ppermute x2, waiting for transfers between devices, alternating(): return lax.ppermute(value, ('sub', 'hor'), pairs)  3.3 us
    pallas_call x1, Pallas kernels, local(): pl.pallas_call(first_kernel, in_specs=[hbm] * 3, out_specs=[vmem] * 4, ou...  2.14 us
    pallas_call x2, Pallas kernels, mend(): pl.pallas_call(functools.partial(mend_kernel, which), in_specs=[vmem] * 7...  1.8 us
  transfers between devices with their start and end apart: 5, of which 1 were waited for; matrix products, arithmetic and copies ran while one was open for 1% of the time, Pallas kernels for 11%

profile of v2, /device:TPU:0, one launch (start us, length us, event | category | flops | bytes accessed | tf_op | source)
XLA Modules:
  0.0 62.8 jit_solution(15203411518008935048)
XLA Ops:
  0.6 0.0 copy-start.2
  0.6 0.0 copy-start
  0.7 0.0 copy-start.1
  0.7 0.0 copy-start.3
  0.7 2.1 %first_pack.1 = (f32[11,16,768]{2,1,0:T(8,128)S(1)}, f32[1,2,12,16,768]{4,3,2,1,0:T(8,128)S(1)}, f32[1,12,16,768]{3,2,1,0:T(8,128)S(1)}, f32[1,12,16,768]{3,2,1,0:T(8,128)S(1)}) custom-call(f32[1,2,12,16,768]{4,3,2,1,0:T(8,128)} %state_hbm.1, f32[1,12,16,768]{3,2,1,0:T(8,128)} %east_hbm.1, f32[1,12,16,768]{3,2,1,0:T(8,128)} %north_hbm.1), custom_call_target="tpu_custom_call" | custom-call | flops 1916928 | bytes 2359296 | tf_op jit(solution)/shard_map/first_pack/pallas_call | solution.py:331
  2.8 1.3 %collective-permute-start.1 = (f32[11,16,768]{2,1,0:T(8,128)S(1)}, f32[11,16,768]{2,1,0:T(8,128)S(1)}, u32[]{:S(2)}, u32[]{:S(2)}) collective-permute-start(f32[11,16,768]{2,1,0:T(8,128)S(1)} %get-tuple-element.20.mine_ref), channel_id=1, source_target_pairs={{1,0},{2,1},{3,2},{4,5},{5,6},{6,7},{9,8},{10,9},{11,10},{12,13},{... | collective-permute-start | bytes 1622024 | tf_op jit(solution)/shard_map/ppermute | solution.py:29
  4.1 0.0 copy-done.2
  4.1 0.0 copy-done
  4.2 4.5 %sweep.1 = (f32[11,16,768]{2,1,0:T(8,128)S(1)}, f32[2,4,16,768]{3,2,1,0:T(8,128)S(1)}, f32[2,8,16,768]{3,2,1,0:T(8,128)S(1)}, f32[2,2,12,32]{3,2,1,0:T(8,128)S(1)}, f32[2,16,32]{2,1,0:T(8,128)S(1)}) custom-call(s32[2,2,12]{2,1,0:T(2,128)S(1)} %copy-done.2, s32[4,2,2,12]{3,2,1,0:T(2,128)S(1)} %copy-done, f32[4,2,2,12]{3,2,1,0:T(2,128)S(1)} %copy-done.1, ...), custom_call_target="tpu_custom_call" | custom-call | flops 15335424 | bytes 3538944 | tf_op jit(solution)/shard_map/sweep/pallas_call | solution.py:346
  8.7 5.6 %collective-permute-start.3 = (f32[11,16,768]{2,1,0:T(8,128)S(1)}, f32[11,16,768]{2,1,0:T(8,128)S(1)}, u32[]{:S(2)}, u32[]{:S(2)}) collective-permute-start(f32[11,16,768]{2,1,0:T(8,128)S(1)} %get-tuple-element.19.mine_ref), channel_id=1, source_target_pairs={{0,1},{1,2},{2,3},{5,4},{6,5},{7,6},{8,9},{9,10},{10,11},{13,12},{... | collective-permute-start | bytes 1622024 | tf_op jit(solution)/shard_map/ppermute | solution.py:29
  14.3 1.3 %collective-permute-start = (f32[2,4,16,768]{3,2,1,0:T(8,128)S(1)}, f32[2,4,16,768]{3,2,1,0:T(8,128)S(1)}, u32[]{:S(2)}, u32[]{:S(2)}) collective-permute-start(f32[2,4,16,768]{3,2,1,0:T(8,128)S(1)} %get-tuple-element.18), channel_id=1, source_target_pairs={{4,0},{8,4},{12,8},{5,1},{9,5},{13,9},{6,2},{10,6},{14,10},{7,3},{... | collective-permute-start | bytes 1179656 | tf_op jit(solution)/shard_map/ppermute | solution.py:20
  15.6 0.0 collective-permute-done.1.other_ref
  15.6 0.9 %mend_a.1 = (f32[2,4,16,768]{3,2,1,0:T(8,128)S(1)}, f32[2,16,32]{2,1,0:T(8,128)S(1)}) custom-call(f32[1,12,16,768]{3,2,1,0:T(8,128)S(1)} %get-tuple-element.16.east_ref, f32[1,12,16,768]{3,2,1,0:T(8,128)S(1)} %get-tuple-element.17.north_ref, f32[11,16,768]{2,1,0:T(8,128)S(1)} %get-tuple-element.19.mine_ref, ...), custom_call_target="tpu_custom_call" | custom-call | flops 2555904 | bytes 2260992 | tf_op jit(solution)/shard_map/mend_a/pallas_call | solution.py:372
  16.5 1.3 %collective-permute-start.2 = (f32[2,4,16,768]{3,2,1,0:T(8,128)S(1)}, f32[2,4,16,768]{3,2,1,0:T(8,128)S(1)}, u32[]{:S(2)}, u32[]{:S(2)}) collective-permute-start(f32[2,4,16,768]{3,2,1,0:T(8,128)S(1)} %get-tuple-element.24), channel_id=1, source_target_pairs={{4,0},{8,4},{12,8},{5,1},{9,5},{13,9},{6,2},{10,6},{14,10},{7,3},{... | collective-permute-start | bytes 1179656 | tf_op jit(solution)/shard_map/ppermute | solution.py:20
  17.8 3.3 %collective-permute-done.3.other_ref = f32[11,16,768]{2,1,0:T(8,128)S(1)} collective-permute-done((f32[11,16,768]{2,1,0:T(8,128)S(1)}, f32[11,16,768]{2,1,0:T(8,128)S(1)}, u32[]{:S(2)}, u32[]{:S(2)}) %collective-permute-start.3) | collective-permute-done | bytes 540704 | tf_op jit(solution)/shard_map/ppermute | solution.py:29
  21.1 0.9 %mend_b.1 = (f32[2,4,16,768]{3,2,1,0:T(8,128)S(1)}, f32[2,16,32]{2,1,0:T(8,128)S(1)}) custom-call(f32[1,12,16,768]{3,2,1,0:T(8,128)S(1)} %get-tuple-element.16.east_ref, f32[1,12,16,768]{3,2,1,0:T(8,128)S(1)} %get-tuple-element.17.north_ref, f32[11,16,768]{2,1,0:T(8,128)S(1)} %get-tuple-element.20.mine_ref, ...), custom_call_target="tpu_custom_call" | custom-call | flops 2555904 | bytes 2260992 | tf_op jit(solution)/shard_map/mend_b/pallas_call | solution.py:372
  22.0 1.3 %collective-permute-start.4 = (f32[2,4,16,768]{3,2,1,0:T(8,128)S(1)}, f32[2,4,16,768]{3,2,1,0:T(8,128)S(1)}, u32[]{:S(2)}, u32[]{:S(2)}) collective-permute-start(f32[2,4,16,768]{3,2,1,0:T(8,128)S(1)} %get-tuple-element.26), channel_id=1, source_target_pairs={{4,0},{8,4},{12,8},{5,1},{9,5},{13,9},{6,2},{10,6},{14,10},{7,3},{... | collective-permute-start | bytes 1179656 | tf_op jit(solution)/shard_map/ppermute | solution.py:20
  23.3 37.1 %all-gather = f32[32,16,32]{2,1,0:T(8,128)S(1)} all-gather(f32[2,16,32]{2,1,0:T(8,128)S(1)} %get-tuple-element.27), channel_id=2, replica_groups=mesh['ens'=2,'sub'=4,'hor'=4] {'sub','hor'}, dimensions={0}, use_global_device_ids=true | all-gather | bytes 69632 | tf_op jit(solution)/shard_map/all_gather | solution.py:388
  60.4 0.7 %dynamic-slice_reduce_fusion = f32[2,4,8]{2,1,0:T(4,128)} fusion(f32[16,2,16,32]{3,2,1,0:T(8,128)S(1)} %bitcast.1, s32[]{:T(128)S(6)} %select_n.6, s32[]{:T(128)S(6)} %select_n.7), kind=kLoop, calls=%fused_computation | loop fusion | flops 960 | bytes 4360 | tf_op jit(solution)/shard_map/reduce_sum | solution.py:394
  61.1 0.0 collective-permute-done.middle_ref
  61.1 0.0 collective-permute-done.2.side_ref
  61.1 0.9 %subtract_most.1.begun_hbm = f32[1,2,12,16,768]{4,3,2,1,0:T(8,128)} custom-call(f32[1,2,12,16,768]{4,3,2,1,0:T(8,128)S(1)} %get-tuple-element.15.state_ref, f32[2,4,16,768]{3,2,1,0:T(8,128)S(1)} %collective-permute-done.middle_ref, f32[2,4,16,768]{3,2,1,0:T(8,128)S(1)} %collective-permute-done.2.side_ref), custom_call_target="tpu_custom_call" | custom-call | flops 196608 | bytes 2359296 | tf_op jit(solution)/shard_map/subtract_most/pallas_call | solution.py:396
  62.0 0.0 collective-permute-done.4.side_ref
  62.1 0.8 %subtract_last.1 = f32[1,2,12,16,768]{4,3,2,1,0:T(8,128)} custom-call(f32[1,2,12,16,768]{4,3,2,1,0:T(8,128)} %subtract_most.1.begun_hbm, f32[1,2,12,16,768]{4,3,2,1,0:T(8,128)S(1)} %get-tuple-element.15.state_ref, f32[2,4,16,768]{3,2,1,0:T(8,128)S(1)} %collective-permute-done.4.side_ref), custom_call_target="tpu_custom_call", output_to_operand_aliasing={{}: (0, {})} | custom-call | flops 98304 | bytes 1179648 | tf_op jit(solution)/shard_map/subtract_last/pallas_call | solution.py:409
  (2 shorter events, 0.0 us)
Async XLA Ops:
  0.6 3.5 %copy-start.2 = (s32[2,2,12]{2,1,0:T(2,128)S(1)}, s32[2,2,12]{2,1,0:T(2,128)}, u32[]{:S(2)}) copy-start(s32[2,2,12]{2,1,0:T(2,128)} %cell_ref.1) | copy-start | bytes 580
  0.6 3.5 %copy-start = (s32[4,2,2,12]{3,2,1,0:T(2,128)S(1)}, s32[4,2,2,12]{3,2,1,0:T(2,128)}, u32[]{:S(2)}) copy-start(s32[4,2,2,12]{3,2,1,0:T(2,128)} %offset_ref.1) | copy-start | bytes 2308
  0.7 3.5 %copy-start.1 = (f32[4,2,2,12]{3,2,1,0:T(2,128)S(1)}, f32[4,2,2,12]{3,2,1,0:T(2,128)}, u32[]{:S(2)}) copy-start(f32[4,2,2,12]{3,2,1,0:T(2,128)} %weight_ref.1) | copy-start | bytes 2308
  0.7 3.5 %copy-start.3 = (s32[32]{0:T(128)S(1)}, s32[32]{0:T(128)}, u32[]{:S(2)}) copy-start(s32[32]{0:T(128)} %owner_ref.1) | copy-start | bytes 388
  2.8 12.7 %collective-permute-start.1 = (f32[11,16,768]{2,1,0:T(8,128)S(1)}, f32[11,16,768]{2,1,0:T(8,128)S(1)}, u32[]{:S(2)}, u32[]{:S(2)}) collective-permute-start(f32[11,16,768]{2,1,0:T(8,128)S(1)} %get-tuple-element.20.mine_ref), channel_id=1, source_target_pairs={{1,0},{2,1},{3,2},{4,5},{5,6},{6,7},{9,8},{10,9},{11,10},{12,13},{... | collective-permute-start | bytes 1622024 | tf_op jit(solution)/shard_map/ppermute | solution.py:29
  8.7 12.4 %collective-permute-start.3 = (f32[11,16,768]{2,1,0:T(8,128)S(1)}, f32[11,16,768]{2,1,0:T(8,128)S(1)}, u32[]{:S(2)}, u32[]{:S(2)}) collective-permute-start(f32[11,16,768]{2,1,0:T(8,128)S(1)} %get-tuple-element.19.mine_ref), channel_id=1, source_target_pairs={{0,1},{1,2},{2,3},{5,4},{6,5},{7,6},{8,9},{9,10},{10,11},{13,12},{... | collective-permute-start | bytes 1622024 | tf_op jit(solution)/shard_map/ppermute | solution.py:29
  14.3 46.9 %collective-permute-start = (f32[2,4,16,768]{3,2,1,0:T(8,128)S(1)}, f32[2,4,16,768]{3,2,1,0:T(8,128)S(1)}, u32[]{:S(2)}, u32[]{:S(2)}) collective-permute-start(f32[2,4,16,768]{3,2,1,0:T(8,128)S(1)} %get-tuple-element.18), channel_id=1, source_target_pairs={{4,0},{8,4},{12,8},{5,1},{9,5},{13,9},{6,2},{10,6},{14,10},{7,3},{... | collective-permute-start | bytes 1179656 | tf_op jit(solution)/shard_map/ppermute | solution.py:20
  16.5 44.6 %collective-permute-start.2 = (f32[2,4,16,768]{3,2,1,0:T(8,128)S(1)}, f32[2,4,16,768]{3,2,1,0:T(8,128)S(1)}, u32[]{:S(2)}, u32[]{:S(2)}) collective-permute-start(f32[2,4,16,768]{3,2,1,0:T(8,128)S(1)} %get-tuple-element.24), channel_id=1, source_target_pairs={{4,0},{8,4},{12,8},{5,1},{9,5},{13,9},{6,2},{10,6},{14,10},{7,3},{... | collective-permute-start | bytes 1179656 | tf_op jit(solution)/shard_map/ppermute | solution.py:20
  22.0 40.1 %collective-permute-start.4 = (f32[2,4,16,768]{3,2,1,0:T(8,128)S(1)}, f32[2,4,16,768]{3,2,1,0:T(8,128)S(1)}, u32[]{:S(2)}, u32[]{:S(2)}) collective-permute-start(f32[2,4,16,768]{3,2,1,0:T(8,128)S(1)} %get-tuple-element.26), channel_id=1, source_target_pairs={{4,0},{8,4},{12,8},{5,1},{9,5},{13,9},{6,2},{10,6},{14,10},{7,3},{... | collective-permute-start | bytes 1179656 | tf_op jit(solution)/shard_map/ppermute | solution.py:20

commit v3 on v2

--- a/solution.py
+++ b/solution.py
@@ -71,42 +71,29 @@
     lax.fori_loop(0, levels // HALF, step, 0)
 
 
-def first_kernel(
-    state_hbm, east_hbm, north_hbm, pack_ref, state_ref, east_ref, north_ref, early_sems, late_sems
-):
-    parts, rows, levels = state_ref.shape[1:4]
+def first_kernel(state_hbm, east_hbm, north_hbm, pack_ref, state_ref, east_ref, north_ref, sems):
+    parts, rows, levels = state_hbm.shape[1:4]
     flip = parity()
     sign = sign_of(flip)
-    start = flip * (rows - STEPS)
-    place = lambda r: start + r + flip * (STEPS - 1 - 2 * r)
-
-    def copies(first_row, count, sems):
-        at = pl.ds(first_row, count)
-        made = [
-            pltpu.make_async_copy(state_hbm.at[0, c, at], state_ref.at[0, c, at], sems.at[c])
-            for c in range(parts)
-        ]
-        made.append(pltpu.make_async_copy(east_hbm.at[0, at], east_ref.at[0, at], sems.at[parts]))
-        made.append(pltpu.make_async_copy(north_hbm.at[0, at], north_ref.at[0, at], sems.at[parts + 1]))
-        return made
-
-    early = copies(start, STEPS, early_sems)
-    late = copies(STEPS * (1 - flip), rows - STEPS, late_sems)
-    for copy in early + late:
+    at_end = pl.ds(flip * (rows - STEPS), STEPS)
+    place = lambda r: r + flip * (STEPS - 1 - 2 * r)
+    copies = [
+        pltpu.make_async_copy(state_hbm.at[0, c, at_end], state_ref.at[c], sems.at[c]) for c in range(parts)
+    ]
+    copies.append(pltpu.make_async_copy(east_hbm.at[0, at_end], east_ref, sems.at[parts]))
+    copies.append(pltpu.make_async_copy(north_hbm.at[0, at_end], north_ref, sems.at[parts + 1]))
+    for copy in copies:
         copy.start()
-    for copy in early:
+    for copy in copies:
         copy.wait()
 
     def half(at):
-        row = [
-            Row(east_ref[0, place(r), at, :] * sign, north_ref[0, place(r), at, :])
-            for r in range(STEPS)
-        ]
-        pack_ref[FLUX_ROWS, at, :] = east_ref[0, place(0), at, :]
-        pack_ref[FLUX_ROWS + 1, at, :] = north_ref[0, place(0), at, :]
-        pack_ref[FLUX_ROWS + 2, at, :] = east_ref[0, place(1), at, :]
+        row = [Row(east_ref[place(r), at, :] * sign, north_ref[place(r), at, :]) for r in range(STEPS)]
+        pack_ref[FLUX_ROWS, at, :] = east_ref[place(0), at, :]
+        pack_ref[FLUX_ROWS + 1, at, :] = north_ref[place(0), at, :]
+        pack_ref[FLUX_ROWS + 2, at, :] = east_ref[place(1), at, :]
         for c in range(parts):
-            field = [state_ref[0, c, place(r), at, :] for r in range(STEPS)]
+            field = [state_ref[c, place(r), at, :] for r in range(STEPS)]
             for k in range(STEPS):
                 pack_ref[2 * k + c, at, :] = row[0].outward * field[0]
                 after = []
@@ -118,109 +105,120 @@
                 field = after
 
     level_halves(levels, half)
-    for copy in late:
-        copy.wait()
+
+
+def as_column(row):
+    count = row.shape[1]
+    here = lax.broadcasted_iota(jnp.int32, (count, count), 0)
+    there = lax.broadcasted_iota(jnp.int32, (count, count), 1)
+    return jnp.sum(jnp.where(here == there, row, 0), axis=1, keepdims=True)
 
 
 def sweep_kernel(
     cell_ref, offset_ref, weight_ref, owner_ref, state_ref, east_ref, north_ref,
     pack_ref, middle_ref, ends_ref, spread_ref, partial_ref,
-    field, plus_ref, minus_ref, centre_ref, ghost_ref,
+    field, to_east, to_west, plus_ref, minus_ref, centre_ref,
 ):
     parts, rows, levels, width = state_ref.shape[1:]
     slots = spread_ref.shape[-1]
-    slot_ids = lax.broadcasted_iota(jnp.int32, (1, slots), 1)
     flip = 1 - parity()
     sign = sign_of(flip)
     end_row = flip * (rows - 1)
     next_row = end_row + 1 - 2 * flip
 
-    def one_row(i, carry):
-        for c in range(2):
-            for s in range(2):
-                total = jnp.zeros((1, slots), jnp.float32)
-                for point in range(offset_ref.shape[0]):
-                    slot = owner_ref[cell_ref[c, s, i] + offset_ref[point, c, s, i]]
-                    total = total + jnp.where(slot_ids == slot, weight_ref[point, c, s, i], 0.0)
-                spread_ref[c, s, pl.ds(i, 1), :] = total
+    nothing = jnp.zeros((levels, width), jnp.float32)
+    for edge in (0, rows + 1):
+        to_east[edge] = nothing
+        to_west[edge] = nothing
+        for slot in range(STEPS):
+            for c in range(parts):
+                field[slot, c, edge] = nothing
+
+    def prepare(i, carry):
+        east_rate = east_ref[0, i]
+        north_rate = north_ref[0, i]
+        to_west[i + 1] = jnp.maximum(east_rate, 0.0)
+        to_east[i + 1] = jnp.maximum(-east_rate, 0.0)
+        centre_ref[i] = 1.0 - jnp.abs(east_rate) - jnp.abs(north_rate)
+        plus_ref[i], minus_ref[i] = north_rates(north_rate)
+        for c in range(parts):
+            field[0, c, i + 1] = state_ref[0, c, i]
         return carry
 
-    lax.fori_loop(0, rows, one_row, 0)
-
-    def half(at):
-        pack_ref[FLUX_ROWS, at, :] = east_ref[0, end_row, at, :]
-        pack_ref[FLUX_ROWS + 1, at, :] = north_ref[0, end_row, at, :]
-        pack_ref[FLUX_ROWS + 2, at, :] = east_ref[0, next_row, at, :]
-        leaving = jnp.maximum(east_ref[0, end_row, at, :] * sign, 0.0)
-
-        def coefficients(i, carry):
-            east_rate = east_ref[0, i, at, :]
-            north_rate = north_ref[0, i, at, :]
-            centre_ref[i] = 1.0 - jnp.abs(east_rate) - jnp.abs(north_rate)
-            plus_ref[i], minus_ref[i] = north_rates(north_rate)
-            return carry
-
-        lax.fori_loop(0, rows, coefficients, 0)
-
-        for k in range(STEPS):
-            if k == 0:
-                read = lambda c, i: state_ref[0, c, i, at, :]
-            else:
-                read = lambda c, i, slot=(k - 1) % 2: field[slot, c, i]
-            for c in range(parts):
-                pack_ref[2 * k + c, at, :] = leaving * read(c, end_row)
-            west = [None] * parts
-            here = [read(c, 0) for c in range(parts)]
-            for i in range(rows):
-                east_here = east_ref[0, i, at, :]
-                leave_west = jnp.maximum(-east_here, 0.0)
-                if i + 1 < rows:
-                    after = [read(c, i + 1) for c in range(parts)]
-                    east_after = jnp.maximum(east_ref[0, i + 1, at, :], 0.0)
-                centre, plus, minus = centre_ref[i], plus_ref[i], minus_ref[i]
-                south_rate = jnp.maximum(north_ref[0, i, at, :LANES], 0.0)
-                north_rate = jnp.maximum(-north_ref[0, i, at, width - LANES:], 0.0)
-                for c in range(parts):
-                    value = here[c]
-                    south = south_rate * value[:, :LANES]
-                    north = north_rate * value[:, width - LANES:]
-                    if k == 0:
-                        ghost_ref[c, 0, i] = south
-                        ghost_ref[c, 1, i] = north
-                    else:
-                        ghost_ref[c, 0, i] += south
-                        ghost_ref[c, 1, i] += north
-                    total = centre * value + shifted(plus * value, minus * value)
-                    if i + 1 < rows:
-                        total = total + east_after * after[c]
-                    if i > 0:
-                        total = total + west[c]
-                    west[c] = leave_west * value
-                    if k < STEPS - 1:
-                        field[k % 2, c, i] = total
-                    elif i < STEPS:
-                        ends_ref[c, i, at, :] = total
-                    elif i >= rows - STEPS:
-                        ends_ref[c, i - rows + 2 * STEPS, at, :] = total
-                    else:
-                        middle_ref[c, i - STEPS, at, :] = total
-                here = after
-
+    lax.fori_loop(0, rows, prepare, 0, unroll=2)
+
+    pack_ref[FLUX_ROWS] = east_ref[0, end_row]
+    pack_ref[FLUX_ROWS + 1] = north_ref[0, end_row]
+    pack_ref[FLUX_ROWS + 2] = east_ref[0, next_row]
+
+    def advance(k, i, c, at):
+        value = field[k, c, i + 1, at, :]
+        total = centre_ref[i, at, :] * value + shifted(plus_ref[i, at, :] * value, minus_ref[i, at, :] * value)
+        total = total + to_west[i + 2, at, :] * field[k, c, i + 2, at, :]
+        return total + to_east[i, at, :] * field[k, c, i, at, :]
+
+    halves = [pl.ds(h * HALF, HALF) for h in range(levels // HALF)]
+    for k in range(STEPS):
+        leaving = jnp.maximum(east_ref[0, end_row] * sign, 0.0)
         for c in range(parts):
-            total = jnp.zeros((HALF, slots), jnp.float32)
-            for s in range(2):
-                lane = 0 if s == 0 else LANES - 1
-                for i in range(rows):
-                    total = total + ghost_ref[c, s, i, :, lane:lane + 1] * spread_ref[c, s, i:i + 1, :]
-            partial_ref[c, at, :] = total
-
-    level_halves(levels, half)
+            pack_ref[2 * k + c] = leaving * field[k, c, end_row + 1]
+
+        if k < STEPS - 1:
+
+            def one_row(i, carry, k=k):
+                for at in halves:
+                    for c in range(parts):
+                        field[k + 1, c, i + 1, at, :] = advance(k, i, c, at)
+                return carry
+
+            lax.fori_loop(0, rows, one_row, 0, unroll=2)
+        else:
+
+            def end_rows(i, carry, k=k):
+                for at in halves:
+                    for c in range(parts):
+                        ends_ref[c, i, at, :] = advance(k, i, c, at)
+                        ends_ref[c, i + STEPS, at, :] = advance(k, i + rows - STEPS, c, at)
+                return carry
+
+            def middle_row(i, carry, k=k):
+                for at in halves:
+                    for c in range(parts):
+                        middle_ref[c, i, at, :] = advance(k, i + STEPS, c, at)
+                return carry
+
+            lax.fori_loop(0, STEPS, end_rows, 0)
+            lax.fori_loop(0, rows - 2 * STEPS, middle_row, 0, unroll=2)
+
+    here = lax.broadcasted_iota(jnp.int32, (slots, slots), 1)
+    placing = jnp.where(as_column(owner_ref[...]) == here, 1.0, 0.0)
+    cells = lax.broadcasted_iota(jnp.int32, (rows, slots), 1)
+    for c in range(parts):
+        for s in range(2):
+            mixing = jnp.zeros((rows, slots), jnp.float32)
+            for point in range(offset_ref.shape[0]):
+                target = as_column(cell_ref[c, s:s + 1, :] + offset_ref[point, c, s:s + 1, :])
+                mixing = mixing + jnp.where(target == cells, as_column(weight_ref[point, c, s:s + 1, :]), 0.0)
+            spread_ref[c, s] = jnp.dot(
+                mixing, placing, precision=lax.Precision.HIGHEST, preferred_element_type=jnp.float32
+            )
+
+    for c in range(parts):
+        total = jnp.zeros((levels, slots), jnp.float32)
+        for i in range(rows):
+            rate = north_ref[0, i]
+            iterates = [field[k, c, i + 1] for k in range(STEPS)]
+            first = sum(value[:, :1] for value in iterates)
+            last = sum(value[:, width - 1:] for value in iterates)
+            total = total + (jnp.maximum(rate[:, :1], 0.0) * first) * spread_ref[c, 0, i:i + 1, :]
+            total = total + (jnp.maximum(-rate[:, width - 1:], 0.0) * last) * spread_ref[c, 1, i:i + 1, :]
+        partial_ref[c] = total
 
 
 def mend_kernel(
     which, east_ref, north_ref, mine_ref, other_ref, ends_ref, spread_ref, partial_ref, out_ref, sum_ref
 ):
-    parts, levels = sum_ref.shape[:2]
+    parts, levels, slots = partial_ref.shape
     rows = spread_ref.shape[2]
     width = east_ref.shape[-1]
     flip = 1 - parity() if which == 0 else parity()
@@ -259,9 +257,26 @@
                 north = jnp.maximum(-rate[:, width - 1:], 0.0) * value[:, width - 1:]
                 total = total + south * spread_ref[c, 0, pl.ds(i, 1), :]
                 total = total + north * spread_ref[c, 1, pl.ds(i, 1), :]
-            sum_ref[c, at, :] = total
+            if which == 0:
+                sum_ref[c, at, :] = total
+            else:
+                share = sum_ref.shape[-1]
+                for p in range(slots // share):
+                    sum_ref[p, c, at, :] = total[:, p * share:(p + 1) * share]
 
     level_halves(levels, half)
+
+
+def join_hor(came_ref, out_ref):
+    subs, parts, share = out_ref.shape[:3]
+    total = jnp.sum(came_ref[...], 0)
+    for s in range(subs):
+        for c in range(parts):
+            out_ref[s, c] = total[c, s * share:(s + 1) * share]
+
+
+def join_sub(came_ref, out_ref):
+    out_ref[...] = jnp.sum(came_ref[...], 0)
 
 
 def subtract_most(state_ref, middle_ref, side_ref, out_hbm, buffer, sems):
@@ -328,24 +343,27 @@
     hbm = pl.BlockSpec(memory_space=pltpu.HBM)
     in_hbm = lambda value: pltpu.with_memory_space_constraint(value, pltpu.HBM)
 
-    first_pack, state, east, north = pl.pallas_call(
+    first_pack = pl.pallas_call(
         first_kernel,
         in_specs=[hbm] * 3,
-        out_specs=[vmem] * 4,
-        out_shape=[
-            f32(PACK_ROWS, levels, width),
-            f32(*adjoint_state.shape), f32(*courant_east.shape), f32(*courant_north.shape),
+        out_specs=vmem,
+        out_shape=f32(PACK_ROWS, levels, width),
+        scratch_shapes=[
+            pltpu.VMEM((parts, STEPS, levels, width), jnp.float32),
+            pltpu.VMEM((STEPS, levels, width), jnp.float32),
+            pltpu.VMEM((STEPS, levels, width), jnp.float32),
+            pltpu.SemaphoreType.DMA((parts + 2,)),
         ],
-        scratch_shapes=[pltpu.SemaphoreType.DMA((parts + 2,)), pltpu.SemaphoreType.DMA((parts + 2,))],
-        compiler_params=PARAMS,
-        cost_estimate=cost(12 * levels * width * 13, 48 * row_bytes),
+        compiler_params=PARAMS,
+        cost_estimate=cost(12 * levels * width * 13, 27 * row_bytes),
         name="first_pack",
     )(in_hbm(adjoint_state), in_hbm(courant_east), in_hbm(courant_north))
     first_came = alternating(first_pack, -1)
 
+    state, east, north = adjoint_state, courant_east, courant_north
     second_pack, middle, ends, spread, partial = pl.pallas_call(
         sweep_kernel,
-        in_specs=[smem] * 4 + [vmem] * 3,
+        in_specs=[vmem] * 7,
         out_specs=[vmem] * 5,
         out_shape=[
             f32(PACK_ROWS, levels, width),
@@ -355,25 +373,29 @@
             f32(parts, levels, slots),
         ],
         scratch_shapes=[
-            pltpu.VMEM((2, parts, rows, HALF, width), jnp.float32),
-            pltpu.VMEM((rows, HALF, width), jnp.float32),
-            pltpu.VMEM((rows, HALF, width), jnp.float32),
-            pltpu.VMEM((rows, HALF, width), jnp.float32),
-            pltpu.VMEM((parts, 2, rows, HALF, LANES), jnp.float32),
+            pltpu.VMEM((STEPS, parts, rows + 2, levels, width), jnp.float32),
+            pltpu.VMEM((rows + 2, levels, width), jnp.float32),
+            pltpu.VMEM((rows + 2, levels, width), jnp.float32),
+            pltpu.VMEM((rows, levels, width), jnp.float32),
+            pltpu.VMEM((rows, levels, width), jnp.float32),
+            pltpu.VMEM((rows, levels, width), jnp.float32),
         ],
         compiler_params=PARAMS,
         cost_estimate=cost(8 * rows * levels * width * 13, 6 * rows * row_bytes),
         name="sweep",
-    )(parent_cell, stencil_offset, stencil_weight, owner_slot, state, east, north)
+    )(parent_cell, stencil_offset, stencil_weight, owner_slot[None], state, east, north)
     middle_came = along(middle, "sub", -1)
     second_came = alternating(second_pack, 1)
 
+    subs, hors = lax.axis_size("sub"), lax.axis_size("hor")
+
     def mend(which, mine, other, so_far):
+        summed = f32(parts, levels, slots) if which == 0 else f32(hors, parts, levels, slots // hors)
         return pl.pallas_call(
             functools.partial(mend_kernel, which),
             in_specs=[vmem] * 7,
             out_specs=[vmem] * 2,
-            out_shape=[f32(parts, STEPS, levels, width), f32(parts, levels, slots)],
+            out_shape=[f32(parts, STEPS, levels, width), summed],
             compiler_params=PARAMS,
             cost_estimate=cost(16 * levels * width * 13, 46 * row_bytes),
             name="mend_" + "ab"[which],
@@ -381,17 +403,27 @@
 
     side_a, partial = mend(0, second_pack, first_came, partial)
     a_came = along(side_a, "sub", -1)
-    side_b, partial = mend(1, first_pack, second_came, partial)
+    side_b, pieces = mend(1, first_pack, second_came, partial)
     b_came = along(side_b, "sub", -1)
 
-    subs, hors = lax.axis_size("sub"), lax.axis_size("hor")
-    gathered = lax.all_gather(partial, ("sub", "hor"))
-    mine_part = lax.dynamic_slice(
-        gathered,
-        (0, 0, lax.axis_index("sub") * (levels // subs), lax.axis_index("hor") * (slots // hors)),
-        (subs * hors, parts, levels // subs, slots // hors),
-    )
-    boundary_gradient = jnp.sum(mine_part, 0)
+    pieces = lax.all_to_all(pieces, "hor", 0, 0, tiled=True)
+    pieces = pl.pallas_call(
+        join_hor,
+        in_specs=[vmem],
+        out_specs=vmem,
+        out_shape=f32(subs, parts, levels // subs, slots // hors),
+        compiler_params=PARAMS,
+        name="join_hor",
+    )(pieces)
+    pieces = lax.all_to_all(pieces, "sub", 0, 0, tiled=True)
+    boundary_gradient = pl.pallas_call(
+        join_sub,
+        in_specs=[vmem],
+        out_specs=vmem,
+        out_shape=f32(parts, levels // subs, slots // hors),
+        compiler_params=PARAMS,
+        name="join_sub",
+    )(pieces)
 
     begun = pl.pallas_call(
         subtract_most,

time: 63.1 us -> 47.3 us (0.75)
  blocking collectives: 37.1 us -> 18.7 us
  Pallas kernels: 10.2 us -> 11.9 us
  local copies, waits for them, and re-layouts: 0.02 us -> 0.86 us
    all_gather x1 -> x0, blocking collectives: 37.1 us -> none  [local(): gathered = lax.all_gather(partial, ('sub', 'hor'))]
    all_to_all x0 -> x2, blocking collectives: none -> 18.7 us  [the longest x1 11.6 us: local(): pieces = lax.all_to_all(pieces, 'hor', 0, 0, tiled=True)]
    pallas_call x2 -> x4, Pallas kernels: 6.63 us -> 7.68 us  [the longest x1 5.04 us: local(): pl.pallas_call(sweep_kernel, in_specs=[vmem] * 7, out_specs=[vmem] * 5, o...]
    pallas_call x2, Pallas kernels: 1.8 us -> 2.51 us  [mend(): pl.pallas_call(functools.partial(mend_kernel, which), in_specs=[vmem] * 7...]
    reduce_sum x1 -> x0, other arithmetic: 0.71 us -> none  [local(): boundary_gradient = jnp.sum(mine_part, 0)]
    all_to_all x0 -> x1, other arithmetic: none -> 0.66 us  [local(): pieces = lax.all_to_all(pieces, 'hor', 0, 0, tiled=True)]
  transfers between devices with their start and end apart: 5 -> 5, of which waited for: 1 -> 1; matrix products, arithmetic and copies ran while one was open for 1% -> 3% of each run, Pallas kernels for 11% -> 19%
where the time goes in v3:
time: 47.3 us; the launch traced here: 47 us
  blocking collectives  18.7 us (40%)
  Pallas kernels  11.9 us (25%)
  starting transfers between devices  10.7 us (23%)
  waiting for transfers between devices  3.31 us (7%)
  local copies, waits for them, and re-layouts  0.86 us (2%)
  between operations  0.84 us (2%)
  other arithmetic  0.66 us (1%)
    all_to_all x1, blocking collectives, local(): pieces = lax.all_to_all(pieces, 'hor', 0, 0, tiled=True)  11.6 us
    all_to_all x1, blocking collectives, local(): pieces = lax.all_to_all(pieces, 'sub', 0, 0, tiled=True)  7.05 us
    ppermute x2, starting transfers between devices, alternating(): return lax.ppermute(value, ('sub', 'hor'), pairs)  6.88 us
    pallas_call x1, Pallas kernels, local(): pl.pallas_call(sweep_kernel, in_specs=[vmem] * 7, out_specs=[vmem] * 5, o...  5.04 us
    ppermute x3, starting transfers between devices, along(): return lax.ppermute(value, axis, pairs)  3.86 us
    ppermute x2, waiting for transfers between devices, alternating(): return lax.ppermute(value, ('sub', 'hor'), pairs)  3.3 us
    pallas_call x2, Pallas kernels, mend(): pl.pallas_call(functools.partial(mend_kernel, which), in_specs=[vmem] * 7...  2.51 us
    pallas_call x1, Pallas kernels, local(): pl.pallas_call(first_kernel, in_specs=[hbm] * 3, out_specs=vmem, out_shap...  2.02 us
  transfers between devices with their start and end apart: 5, of which 1 were waited for; matrix products, arithmetic and copies ran while one was open for 3% of the time, Pallas kernels for 19%

profile of v3, /device:TPU:0, one launch (start us, length us, event | category | flops | bytes accessed | tf_op | source)
XLA Modules:
  0.0 47.0 jit_solution(504608958643126351)
XLA Ops:
  0.7 2.0 %first_pack.1.mine_ref = f32[11,16,768]{2,1,0:T(8,128)S(1)} custom-call(f32[1,2,12,16,768]{4,3,2,1,0:T(8,128)} %state_ref.5, f32[1,12,16,768]{3,2,1,0:T(8,128)} %east_ref.5, f32[1,12,16,768]{3,2,1,0:T(8,128)} %north_ref.5), custom_call_target="tpu_custom_call" | custom-call | flops 1916928 | bytes 1327104 | tf_op jit(solution)/shard_map/first_pack/pallas_call | solution.py:346
  2.7 1.3 %collective-permute-start.1 = (f32[11,16,768]{2,1,0:T(8,128)S(1)}, f32[11,16,768]{2,1,0:T(8,128)S(1)}, u32[]{:S(2)}, u32[]{:S(2)}) collective-permute-start(f32[11,16,768]{2,1,0:T(8,128)S(1)} %first_pack.1.mine_ref), channel_id=1, source_target_pairs={{1,0},{2,1},{3,2},{4,5},{5,6},{6,7},{9,8},{10,9},{11,10},{12,13},{... | collective-permute-start | bytes 1622024 | tf_op jit(solution)/shard_map/ppermute | solution.py:29
  4.1 5.0 %sweep.1 = (f32[11,16,768]{2,1,0:T(8,128)S(1)}, f32[2,4,16,768]{3,2,1,0:T(8,128)S(1)}, f32[2,8,16,768]{3,2,1,0:T(8,128)S(1)}, f32[2,2,12,32]{3,2,1,0:T(8,128)S(1)}, f32[2,16,32]{2,1,0:T(8,128)S(1)}) custom-call(s32[2,2,12]{2,1,0:T(2,128)S(1)} %copy-done.5, s32[4,2,2,12]{3,2,1,0:T(2,128)S(1)} %copy-done.3, f32[4,2,2,12]{3,2,1,0:T(2,128)S(1)} %copy-done.4, ...), custom_call_target="tpu_custom_call" | custom-call | flops 15335424 | bytes 3538944 | tf_op jit(solution)/shard_map/sweep/pallas_call | solution.py:364
  9.1 5.6 %collective-permute-start.3 = (f32[11,16,768]{2,1,0:T(8,128)S(1)}, f32[11,16,768]{2,1,0:T(8,128)S(1)}, u32[]{:S(2)}, u32[]{:S(2)}) collective-permute-start(f32[11,16,768]{2,1,0:T(8,128)S(1)} %get-tuple-element.12.mine_ref), channel_id=1, source_target_pairs={{0,1},{1,2},{2,3},{5,4},{6,5},{7,6},{8,9},{9,10},{10,11},{13,12},{... | collective-permute-start | bytes 1622024 | tf_op jit(solution)/shard_map/ppermute | solution.py:29
  14.7 1.3 %collective-permute-start = (f32[2,4,16,768]{3,2,1,0:T(8,128)S(1)}, f32[2,4,16,768]{3,2,1,0:T(8,128)S(1)}, u32[]{:S(2)}, u32[]{:S(2)}) collective-permute-start(f32[2,4,16,768]{3,2,1,0:T(8,128)S(1)} %get-tuple-element.11), channel_id=1, source_target_pairs={{4,0},{8,4},{12,8},{5,1},{9,5},{13,9},{6,2},{10,6},{14,10},{7,3},{... | collective-permute-start | bytes 1179656 | tf_op jit(solution)/shard_map/ppermute | solution.py:20
  16.0 0.0 collective-permute-done.1.other_ref
  16.0 0.9 %mend_a.1 = (f32[2,4,16,768]{3,2,1,0:T(8,128)S(1)}, f32[2,16,32]{2,1,0:T(8,128)S(1)}) custom-call(f32[1,12,16,768]{3,2,1,0:T(8,128)S(1)} %copy-done.1, f32[1,12,16,768]{3,2,1,0:T(8,128)S(1)} %copy-done.2, f32[11,16,768]{2,1,0:T(8,128)S(1)} %get-tuple-element.12.mine_ref, f32[11,16,768]{2,1,0:T(8,128)S(1)} %collective-permute-done.1.other_ref, ...), custom_call_target="tpu_custom_call" | custom-call | flops 2555904 | bytes 2260992 | tf_op jit(solution)/shard_map/mend_a/pallas_call | solution.py:394
  17.0 1.3 %collective-permute-start.2 = (f32[2,4,16,768]{3,2,1,0:T(8,128)S(1)}, f32[2,4,16,768]{3,2,1,0:T(8,128)S(1)}, u32[]{:S(2)}, u32[]{:S(2)}) collective-permute-start(f32[2,4,16,768]{3,2,1,0:T(8,128)S(1)} %get-tuple-element.16), channel_id=1, source_target_pairs={{4,0},{8,4},{12,8},{5,1},{9,5},{13,9},{6,2},{10,6},{14,10},{7,3},{... | collective-permute-start | bytes 1179656 | tf_op jit(solution)/shard_map/ppermute | solution.py:20
  18.3 3.3 %collective-permute-done.3.other_ref = f32[11,16,768]{2,1,0:T(8,128)S(1)} collective-permute-done((f32[11,16,768]{2,1,0:T(8,128)S(1)}, f32[11,16,768]{2,1,0:T(8,128)S(1)}, u32[]{:S(2)}, u32[]{:S(2)}) %collective-permute-start.3) | collective-permute-done | bytes 540704 | tf_op jit(solution)/shard_map/ppermute | solution.py:29
  21.6 1.6 %mend_b.1 = (f32[2,4,16,768]{3,2,1,0:T(8,128)}, f32[4,2,16,8]{3,2,1,0:T(8,128)S(1)}) custom-call(f32[1,12,16,768]{3,2,1,0:T(8,128)S(1)} %copy-done.1, f32[1,12,16,768]{3,2,1,0:T(8,128)S(1)} %copy-done.2, f32[11,16,768]{2,1,0:T(8,128)S(1)} %first_pack.1.mine_ref, f32[11,16,768]{2,1,0:T(8,128)S(1)} %collective-permute-done.3.other_ref, ...), custom_call_target="tpu_custom_call" | custom-call | flops 2555904 | bytes 2260992 | tf_op jit(solution)/shard_map/mend_b/pallas_call | solution.py:394
  23.2 1.3 %collective-permute-start.4 = (f32[2,4,16,768]{3,2,1,0:T(8,128)}, f32[2,4,16,768]{3,2,1,0:T(8,128)S(1)}, u32[]{:S(2)}, u32[]{:S(2)}) collective-permute-start(f32[2,4,16,768]{3,2,1,0:T(8,128)} %get-tuple-element.18), channel_id=1, source_target_pairs={{4,0},{8,4},{12,8},{5,1},{9,5},{13,9},{6,2},{10,6},{14,10},{7,3},{... | collective-permute-start | bytes 1179656 | tf_op jit(solution)/shard_map/ppermute | solution.py:20
  24.5 0.1 copy.10
  24.5 0.1 reshape.4
  24.6 11.6 %all_to_all.10 = f32[4,1,256]{2,1,0:T(1,128)S(1)} all-to-all(f32[4,1,256]{2,1,0:T(1,128)S(1)} %reshape.4), channel_id=1, replica_groups=mesh['ens'=2,'sub'=4,'hor'=4] {'hor'}, dimensions={0} | all-to-all | bytes 8192 | tf_op jit(solution)/shard_map/all_to_all | solution.py:409
  36.2 0.5 %broadcast = f32[]{:T(128)} broadcast(f32[]{:T(128)} %constant.3), dimensions={} | broadcast | bytes 8 | tf_op jit(solution)/shard_map/all_to_all | solution.py:409
  36.7 0.7 %reduce = f32[4,256]{1,0:T(4,128)S(1)} reduce(f32[4,1,256]{2,1,0:T(1,128)S(1)} %all_to_all.10, f32[]{:T(128)} %broadcast), dimensions={1}, to_apply=%all_to_all.6.reduce_sub_computation | reduce | bytes 8196 | tf_op jit(solution)/shard_map/all_to_all | solution.py:409
  37.4 0.1 reshape.5
  37.5 0.1 copy.11.came_ref
  37.6 7.0 %all_to_all.11.came_ref = f32[4,2,4,8]{3,2,1,0:T(4,128)S(1)} all-to-all(f32[4,2,4,8]{3,2,1,0:T(4,128)S(1)} %join_hor.1), channel_id=1, replica_groups=mesh['ens'=2,'sub'=4,'hor'=4] {'sub'}, dimensions={0} | all-to-all | bytes 2048 | tf_op jit(solution)/shard_map/all_to_all | solution.py:418
  44.6 0.6 %join_sub.1 = f32[2,4,8]{2,1,0:T(4,128)} custom-call(f32[4,2,4,8]{3,2,1,0:T(4,128)S(1)} %all_to_all.11.came_ref), custom_call_target="tpu_custom_call" | custom-call | tf_op jit(solution)/shard_map/join_sub/pallas_call | solution.py:419
  45.2 0.0 collective-permute-done.middle_ref
  45.2 0.9 %subtract_most.1.begun_hbm = f32[1,2,12,16,768]{4,3,2,1,0:T(8,128)} custom-call(f32[1,2,12,16,768]{4,3,2,1,0:T(8,128)S(1)} %copy-done, f32[2,4,16,768]{3,2,1,0:T(8,128)S(1)} %collective-permute-done.middle_ref, f32[2,4,16,768]{3,2,1,0:T(8,128)S(1)} %collective-permute-done.2.side_ref), custom_call_target="tpu_custom_call" | custom-call | flops 196608 | bytes 2359296 | tf_op jit(solution)/shard_map/subtract_most/pallas_call | solution.py:428
  46.2 0.0 collective-permute-done.4.side_ref
  46.2 0.8 %subtract_last.1 = f32[1,2,12,16,768]{4,3,2,1,0:T(8,128)} custom-call(f32[1,2,12,16,768]{4,3,2,1,0:T(8,128)} %subtract_most.1.begun_hbm, f32[1,2,12,16,768]{4,3,2,1,0:T(8,128)S(1)} %copy-done, f32[2,4,16,768]{3,2,1,0:T(8,128)S(1)} %collective-permute-done.4.side_ref), custom_call_target="tpu_custom_call", output_to_operand_aliasing={{}: (0, {})} | custom-call | flops 98304 | bytes 1179648 | tf_op jit(solution)/shard_map/subtract_last/pallas_call | solution.py:441
  (16 shorter events, 0.1 us)
Async XLA Ops:
  0.6 3.4 %copy-start = (f32[1,2,12,16,768]{4,3,2,1,0:T(8,128)S(1)}, f32[1,2,12,16,768]{4,3,2,1,0:T(8,128)}, u32[]{:S(2)}) copy-start(f32[1,2,12,16,768]{4,3,2,1,0:T(8,128)} %state_ref.5) | copy-start | bytes 3538948
  0.6 3.4 %copy-start.1 = (f32[1,12,16,768]{3,2,1,0:T(8,128)S(1)}, f32[1,12,16,768]{3,2,1,0:T(8,128)}, u32[]{:S(2)}) copy-start(f32[1,12,16,768]{3,2,1,0:T(8,128)} %east_ref.5) | copy-start | bytes 1769476
  0.7 3.4 %copy-start.2 = (f32[1,12,16,768]{3,2,1,0:T(8,128)S(1)}, f32[1,12,16,768]{3,2,1,0:T(8,128)}, u32[]{:S(2)}) copy-start(f32[1,12,16,768]{3,2,1,0:T(8,128)} %north_ref.5) | copy-start | bytes 1769476
  0.7 3.4 %copy-start.6 = (s32[32]{0:T(128)S(1)}, s32[32]{0:T(128)}, u32[]{:S(2)}) copy-start(s32[32]{0:T(128)} %param.13) | copy-start | bytes 388
  0.7 3.4 %copy-start.5 = (s32[2,2,12]{2,1,0:T(2,128)S(1)}, s32[2,2,12]{2,1,0:T(2,128)}, u32[]{:S(2)}) copy-start(s32[2,2,12]{2,1,0:T(2,128)} %cell_ref.1) | copy-start | bytes 580
  0.7 3.4 %copy-start.3 = (s32[4,2,2,12]{3,2,1,0:T(2,128)S(1)}, s32[4,2,2,12]{3,2,1,0:T(2,128)}, u32[]{:S(2)}) copy-start(s32[4,2,2,12]{3,2,1,0:T(2,128)} %offset_ref.1) | copy-start | bytes 2308
  0.7 3.4 %copy-start.4 = (f32[4,2,2,12]{3,2,1,0:T(2,128)S(1)}, f32[4,2,2,12]{3,2,1,0:T(2,128)}, u32[]{:S(2)}) copy-start(f32[4,2,2,12]{3,2,1,0:T(2,128)} %weight_ref.1) | copy-start | bytes 2308
  2.7 13.3 %collective-permute-start.1 = (f32[11,16,768]{2,1,0:T(8,128)S(1)}, f32[11,16,768]{2,1,0:T(8,128)S(1)}, u32[]{:S(2)}, u32[]{:S(2)}) collective-permute-start(f32[11,16,768]{2,1,0:T(8,128)S(1)} %first_pack.1.mine_ref), channel_id=1, source_target_pairs={{1,0},{2,1},{3,2},{4,5},{5,6},{6,7},{9,8},{10,9},{11,10},{12,13},{... | collective-permute-start | bytes 1622024 | tf_op jit(solution)/shard_map/ppermute | solution.py:29
  9.1 12.4 %collective-permute-start.3 = (f32[11,16,768]{2,1,0:T(8,128)S(1)}, f32[11,16,768]{2,1,0:T(8,128)S(1)}, u32[]{:S(2)}, u32[]{:S(2)}) collective-permute-start(f32[11,16,768]{2,1,0:T(8,128)S(1)} %get-tuple-element.12.mine_ref), channel_id=1, source_target_pairs={{0,1},{1,2},{2,3},{5,4},{6,5},{7,6},{8,9},{9,10},{10,11},{13,12},{... | collective-permute-start | bytes 1622024 | tf_op jit(solution)/shard_map/ppermute | solution.py:29
  14.7 30.5 %collective-permute-start = (f32[2,4,16,768]{3,2,1,0:T(8,128)S(1)}, f32[2,4,16,768]{3,2,1,0:T(8,128)S(1)}, u32[]{:S(2)}, u32[]{:S(2)}) collective-permute-start(f32[2,4,16,768]{3,2,1,0:T(8,128)S(1)} %get-tuple-element.11), channel_id=1, source_target_pairs={{4,0},{8,4},{12,8},{5,1},{9,5},{13,9},{6,2},{10,6},{14,10},{7,3},{... | collective-permute-start | bytes 1179656 | tf_op jit(solution)/shard_map/ppermute | solution.py:20
  17.0 28.3 %collective-permute-start.2 = (f32[2,4,16,768]{3,2,1,0:T(8,128)S(1)}, f32[2,4,16,768]{3,2,1,0:T(8,128)S(1)}, u32[]{:S(2)}, u32[]{:S(2)}) collective-permute-start(f32[2,4,16,768]{3,2,1,0:T(8,128)S(1)} %get-tuple-element.16), channel_id=1, source_target_pairs={{4,0},{8,4},{12,8},{5,1},{9,5},{13,9},{6,2},{10,6},{14,10},{7,3},{... | collective-permute-start | bytes 1179656 | tf_op jit(solution)/shard_map/ppermute | solution.py:20
  23.2 23.0 %collective-permute-start.4 = (f32[2,4,16,768]{3,2,1,0:T(8,128)}, f32[2,4,16,768]{3,2,1,0:T(8,128)S(1)}, u32[]{:S(2)}, u32[]{:S(2)}) collective-permute-start(f32[2,4,16,768]{3,2,1,0:T(8,128)} %get-tuple-element.18), channel_id=1, source_target_pairs={{4,0},{8,4},{12,8},{5,1},{9,5},{13,9},{6,2},{10,6},{14,10},{7,3},{... | collective-permute-start | bytes 1179656 | tf_op jit(solution)/shard_map/ppermute | solution.py:20

commit v4 on v3

v4 whole, which is shorter than its diff:
```python
import functools

import jax
import jax.numpy as jnp
from jax import lax
from jax.experimental import pallas as pl
from jax.experimental.pallas import tpu as pltpu
from jax.sharding import PartitionSpec as P

STEPS = 4
HALF = 8
FLUX_ROWS = 2 * STEPS
PACK_ROWS = FLUX_ROWS + 3
LANES = 128


def along(value, axis, step_of):
    peers = lax.axis_size(axis)
    pairs = [(i, i + step_of) for i in range(peers) if 0 <= i + step_of < peers]
    return lax.ppermute(value, axis, pairs)


def alternating(value, sign):
    subs, hors = lax.axis_size("sub"), lax.axis_size("hor")
    pairs = []
    for s in range(subs):
        step = sign if s % 2 == 0 else -sign
        pairs += [(s * hors + h, s * hors + h + step) for h in range(hors) if 0 <= h + step < hors]
    return lax.ppermute(value, ("sub", "hor"), pairs)


def parity():
    return lax.rem(lax.axis_index("sub"), 2)


def sign_of(flip):
    return jnp.where(flip == 1, jnp.float32(-1.0), jnp.float32(1.0))


def north_rates(north_rate):
    width = north_rate.shape[-1]
    column = lax.broadcasted_iota(jnp.int32, north_rate.shape, len(north_rate.shape) - 1)
    plus = jnp.where(column == 0, 0.0, jnp.maximum(north_rate, 0.0))
    minus = jnp.where(column == width - 1, 0.0, jnp.maximum(-north_rate, 0.0))
    return plus, minus


def shifted(flux_plus, flux_minus):
    width = flux_plus.shape[-1]
    axis = len(flux_plus.shape) - 1
    return pltpu.roll(flux_plus, width - 1, axis) + pltpu.roll(flux_minus, 1, axis)


class Row:
    def __init__(self, east_rate, north_rate=None):
        self.outward = jnp.maximum(east_rate, 0.0)
        self.inward = jnp.maximum(-east_rate, 0.0)
        if north_rate is not None:
            self.centre = 1.0 - jnp.abs(east_rate) - jnp.abs(north_rate)
            self.plus, self.minus = north_rates(north_rate)

    def stay(self, value):
        return self.centre * value + shifted(self.plus * value, self.minus * value)


def level_halves(levels, body):
    def step(h, carry):
        body(pl.ds(pl.multiple_of(h * HALF, HALF), HALF))
        return carry

    lax.fori_loop(0, levels // HALF, step, 0)


def first_kernel(state_hbm, east_hbm, north_hbm, pack_ref, state_ref, east_ref, north_ref, sems):
    parts, rows, levels = state_hbm.shape[1:4]
    flip = parity()
    sign = sign_of(flip)
    at_end = pl.ds(flip * (rows - STEPS), STEPS)
    place = lambda r: r + flip * (STEPS - 1 - 2 * r)
    halves = levels // HALF
    copies = []
    for h in range(halves):
        at = pl.ds(h * HALF, HALF)
        sem = sems.at[h]
        batch = [
            pltpu.make_async_copy(state_hbm.at[0, c, at_end, at], state_ref.at[c, :, at], sem.at[c])
            for c in range(parts)
        ]
        batch.append(pltpu.make_async_copy(east_hbm.at[0, at_end, at], east_ref.at[:, at], sem.at[parts]))
        batch.append(pltpu.make_async_copy(north_hbm.at[0, at_end, at], north_ref.at[:, at], sem.at[parts + 1]))
        copies.append(batch)
        for copy in batch:
            copy.start()

    def half(at):
        row = [Row(east_ref[place(r), at, :] * sign, north_ref[place(r), at, :]) for r in range(STEPS)]
        pack_ref[FLUX_ROWS, at, :] = east_ref[place(0), at, :]
        pack_ref[FLUX_ROWS + 1, at, :] = north_ref[place(0), at, :]
        pack_ref[FLUX_ROWS + 2, at, :] = east_ref[place(1), at, :]
        for c in range(parts):
            field = [state_ref[c, place(r), at, :] for r in range(STEPS)]
            for k in range(STEPS):
                pack_ref[2 * k + c, at, :] = row[0].outward * field[0]
                after = []
                for r in range(STEPS - 1 - k):
                    value = row[r].stay(field[r]) + row[r + 1].outward * field[r + 1]
                    if r > 0:
                        value = value + row[r - 1].inward * field[r - 1]
                    after.append(value)
                field = after

    for h in range(halves):
        for copy in copies[h]:
            copy.wait()
        half(pl.ds(h * HALF, HALF))


def as_column(row):
    count = row.shape[1]
    here = lax.broadcasted_iota(jnp.int32, (count, count), 0)
    there = lax.broadcasted_iota(jnp.int32, (count, count), 1)
    return jnp.sum(jnp.where(here == there, row, 0), axis=1, keepdims=True)


def sweep_kernel(
    state_ref, east_ref, north_ref, pack_ref, middle_ref, ends_ref, column_ref,
    field, plus_ref, minus_ref, centre_ref,
):
    parts, rows, levels, width = state_ref.shape[1:]
    flip = 1 - parity()
    sign = sign_of(flip)
    end_row = flip * (rows - 1)
    next_row = end_row + 1 - 2 * flip

    def half(at):
        pack_ref[FLUX_ROWS, at, :] = east_ref[0, end_row, at, :]
        pack_ref[FLUX_ROWS + 1, at, :] = north_ref[0, end_row, at, :]
        pack_ref[FLUX_ROWS + 2, at, :] = east_ref[0, next_row, at, :]

        for k in range(STEPS):
            if k == 0:
                read = lambda c, i: state_ref[0, c, i, at, :]
            else:
                read = lambda c, i, slot=k - 1: field[slot, c, i]
            leaving = jnp.maximum(east_ref[0, end_row, at, :] * sign, 0.0)
            for c in range(parts):
                pack_ref[2 * k + c, at, :] = leaving * read(c, end_row)
            west = [None] * parts
            here = [read(c, 0) for c in range(parts)]
            east_here = east_ref[0, 0, at, :]
            for i in range(rows):
                leave_west = jnp.maximum(-east_here, 0.0)
                if k == 0:
                    north_rate = north_ref[0, i, at, :]
                    centre = 1.0 - jnp.abs(east_here) - jnp.abs(north_rate)
                    plus, minus = north_rates(north_rate)
                    centre_ref[i], plus_ref[i], minus_ref[i] = centre, plus, minus
                else:
                    centre, plus, minus = centre_ref[i], plus_ref[i], minus_ref[i]
                if i + 1 < rows:
                    east_here = east_ref[0, i + 1, at, :]
                    east_after = jnp.maximum(east_here, 0.0)
                for c in range(parts):
                    value = here[c]
                    total = centre * value + shifted(plus * value, minus * value)
                    if i > 0:
                        total = total + west[c]
                    if i + 1 < rows:
                        west[c] = leave_west * value
                        here[c] = read(c, i + 1)
                        total = total + east_after * here[c]
                    if k < STEPS - 1:
                        field[k, c, i] = total
                    elif i < STEPS:
                        ends_ref[c, i, at, :] = total
                    elif i >= rows - STEPS:
                        ends_ref[c, i - rows + 2 * STEPS, at, :] = total
                    else:
                        middle_ref[c, i - STEPS, at, :] = total

        def columns(i, carry):
            for c in range(parts):
                value = state_ref[0, c, i, at, :]
                first, last = value[:, :LANES], value[:, width - LANES:]
                for slot in range(STEPS - 1):
                    first = first + field[slot, c, i, :, :LANES]
                    last = last + field[slot, c, i, :, width - LANES:]
                column_ref[c, 0, i, at, :] = first
                column_ref[c, 1, i, at, :] = last
            return carry

        lax.fori_loop(0, rows, columns, 0, unroll=2)

    level_halves(levels, half)


def ghost_kernel(
    cell_ref, offset_ref, weight_ref, owner_ref, column_ref, north_hbm, spread_ref, partial_ref, first_rate, last_rate, sems
):
    parts, _, rows, levels, _ = column_ref.shape
    slots = spread_ref.shape[-1]
    width = north_hbm.shape[-1]
    copies = [
        pltpu.make_async_copy(north_hbm.at[0, :, :, pl.ds(0, LANES)], first_rate, sems.at[0]),
        pltpu.make_async_copy(north_hbm.at[0, :, :, pl.ds(width - LANES, LANES)], last_rate, sems.at[1]),
    ]
    for copy in copies:
        copy.start()

    here = lax.broadcasted_iota(jnp.int32, (slots, slots), 1)
    placing = jnp.where(as_column(owner_ref[...]) == here, 1.0, 0.0)
    cells = lax.broadcasted_iota(jnp.int32, (rows, slots), 1)
    for c in range(parts):
        for s in range(2):
            mixing = jnp.zeros((rows, slots), jnp.float32)
            for point in range(offset_ref.shape[0]):
                target = as_column(cell_ref[c, s:s + 1, :] + offset_ref[point, c, s:s + 1, :])
                mixing = mixing + jnp.where(target == cells, as_column(weight_ref[point, c, s:s + 1, :]), 0.0)
            spread_ref[c, s] = jnp.dot(
                mixing, placing, precision=lax.Precision.HIGHEST, preferred_element_type=jnp.float32
            )

    for copy in copies:
        copy.wait()
    for c in range(parts):
        total = jnp.zeros((levels, slots), jnp.float32)
        for i in range(rows):
            south = jnp.maximum(first_rate[i, :, :1], 0.0) * column_ref[c, 0, i, :, :1]
            north = jnp.maximum(-last_rate[i, :, LANES - 1:], 0.0) * column_ref[c, 1, i, :, LANES - 1:]
            total = total + south * spread_ref[c, 0, i:i + 1, :]
            total = total + north * spread_ref[c, 1, i:i + 1, :]
        partial_ref[c] = total


def mend_kernel(
    which, east_ref, north_ref, mine_ref, other_ref, ends_ref, spread_ref, partial_ref, out_ref, sum_ref
):
    parts, levels, slots = partial_ref.shape
    rows = spread_ref.shape[2]
    width = east_ref.shape[-1]
    flip = 1 - parity() if which == 0 else parity()
    sign = sign_of(flip)
    turn = lambda r: r + flip * (STEPS - 1 - 2 * r)
    place = lambda r: flip * (rows - STEPS) + turn(r)

    def half(at):
        own = [Row(east_ref[0, place(r), at, :] * sign, north_ref[0, place(r), at, :]) for r in range(STEPS - 1)]
        near = Row(other_ref[FLUX_ROWS, at, :] * sign, other_ref[FLUX_ROWS + 1, at, :])
        far = Row(other_ref[FLUX_ROWS + 2, at, :] * sign)
        for c in range(parts):
            mine = lambda k: mine_ref[2 * k + c, at, :]
            theirs = lambda k: other_ref[2 * k + c, at, :]
            a0 = theirs(0)
            n1 = mine(0)
            b0 = own[0].stay(a0) + near.inward * n1 + theirs(1)
            b1 = own[0].inward * a0
            bn1 = near.stay(n1) + own[0].outward * a0 + mine(1)
            bn2 = near.outward * n1
            c0 = own[0].stay(b0) + near.inward * bn1 + own[1].outward * b1 + theirs(2)
            c1 = own[1].stay(b1) + own[0].inward * b0
            c2 = own[1].inward * b1
            cn1 = near.stay(bn1) + own[0].outward * b0 + far.inward * bn2 + mine(2)
            d0 = own[0].stay(c0) + near.inward * cn1 + own[1].outward * c1 + theirs(3)
            d1 = own[1].stay(c1) + own[0].inward * c0 + own[2].outward * c2
            d2 = own[2].stay(c2) + own[1].inward * c1
            d3 = own[2].inward * c2
            for r, value in enumerate((d0, d1, d2, d3)):
                out_ref[c, turn(r), at, :] = ends_ref[c, flip * STEPS + turn(r), at, :] + value
            total = partial_ref[c, at, :]
            for r, value in enumerate((a0 + b0 + c0, b1 + c1, c2)):
                i = place(r)
                rate = north_ref[0, i, at, :]
                south = jnp.maximum(rate[:, :1], 0.0) * value[:, :1]
                north = jnp.maximum(-rate[:, width - 1:], 0.0) * value[:, width - 1:]
                total = total + south * spread_ref[c, 0, pl.ds(i, 1), :]
                total = total + north * spread_ref[c, 1, pl.ds(i, 1), :]
            sum_ref[c, at, :] = total

    level_halves(levels, half)


def pieces_kernel(total_ref, out_hbm, buffer, sem):
    parts, levels, slots = total_ref.shape
    peers, height, lanes = buffer.shape
    share = height // parts
    subs = levels // share
    each = peers // subs
    for s in range(subs):
        block = jnp.concatenate([total_ref[c, s * share:(s + 1) * share, :] for c in range(parts)], 0)
        if lanes > slots:
            block = jnp.concatenate([block, jnp.zeros((height, lanes - slots), jnp.float32)], 1)

        def give(p, carry, s=s, block=block):
            buffer[s * each + p] = block
            return carry

        lax.fori_loop(0, each, give, 0, unroll=4)
    copy = pltpu.make_async_copy(buffer, out_hbm, sem)
    copy.start()
    copy.wait()


def join_kernel(came_ref, out_ref):
    parts, share, mine = out_ref.shape
    lanes = came_ref.shape[-1]
    start = lax.axis_index("hor") * mine
    from_slot = lax.broadcasted_iota(jnp.int32, (lanes, mine), 0)
    to_slot = lax.broadcasted_iota(jnp.int32, (lanes, mine), 1)
    pick = jnp.where(from_slot == to_slot + start, 1.0, 0.0)
    total = jnp.sum(came_ref[...], 0)
    total = jnp.dot(total, pick, precision=lax.Precision.HIGHEST, preferred_element_type=jnp.float32)
    for c in range(parts):
        out_ref[c] = total[c * share:(c + 1) * share]


def subtract_kernel(state_ref, middle_ref, a_ref, b_ref, out_hbm, buffer, sems):
    parts, inner = middle_ref.shape[:2]
    rows = state_ref.shape[2]
    a_start = parity() * (rows - STEPS)
    b_start = (1 - parity()) * (rows - STEPS)
    copies = []
    for start, other in ((STEPS, middle_ref), (a_start, a_ref), (b_start, b_ref)):
        for c in range(parts):
            count = other.shape[1]
            for r in range(count):
                buffer[c, start + r] = state_ref[0, c, start + r] - other[c, r]
            at = pl.ds(start, count)
            copy = pltpu.make_async_copy(buffer.at[c, at], out_hbm.at[0, c, at], sems.at[len(copies)])
            copy.start()
            copies.append(copy)
    for copy in copies:
        copy.wait()


def cost(flops, moved):
    return pl.CostEstimate(flops=flops, bytes_accessed=moved, transcendentals=0)


PARAMS = pltpu.CompilerParams(vmem_limit_bytes=24 * 1024 * 1024)


def local(
    adjoint_state,
    courant_east,
    courant_north,
    parent_cell,
    stencil_offset,
    stencil_weight,
    owner_slot,
):
    _, parts, rows, levels, width = adjoint_state.shape
    slots = owner_slot.shape[0]
    inner = rows - 2 * STEPS
    row_bytes = levels * width * 4
    f32 = lambda *shape: jax.ShapeDtypeStruct(shape, jnp.float32)
    vmem = pl.BlockSpec(memory_space=pltpu.VMEM)
    smem = pl.BlockSpec(memory_space=pltpu.SMEM)
    hbm = pl.BlockSpec(memory_space=pltpu.HBM)
    in_hbm = lambda value: pltpu.with_memory_space_constraint(value, pltpu.HBM)

    first_pack = pl.pallas_call(
        first_kernel,
        in_specs=[hbm] * 3,
        out_specs=vmem,
        out_shape=f32(PACK_ROWS, levels, width),
        scratch_shapes=[
            pltpu.VMEM((parts, STEPS, levels, width), jnp.float32),
            pltpu.VMEM((STEPS, levels, width), jnp.float32),
            pltpu.VMEM((STEPS, levels, width), jnp.float32),
            pltpu.SemaphoreType.DMA((levels // HALF, parts + 2)),
        ],
        compiler_params=PARAMS,
        cost_estimate=cost(12 * levels * width * 13, 27 * row_bytes),
        name="first_pack",
    )(in_hbm(adjoint_state), in_hbm(courant_east), in_hbm(courant_north))
    first_came = alternating(first_pack, -1)

    state, east, north = adjoint_state, courant_east, courant_north
    second_pack, middle, ends, columns = pl.pallas_call(
        sweep_kernel,
        in_specs=[vmem] * 3,
        out_specs=[vmem] * 4,
        out_shape=[
            f32(PACK_ROWS, levels, width),
            f32(parts, inner, levels, width),
            f32(parts, 2 * STEPS, levels, width),
            f32(parts, 2, rows, levels, LANES),
        ],
        scratch_shapes=[
            pltpu.VMEM((STEPS - 1, parts, rows, HALF, width), jnp.float32),
            pltpu.VMEM((rows, HALF, width), jnp.float32),
            pltpu.VMEM((rows, HALF, width), jnp.float32),
            pltpu.VMEM((rows, HALF, width), jnp.float32),
        ],
        compiler_params=PARAMS,
        cost_estimate=cost(8 * rows * levels * width * 13, 6 * rows * row_bytes),
        name="sweep",
    )(state, east, north)
    middle_came = along(middle, "sub", -1)
    second_came = alternating(second_pack, 1)

    spread, partial = pl.pallas_call(
        ghost_kernel,
        in_specs=[vmem] * 5 + [hbm],
        out_specs=[vmem] * 2,
        out_shape=[f32(parts, 2, rows, slots), f32(parts, levels, slots)],
        scratch_shapes=[
            pltpu.VMEM((rows, levels, LANES), jnp.float32),
            pltpu.VMEM((rows, levels, LANES), jnp.float32),
            pltpu.SemaphoreType.DMA((2,)),
        ],
        compiler_params=PARAMS,
        cost_estimate=cost(parts * rows * levels * slots * 8, 4 * rows * levels * LANES * 8),
        name="ghost_sums",
    )(parent_cell, stencil_offset, stencil_weight, owner_slot[None], columns, in_hbm(courant_north))

    subs, hors = lax.axis_size("sub"), lax.axis_size("hor")

    def mend(which, mine, other, so_far):
        return pl.pallas_call(
            functools.partial(mend_kernel, which),
            in_specs=[vmem] * 7,
            out_specs=[vmem] * 2,
            out_shape=[f32(parts, STEPS, levels, width), f32(parts, levels, slots)],
            compiler_params=PARAMS,
            cost_estimate=cost(16 * levels * width * 13, 46 * row_bytes),
            name="mend_" + "ab"[which],
        )(east, north, mine, other, ends, spread, so_far)

    side_a, partial = mend(0, second_pack, first_came, partial)
    a_came = along(side_a, "sub", -1)
    side_b, partial = mend(1, first_pack, second_came, partial)
    b_came = along(side_b, "sub", -1)

    piece = (subs * hors, parts * levels // subs, -(-slots // LANES) * LANES)
    pieces = pl.pallas_call(
        pieces_kernel,
        in_specs=[vmem],
        out_specs=hbm,
        out_shape=pltpu.HBM(piece, jnp.float32),
        scratch_shapes=[pltpu.VMEM(piece, jnp.float32), pltpu.SemaphoreType.DMA],
        compiler_params=PARAMS,
        name="pieces",
    )(partial)
    pieces = lax.all_to_all(pieces, ("sub", "hor"), 0, 0, tiled=True)
    boundary_gradient = pl.pallas_call(
        join_kernel,
        in_specs=[vmem],
        out_specs=vmem,
        out_shape=f32(parts, levels // subs, slots // hors),
        compiler_params=PARAMS,
        name="join",
    )(pieces)

    adjoint_result = pl.pallas_call(
        subtract_kernel,
        in_specs=[vmem] * 4,
        out_specs=hbm,
        out_shape=f32(*adjoint_state.shape),
        scratch_shapes=[
            pltpu.VMEM((parts, rows, levels, width), jnp.float32),
            pltpu.SemaphoreType.DMA((3 * parts,)),
        ],
        compiler_params=PARAMS,
        cost_estimate=cost(parts * rows * levels * width, 6 * rows * row_bytes),
        name="subtract",
    )(state, middle_came, a_came, b_came)
    return (adjoint_result, boundary_gradient)


def solution(mesh):
    in_specs = (
        P(("ens", "sub"), None, "hor", None, None),
        P(("ens", "sub"), "hor", None, None),
        P(("ens", "sub"), "hor", None, None),
        P(None, None, "hor"),
        P(None, None, None, "hor"),
        P(None, None, None, "hor"),
        P(),
    )
    out_specs = (P(("ens", "sub"), None, "hor", None, None), P("ens", "sub", "hor"))
    return jax.shard_map(local, mesh=mesh, in_specs=in_specs, out_specs=out_specs, check_vma=False)
```

time: 47.3 us -> 39.2 us (0.83)
  blocking collectives: 18.7 us -> 14.7 us
  Pallas kernels: 11.9 us -> 10.4 us
  waiting for transfers between devices: 3.31 us -> 1.97 us
  local copies, waits for them, and re-layouts: 0.86 us -> 0.05 us
  other arithmetic: 0.66 us -> 0 us
    all_to_all x2 -> x1, blocking collectives: 18.7 us -> 14.7 us  [local(): pieces = lax.all_to_all(pieces, ('sub', 'hor'), 0, 0, tiled=True)]
    ppermute x2, waiting for transfers between devices: 3.3 us -> 1.96 us  [alternating(): return lax.ppermute(value, ('sub', 'hor'), pairs)]
    pallas_call x2, Pallas kernels: 2.51 us -> 1.8 us  [mend(): pl.pallas_call(functools.partial(mend_kernel, which), in_specs=[vmem] * 7...]
    all_to_all x1 -> x0, other arithmetic: 0.66 us -> none  [local(): pieces = lax.all_to_all(pieces, 'hor', 0, 0, tiled=True)]
    pallas_call x5, Pallas kernels: 7.37 us -> 6.75 us  [the longest x1 2.99 us: local(): pl.pallas_call(sweep_kernel, in_specs=[vmem] * 3, out_specs=[vmem] * 4, o...]
    all_to_all x2 -> x0, local copies, waits for them, and re-layouts: 0.59 us -> none  [local(): pieces = lax.all_to_all(pieces, 'hor', 0, 0, tiled=True)]
  transfers between devices with their start and end apart: 5 -> 5, of which waited for: 1 -> 1; matrix products, arithmetic and copies ran while one was open for 3% -> 0% of each run, Pallas kernels for 19% -> 19%
where the time goes in v4:
time: 39.2 us; the launch traced here: 38.9 us
  blocking collectives  14.7 us (38%)
  starting transfers between devices  10.9 us (28%)
  Pallas kernels  10.4 us (27%)
  waiting for transfers between devices  1.97 us (5%)
  between operations  0.86 us (2%)
    all_to_all x1, blocking collectives, local(): pieces = lax.all_to_all(pieces, ('sub', 'hor'), 0, 0, tiled=True)  14.7 us
    ppermute x2, starting transfers between devices, alternating(): return lax.ppermute(value, ('sub', 'hor'), pairs)  7.01 us
    ppermute x3, starting transfers between devices, along(): return lax.ppermute(value, axis, pairs)  3.88 us
    pallas_call x1, Pallas kernels, local(): pl.pallas_call(sweep_kernel, in_specs=[vmem] * 3, out_specs=[vmem] * 4, o...  2.99 us
    ppermute x2, waiting for transfers between devices, alternating(): return lax.ppermute(value, ('sub', 'hor'), pairs)  1.96 us
    pallas_call x1, Pallas kernels, local(): pl.pallas_call(first_kernel, in_specs=[hbm] * 3, out_specs=vmem, out_shap...  1.87 us
    pallas_call x2, Pallas kernels, mend(): pl.pallas_call(functools.partial(mend_kernel, which), in_specs=[vmem] * 7...  1.8 us
    pallas_call x1, Pallas kernels, local(): pl.pallas_call(ghost_kernel, in_specs=[vmem] * 5 + [hbm], out_specs=[vmem...  1.28 us
  transfers between devices with their start and end apart: 5, of which 1 were waited for; matrix products, arithmetic and copies ran while one was open for 0% of the time, Pallas kernels for 19%

profile of v4, /device:TPU:0, one launch (start us, length us, event | category | flops | bytes accessed | tf_op | source)
XLA Modules:
  0.0 38.9 jit_solution(15633933851153151898)
XLA Ops:
  0.6 0.0 copy-start
  0.7 1.9 %first_pack.1.mine_ref = f32[11,16,768]{2,1,0:T(8,128)S(1)} custom-call(f32[1,2,12,16,768]{4,3,2,1,0:T(8,128)} %state_ref.3, f32[1,12,16,768]{3,2,1,0:T(8,128)} %east_ref.5, f32[1,12,16,768]{3,2,1,0:T(8,128)} %north_ref.5), custom_call_target="tpu_custom_call" | custom-call | flops 1916928 | bytes 1327104 | tf_op jit(solution)/shard_map/first_pack/pallas_call | solution.py:361
  2.5 0.0 copy-start.4
  2.6 0.0 copy-start.5
  2.6 0.0 copy-start.6
  2.6 0.0 copy-start.7
  2.6 0.0 copy-start.1
  2.6 1.4 %collective-permute-start.1 = (f32[11,16,768]{2,1,0:T(8,128)S(1)}, f32[11,16,768]{2,1,0:T(8,128)S(1)}, u32[]{:S(2)}, u32[]{:S(2)}) collective-permute-start(f32[11,16,768]{2,1,0:T(8,128)S(1)} %first_pack.1.mine_ref), channel_id=1, source_target_pairs={{1,0},{2,1},{3,2},{4,5},{5,6},{6,7},{9,8},{10,9},{11,10},{12,13},{... | collective-permute-start | bytes 1622024 | tf_op jit(solution)/shard_map/ppermute | solution.py:29
  4.1 3.0 %sweep.1 = (f32[11,16,768]{2,1,0:T(8,128)S(1)}, f32[2,4,16,768]{3,2,1,0:T(8,128)S(1)}, f32[2,8,16,768]{3,2,1,0:T(8,128)S(1)}, f32[2,2,12,16,128]{4,3,2,1,0:T(8,128)S(1)}) custom-call(f32[1,2,12,16,768]{4,3,2,1,0:T(8,128)S(1)} %copy-done.2, f32[1,12,16,768]{3,2,1,0:T(8,128)S(1)} %copy-done.3, f32[1,12,16,768]{3,2,1,0:T(8,128)S(1)} %copy-done), custom_call_target="tpu_custom_call" | custom-call | flops 15335424 | bytes 3538944 | tf_op jit(solution)/shard_map/sweep/pallas_call | solution.py:379
  7.1 5.6 %collective-permute-start.3 = (f32[11,16,768]{2,1,0:T(8,128)S(1)}, f32[11,16,768]{2,1,0:T(8,128)S(1)}, u32[]{:S(2)}, u32[]{:S(2)}) collective-permute-start(f32[11,16,768]{2,1,0:T(8,128)S(1)} %get-tuple-element.13.mine_ref), channel_id=1, source_target_pairs={{0,1},{1,2},{2,3},{5,4},{6,5},{7,6},{8,9},{9,10},{10,11},{13,12},{... | collective-permute-start | bytes 1622024 | tf_op jit(solution)/shard_map/ppermute | solution.py:29
  12.7 1.3 %collective-permute-start = (f32[2,4,16,768]{3,2,1,0:T(8,128)S(1)}, f32[2,4,16,768]{3,2,1,0:T(8,128)S(1)}, u32[]{:S(2)}, u32[]{:S(2)}) collective-permute-start(f32[2,4,16,768]{3,2,1,0:T(8,128)S(1)} %get-tuple-element.12), channel_id=1, source_target_pairs={{4,0},{8,4},{12,8},{5,1},{9,5},{13,9},{6,2},{10,6},{14,10},{7,3},{... | collective-permute-start | bytes 1179656 | tf_op jit(solution)/shard_map/ppermute | solution.py:20
  14.0 1.3 %ghost_sums.1 = (f32[2,2,12,32]{3,2,1,0:T(8,128)S(1)}, f32[2,16,32]{2,1,0:T(8,128)S(1)}) custom-call(s32[2,2,12]{2,1,0:T(2,128)S(1)} %copy-done.6, s32[4,2,2,12]{3,2,1,0:T(2,128)S(1)} %copy-done.4, f32[4,2,2,12]{3,2,1,0:T(2,128)S(1)} %copy-done.5, s32[1,32]{1,0:T(1,128)S(1)} %bitcast.1, f32[2,2,12,16,128]{4,3,2,1,0:T(8,128)S(1)} %get-tuple-element.15.column_ref, ...), custom_call_target="tpu_custom_call" | custom-call | flops 98304 | bytes 786432 | tf_op jit(solution)/shard_map/ghost_sums/pallas_call | solution.py:402
  15.3 0.0 collective-permute-done.1.other_ref
  15.3 0.9 %mend_a.1 = (f32[2,4,16,768]{3,2,1,0:T(8,128)S(1)}, f32[2,16,32]{2,1,0:T(8,128)S(1)}) custom-call(f32[1,12,16,768]{3,2,1,0:T(8,128)S(1)} %copy-done.3, f32[1,12,16,768]{3,2,1,0:T(8,128)S(1)} %copy-done.1, f32[11,16,768]{2,1,0:T(8,128)S(1)} %get-tuple-element.13.mine_ref, f32[11,16,768]{2,1,0:T(8,128)S(1)} %collective-permute-done.1.other_ref, ...), custom_call_target="tpu_custom_call" | custom-call | flops 2555904 | bytes 2260992 | tf_op jit(solution)/shard_map/mend_a/pallas_call | solution.py:420
  16.2 1.3 %collective-permute-start.2 = (f32[2,4,16,768]{3,2,1,0:T(8,128)S(1)}, f32[2,4,16,768]{3,2,1,0:T(8,128)S(1)}, u32[]{:S(2)}, u32[]{:S(2)}) collective-permute-start(f32[2,4,16,768]{3,2,1,0:T(8,128)S(1)} %get-tuple-element.18), channel_id=1, source_target_pairs={{4,0},{8,4},{12,8},{5,1},{9,5},{13,9},{6,2},{10,6},{14,10},{7,3},{... | collective-permute-start | bytes 1179656 | tf_op jit(solution)/shard_map/ppermute | solution.py:20
  17.5 2.0 %collective-permute-done.3.other_ref = f32[11,16,768]{2,1,0:T(8,128)S(1)} collective-permute-done((f32[11,16,768]{2,1,0:T(8,128)S(1)}, f32[11,16,768]{2,1,0:T(8,128)S(1)}, u32[]{:S(2)}, u32[]{:S(2)}) %collective-permute-start.3) | collective-permute-done | bytes 540704 | tf_op jit(solution)/shard_map/ppermute | solution.py:29
  19.5 0.9 %mend_b.1 = (f32[2,4,16,768]{3,2,1,0:T(8,128)S(1)}, f32[2,16,32]{2,1,0:T(8,128)S(1)}) custom-call(f32[1,12,16,768]{3,2,1,0:T(8,128)S(1)} %copy-done.3, f32[1,12,16,768]{3,2,1,0:T(8,128)S(1)} %copy-done.1, f32[11,16,768]{2,1,0:T(8,128)S(1)} %first_pack.1.mine_ref, f32[11,16,768]{2,1,0:T(8,128)S(1)} %collective-permute-done.3.other_ref, ...), custom_call_target="tpu_custom_call" | custom-call | flops 2555904 | bytes 2260992 | tf_op jit(solution)/shard_map/mend_b/pallas_call | solution.py:420
  20.4 1.3 %collective-permute-start.4 = (f32[2,4,16,768]{3,2,1,0:T(8,128)S(1)}, f32[2,4,16,768]{3,2,1,0:T(8,128)S(1)}, u32[]{:S(2)}, u32[]{:S(2)}) collective-permute-start(f32[2,4,16,768]{3,2,1,0:T(8,128)S(1)} %get-tuple-element.20), channel_id=1, source_target_pairs={{4,0},{8,4},{12,8},{5,1},{9,5},{13,9},{6,2},{10,6},{14,10},{7,3},{... | collective-permute-start | bytes 1179656 | tf_op jit(solution)/shard_map/ppermute | solution.py:20
  21.7 0.6 %pieces.1 = f32[16,8,128]{2,1,0:T(8,128)} custom-call(f32[2,16,32]{2,1,0:T(8,128)S(1)} %get-tuple-element.21.total_ref), custom_call_target="tpu_custom_call" | custom-call | tf_op jit(solution)/shard_map/pieces/pallas_call | solution.py:436
  22.3 14.7 %all_to_all.5.came_ref = f32[16,8,128]{2,1,0:T(8,128)S(1)} all-to-all(f32[16,8,128]{2,1,0:T(8,128)} %pieces.1), channel_id=1, replica_groups=mesh['ens'=2,'sub'=4,'hor'=4] {'sub','hor'}, dimensions={0} | all-to-all | bytes 131072 | tf_op jit(solution)/shard_map/all_to_all | solution.py:445
  37.0 0.8 %join.1 = f32[2,4,8]{2,1,0:T(4,128)} custom-call(f32[16,8,128]{2,1,0:T(8,128)S(1)} %all_to_all.5.came_ref), custom_call_target="tpu_custom_call" | custom-call | tf_op jit(solution)/shard_map/join/pallas_call | solution.py:446
  37.8 0.0 collective-permute-done.middle_ref
  37.8 0.0 collective-permute-done.2.a_ref
  37.8 1.1 %subtract.1 = f32[1,2,12,16,768]{4,3,2,1,0:T(8,128)} custom-call(f32[1,2,12,16,768]{4,3,2,1,0:T(8,128)S(1)} %copy-done.2, f32[2,4,16,768]{3,2,1,0:T(8,128)S(1)} %collective-permute-done.middle_ref, f32[2,4,16,768]{3,2,1,0:T(8,128)S(1)} %collective-permute-done.2.a_ref, f32[2,4,16,768]{3,2,1,0:T(8,128)S(1)} %collective-permute-done.4.b_ref), custom_call_target="tpu_custom_call" | custom-call | flops 294912 | bytes 3538944 | tf_op jit(solution)/shard_map/subtract/pallas_call | solution.py:455
  (11 shorter events, 0.0 us)
Async XLA Ops:
  0.6 3.4 %copy-start = (f32[1,12,16,768]{3,2,1,0:T(8,128)S(1)}, f32[1,12,16,768]{3,2,1,0:T(8,128)}, u32[]{:S(2)}) copy-start(f32[1,12,16,768]{3,2,1,0:T(8,128)} %north_ref.5) | copy-start | bytes 1769476
  0.6 3.4 %copy-start.3 = (f32[1,12,16,768]{3,2,1,0:T(8,128)S(1)}, f32[1,12,16,768]{3,2,1,0:T(8,128)}, u32[]{:S(2)}) copy-start(f32[1,12,16,768]{3,2,1,0:T(8,128)} %east_ref.5) | copy-start | bytes 1769476
  0.7 3.4 %copy-start.2 = (f32[1,2,12,16,768]{4,3,2,1,0:T(8,128)S(1)}, f32[1,2,12,16,768]{4,3,2,1,0:T(8,128)}, u32[]{:S(2)}) copy-start(f32[1,2,12,16,768]{4,3,2,1,0:T(8,128)} %state_ref.3) | copy-start | bytes 3538948
  2.5 11.4 %copy-start.4 = (s32[4,2,2,12]{3,2,1,0:T(2,128)S(1)}, s32[4,2,2,12]{3,2,1,0:T(2,128)}, u32[]{:S(2)}) copy-start(s32[4,2,2,12]{3,2,1,0:T(2,128)} %offset_ref.1) | copy-start | bytes 2308
  2.6 11.4 %copy-start.5 = (f32[4,2,2,12]{3,2,1,0:T(2,128)S(1)}, f32[4,2,2,12]{3,2,1,0:T(2,128)}, u32[]{:S(2)}) copy-start(f32[4,2,2,12]{3,2,1,0:T(2,128)} %weight_ref.1) | copy-start | bytes 2308
  2.6 11.4 %copy-start.6 = (s32[2,2,12]{2,1,0:T(2,128)S(1)}, s32[2,2,12]{2,1,0:T(2,128)}, u32[]{:S(2)}) copy-start(s32[2,2,12]{2,1,0:T(2,128)} %cell_ref.1) | copy-start | bytes 580
  2.6 11.4 %copy-start.7 = (s32[32]{0:T(128)S(1)}, s32[32]{0:T(128)}, u32[]{:S(2)}) copy-start(s32[32]{0:T(128)} %param.13) | copy-start | bytes 388
  2.6 12.7 %copy-start.1 = (f32[1,12,16,768]{3,2,1,0:T(8,128)S(1)}, f32[1,12,16,768]{3,2,1,0:T(8,128)}, u32[]{:S(2)}) copy-start(f32[1,12,16,768]{3,2,1,0:T(8,128)} %north_ref.5) | copy-start | bytes 1769476
  2.6 12.7 %collective-permute-start.1 = (f32[11,16,768]{2,1,0:T(8,128)S(1)}, f32[11,16,768]{2,1,0:T(8,128)S(1)}, u32[]{:S(2)}, u32[]{:S(2)}) collective-permute-start(f32[11,16,768]{2,1,0:T(8,128)S(1)} %first_pack.1.mine_ref), channel_id=1, source_target_pairs={{1,0},{2,1},{3,2},{4,5},{5,6},{6,7},{9,8},{10,9},{11,10},{12,13},{... | collective-permute-start | bytes 1622024 | tf_op jit(solution)/shard_map/ppermute | solution.py:29
  7.1 12.4 %collective-permute-start.3 = (f32[11,16,768]{2,1,0:T(8,128)S(1)}, f32[11,16,768]{2,1,0:T(8,128)S(1)}, u32[]{:S(2)}, u32[]{:S(2)}) collective-permute-start(f32[11,16,768]{2,1,0:T(8,128)S(1)} %get-tuple-element.13.mine_ref), channel_id=1, source_target_pairs={{0,1},{1,2},{2,3},{5,4},{6,5},{7,6},{8,9},{9,10},{10,11},{13,12},{... | collective-permute-start | bytes 1622024 | tf_op jit(solution)/shard_map/ppermute | solution.py:29
  12.7 25.1 %collective-permute-start = (f32[2,4,16,768]{3,2,1,0:T(8,128)S(1)}, f32[2,4,16,768]{3,2,1,0:T(8,128)S(1)}, u32[]{:S(2)}, u32[]{:S(2)}) collective-permute-start(f32[2,4,16,768]{3,2,1,0:T(8,128)S(1)} %get-tuple-element.12), channel_id=1, source_target_pairs={{4,0},{8,4},{12,8},{5,1},{9,5},{13,9},{6,2},{10,6},{14,10},{7,3},{... | collective-permute-start | bytes 1179656 | tf_op jit(solution)/shard_map/ppermute | solution.py:20
  16.2 21.6 %collective-permute-start.2 = (f32[2,4,16,768]{3,2,1,0:T(8,128)S(1)}, f32[2,4,16,768]{3,2,1,0:T(8,128)S(1)}, u32[]{:S(2)}, u32[]{:S(2)}) collective-permute-start(f32[2,4,16,768]{3,2,1,0:T(8,128)S(1)} %get-tuple-element.18), channel_id=1, source_target_pairs={{4,0},{8,4},{12,8},{5,1},{9,5},{13,9},{6,2},{10,6},{14,10},{7,3},{... | collective-permute-start | bytes 1179656 | tf_op jit(solution)/shard_map/ppermute | solution.py:20
  20.4 17.4 %collective-permute-start.4 = (f32[2,4,16,768]{3,2,1,0:T(8,128)S(1)}, f32[2,4,16,768]{3,2,1,0:T(8,128)S(1)}, u32[]{:S(2)}, u32[]{:S(2)}) collective-permute-start(f32[2,4,16,768]{3,2,1,0:T(8,128)S(1)} %get-tuple-element.20), channel_id=1, source_target_pairs={{4,0},{8,4},{12,8},{5,1},{9,5},{13,9},{6,2},{10,6},{14,10},{7,3},{... | collective-permute-start | bytes 1179656 | tf_op jit(solution)/shard_map/ppermute | solution.py:20

commit v5 on v4

--- a/solution.py
+++ b/solution.py
@@ -279,22 +279,14 @@
     level_halves(levels, half)
 
 
-def pieces_kernel(total_ref, out_hbm, buffer, sem):
+def widen_kernel(total_ref, out_hbm, buffer, sem):
     parts, levels, slots = total_ref.shape
-    peers, height, lanes = buffer.shape
-    share = height // parts
-    subs = levels // share
-    each = peers // subs
-    for s in range(subs):
-        block = jnp.concatenate([total_ref[c, s * share:(s + 1) * share, :] for c in range(parts)], 0)
+    lanes = buffer.shape[-1]
+    for c in range(parts):
+        block = total_ref[c]
         if lanes > slots:
-            block = jnp.concatenate([block, jnp.zeros((height, lanes - slots), jnp.float32)], 1)
-
-        def give(p, carry, s=s, block=block):
-            buffer[s * each + p] = block
-            return carry
-
-        lax.fori_loop(0, each, give, 0, unroll=4)
+            block = jnp.concatenate([block, jnp.zeros((levels, lanes - slots), jnp.float32)], 1)
+        buffer[c * levels:(c + 1) * levels] = block
     copy = pltpu.make_async_copy(buffer, out_hbm, sem)
     copy.start()
     copy.wait()
@@ -302,15 +294,19 @@
 
 def join_kernel(came_ref, out_ref):
     parts, share, mine = out_ref.shape
-    lanes = came_ref.shape[-1]
-    start = lax.axis_index("hor") * mine
+    peers, height, lanes = came_ref.shape
+    levels = height // parts
     from_slot = lax.broadcasted_iota(jnp.int32, (lanes, mine), 0)
     to_slot = lax.broadcasted_iota(jnp.int32, (lanes, mine), 1)
-    pick = jnp.where(from_slot == to_slot + start, 1.0, 0.0)
+    pick = jnp.where(from_slot == to_slot + lax.axis_index("hor") * mine, 1.0, 0.0)
     total = jnp.sum(came_ref[...], 0)
     total = jnp.dot(total, pick, precision=lax.Precision.HIGHEST, preferred_element_type=jnp.float32)
     for c in range(parts):
-        out_ref[c] = total[c * share:(c + 1) * share]
+        chosen = jnp.zeros((share, mine), jnp.float32)
+        for s in range(levels // share):
+            block = total[c * levels + s * share:c * levels + (s + 1) * share]
+            chosen = jnp.where(lax.axis_index("sub") == s, block, chosen)
+        out_ref[c] = chosen
 
 
 def subtract_kernel(state_ref, middle_ref, a_ref, b_ref, out_hbm, buffer, sems):
@@ -432,17 +428,17 @@
     side_b, partial = mend(1, first_pack, second_came, partial)
     b_came = along(side_b, "sub", -1)
 
-    piece = (subs * hors, parts * levels // subs, -(-slots // LANES) * LANES)
-    pieces = pl.pallas_call(
-        pieces_kernel,
+    piece = (parts * levels, -(-slots // LANES) * LANES)
+    piece = pl.pallas_call(
+        widen_kernel,
         in_specs=[vmem],
         out_specs=hbm,
         out_shape=pltpu.HBM(piece, jnp.float32),
         scratch_shapes=[pltpu.VMEM(piece, jnp.float32), pltpu.SemaphoreType.DMA],
         compiler_params=PARAMS,
-        name="pieces",
+        name="widen",
     )(partial)
-    pieces = lax.all_to_all(pieces, ("sub", "hor"), 0, 0, tiled=True)
+    pieces = lax.all_gather(piece, ("sub", "hor"))
     boundary_gradient = pl.pallas_call(
         join_kernel,
         in_specs=[vmem],

time: 39.2 us -> 62 us (1.58)
  blocking collectives: 14.7 us -> 37.6 us
    all_gather x0 -> x1, blocking collectives: none -> 37.6 us  [local(): pieces = lax.all_gather(piece, ('sub', 'hor'))]
    all_to_all x1 -> x0, blocking collectives: 14.7 us -> none  [local(): pieces = lax.all_to_all(pieces, ('sub', 'hor'), 0, 0, tiled=True)]
  transfers between devices with their start and end apart: 5 -> 5, of which waited for: 1 -> 1; matrix products, arithmetic and copies ran while one was open for 0% -> 0% of each run, Pallas kernels for 19% -> 12%
where the time goes in v5:
time: 62 us; the launch traced here: 61.7 us
  blocking collectives  37.6 us (61%)
  starting transfers between devices  10.9 us (18%)
  Pallas kernels  10.4 us (17%)
  waiting for transfers between devices  1.98 us (3%)
  between operations  0.86 us (1%)
    all_gather x1, blocking collectives, local(): pieces = lax.all_gather(piece, ('sub', 'hor'))  37.6 us
    ppermute x2, starting transfers between devices, alternating(): return lax.ppermute(value, ('sub', 'hor'), pairs)  7.01 us
    ppermute x3, starting transfers between devices, along(): return lax.ppermute(value, axis, pairs)  3.88 us
    pallas_call x1, Pallas kernels, local(): pl.pallas_call(sweep_kernel, in_specs=[vmem] * 3, out_specs=[vmem] * 4, o...  2.99 us
    ppermute x2, waiting for transfers between devices, alternating(): return lax.ppermute(value, ('sub', 'hor'), pairs)  1.97 us
    pallas_call x1, Pallas kernels, local(): pl.pallas_call(first_kernel, in_specs=[hbm] * 3, out_specs=vmem, out_shap...  1.87 us
    pallas_call x2, Pallas kernels, mend(): pl.pallas_call(functools.partial(mend_kernel, which), in_specs=[vmem] * 7...  1.8 us
    pallas_call x1, Pallas kernels, local(): pl.pallas_call(ghost_kernel, in_specs=[vmem] * 5 + [hbm], out_specs=[vmem...  1.27 us
  transfers between devices with their start and end apart: 5, of which 1 were waited for; matrix products, arithmetic and copies ran while one was open for 0% of the time, Pallas kernels for 12%

profile of v5, /device:TPU:0, one launch (start us, length us, event | category | flops | bytes accessed | tf_op | source)
XLA Modules:
  0.0 61.7 jit_solution(1244437685448356156)
XLA Ops:
  0.6 0.0 copy-start
  0.7 1.9 %first_pack.1.mine_ref = f32[11,16,768]{2,1,0:T(8,128)S(1)} custom-call(f32[1,2,12,16,768]{4,3,2,1,0:T(8,128)} %state_ref.3, f32[1,12,16,768]{3,2,1,0:T(8,128)} %east_ref.5, f32[1,12,16,768]{3,2,1,0:T(8,128)} %north_ref.5), custom_call_target="tpu_custom_call" | custom-call | flops 1916928 | bytes 1327104 | tf_op jit(solution)/shard_map/first_pack/pallas_call | solution.py:357
  2.5 0.0 copy-start.4
  2.6 0.0 copy-start.5
  2.6 0.0 copy-start.6
  2.6 0.0 copy-start.7
  2.6 0.0 copy-start.1
  2.6 1.4 %collective-permute-start.1 = (f32[11,16,768]{2,1,0:T(8,128)S(1)}, f32[11,16,768]{2,1,0:T(8,128)S(1)}, u32[]{:S(2)}, u32[]{:S(2)}) collective-permute-start(f32[11,16,768]{2,1,0:T(8,128)S(1)} %first_pack.1.mine_ref), channel_id=1, source_target_pairs={{1,0},{2,1},{3,2},{4,5},{5,6},{6,7},{9,8},{10,9},{11,10},{12,13},{... | collective-permute-start | bytes 1622024 | tf_op jit(solution)/shard_map/ppermute | solution.py:29
  4.1 3.0 %sweep.1 = (f32[11,16,768]{2,1,0:T(8,128)S(1)}, f32[2,4,16,768]{3,2,1,0:T(8,128)S(1)}, f32[2,8,16,768]{3,2,1,0:T(8,128)S(1)}, f32[2,2,12,16,128]{4,3,2,1,0:T(8,128)S(1)}) custom-call(f32[1,2,12,16,768]{4,3,2,1,0:T(8,128)S(1)} %copy-done.2, f32[1,12,16,768]{3,2,1,0:T(8,128)S(1)} %copy-done.3, f32[1,12,16,768]{3,2,1,0:T(8,128)S(1)} %copy-done), custom_call_target="tpu_custom_call" | custom-call | flops 15335424 | bytes 3538944 | tf_op jit(solution)/shard_map/sweep/pallas_call | solution.py:375
  7.1 5.6 %collective-permute-start.3 = (f32[11,16,768]{2,1,0:T(8,128)S(1)}, f32[11,16,768]{2,1,0:T(8,128)S(1)}, u32[]{:S(2)}, u32[]{:S(2)}) collective-permute-start(f32[11,16,768]{2,1,0:T(8,128)S(1)} %get-tuple-element.13.mine_ref), channel_id=1, source_target_pairs={{0,1},{1,2},{2,3},{5,4},{6,5},{7,6},{8,9},{9,10},{10,11},{13,12},{... | collective-permute-start | bytes 1622024 | tf_op jit(solution)/shard_map/ppermute | solution.py:29
  12.7 1.3 %collective-permute-start = (f32[2,4,16,768]{3,2,1,0:T(8,128)S(1)}, f32[2,4,16,768]{3,2,1,0:T(8,128)S(1)}, u32[]{:S(2)}, u32[]{:S(2)}) collective-permute-start(f32[2,4,16,768]{3,2,1,0:T(8,128)S(1)} %get-tuple-element.12), channel_id=1, source_target_pairs={{4,0},{8,4},{12,8},{5,1},{9,5},{13,9},{6,2},{10,6},{14,10},{7,3},{... | collective-permute-start | bytes 1179656 | tf_op jit(solution)/shard_map/ppermute | solution.py:20
  14.0 1.3 %ghost_sums.1 = (f32[2,2,12,32]{3,2,1,0:T(8,128)S(1)}, f32[2,16,32]{2,1,0:T(8,128)S(1)}) custom-call(s32[2,2,12]{2,1,0:T(2,128)S(1)} %copy-done.6, s32[4,2,2,12]{3,2,1,0:T(2,128)S(1)} %copy-done.4, f32[4,2,2,12]{3,2,1,0:T(2,128)S(1)} %copy-done.5, s32[1,32]{1,0:T(1,128)S(1)} %bitcast.3, f32[2,2,12,16,128]{4,3,2,1,0:T(8,128)S(1)} %get-tuple-element.15.column_ref, ...), custom_call_target="tpu_custom_call" | custom-call | flops 98304 | bytes 786432 | tf_op jit(solution)/shard_map/ghost_sums/pallas_call | solution.py:398
  15.3 0.9 %mend_a.1 = (f32[2,4,16,768]{3,2,1,0:T(8,128)S(1)}, f32[2,16,32]{2,1,0:T(8,128)S(1)}) custom-call(f32[1,12,16,768]{3,2,1,0:T(8,128)S(1)} %copy-done.3, f32[1,12,16,768]{3,2,1,0:T(8,128)S(1)} %copy-done.1, f32[11,16,768]{2,1,0:T(8,128)S(1)} %get-tuple-element.13.mine_ref, f32[11,16,768]{2,1,0:T(8,128)S(1)} %collective-permute-done.1.other_ref, ...), custom_call_target="tpu_custom_call" | custom-call | flops 2555904 | bytes 2260992 | tf_op jit(solution)/shard_map/mend_a/pallas_call | solution.py:416
  16.2 1.3 %collective-permute-start.2 = (f32[2,4,16,768]{3,2,1,0:T(8,128)S(1)}, f32[2,4,16,768]{3,2,1,0:T(8,128)S(1)}, u32[]{:S(2)}, u32[]{:S(2)}) collective-permute-start(f32[2,4,16,768]{3,2,1,0:T(8,128)S(1)} %get-tuple-element.18), channel_id=1, source_target_pairs={{4,0},{8,4},{12,8},{5,1},{9,5},{13,9},{6,2},{10,6},{14,10},{7,3},{... | collective-permute-start | bytes 1179656 | tf_op jit(solution)/shard_map/ppermute | solution.py:20
  17.5 2.0 %collective-permute-done.3.other_ref = f32[11,16,768]{2,1,0:T(8,128)S(1)} collective-permute-done((f32[11,16,768]{2,1,0:T(8,128)S(1)}, f32[11,16,768]{2,1,0:T(8,128)S(1)}, u32[]{:S(2)}, u32[]{:S(2)}) %collective-permute-start.3) | collective-permute-done | bytes 540704 | tf_op jit(solution)/shard_map/ppermute | solution.py:29
  19.5 0.9 %mend_b.1 = (f32[2,4,16,768]{3,2,1,0:T(8,128)S(1)}, f32[2,16,32]{2,1,0:T(8,128)S(1)}) custom-call(f32[1,12,16,768]{3,2,1,0:T(8,128)S(1)} %copy-done.3, f32[1,12,16,768]{3,2,1,0:T(8,128)S(1)} %copy-done.1, f32[11,16,768]{2,1,0:T(8,128)S(1)} %first_pack.1.mine_ref, f32[11,16,768]{2,1,0:T(8,128)S(1)} %collective-permute-done.3.other_ref, ...), custom_call_target="tpu_custom_call" | custom-call | flops 2555904 | bytes 2260992 | tf_op jit(solution)/shard_map/mend_b/pallas_call | solution.py:416
  20.4 1.3 %collective-permute-start.4 = (f32[2,4,16,768]{3,2,1,0:T(8,128)S(1)}, f32[2,4,16,768]{3,2,1,0:T(8,128)S(1)}, u32[]{:S(2)}, u32[]{:S(2)}) collective-permute-start(f32[2,4,16,768]{3,2,1,0:T(8,128)S(1)} %get-tuple-element.20), channel_id=1, source_target_pairs={{4,0},{8,4},{12,8},{5,1},{9,5},{13,9},{6,2},{10,6},{14,10},{7,3},{... | collective-permute-start | bytes 1179656 | tf_op jit(solution)/shard_map/ppermute | solution.py:20
  21.7 0.6 widen.1
  22.3 37.6 %all-gather = f32[512,128]{1,0:T(8,128)S(1)} all-gather(f32[32,128]{1,0:T(8,128)} %widen.1), channel_id=2, replica_groups=mesh['ens'=2,'sub'=4,'hor'=4] {'sub','hor'}, dimensions={0}, use_global_device_ids=true | all-gather | bytes 278528 | tf_op jit(solution)/shard_map/all_gather | solution.py:441
  59.9 0.8 %join.1 = f32[2,4,8]{2,1,0:T(4,128)} custom-call(f32[16,32,128]{2,1,0:T(8,128)S(1)} %bitcast.2), custom_call_target="tpu_custom_call" | custom-call | tf_op jit(solution)/shard_map/join/pallas_call | solution.py:442
  60.7 0.0 collective-permute-done.middle_ref
  60.7 0.0 collective-permute-done.2.a_ref
  60.7 0.0 collective-permute-done.4.b_ref
  60.7 1.1 %subtract.1 = f32[1,2,12,16,768]{4,3,2,1,0:T(8,128)} custom-call(f32[1,2,12,16,768]{4,3,2,1,0:T(8,128)S(1)} %copy-done.2, f32[2,4,16,768]{3,2,1,0:T(8,128)S(1)} %collective-permute-done.middle_ref, f32[2,4,16,768]{3,2,1,0:T(8,128)S(1)} %collective-permute-done.2.a_ref, f32[2,4,16,768]{3,2,1,0:T(8,128)S(1)} %collective-permute-done.4.b_ref), custom_call_target="tpu_custom_call" | custom-call | flops 294912 | bytes 3538944 | tf_op jit(solution)/shard_map/subtract/pallas_call | solution.py:451
  (11 shorter events, 0.0 us)
Async XLA Ops:
  0.6 3.4 %copy-start = (f32[1,12,16,768]{3,2,1,0:T(8,128)S(1)}, f32[1,12,16,768]{3,2,1,0:T(8,128)}, u32[]{:S(2)}) copy-start(f32[1,12,16,768]{3,2,1,0:T(8,128)} %north_ref.5) | copy-start | bytes 1769476
  0.6 3.4 %copy-start.3 = (f32[1,12,16,768]{3,2,1,0:T(8,128)S(1)}, f32[1,12,16,768]{3,2,1,0:T(8,128)}, u32[]{:S(2)}) copy-start(f32[1,12,16,768]{3,2,1,0:T(8,128)} %east_ref.5) | copy-start | bytes 1769476
  0.7 3.4 %copy-start.2 = (f32[1,2,12,16,768]{4,3,2,1,0:T(8,128)S(1)}, f32[1,2,12,16,768]{4,3,2,1,0:T(8,128)}, u32[]{:S(2)}) copy-start(f32[1,2,12,16,768]{4,3,2,1,0:T(8,128)} %state_ref.3) | copy-start | bytes 3538948
  2.5 11.4 %copy-start.4 = (s32[4,2,2,12]{3,2,1,0:T(2,128)S(1)}, s32[4,2,2,12]{3,2,1,0:T(2,128)}, u32[]{:S(2)}) copy-start(s32[4,2,2,12]{3,2,1,0:T(2,128)} %offset_ref.1) | copy-start | bytes 2308
  2.6 11.4 %copy-start.5 = (f32[4,2,2,12]{3,2,1,0:T(2,128)S(1)}, f32[4,2,2,12]{3,2,1,0:T(2,128)}, u32[]{:S(2)}) copy-start(f32[4,2,2,12]{3,2,1,0:T(2,128)} %weight_ref.1) | copy-start | bytes 2308
  2.6 11.4 %copy-start.6 = (s32[2,2,12]{2,1,0:T(2,128)S(1)}, s32[2,2,12]{2,1,0:T(2,128)}, u32[]{:S(2)}) copy-start(s32[2,2,12]{2,1,0:T(2,128)} %cell_ref.1) | copy-start | bytes 580
  2.6 11.4 %copy-start.7 = (s32[32]{0:T(128)S(1)}, s32[32]{0:T(128)}, u32[]{:S(2)}) copy-start(s32[32]{0:T(128)} %param.13) | copy-start | bytes 388
  2.6 12.7 %copy-start.1 = (f32[1,12,16,768]{3,2,1,0:T(8,128)S(1)}, f32[1,12,16,768]{3,2,1,0:T(8,128)}, u32[]{:S(2)}) copy-start(f32[1,12,16,768]{3,2,1,0:T(8,128)} %north_ref.5) | copy-start | bytes 1769476
  2.6 12.7 %collective-permute-start.1 = (f32[11,16,768]{2,1,0:T(8,128)S(1)}, f32[11,16,768]{2,1,0:T(8,128)S(1)}, u32[]{:S(2)}, u32[]{:S(2)}) collective-permute-start(f32[11,16,768]{2,1,0:T(8,128)S(1)} %first_pack.1.mine_ref), channel_id=1, source_target_pairs={{1,0},{2,1},{3,2},{4,5},{5,6},{6,7},{9,8},{10,9},{11,10},{12,13},{... | collective-permute-start | bytes 1622024 | tf_op jit(solution)/shard_map/ppermute | solution.py:29
  7.1 12.4 %collective-permute-start.3 = (f32[11,16,768]{2,1,0:T(8,128)S(1)}, f32[11,16,768]{2,1,0:T(8,128)S(1)}, u32[]{:S(2)}, u32[]{:S(2)}) collective-permute-start(f32[11,16,768]{2,1,0:T(8,128)S(1)} %get-tuple-element.13.mine_ref), channel_id=1, source_target_pairs={{0,1},{1,2},{2,3},{5,4},{6,5},{7,6},{8,9},{9,10},{10,11},{13,12},{... | collective-permute-start | bytes 1622024 | tf_op jit(solution)/shard_map/ppermute | solution.py:29
  12.7 48.0 %collective-permute-start = (f32[2,4,16,768]{3,2,1,0:T(8,128)S(1)}, f32[2,4,16,768]{3,2,1,0:T(8,128)S(1)}, u32[]{:S(2)}, u32[]{:S(2)}) collective-permute-start(f32[2,4,16,768]{3,2,1,0:T(8,128)S(1)} %get-tuple-element.12), channel_id=1, source_target_pairs={{4,0},{8,4},{12,8},{5,1},{9,5},{13,9},{6,2},{10,6},{14,10},{7,3},{... | collective-permute-start | bytes 1179656 | tf_op jit(solution)/shard_map/ppermute | solution.py:20
  16.2 44.4 %collective-permute-start.2 = (f32[2,4,16,768]{3,2,1,0:T(8,128)S(1)}, f32[2,4,16,768]{3,2,1,0:T(8,128)S(1)}, u32[]{:S(2)}, u32[]{:S(2)}) collective-permute-start(f32[2,4,16,768]{3,2,1,0:T(8,128)S(1)} %get-tuple-element.18), channel_id=1, source_target_pairs={{4,0},{8,4},{12,8},{5,1},{9,5},{13,9},{6,2},{10,6},{14,10},{7,3},{... | collective-permute-start | bytes 1179656 | tf_op jit(solution)/shard_map/ppermute | solution.py:20
  20.4 40.3 %collective-permute-start.4 = (f32[2,4,16,768]{3,2,1,0:T(8,128)S(1)}, f32[2,4,16,768]{3,2,1,0:T(8,128)S(1)}, u32[]{:S(2)}, u32[]{:S(2)}) collective-permute-start(f32[2,4,16,768]{3,2,1,0:T(8,128)S(1)} %get-tuple-element.20), channel_id=1, source_target_pairs={{4,0},{8,4},{12,8},{5,1},{9,5},{13,9},{6,2},{10,6},{14,10},{7,3},{... | collective-permute-start | bytes 1179656 | tf_op jit(solution)/shard_map/ppermute | solution.py:20

commit v6 on v4

--- a/solution.py
+++ b/solution.py
@@ -232,22 +232,17 @@
         partial_ref[c] = total
 
 
-def mend_kernel(
-    which, east_ref, north_ref, mine_ref, other_ref, ends_ref, spread_ref, partial_ref, out_ref, sum_ref
-):
-    parts, levels, slots = partial_ref.shape
-    rows = spread_ref.shape[2]
-    width = east_ref.shape[-1]
-    flip = 1 - parity() if which == 0 else parity()
+def mend_side(flip, east_ref, north_ref, mine_ref, other_ref, store, store_column):
+    levels, width = mine_ref.shape[1:]
+    rows = east_ref.shape[1]
     sign = sign_of(flip)
-    turn = lambda r: r + flip * (STEPS - 1 - 2 * r)
-    place = lambda r: flip * (rows - STEPS) + turn(r)
+    place = lambda r: flip * (rows - STEPS) + r + flip * (STEPS - 1 - 2 * r)
 
     def half(at):
         own = [Row(east_ref[0, place(r), at, :] * sign, north_ref[0, place(r), at, :]) for r in range(STEPS - 1)]
         near = Row(other_ref[FLUX_ROWS, at, :] * sign, other_ref[FLUX_ROWS + 1, at, :])
         far = Row(other_ref[FLUX_ROWS + 2, at, :] * sign)
-        for c in range(parts):
+        for c in range(FLUX_ROWS // STEPS):
             mine = lambda k: mine_ref[2 * k + c, at, :]
             theirs = lambda k: other_ref[2 * k + c, at, :]
             a0 = theirs(0)
@@ -265,65 +260,96 @@
             d2 = own[2].stay(c2) + own[1].inward * c1
             d3 = own[2].inward * c2
             for r, value in enumerate((d0, d1, d2, d3)):
-                out_ref[c, turn(r), at, :] = ends_ref[c, flip * STEPS + turn(r), at, :] + value
-            total = partial_ref[c, at, :]
-            for r, value in enumerate((a0 + b0 + c0, b1 + c1, c2)):
-                i = place(r)
-                rate = north_ref[0, i, at, :]
-                south = jnp.maximum(rate[:, :1], 0.0) * value[:, :1]
-                north = jnp.maximum(-rate[:, width - 1:], 0.0) * value[:, width - 1:]
+                store(c, r, at, value)
+            for r, pieces in enumerate(((a0, b0, c0), (b1, c1), (c2,))):
+                store_column(c, 0, r, at, sum(value[:, :LANES] for value in pieces))
+                store_column(c, 1, r, at, sum(value[:, width - LANES:] for value in pieces))
+
+    level_halves(levels, half)
+
+
+def mend_a_kernel(east_ref, north_ref, mine_ref, other_ref, ends_ref, middle_ref, out_ref, column_ref):
+    parts, inner = middle_ref.shape[:2]
+    flip = 1 - parity()
+    turn = lambda r: r + flip * (STEPS - 1 - 2 * r)
+
+    def store(c, r, at, value):
+        out_ref[c, inner + turn(r), at, :] = ends_ref[c, flip * STEPS + turn(r), at, :] + value
+
+    def store_column(c, s, r, at, value):
+        column_ref[c, s, r, at, :] = value
+
+    mend_side(flip, east_ref, north_ref, mine_ref, other_ref, store, store_column)
+    for c in range(parts):
+        for i in range(inner):
+            out_ref[c, i] = middle_ref[c, i]
+
+
+def mend_b_kernel(
+    east_ref, north_ref, mine_ref, other_ref, ends_ref, a_column_ref, spread_ref, partial_ref,
+    out_ref, sum_ref, b_column_ref,
+):
+    parts, levels, slots = partial_ref.shape
+    rows = east_ref.shape[1]
+    width = east_ref.shape[-1]
+    flip = parity()
+    turn = lambda r: r + flip * (STEPS - 1 - 2 * r)
+
+    def store(c, r, at, value):
+        out_ref[c, turn(r), at, :] = ends_ref[c, flip * STEPS + turn(r), at, :] + value
+
+    def store_column(c, s, r, at, value):
+        b_column_ref[c, s, r, at, :] = value
+
+    mend_side(flip, east_ref, north_ref, mine_ref, other_ref, store, store_column)
+    for c in range(parts):
+        total = partial_ref[c]
+        for side, column_ref in ((1 - flip, a_column_ref), (flip, b_column_ref)):
+            for r in range(STEPS - 1):
+                i = r + side * (rows - 1 - 2 * r)
+                south = jnp.maximum(north_ref[0, i, :, :1], 0.0) * column_ref[c, 0, r, :, :1]
+                north = jnp.maximum(-north_ref[0, i, :, width - 1:], 0.0) * column_ref[c, 1, r, :, LANES - 1:]
                 total = total + south * spread_ref[c, 0, pl.ds(i, 1), :]
                 total = total + north * spread_ref[c, 1, pl.ds(i, 1), :]
-            sum_ref[c, at, :] = total
-
-    level_halves(levels, half)
+        sum_ref[c] = total
 
 
 def pieces_kernel(total_ref, out_hbm, buffer, sem):
     parts, levels, slots = total_ref.shape
-    peers, height, lanes = buffer.shape
-    share = height // parts
+    peers, _, share, mine = buffer.shape
     subs = levels // share
     each = peers // subs
-    for s in range(subs):
-        block = jnp.concatenate([total_ref[c, s * share:(s + 1) * share, :] for c in range(parts)], 0)
-        if lanes > slots:
-            block = jnp.concatenate([block, jnp.zeros((height, lanes - slots), jnp.float32)], 1)
-
-        def give(p, carry, s=s, block=block):
-            buffer[s * each + p] = block
-            return carry
-
-        lax.fori_loop(0, each, give, 0, unroll=4)
+    from_slot = lax.broadcasted_iota(jnp.int32, (slots, mine), 0)
+    to_slot = lax.broadcasted_iota(jnp.int32, (slots, mine), 1)
+    total = jnp.concatenate([total_ref[c] for c in range(parts)], 0)
+    for p in range(each):
+        pick = jnp.where(from_slot == to_slot + p * mine, 1.0, 0.0)
+        block = jnp.dot(total, pick, precision=lax.Precision.HIGHEST, preferred_element_type=jnp.float32)
+        for s in range(subs):
+            for c in range(parts):
+                at = c * levels + s * share
+                buffer[s * each + p, c] = block[at:at + share]
     copy = pltpu.make_async_copy(buffer, out_hbm, sem)
     copy.start()
     copy.wait()
 
 
 def join_kernel(came_ref, out_ref):
-    parts, share, mine = out_ref.shape
-    lanes = came_ref.shape[-1]
-    start = lax.axis_index("hor") * mine
-    from_slot = lax.broadcasted_iota(jnp.int32, (lanes, mine), 0)
-    to_slot = lax.broadcasted_iota(jnp.int32, (lanes, mine), 1)
-    pick = jnp.where(from_slot == to_slot + start, 1.0, 0.0)
-    total = jnp.sum(came_ref[...], 0)
-    total = jnp.dot(total, pick, precision=lax.Precision.HIGHEST, preferred_element_type=jnp.float32)
-    for c in range(parts):
-        out_ref[c] = total[c * share:(c + 1) * share]
-
-
-def subtract_kernel(state_ref, middle_ref, a_ref, b_ref, out_hbm, buffer, sems):
-    parts, inner = middle_ref.shape[:2]
-    rows = state_ref.shape[2]
+    out_ref[...] = jnp.sum(came_ref[...], 0)
+
+
+def subtract_kernel(state_ref, a_ref, b_ref, out_hbm, buffer, sems):
+    parts, rows = state_ref.shape[1:3]
+    inner = rows - 2 * STEPS
     a_start = parity() * (rows - STEPS)
     b_start = (1 - parity()) * (rows - STEPS)
     copies = []
-    for start, other in ((STEPS, middle_ref), (a_start, a_ref), (b_start, b_ref)):
+    for start, other, first, count in (
+        (STEPS, a_ref, 0, inner), (a_start, a_ref, inner, STEPS), (b_start, b_ref, 0, STEPS),
+    ):
         for c in range(parts):
-            count = other.shape[1]
             for r in range(count):
-                buffer[c, start + r] = state_ref[0, c, start + r] - other[c, r]
+                buffer[c, start + r] = state_ref[0, c, start + r] - other[c, first + r]
             at = pl.ds(start, count)
             copy = pltpu.make_async_copy(buffer.at[c, at], out_hbm.at[0, c, at], sems.at[len(copies)])
             copy.start()
@@ -396,7 +422,6 @@
         cost_estimate=cost(8 * rows * levels * width * 13, 6 * rows * row_bytes),
         name="sweep",
     )(state, east, north)
-    middle_came = along(middle, "sub", -1)
     second_came = alternating(second_pack, 1)
 
     spread, partial = pl.pallas_call(
@@ -416,23 +441,30 @@
 
     subs, hors = lax.axis_size("sub"), lax.axis_size("hor")
 
-    def mend(which, mine, other, so_far):
-        return pl.pallas_call(
-            functools.partial(mend_kernel, which),
-            in_specs=[vmem] * 7,
-            out_specs=[vmem] * 2,
-            out_shape=[f32(parts, STEPS, levels, width), f32(parts, levels, slots)],
-            compiler_params=PARAMS,
-            cost_estimate=cost(16 * levels * width * 13, 46 * row_bytes),
-            name="mend_" + "ab"[which],
-        )(east, north, mine, other, ends, spread, so_far)
-
-    side_a, partial = mend(0, second_pack, first_came, partial)
+    column_shape = (parts, 2, STEPS - 1, levels, LANES)
+    side_a, a_columns = pl.pallas_call(
+        mend_a_kernel,
+        in_specs=[vmem] * 6,
+        out_specs=[vmem] * 2,
+        out_shape=[f32(parts, inner + STEPS, levels, width), f32(*column_shape)],
+        compiler_params=PARAMS,
+        cost_estimate=cost(16 * levels * width * 13, 54 * row_bytes),
+        name="mend_a",
+    )(east, north, second_pack, first_came, ends, middle)
     a_came = along(side_a, "sub", -1)
-    side_b, partial = mend(1, first_pack, second_came, partial)
+    side_b, partial = pl.pallas_call(
+        mend_b_kernel,
+        in_specs=[vmem] * 8,
+        out_specs=[vmem] * 2,
+        out_shape=[f32(parts, STEPS, levels, width), f32(parts, levels, slots)],
+        scratch_shapes=[pltpu.VMEM(column_shape, jnp.float32)],
+        compiler_params=PARAMS,
+        cost_estimate=cost(16 * levels * width * 13, 46 * row_bytes),
+        name="mend_b",
+    )(east, north, first_pack, second_came, ends, a_columns, spread, partial)
     b_came = along(side_b, "sub", -1)
 
-    piece = (subs * hors, parts * levels // subs, -(-slots // LANES) * LANES)
+    piece = (subs * hors, parts, levels // subs, slots // hors)
     pieces = pl.pallas_call(
         pieces_kernel,
         in_specs=[vmem],
@@ -454,7 +486,7 @@
 
     adjoint_result = pl.pallas_call(
         subtract_kernel,
-        in_specs=[vmem] * 4,
+        in_specs=[vmem] * 3,
         out_specs=hbm,
         out_shape=f32(*adjoint_state.shape),
         scratch_shapes=[
@@ -464,7 +496,7 @@
         compiler_params=PARAMS,
         cost_estimate=cost(parts * rows * levels * width, 6 * rows * row_bytes),
         name="subtract",
-    )(state, middle_came, a_came, b_came)
+    )(state, a_came, b_came)
     return (adjoint_result, boundary_gradient)
 
 

time: 39.2 us -> 39 us (level)
  starting transfers between devices: 10.9 us -> 9.6 us
  waiting for transfers between devices: 1.97 us -> 3.25 us
    ppermute x2, waiting for transfers between devices: 1.96 us -> 3.24 us  [alternating(): return lax.ppermute(value, ('sub', 'hor'), pairs)]
    ppermute x3 -> x2, starting transfers between devices: 3.88 us -> 2.72 us  [along(): return lax.ppermute(value, axis, pairs)]
  transfers between devices with their start and end apart: 5 -> 4, of which waited for: 1 -> 2; matrix products, arithmetic and copies ran while one was open for 0% -> 0% of each run, Pallas kernels for 19% -> 19%
where the time goes in v6:
time: 39 us; the launch traced here: 38.7 us
  blocking collectives  14.7 us (38%)
  Pallas kernels  10.4 us (27%)
  starting transfers between devices  9.6 us (25%)
  waiting for transfers between devices  3.25 us (8%)
  between operations  0.8 us (2%)
    all_to_all x1, blocking collectives, local(): pieces = lax.all_to_all(pieces, ('sub', 'hor'), 0, 0, tiled=True)  14.7 us
    ppermute x2, starting transfers between devices, alternating(): return lax.ppermute(value, ('sub', 'hor'), pairs)  6.88 us
    ppermute x2, waiting for transfers between devices, alternating(): return lax.ppermute(value, ('sub', 'hor'), pairs)  3.24 us
    pallas_call x1, Pallas kernels, local(): pl.pallas_call(sweep_kernel, in_specs=[vmem] * 3, out_specs=[vmem] * 4, o...  2.99 us
    ppermute x2, starting transfers between devices, along(): return lax.ppermute(value, axis, pairs)  2.72 us
    pallas_call x1, Pallas kernels, local(): pl.pallas_call(first_kernel, in_specs=[hbm] * 3, out_specs=vmem, out_shap...  1.87 us
    pallas_call x1, Pallas kernels, local(): pl.pallas_call(ghost_kernel, in_specs=[vmem] * 5 + [hbm], out_specs=[vmem...  1.27 us
    pallas_call x1, Pallas kernels, local(): pl.pallas_call(subtract_kernel, in_specs=[vmem] * 3, out_specs=hbm, out_s...  1.07 us
  transfers between devices with their start and end apart: 4, of which 2 were waited for; matrix products, arithmetic and copies ran while one was open for 0% of the time, Pallas kernels for 19%

profile of v6, /device:TPU:0, one launch (start us, length us, event | category | flops | bytes accessed | tf_op | source)
XLA Modules:
  0.0 38.7 jit_solution(16889571516891239027)
XLA Ops:
  0.6 0.0 copy-start
  0.6 0.0 copy-start.3
  0.7 0.0 copy-start.2
  0.7 1.9 %first_pack.1.mine_ref = f32[11,16,768]{2,1,0:T(8,128)S(1)} custom-call(f32[1,2,12,16,768]{4,3,2,1,0:T(8,128)} %state_ref.3, f32[1,12,16,768]{3,2,1,0:T(8,128)} %east_ref.5, f32[1,12,16,768]{3,2,1,0:T(8,128)} %north_ref.5), custom_call_target="tpu_custom_call" | custom-call | flops 1916928 | bytes 1327104 | tf_op jit(solution)/shard_map/first_pack/pallas_call | solution.py:387
  2.5 1.3 %collective-permute-start = (f32[11,16,768]{2,1,0:T(8,128)S(1)}, f32[11,16,768]{2,1,0:T(8,128)S(1)}, u32[]{:S(2)}, u32[]{:S(2)}) collective-permute-start(f32[11,16,768]{2,1,0:T(8,128)S(1)} %first_pack.1.mine_ref), channel_id=1, source_target_pairs={{1,0},{2,1},{3,2},{4,5},{5,6},{6,7},{9,8},{10,9},{11,10},{12,13},{... | collective-permute-start | bytes 1622024 | tf_op jit(solution)/shard_map/ppermute | solution.py:29
  3.8 0.0 copy-done
  3.9 0.0 copy-done.3
  3.9 3.0 %sweep.1 = (f32[11,16,768]{2,1,0:T(8,128)S(1)}, f32[2,4,16,768]{3,2,1,0:T(8,128)S(1)}, f32[2,8,16,768]{3,2,1,0:T(8,128)S(1)}, f32[2,2,12,16,128]{4,3,2,1,0:T(8,128)S(1)}) custom-call(f32[1,2,12,16,768]{4,3,2,1,0:T(8,128)S(1)} %copy-done.2, f32[1,12,16,768]{3,2,1,0:T(8,128)S(1)} %copy-done.3, f32[1,12,16,768]{3,2,1,0:T(8,128)S(1)} %copy-done), custom_call_target="tpu_custom_call" | custom-call | flops 15335424 | bytes 3538944 | tf_op jit(solution)/shard_map/sweep/pallas_call | solution.py:405
  6.9 5.6 %collective-permute-start.2 = (f32[11,16,768]{2,1,0:T(8,128)S(1)}, f32[11,16,768]{2,1,0:T(8,128)S(1)}, u32[]{:S(2)}, u32[]{:S(2)}) collective-permute-start(f32[11,16,768]{2,1,0:T(8,128)S(1)} %get-tuple-element.12.mine_ref), channel_id=1, source_target_pairs={{0,1},{1,2},{2,3},{5,4},{6,5},{7,6},{8,9},{9,10},{10,11},{13,12},{... | collective-permute-start | bytes 1622024 | tf_op jit(solution)/shard_map/ppermute | solution.py:29
  12.5 2.5 %collective-permute-done.other_ref = f32[11,16,768]{2,1,0:T(8,128)S(1)} collective-permute-done((f32[11,16,768]{2,1,0:T(8,128)S(1)}, f32[11,16,768]{2,1,0:T(8,128)S(1)}, u32[]{:S(2)}, u32[]{:S(2)}) %collective-permute-start) | collective-permute-done | bytes 540704 | tf_op jit(solution)/shard_map/ppermute | solution.py:29
  15.0 0.8 %mend_a.1 = (f32[2,8,16,768]{3,2,1,0:T(8,128)S(1)}, f32[2,2,3,16,128]{4,3,2,1,0:T(8,128)S(1)}) custom-call(f32[1,12,16,768]{3,2,1,0:T(8,128)S(1)} %copy-done.3, f32[1,12,16,768]{3,2,1,0:T(8,128)S(1)} %copy-done, f32[11,16,768]{2,1,0:T(8,128)S(1)} %get-tuple-element.12.mine_ref, f32[11,16,768]{2,1,0:T(8,128)S(1)} %collective-permute-done.other_ref, ...), custom_call_target="tpu_custom_call" | custom-call | flops 2555904 | bytes 2654208 | tf_op jit(solution)/shard_map/mend_a/pallas_call | solution.py:445
  15.8 0.0 copy-start.1
  15.8 1.4 %collective-permute-start.1 = (f32[2,8,16,768]{3,2,1,0:T(8,128)S(1)}, f32[2,8,16,768]{3,2,1,0:T(8,128)S(1)}, u32[]{:S(2)}, u32[]{:S(2)}) collective-permute-start(f32[2,8,16,768]{3,2,1,0:T(8,128)S(1)} %get-tuple-element.15), channel_id=1, source_target_pairs={{4,0},{8,4},{12,8},{5,1},{9,5},{13,9},{6,2},{10,6},{14,10},{7,3},{... | collective-permute-start | bytes 2359304 | tf_op jit(solution)/shard_map/ppermute | solution.py:20
  17.3 1.3 %ghost_sums.1 = (f32[2,2,12,32]{3,2,1,0:T(8,128)S(1)}, f32[2,16,32]{2,1,0:T(8,128)S(1)}) custom-call(s32[2,2,12]{2,1,0:T(2,128)S(1)} %copy-done.6, s32[4,2,2,12]{3,2,1,0:T(2,128)S(1)} %copy-done.4, f32[4,2,2,12]{3,2,1,0:T(2,128)S(1)} %copy-done.5, s32[1,32]{1,0:T(1,128)S(1)} %bitcast.1, f32[2,2,12,16,128]{4,3,2,1,0:T(8,128)S(1)} %get-tuple-element.17.column_ref, ...), custom_call_target="tpu_custom_call" | custom-call | flops 98304 | bytes 786432 | tf_op jit(solution)/shard_map/ghost_sums/pallas_call | solution.py:427
  18.5 0.7 %collective-permute-done.2.other_ref = f32[11,16,768]{2,1,0:T(8,128)S(1)} collective-permute-done((f32[11,16,768]{2,1,0:T(8,128)S(1)}, f32[11,16,768]{2,1,0:T(8,128)S(1)}, u32[]{:S(2)}, u32[]{:S(2)}) %collective-permute-start.2) | collective-permute-done | bytes 540704 | tf_op jit(solution)/shard_map/ppermute | solution.py:29
  19.3 0.0 copy-done.1
  19.3 0.9 %mend_b.1 = (f32[2,4,16,768]{3,2,1,0:T(8,128)S(1)}, f32[2,16,32]{2,1,0:T(8,128)S(1)}) custom-call(f32[1,12,16,768]{3,2,1,0:T(8,128)S(1)} %copy-done.3, f32[1,12,16,768]{3,2,1,0:T(8,128)S(1)} %copy-done.1, f32[11,16,768]{2,1,0:T(8,128)S(1)} %first_pack.1.mine_ref, f32[11,16,768]{2,1,0:T(8,128)S(1)} %collective-permute-done.2.other_ref, ...), custom_call_target="tpu_custom_call" | custom-call | flops 2555904 | bytes 2260992 | tf_op jit(solution)/shard_map/mend_b/pallas_call | solution.py:455
  20.2 1.3 %collective-permute-start.3 = (f32[2,4,16,768]{3,2,1,0:T(8,128)S(1)}, f32[2,4,16,768]{3,2,1,0:T(8,128)S(1)}, u32[]{:S(2)}, u32[]{:S(2)}) collective-permute-start(f32[2,4,16,768]{3,2,1,0:T(8,128)S(1)} %get-tuple-element.20), channel_id=1, source_target_pairs={{4,0},{8,4},{12,8},{5,1},{9,5},{13,9},{6,2},{10,6},{14,10},{7,3},{... | collective-permute-start | bytes 1179656 | tf_op jit(solution)/shard_map/ppermute | solution.py:20
  21.5 0.9 %pieces.1 = f32[16,2,4,8]{3,2,1,0:T(4,128)} custom-call(f32[2,16,32]{2,1,0:T(8,128)S(1)} %get-tuple-element.21.total_ref), custom_call_target="tpu_custom_call" | custom-call | tf_op jit(solution)/shard_map/pieces/pallas_call | solution.py:468
  22.3 14.7 %all_to_all.5.came_ref = f32[16,2,4,8]{3,2,1,0:T(4,128)S(1)} all-to-all(f32[16,2,4,8]{3,2,1,0:T(4,128)} %pieces.1), channel_id=1, replica_groups=mesh['ens'=2,'sub'=4,'hor'=4] {'sub','hor'}, dimensions={0} | all-to-all | bytes 8192 | tf_op jit(solution)/shard_map/all_to_all | solution.py:477
  37.0 0.6 %join.1 = f32[2,4,8]{2,1,0:T(4,128)} custom-call(f32[16,2,4,8]{3,2,1,0:T(4,128)S(1)} %all_to_all.5.came_ref), custom_call_target="tpu_custom_call" | custom-call | tf_op jit(solution)/shard_map/join/pallas_call | solution.py:478
  37.6 0.0 collective-permute-done.3.b_ref
  37.6 0.0 collective-permute-done.1.a_ref
  37.6 1.1 %subtract.1 = f32[1,2,12,16,768]{4,3,2,1,0:T(8,128)} custom-call(f32[1,2,12,16,768]{4,3,2,1,0:T(8,128)S(1)} %copy-done.2, f32[2,8,16,768]{3,2,1,0:T(8,128)S(1)} %collective-permute-done.1.a_ref, f32[2,4,16,768]{3,2,1,0:T(8,128)S(1)} %collective-permute-done.3.b_ref), custom_call_target="tpu_custom_call" | custom-call | flops 294912 | bytes 3538944 | tf_op jit(solution)/shard_map/subtract/pallas_call | solution.py:487
  (9 shorter events, 0.0 us)
Async XLA Ops:
  0.6 3.2 %copy-start = (f32[1,12,16,768]{3,2,1,0:T(8,128)S(1)}, f32[1,12,16,768]{3,2,1,0:T(8,128)}, u32[]{:S(2)}) copy-start(f32[1,12,16,768]{3,2,1,0:T(8,128)} %north_ref.5) | copy-start | bytes 1769476
  0.6 3.2 %copy-start.3 = (f32[1,12,16,768]{3,2,1,0:T(8,128)S(1)}, f32[1,12,16,768]{3,2,1,0:T(8,128)}, u32[]{:S(2)}) copy-start(f32[1,12,16,768]{3,2,1,0:T(8,128)} %east_ref.5) | copy-start | bytes 1769476
  0.7 3.2 %copy-start.2 = (f32[1,2,12,16,768]{4,3,2,1,0:T(8,128)S(1)}, f32[1,2,12,16,768]{4,3,2,1,0:T(8,128)}, u32[]{:S(2)}) copy-start(f32[1,2,12,16,768]{4,3,2,1,0:T(8,128)} %state_ref.3) | copy-start | bytes 3538948
  2.5 12.4 %collective-permute-start = (f32[11,16,768]{2,1,0:T(8,128)S(1)}, f32[11,16,768]{2,1,0:T(8,128)S(1)}, u32[]{:S(2)}, u32[]{:S(2)}) collective-permute-start(f32[11,16,768]{2,1,0:T(8,128)S(1)} %first_pack.1.mine_ref), channel_id=1, source_target_pairs={{1,0},{2,1},{3,2},{4,5},{5,6},{6,7},{9,8},{10,9},{11,10},{12,13},{... | collective-permute-start | bytes 1622024 | tf_op jit(solution)/shard_map/ppermute | solution.py:29
  6.9 12.4 %collective-permute-start.2 = (f32[11,16,768]{2,1,0:T(8,128)S(1)}, f32[11,16,768]{2,1,0:T(8,128)S(1)}, u32[]{:S(2)}, u32[]{:S(2)}) collective-permute-start(f32[11,16,768]{2,1,0:T(8,128)S(1)} %get-tuple-element.12.mine_ref), channel_id=1, source_target_pairs={{0,1},{1,2},{2,3},{5,4},{6,5},{7,6},{8,9},{9,10},{10,11},{13,12},{... | collective-permute-start | bytes 1622024 | tf_op jit(solution)/shard_map/ppermute | solution.py:29
  15.0 2.3 %copy-start.4 = (s32[4,2,2,12]{3,2,1,0:T(2,128)S(1)}, s32[4,2,2,12]{3,2,1,0:T(2,128)}, u32[]{:S(2)}) copy-start(s32[4,2,2,12]{3,2,1,0:T(2,128)} %offset_ref.1) | copy-start | bytes 2308
  15.0 2.3 %copy-start.5 = (f32[4,2,2,12]{3,2,1,0:T(2,128)S(1)}, f32[4,2,2,12]{3,2,1,0:T(2,128)}, u32[]{:S(2)}) copy-start(f32[4,2,2,12]{3,2,1,0:T(2,128)} %weight_ref.1) | copy-start | bytes 2308
  15.0 2.3 %copy-start.6 = (s32[2,2,12]{2,1,0:T(2,128)S(1)}, s32[2,2,12]{2,1,0:T(2,128)}, u32[]{:S(2)}) copy-start(s32[2,2,12]{2,1,0:T(2,128)} %cell_ref.1) | copy-start | bytes 580
  15.0 2.3 %copy-start.7 = (s32[32]{0:T(128)S(1)}, s32[32]{0:T(128)}, u32[]{:S(2)}) copy-start(s32[32]{0:T(128)} %param.13) | copy-start | bytes 388
  15.8 3.5 %copy-start.1 = (f32[1,12,16,768]{3,2,1,0:T(8,128)S(1)}, f32[1,12,16,768]{3,2,1,0:T(8,128)}, u32[]{:S(2)}) copy-start(f32[1,12,16,768]{3,2,1,0:T(8,128)} %north_ref.5) | copy-start | bytes 1769476
  15.8 21.8 %collective-permute-start.1 = (f32[2,8,16,768]{3,2,1,0:T(8,128)S(1)}, f32[2,8,16,768]{3,2,1,0:T(8,128)S(1)}, u32[]{:S(2)}, u32[]{:S(2)}) collective-permute-start(f32[2,8,16,768]{3,2,1,0:T(8,128)S(1)} %get-tuple-element.15), channel_id=1, source_target_pairs={{4,0},{8,4},{12,8},{5,1},{9,5},{13,9},{6,2},{10,6},{14,10},{7,3},{... | collective-permute-start | bytes 2359304 | tf_op jit(solution)/shard_map/ppermute | solution.py:20
  20.2 17.5 %collective-permute-start.3 = (f32[2,4,16,768]{3,2,1,0:T(8,128)S(1)}, f32[2,4,16,768]{3,2,1,0:T(8,128)S(1)}, u32[]{:S(2)}, u32[]{:S(2)}) collective-permute-start(f32[2,4,16,768]{3,2,1,0:T(8,128)S(1)} %get-tuple-element.20), channel_id=1, source_target_pairs={{4,0},{8,4},{12,8},{5,1},{9,5},{13,9},{6,2},{10,6},{14,10},{7,3},{... | collective-permute-start | bytes 1179656 | tf_op jit(solution)/shard_map/ppermute | solution.py:20

commit v7 on v6

--- a/solution.py
+++ b/solution.py
@@ -334,8 +334,11 @@
     copy.wait()
 
 
-def join_kernel(came_ref, out_ref):
-    out_ref[...] = jnp.sum(came_ref[...], 0)
+def join_kernel(came_hbm, out_ref, buffer, sem):
+    copy = pltpu.make_async_copy(came_hbm, buffer, sem)
+    copy.start()
+    copy.wait()
+    out_ref[...] = jnp.sum(buffer[...], 0)
 
 
 def subtract_kernel(state_ref, a_ref, b_ref, out_hbm, buffer, sems):
@@ -477,12 +480,13 @@
     pieces = lax.all_to_all(pieces, ("sub", "hor"), 0, 0, tiled=True)
     boundary_gradient = pl.pallas_call(
         join_kernel,
-        in_specs=[vmem],
+        in_specs=[hbm],
         out_specs=vmem,
         out_shape=f32(parts, levels // subs, slots // hors),
+        scratch_shapes=[pltpu.VMEM(piece, jnp.float32), pltpu.SemaphoreType.DMA],
         compiler_params=PARAMS,
         name="join",
-    )(pieces)
+    )(in_hbm(pieces))
 
     adjoint_result = pl.pallas_call(
         subtract_kernel,

time: 39 us -> 40 us (1.026)
  Pallas kernels: 10.4 us -> 11.2 us
    pallas_call x1, Pallas kernels: 0.61 us -> 1.46 us  [local(): pl.pallas_call(join_kernel, in_specs=[hbm], out_specs=vmem, out_shape=f32...]
  transfers between devices with their start and end apart: 4 -> 4, of which waited for: 2 -> 2; matrix products, arithmetic and copies ran while one was open for 0% -> 0% of each run, Pallas kernels for 19% -> 21%
where the time goes in v7:
time: 40 us; the launch traced here: 39.7 us
  blocking collectives  14.8 us (37%)
  Pallas kernels  11.2 us (28%)
  starting transfers between devices  9.6 us (24%)
  waiting for transfers between devices  3.25 us (8%)
  between operations  0.82 us (2%)
    all_to_all x1, blocking collectives, local(): pieces = lax.all_to_all(pieces, ('sub', 'hor'), 0, 0, tiled=True)  14.8 us
    ppermute x2, starting transfers between devices, alternating(): return lax.ppermute(value, ('sub', 'hor'), pairs)  6.88 us
    ppermute x2, waiting for transfers between devices, alternating(): return lax.ppermute(value, ('sub', 'hor'), pairs)  3.24 us
    pallas_call x1, Pallas kernels, local(): pl.pallas_call(sweep_kernel, in_specs=[vmem] * 3, out_specs=[vmem] * 4, o...  2.99 us
    ppermute x2, starting transfers between devices, along(): return lax.ppermute(value, axis, pairs)  2.72 us
    pallas_call x1, Pallas kernels, local(): pl.pallas_call(first_kernel, in_specs=[hbm] * 3, out_specs=vmem, out_shap...  1.87 us
    pallas_call x1, Pallas kernels, local(): pl.pallas_call(join_kernel, in_specs=[hbm], out_specs=vmem, out_shape=f32...  1.46 us
    pallas_call x1, Pallas kernels, local(): pl.pallas_call(ghost_kernel, in_specs=[vmem] * 5 + [hbm], out_specs=[vmem...  1.27 us
  transfers between devices with their start and end apart: 4, of which 2 were waited for; matrix products, arithmetic and copies ran while one was open for 0% of the time, Pallas kernels for 21%

profile of v7, /device:TPU:0, one launch (start us, length us, event | category | flops | bytes accessed | tf_op | source)
XLA Modules:
  0.0 39.7 jit_solution(579865780620757753)
XLA Ops:
  0.6 0.0 copy-start
  0.6 0.0 copy-start.3
  0.7 0.0 copy-start.2
  0.7 1.9 %first_pack.1.mine_ref = f32[11,16,768]{2,1,0:T(8,128)S(1)} custom-call(f32[1,2,12,16,768]{4,3,2,1,0:T(8,128)} %state_ref.3, f32[1,12,16,768]{3,2,1,0:T(8,128)} %east_ref.5, f32[1,12,16,768]{3,2,1,0:T(8,128)} %north_ref.5), custom_call_target="tpu_custom_call" | custom-call | flops 1916928 | bytes 1327104 | tf_op jit(solution)/shard_map/first_pack/pallas_call | solution.py:390
  2.5 1.3 %collective-permute-start = (f32[11,16,768]{2,1,0:T(8,128)S(1)}, f32[11,16,768]{2,1,0:T(8,128)S(1)}, u32[]{:S(2)}, u32[]{:S(2)}) collective-permute-start(f32[11,16,768]{2,1,0:T(8,128)S(1)} %first_pack.1.mine_ref), channel_id=1, source_target_pairs={{1,0},{2,1},{3,2},{4,5},{5,6},{6,7},{9,8},{10,9},{11,10},{12,13},{... | collective-permute-start | bytes 1622024 | tf_op jit(solution)/shard_map/ppermute | solution.py:29
  3.8 0.0 copy-done
  3.9 0.0 copy-done.3
  3.9 3.0 %sweep.1 = (f32[11,16,768]{2,1,0:T(8,128)S(1)}, f32[2,4,16,768]{3,2,1,0:T(8,128)S(1)}, f32[2,8,16,768]{3,2,1,0:T(8,128)S(1)}, f32[2,2,12,16,128]{4,3,2,1,0:T(8,128)S(1)}) custom-call(f32[1,2,12,16,768]{4,3,2,1,0:T(8,128)S(1)} %copy-done.2, f32[1,12,16,768]{3,2,1,0:T(8,128)S(1)} %copy-done.3, f32[1,12,16,768]{3,2,1,0:T(8,128)S(1)} %copy-done), custom_call_target="tpu_custom_call" | custom-call | flops 15335424 | bytes 3538944 | tf_op jit(solution)/shard_map/sweep/pallas_call | solution.py:408
  6.9 5.6 %collective-permute-start.2 = (f32[11,16,768]{2,1,0:T(8,128)S(1)}, f32[11,16,768]{2,1,0:T(8,128)S(1)}, u32[]{:S(2)}, u32[]{:S(2)}) collective-permute-start(f32[11,16,768]{2,1,0:T(8,128)S(1)} %get-tuple-element.12.mine_ref), channel_id=1, source_target_pairs={{0,1},{1,2},{2,3},{5,4},{6,5},{7,6},{8,9},{9,10},{10,11},{13,12},{... | collective-permute-start | bytes 1622024 | tf_op jit(solution)/shard_map/ppermute | solution.py:29
  12.5 2.5 %collective-permute-done.other_ref = f32[11,16,768]{2,1,0:T(8,128)S(1)} collective-permute-done((f32[11,16,768]{2,1,0:T(8,128)S(1)}, f32[11,16,768]{2,1,0:T(8,128)S(1)}, u32[]{:S(2)}, u32[]{:S(2)}) %collective-permute-start) | collective-permute-done | bytes 540704 | tf_op jit(solution)/shard_map/ppermute | solution.py:29
  15.0 0.8 %mend_a.1 = (f32[2,8,16,768]{3,2,1,0:T(8,128)S(1)}, f32[2,2,3,16,128]{4,3,2,1,0:T(8,128)S(1)}) custom-call(f32[1,12,16,768]{3,2,1,0:T(8,128)S(1)} %copy-done.3, f32[1,12,16,768]{3,2,1,0:T(8,128)S(1)} %copy-done, f32[11,16,768]{2,1,0:T(8,128)S(1)} %get-tuple-element.12.mine_ref, f32[11,16,768]{2,1,0:T(8,128)S(1)} %collective-permute-done.other_ref, ...), custom_call_target="tpu_custom_call" | custom-call | flops 2555904 | bytes 2654208 | tf_op jit(solution)/shard_map/mend_a/pallas_call | solution.py:448
  15.8 0.0 copy-start.1
  15.8 1.4 %collective-permute-start.1 = (f32[2,8,16,768]{3,2,1,0:T(8,128)S(1)}, f32[2,8,16,768]{3,2,1,0:T(8,128)S(1)}, u32[]{:S(2)}, u32[]{:S(2)}) collective-permute-start(f32[2,8,16,768]{3,2,1,0:T(8,128)S(1)} %get-tuple-element.15), channel_id=1, source_target_pairs={{4,0},{8,4},{12,8},{5,1},{9,5},{13,9},{6,2},{10,6},{14,10},{7,3},{... | collective-permute-start | bytes 2359304 | tf_op jit(solution)/shard_map/ppermute | solution.py:20
  17.3 1.3 %ghost_sums.1 = (f32[2,2,12,32]{3,2,1,0:T(8,128)S(1)}, f32[2,16,32]{2,1,0:T(8,128)S(1)}) custom-call(s32[2,2,12]{2,1,0:T(2,128)S(1)} %copy-done.6, s32[4,2,2,12]{3,2,1,0:T(2,128)S(1)} %copy-done.4, f32[4,2,2,12]{3,2,1,0:T(2,128)S(1)} %copy-done.5, s32[1,32]{1,0:T(1,128)S(1)} %bitcast.1, f32[2,2,12,16,128]{4,3,2,1,0:T(8,128)S(1)} %get-tuple-element.17.column_ref, ...), custom_call_target="tpu_custom_call" | custom-call | flops 98304 | bytes 786432 | tf_op jit(solution)/shard_map/ghost_sums/pallas_call | solution.py:430
  18.5 0.7 %collective-permute-done.2.other_ref = f32[11,16,768]{2,1,0:T(8,128)S(1)} collective-permute-done((f32[11,16,768]{2,1,0:T(8,128)S(1)}, f32[11,16,768]{2,1,0:T(8,128)S(1)}, u32[]{:S(2)}, u32[]{:S(2)}) %collective-permute-start.2) | collective-permute-done | bytes 540704 | tf_op jit(solution)/shard_map/ppermute | solution.py:29
  19.3 0.0 copy-done.1
  19.3 0.9 %mend_b.1 = (f32[2,4,16,768]{3,2,1,0:T(8,128)S(1)}, f32[2,16,32]{2,1,0:T(8,128)S(1)}) custom-call(f32[1,12,16,768]{3,2,1,0:T(8,128)S(1)} %copy-done.3, f32[1,12,16,768]{3,2,1,0:T(8,128)S(1)} %copy-done.1, f32[11,16,768]{2,1,0:T(8,128)S(1)} %first_pack.1.mine_ref, f32[11,16,768]{2,1,0:T(8,128)S(1)} %collective-permute-done.2.other_ref, ...), custom_call_target="tpu_custom_call" | custom-call | flops 2555904 | bytes 2260992 | tf_op jit(solution)/shard_map/mend_b/pallas_call | solution.py:458
  20.2 1.3 %collective-permute-start.3 = (f32[2,4,16,768]{3,2,1,0:T(8,128)S(1)}, f32[2,4,16,768]{3,2,1,0:T(8,128)S(1)}, u32[]{:S(2)}, u32[]{:S(2)}) collective-permute-start(f32[2,4,16,768]{3,2,1,0:T(8,128)S(1)} %get-tuple-element.20), channel_id=1, source_target_pairs={{4,0},{8,4},{12,8},{5,1},{9,5},{13,9},{6,2},{10,6},{14,10},{7,3},{... | collective-permute-start | bytes 1179656 | tf_op jit(solution)/shard_map/ppermute | solution.py:20
  21.5 0.9 %pieces.1 = f32[16,2,4,8]{3,2,1,0:T(4,128)} custom-call(f32[2,16,32]{2,1,0:T(8,128)S(1)} %get-tuple-element.21.total_ref), custom_call_target="tpu_custom_call" | custom-call | tf_op jit(solution)/shard_map/pieces/pallas_call | solution.py:471
  22.3 14.8 %all_to_all.5.came_hbm = f32[16,2,4,8]{3,2,1,0:T(4,128)} all-to-all(f32[16,2,4,8]{3,2,1,0:T(4,128)} %pieces.1), channel_id=1, replica_groups=mesh['ens'=2,'sub'=4,'hor'=4] {'sub','hor'}, dimensions={0} | all-to-all | bytes 8192 | tf_op jit(solution)/shard_map/all_to_all | solution.py:480
  37.1 1.5 %join.1 = f32[2,4,8]{2,1,0:T(4,128)} custom-call(f32[16,2,4,8]{3,2,1,0:T(4,128)} %all_to_all.5.came_hbm), custom_call_target="tpu_custom_call" | custom-call | tf_op jit(solution)/shard_map/join/pallas_call | solution.py:481
  38.6 0.0 collective-permute-done.3.b_ref
  38.6 0.0 collective-permute-done.1.a_ref
  38.6 1.1 %subtract.1 = f32[1,2,12,16,768]{4,3,2,1,0:T(8,128)} custom-call(f32[1,2,12,16,768]{4,3,2,1,0:T(8,128)S(1)} %copy-done.2, f32[2,8,16,768]{3,2,1,0:T(8,128)S(1)} %collective-permute-done.1.a_ref, f32[2,4,16,768]{3,2,1,0:T(8,128)S(1)} %collective-permute-done.3.b_ref), custom_call_target="tpu_custom_call" | custom-call | flops 294912 | bytes 3538944 | tf_op jit(solution)/shard_map/subtract/pallas_call | solution.py:491
  (9 shorter events, 0.0 us)
Async XLA Ops:
  0.6 3.2 %copy-start = (f32[1,12,16,768]{3,2,1,0:T(8,128)S(1)}, f32[1,12,16,768]{3,2,1,0:T(8,128)}, u32[]{:S(2)}) copy-start(f32[1,12,16,768]{3,2,1,0:T(8,128)} %north_ref.5) | copy-start | bytes 1769476
  0.6 3.2 %copy-start.3 = (f32[1,12,16,768]{3,2,1,0:T(8,128)S(1)}, f32[1,12,16,768]{3,2,1,0:T(8,128)}, u32[]{:S(2)}) copy-start(f32[1,12,16,768]{3,2,1,0:T(8,128)} %east_ref.5) | copy-start | bytes 1769476
  0.7 3.2 %copy-start.2 = (f32[1,2,12,16,768]{4,3,2,1,0:T(8,128)S(1)}, f32[1,2,12,16,768]{4,3,2,1,0:T(8,128)}, u32[]{:S(2)}) copy-start(f32[1,2,12,16,768]{4,3,2,1,0:T(8,128)} %state_ref.3) | copy-start | bytes 3538948
  2.5 12.4 %collective-permute-start = (f32[11,16,768]{2,1,0:T(8,128)S(1)}, f32[11,16,768]{2,1,0:T(8,128)S(1)}, u32[]{:S(2)}, u32[]{:S(2)}) collective-permute-start(f32[11,16,768]{2,1,0:T(8,128)S(1)} %first_pack.1.mine_ref), channel_id=1, source_target_pairs={{1,0},{2,1},{3,2},{4,5},{5,6},{6,7},{9,8},{10,9},{11,10},{12,13},{... | collective-permute-start | bytes 1622024 | tf_op jit(solution)/shard_map/ppermute | solution.py:29
  6.9 12.4 %collective-permute-start.2 = (f32[11,16,768]{2,1,0:T(8,128)S(1)}, f32[11,16,768]{2,1,0:T(8,128)S(1)}, u32[]{:S(2)}, u32[]{:S(2)}) collective-permute-start(f32[11,16,768]{2,1,0:T(8,128)S(1)} %get-tuple-element.12.mine_ref), channel_id=1, source_target_pairs={{0,1},{1,2},{2,3},{5,4},{6,5},{7,6},{8,9},{9,10},{10,11},{13,12},{... | collective-permute-start | bytes 1622024 | tf_op jit(solution)/shard_map/ppermute | solution.py:29
  15.0 2.3 %copy-start.4 = (s32[4,2,2,12]{3,2,1,0:T(2,128)S(1)}, s32[4,2,2,12]{3,2,1,0:T(2,128)}, u32[]{:S(2)}) copy-start(s32[4,2,2,12]{3,2,1,0:T(2,128)} %offset_ref.1) | copy-start | bytes 2308
  15.0 2.3 %copy-start.5 = (f32[4,2,2,12]{3,2,1,0:T(2,128)S(1)}, f32[4,2,2,12]{3,2,1,0:T(2,128)}, u32[]{:S(2)}) copy-start(f32[4,2,2,12]{3,2,1,0:T(2,128)} %weight_ref.1) | copy-start | bytes 2308
  15.0 2.3 %copy-start.6 = (s32[2,2,12]{2,1,0:T(2,128)S(1)}, s32[2,2,12]{2,1,0:T(2,128)}, u32[]{:S(2)}) copy-start(s32[2,2,12]{2,1,0:T(2,128)} %cell_ref.1) | copy-start | bytes 580
  15.0 2.3 %copy-start.7 = (s32[32]{0:T(128)S(1)}, s32[32]{0:T(128)}, u32[]{:S(2)}) copy-start(s32[32]{0:T(128)} %param.13) | copy-start | bytes 388
  15.8 3.5 %copy-start.1 = (f32[1,12,16,768]{3,2,1,0:T(8,128)S(1)}, f32[1,12,16,768]{3,2,1,0:T(8,128)}, u32[]{:S(2)}) copy-start(f32[1,12,16,768]{3,2,1,0:T(8,128)} %north_ref.5) | copy-start | bytes 1769476
  15.8 22.8 %collective-permute-start.1 = (f32[2,8,16,768]{3,2,1,0:T(8,128)S(1)}, f32[2,8,16,768]{3,2,1,0:T(8,128)S(1)}, u32[]{:S(2)}, u32[]{:S(2)}) collective-permute-start(f32[2,8,16,768]{3,2,1,0:T(8,128)S(1)} %get-tuple-element.15), channel_id=1, source_target_pairs={{4,0},{8,4},{12,8},{5,1},{9,5},{13,9},{6,2},{10,6},{14,10},{7,3},{... | collective-permute-start | bytes 2359304 | tf_op jit(solution)/shard_map/ppermute | solution.py:20
  20.2 18.4 %collective-permute-start.3 = (f32[2,4,16,768]{3,2,1,0:T(8,128)S(1)}, f32[2,4,16,768]{3,2,1,0:T(8,128)S(1)}, u32[]{:S(2)}, u32[]{:S(2)}) collective-permute-start(f32[2,4,16,768]{3,2,1,0:T(8,128)S(1)} %get-tuple-element.20), channel_id=1, source_target_pairs={{4,0},{8,4},{12,8},{5,1},{9,5},{13,9},{6,2},{10,6},{14,10},{7,3},{... | collective-permute-start | bytes 1179656 | tf_op jit(solution)/shard_map/ppermute | solution.py:20

commit v8 on v6

--- a/solution.py
+++ b/solution.py
@@ -12,6 +12,9 @@
 FLUX_ROWS = 2 * STEPS
 PACK_ROWS = FLUX_ROWS + 3
 LANES = 128
+EXTRA = PACK_ROWS
+TARGETS = 4 * LANES
+WEIGHTS = 5 * LANES
 
 
 def along(value, axis, step_of):
@@ -29,6 +32,19 @@
     return lax.ppermute(value, ("sub", "hor"), pairs)
 
 
+def added_up(value):
+    sizes = {axis: lax.axis_size(axis) for axis in ("sub", "hor")}
+    if any(size & (size - 1) for size in sizes.values()):
+        return lax.psum(value, ("sub", "hor"))
+    steps = {axis: [1 << n for n in range(size.bit_length() - 1)] for axis, size in sizes.items()}
+    order = [("sub", step) for step in steps["sub"][:1]]
+    order += [("hor", step) for step in steps["hor"]]
+    order += [("sub", step) for step in steps["sub"][1:]]
+    for axis, step in order:
+        value = value + lax.ppermute(value, axis, [(i, i ^ step) for i in range(sizes[axis])])
+    return value
+
+
 def parity():
     return lax.rem(lax.axis_index("sub"), 2)
 
@@ -71,9 +87,14 @@
     lax.fori_loop(0, levels // HALF, step, 0)
 
 
-def first_kernel(state_hbm, east_hbm, north_hbm, pack_ref, state_ref, east_ref, north_ref, sems):
-    parts, rows, levels = state_hbm.shape[1:4]
-    flip = parity()
+def pack_kernel(which, *refs):
+    if which == 0:
+        state_hbm, east_hbm, north_hbm, cell_hbm, offset_hbm, weight_hbm = refs[:6]
+        pack_ref, state_ref, east_ref, north_ref, cell_ref, offset_ref, weight_ref, sems, small_sems = refs[6:]
+    else:
+        state_hbm, east_hbm, north_hbm, pack_ref, state_ref, east_ref, north_ref, sems = refs
+    parts, rows, levels, width = state_hbm.shape[1:]
+    flip = parity() if which == 0 else 1 - parity()
     sign = sign_of(flip)
     at_end = pl.ds(flip * (rows - STEPS), STEPS)
     place = lambda r: r + flip * (STEPS - 1 - 2 * r)
@@ -91,12 +112,26 @@
         copies.append(batch)
         for copy in batch:
             copy.start()
+    if which == 0:
+        small = [
+            pltpu.make_async_copy(source, target, small_sems.at[n])
+            for n, (source, target) in enumerate(
+                ((cell_hbm, cell_ref), (offset_hbm, offset_ref), (weight_hbm, weight_ref))
+            )
+        ]
+        for copy in small:
+            copy.start()
 
     def half(at):
         row = [Row(east_ref[place(r), at, :] * sign, north_ref[place(r), at, :]) for r in range(STEPS)]
         pack_ref[FLUX_ROWS, at, :] = east_ref[place(0), at, :]
         pack_ref[FLUX_ROWS + 1, at, :] = north_ref[place(0), at, :]
         pack_ref[FLUX_ROWS + 2, at, :] = east_ref[place(1), at, :]
+        if which == 0:
+            for r in (1, 2):
+                lanes = (2 * r - 2) * LANES
+                pack_ref[EXTRA, at, lanes:lanes + LANES] = north_ref[place(r), at, :LANES]
+                pack_ref[EXTRA, at, lanes + LANES:lanes + 2 * LANES] = north_ref[place(r), at, width - LANES:]
         for c in range(parts):
             field = [state_ref[c, place(r), at, :] for r in range(STEPS)]
             for k in range(STEPS):
@@ -114,6 +149,17 @@
             copy.wait()
         half(pl.ds(h * HALF, HALF))
 
+    if which == 0:
+        for copy in small:
+            copy.wait()
+        n = 0
+        for point in range(offset_ref.shape[0]):
+            for c in range(parts):
+                target = (cell_ref[c] + offset_ref[point, c]).astype(jnp.float32)
+                pack_ref[EXTRA, n:n + 2, TARGETS:TARGETS + rows] = target
+                pack_ref[EXTRA, n:n + 2, WEIGHTS:WEIGHTS + rows] = weight_ref[point, c]
+                n += 2
+
 
 def as_column(row):
     count = row.shape[1]
@@ -123,28 +169,17 @@
 
 
 def sweep_kernel(
-    state_ref, east_ref, north_ref, pack_ref, middle_ref, ends_ref, column_ref,
+    state_ref, east_ref, north_ref, middle_ref, ends_ref, column_ref,
     field, plus_ref, minus_ref, centre_ref,
 ):
     parts, rows, levels, width = state_ref.shape[1:]
-    flip = 1 - parity()
-    sign = sign_of(flip)
-    end_row = flip * (rows - 1)
-    next_row = end_row + 1 - 2 * flip
 
     def half(at):
-        pack_ref[FLUX_ROWS, at, :] = east_ref[0, end_row, at, :]
-        pack_ref[FLUX_ROWS + 1, at, :] = north_ref[0, end_row, at, :]
-        pack_ref[FLUX_ROWS + 2, at, :] = east_ref[0, next_row, at, :]
-
         for k in range(STEPS):
             if k == 0:
                 read = lambda c, i: state_ref[0, c, i, at, :]
             else:
                 read = lambda c, i, slot=k - 1: field[slot, c, i]
-            leaving = jnp.maximum(east_ref[0, end_row, at, :] * sign, 0.0)
-            for c in range(parts):
-                pack_ref[2 * k + c, at, :] = leaving * read(c, end_row)
             west = [None] * parts
             here = [read(c, 0) for c in range(parts)]
             east_here = east_ref[0, 0, at, :]
@@ -194,42 +229,74 @@
     level_halves(levels, half)
 
 
-def ghost_kernel(
-    cell_ref, offset_ref, weight_ref, owner_ref, column_ref, north_hbm, spread_ref, partial_ref, first_rate, last_rate, sems
+def mix(targets, weights, cells, total):
+    for target, weight in zip(targets, weights):
+        total = total + jnp.where(as_column(target) == cells, as_column(weight), 0.0)
+    return total
+
+
+def ghost_base_kernel(
+    cell_ref, offset_ref, weight_ref, column_ref, north_ref, mixing_ref, partial_ref
 ):
     parts, _, rows, levels, _ = column_ref.shape
-    slots = spread_ref.shape[-1]
-    width = north_hbm.shape[-1]
-    copies = [
-        pltpu.make_async_copy(north_hbm.at[0, :, :, pl.ds(0, LANES)], first_rate, sems.at[0]),
-        pltpu.make_async_copy(north_hbm.at[0, :, :, pl.ds(width - LANES, LANES)], last_rate, sems.at[1]),
-    ]
-    for copy in copies:
-        copy.start()
-
-    here = lax.broadcasted_iota(jnp.int32, (slots, slots), 1)
-    placing = jnp.where(as_column(owner_ref[...]) == here, 1.0, 0.0)
+    slots = mixing_ref.shape[-1]
+    width = north_ref.shape[-1]
+    points = range(offset_ref.shape[0])
     cells = lax.broadcasted_iota(jnp.int32, (rows, slots), 1)
     for c in range(parts):
         for s in range(2):
-            mixing = jnp.zeros((rows, slots), jnp.float32)
-            for point in range(offset_ref.shape[0]):
-                target = as_column(cell_ref[c, s:s + 1, :] + offset_ref[point, c, s:s + 1, :])
-                mixing = mixing + jnp.where(target == cells, as_column(weight_ref[point, c, s:s + 1, :]), 0.0)
-            spread_ref[c, s] = jnp.dot(
-                mixing, placing, precision=lax.Precision.HIGHEST, preferred_element_type=jnp.float32
+            mixing_ref[c, s] = mix(
+                [cell_ref[c, s:s + 1, :] + offset_ref[point, c, s:s + 1, :] for point in points],
+                [weight_ref[point, c, s:s + 1, :] for point in points],
+                cells, jnp.zeros((rows, slots), jnp.float32),
             )
 
-    for copy in copies:
-        copy.wait()
     for c in range(parts):
         total = jnp.zeros((levels, slots), jnp.float32)
         for i in range(rows):
-            south = jnp.maximum(first_rate[i, :, :1], 0.0) * column_ref[c, 0, i, :, :1]
-            north = jnp.maximum(-last_rate[i, :, LANES - 1:], 0.0) * column_ref[c, 1, i, :, LANES - 1:]
-            total = total + south * spread_ref[c, 0, i:i + 1, :]
-            total = total + north * spread_ref[c, 1, i:i + 1, :]
+            south = jnp.maximum(north_ref[0, i, :, :1], 0.0) * column_ref[c, 0, i, :, :1]
+            north = jnp.maximum(-north_ref[0, i, :, width - 1:], 0.0) * column_ref[c, 1, i, :, LANES - 1:]
+            total = total + south * mixing_ref[c, 0, i:i + 1, :]
+            total = total + north * mixing_ref[c, 1, i:i + 1, :]
         partial_ref[c] = total
+
+
+def ghost_kernel(north_ref, other_ref, column_ref, mixing_ref, partial_ref, sum_ref, near_mixing):
+    parts, levels, slots = partial_ref.shape
+    rows = mixing_ref.shape[2]
+    width = north_ref.shape[-1]
+    flip = 1 - parity()
+    cells = lax.broadcasted_iota(jnp.int32, (rows, slots), 1).astype(jnp.float32)
+    points = (WEIGHTS - TARGETS) // LANES * 4
+    for c in range(parts):
+        for s in range(2):
+            at = [(point * parts + c) * 2 + s for point in range(points)]
+            near_mixing[c, s] = mix(
+                [other_ref[EXTRA, n:n + 1, TARGETS:TARGETS + rows] for n in at],
+                [other_ref[EXTRA, n:n + 1, WEIGHTS:WEIGHTS + rows] for n in at],
+                cells, jnp.zeros((rows, slots), jnp.float32),
+            )
+    for c in range(parts):
+        total = partial_ref[c]
+        for r in range(STEPS - 1):
+            i = r + flip * (rows - 1 - 2 * r)
+            south = jnp.maximum(north_ref[0, i, :, :1], 0.0) * column_ref[c, 0, r, :, :1]
+            north = jnp.maximum(-north_ref[0, i, :, width - 1:], 0.0) * column_ref[c, 1, r, :, LANES - 1:]
+            total = total + south * mixing_ref[c, 0, pl.ds(i, 1), :]
+            total = total + north * mixing_ref[c, 1, pl.ds(i, 1), :]
+            i = r + (1 - flip) * (rows - 1 - 2 * r)
+            if r == 0:
+                first_rate = other_ref[FLUX_ROWS + 1, :, :LANES]
+                last_rate = other_ref[FLUX_ROWS + 1, :, width - LANES:]
+            else:
+                lanes = (2 * r - 2) * LANES
+                first_rate = other_ref[EXTRA, :, lanes:lanes + LANES]
+                last_rate = other_ref[EXTRA, :, lanes + LANES:lanes + 2 * LANES]
+            south = jnp.maximum(first_rate[:, :1], 0.0) * column_ref[c, 0, STEPS - 1 + r, :, :1]
+            north = jnp.maximum(-last_rate[:, LANES - 1:], 0.0) * column_ref[c, 1, STEPS - 1 + r, :, LANES - 1:]
+            total = total + south * near_mixing[c, 0, pl.ds(i, 1), :]
+            total = total + north * near_mixing[c, 1, pl.ds(i, 1), :]
+        sum_ref[c] = total
 
 
 def mend_side(flip, east_ref, north_ref, mine_ref, other_ref, store, store_column):
@@ -261,14 +328,27 @@
             d3 = own[2].inward * c2
             for r, value in enumerate((d0, d1, d2, d3)):
                 store(c, r, at, value)
-            for r, pieces in enumerate(((a0, b0, c0), (b1, c1), (c2,))):
-                store_column(c, 0, r, at, sum(value[:, :LANES] for value in pieces))
-                store_column(c, 1, r, at, sum(value[:, width - LANES:] for value in pieces))
+            if store_column is not None:
+                tiles = (slice(0, LANES), slice(width - LANES, width))
+                for s, lanes in enumerate(tiles):
+                    tile = lambda value: value[:, lanes]
+                    rate = other_ref[EXTRA, at, s * LANES:(s + 1) * LANES]
+                    stays = 1.0 - jnp.abs(other_ref[FLUX_ROWS + 2, at, lanes]) - jnp.abs(rate)
+                    drift = jnp.maximum(rate if s == 0 else -rate, 0.0) * tile(bn2)
+                    cn2 = stays * tile(bn2) + pltpu.roll(drift, LANES - 1 if s == 0 else 1, 1)
+                    cn2 = cn2 + tile(near.outward) * tile(bn1)
+                    cn3 = tile(far.outward) * tile(bn2)
+                    sums = (
+                        tile(a0) + tile(b0) + tile(c0), tile(b1) + tile(c1), tile(c2),
+                        tile(n1) + tile(bn1) + tile(cn1), tile(bn2) + cn2, cn3,
+                    )
+                    for r, value in enumerate(sums):
+                        store_column(c, s, r, at, value)
 
     level_halves(levels, half)
 
 
-def mend_a_kernel(east_ref, north_ref, mine_ref, other_ref, ends_ref, middle_ref, out_ref, column_ref):
+def mend_a_kernel(east_ref, north_ref, mine_ref, other_ref, ends_ref, middle_ref, base_ref, out_ref, column_ref):
     parts, inner = middle_ref.shape[:2]
     flip = 1 - parity()
     turn = lambda r: r + flip * (STEPS - 1 - 2 * r)
@@ -285,57 +365,27 @@
             out_ref[c, i] = middle_ref[c, i]
 
 
-def mend_b_kernel(
-    east_ref, north_ref, mine_ref, other_ref, ends_ref, a_column_ref, spread_ref, partial_ref,
-    out_ref, sum_ref, b_column_ref,
-):
-    parts, levels, slots = partial_ref.shape
-    rows = east_ref.shape[1]
-    width = east_ref.shape[-1]
+def mend_b_kernel(east_ref, north_ref, mine_ref, other_ref, ends_ref, out_ref):
     flip = parity()
     turn = lambda r: r + flip * (STEPS - 1 - 2 * r)
 
     def store(c, r, at, value):
         out_ref[c, turn(r), at, :] = ends_ref[c, flip * STEPS + turn(r), at, :] + value
 
-    def store_column(c, s, r, at, value):
-        b_column_ref[c, s, r, at, :] = value
-
-    mend_side(flip, east_ref, north_ref, mine_ref, other_ref, store, store_column)
+    mend_side(flip, east_ref, north_ref, mine_ref, other_ref, store, None)
+
+
+def pick_kernel(total_ref, owner_ref, out_ref):
+    parts, share, mine = out_ref.shape
+    slots = owner_ref.shape[-1]
+    to_slot = lax.broadcasted_iota(jnp.int32, (slots, mine), 1) + lax.axis_index("hor") * mine
+    pick = jnp.where(as_column(owner_ref[...]) == to_slot, 1.0, 0.0)
     for c in range(parts):
-        total = partial_ref[c]
-        for side, column_ref in ((1 - flip, a_column_ref), (flip, b_column_ref)):
-            for r in range(STEPS - 1):
-                i = r + side * (rows - 1 - 2 * r)
-                south = jnp.maximum(north_ref[0, i, :, :1], 0.0) * column_ref[c, 0, r, :, :1]
-                north = jnp.maximum(-north_ref[0, i, :, width - 1:], 0.0) * column_ref[c, 1, r, :, LANES - 1:]
-                total = total + south * spread_ref[c, 0, pl.ds(i, 1), :]
-                total = total + north * spread_ref[c, 1, pl.ds(i, 1), :]
-        sum_ref[c] = total
-
-
-def pieces_kernel(total_ref, out_hbm, buffer, sem):
-    parts, levels, slots = total_ref.shape
-    peers, _, share, mine = buffer.shape
-    subs = levels // share
-    each = peers // subs
-    from_slot = lax.broadcasted_iota(jnp.int32, (slots, mine), 0)
-    to_slot = lax.broadcasted_iota(jnp.int32, (slots, mine), 1)
-    total = jnp.concatenate([total_ref[c] for c in range(parts)], 0)
-    for p in range(each):
-        pick = jnp.where(from_slot == to_slot + p * mine, 1.0, 0.0)
-        block = jnp.dot(total, pick, precision=lax.Precision.HIGHEST, preferred_element_type=jnp.float32)
-        for s in range(subs):
-            for c in range(parts):
-                at = c * levels + s * share
-                buffer[s * each + p, c] = block[at:at + share]
-    copy = pltpu.make_async_copy(buffer, out_hbm, sem)
-    copy.start()
-    copy.wait()
-
-
-def join_kernel(came_ref, out_ref):
-    out_ref[...] = jnp.sum(came_ref[...], 0)
+        chosen = jnp.zeros((share, slots), jnp.float32)
+        for s in range(total_ref.shape[1] // share):
+            block = total_ref[c, s * share:(s + 1) * share, :]
+            chosen = jnp.where(lax.axis_index("sub") == s, block, chosen)
+        out_ref[c] = jnp.dot(chosen, pick, precision=lax.Precision.HIGHEST, preferred_element_type=jnp.float32)
 
 
 def subtract_kernel(state_ref, a_ref, b_ref, out_hbm, buffer, sems):
@@ -384,30 +434,40 @@
     hbm = pl.BlockSpec(memory_space=pltpu.HBM)
     in_hbm = lambda value: pltpu.with_memory_space_constraint(value, pltpu.HBM)
 
-    first_pack = pl.pallas_call(
-        first_kernel,
-        in_specs=[hbm] * 3,
-        out_specs=vmem,
-        out_shape=f32(PACK_ROWS, levels, width),
-        scratch_shapes=[
-            pltpu.VMEM((parts, STEPS, levels, width), jnp.float32),
-            pltpu.VMEM((STEPS, levels, width), jnp.float32),
-            pltpu.VMEM((STEPS, levels, width), jnp.float32),
-            pltpu.SemaphoreType.DMA((levels // HALF, parts + 2)),
-        ],
-        compiler_params=PARAMS,
-        cost_estimate=cost(12 * levels * width * 13, 27 * row_bytes),
-        name="first_pack",
-    )(in_hbm(adjoint_state), in_hbm(courant_east), in_hbm(courant_north))
+    subs, hors = lax.axis_size("sub"), lax.axis_size("hor")
+    small = [parent_cell, stencil_offset, stencil_weight]
+
+    def pack(which):
+        extra = small if which == 0 else []
+        return pl.pallas_call(
+            functools.partial(pack_kernel, which),
+            in_specs=[hbm] * (3 + len(extra)),
+            out_specs=vmem,
+            out_shape=f32(PACK_ROWS + 1 - which, levels, width),
+            scratch_shapes=[
+                pltpu.VMEM((parts, STEPS, levels, width), jnp.float32),
+                pltpu.VMEM((STEPS, levels, width), jnp.float32),
+                pltpu.VMEM((STEPS, levels, width), jnp.float32),
+            ]
+            + [pltpu.VMEM(value.shape, value.dtype) for value in extra]
+            + [pltpu.SemaphoreType.DMA((levels // HALF, parts + 2))]
+            + [pltpu.SemaphoreType.DMA((3,)) for _ in extra[:1]],
+            compiler_params=PARAMS,
+            cost_estimate=cost(12 * levels * width * 13, 28 * row_bytes),
+            name="pack_" + "ab"[which],
+        )(*[in_hbm(value) for value in [adjoint_state, courant_east, courant_north] + extra])
+
+    first_pack = pack(0)
     first_came = alternating(first_pack, -1)
+    second_pack = pack(1)
+    second_came = alternating(second_pack, 1)
 
     state, east, north = adjoint_state, courant_east, courant_north
-    second_pack, middle, ends, columns = pl.pallas_call(
+    middle, ends, columns = pl.pallas_call(
         sweep_kernel,
         in_specs=[vmem] * 3,
-        out_specs=[vmem] * 4,
+        out_specs=[vmem] * 3,
         out_shape=[
-            f32(PACK_ROWS, levels, width),
             f32(parts, inner, levels, width),
             f32(parts, 2 * STEPS, levels, width),
             f32(parts, 2, rows, levels, LANES),
@@ -422,67 +482,58 @@
         cost_estimate=cost(8 * rows * levels * width * 13, 6 * rows * row_bytes),
         name="sweep",
     )(state, east, north)
-    second_came = alternating(second_pack, 1)
-
-    spread, partial = pl.pallas_call(
-        ghost_kernel,
-        in_specs=[vmem] * 5 + [hbm],
+
+    mixing, base = pl.pallas_call(
+        ghost_base_kernel,
+        in_specs=[vmem] * 5,
         out_specs=[vmem] * 2,
         out_shape=[f32(parts, 2, rows, slots), f32(parts, levels, slots)],
-        scratch_shapes=[
-            pltpu.VMEM((rows, levels, LANES), jnp.float32),
-            pltpu.VMEM((rows, levels, LANES), jnp.float32),
-            pltpu.SemaphoreType.DMA((2,)),
-        ],
         compiler_params=PARAMS,
         cost_estimate=cost(parts * rows * levels * slots * 8, 4 * rows * levels * LANES * 8),
-        name="ghost_sums",
-    )(parent_cell, stencil_offset, stencil_weight, owner_slot[None], columns, in_hbm(courant_north))
-
-    subs, hors = lax.axis_size("sub"), lax.axis_size("hor")
-
-    column_shape = (parts, 2, STEPS - 1, levels, LANES)
+        name="ghost_base",
+    )(*small, columns, north)
+
+    column_shape = (parts, 2, 2 * (STEPS - 1), levels, LANES)
     side_a, a_columns = pl.pallas_call(
         mend_a_kernel,
-        in_specs=[vmem] * 6,
+        in_specs=[vmem] * 7,
         out_specs=[vmem] * 2,
         out_shape=[f32(parts, inner + STEPS, levels, width), f32(*column_shape)],
         compiler_params=PARAMS,
         cost_estimate=cost(16 * levels * width * 13, 54 * row_bytes),
         name="mend_a",
-    )(east, north, second_pack, first_came, ends, middle)
+    )(east, north, second_pack, first_came, ends, middle, base)
     a_came = along(side_a, "sub", -1)
-    side_b, partial = pl.pallas_call(
+    total = pl.pallas_call(
+        ghost_kernel,
+        in_specs=[vmem] * 5,
+        out_specs=vmem,
+        out_shape=f32(parts, levels, slots),
+        scratch_shapes=[pltpu.VMEM((parts, 2, rows, slots), jnp.float32)],
+        compiler_params=PARAMS,
+        cost_estimate=cost(parts * levels * slots * 64, 8 * row_bytes),
+        name="ghost",
+    )(north, first_came, a_columns, mixing, base)
+    side_b = pl.pallas_call(
         mend_b_kernel,
-        in_specs=[vmem] * 8,
-        out_specs=[vmem] * 2,
-        out_shape=[f32(parts, STEPS, levels, width), f32(parts, levels, slots)],
-        scratch_shapes=[pltpu.VMEM(column_shape, jnp.float32)],
+        in_specs=[vmem] * 5,
+        out_specs=vmem,
+        out_shape=f32(parts, STEPS, levels, width),
         compiler_params=PARAMS,
         cost_estimate=cost(16 * levels * width * 13, 46 * row_bytes),
         name="mend_b",
-    )(east, north, first_pack, second_came, ends, a_columns, spread, partial)
+    )(east, north, first_pack, second_came, ends)
     b_came = along(side_b, "sub", -1)
 
-    piece = (subs * hors, parts, levels // subs, slots // hors)
-    pieces = pl.pallas_call(
-        pieces_kernel,
-        in_specs=[vmem],
-        out_specs=hbm,
-        out_shape=pltpu.HBM(piece, jnp.float32),
-        scratch_shapes=[pltpu.VMEM(piece, jnp.float32), pltpu.SemaphoreType.DMA],
-        compiler_params=PARAMS,
-        name="pieces",
-    )(partial)
-    pieces = lax.all_to_all(pieces, ("sub", "hor"), 0, 0, tiled=True)
+    total = added_up(total)
     boundary_gradient = pl.pallas_call(
-        join_kernel,
-        in_specs=[vmem],
+        pick_kernel,
+        in_specs=[vmem] * 2,
         out_specs=vmem,
         out_shape=f32(parts, levels // subs, slots // hors),
         compiler_params=PARAMS,
-        name="join",
-    )(pieces)
+        name="pick",
+    )(total, owner_slot[None])
 
     adjoint_result = pl.pallas_call(
         subtract_kernel,

time: 39 us -> 39.4 us (1.010)
  blocking collectives: 14.7 us -> 0 us
  starting transfers between devices: 9.6 us -> 18.8 us
  waiting for transfers between devices: 3.25 us -> 8.94 us
    all_to_all x1 -> x0, blocking collectives: 14.7 us -> none  [local(): pieces = lax.all_to_all(pieces, ('sub', 'hor'), 0, 0, tiled=True)]
    ppermute x0 -> x4, starting transfers between devices: none -> 9.05 us  [added_up(): lax.ppermute(value, axis, [(i, i ^ step) for i in range(sizes[axis])])]
    ppermute x0 -> x4, waiting for transfers between devices: none -> 6.19 us  [added_up(): lax.ppermute(value, axis, [(i, i ^ step) for i in range(sizes[axis])])]
    ppermute x2, waiting for transfers between devices: 3.24 us -> 2.75 us  [alternating(): return lax.ppermute(value, ('sub', 'hor'), pairs)]
    pallas_call x7 -> x8, Pallas kernels: 9.29 us -> 9.38 us  [the longest x2 3.5 us: pack(): pl.pallas_call(functools.partial(pack_kernel, which), in_specs=[hbm] * (3...]
  transfers between devices with their start and end apart: 4 -> 8, of which waited for: 2 -> 6; matrix products, arithmetic and copies ran while one was open for 0% -> 0% of each run, Pallas kernels for 19% -> 19%
where the time goes in v8:
time: 39.4 us; the launch traced here: 39.1 us
  starting transfers between devices  18.8 us (48%)
  Pallas kernels  10.4 us (26%)
  waiting for transfers between devices  8.94 us (23%)
  between operations  0.82 us (2%)
    ppermute x4, starting transfers between devices, added_up(): lax.ppermute(value, axis, [(i, i ^ step) for i in range(sizes[axis])])  9.05 us
    ppermute x2, starting transfers between devices, alternating(): return lax.ppermute(value, ('sub', 'hor'), pairs)  7.15 us
    ppermute x4, waiting for transfers between devices, added_up(): lax.ppermute(value, axis, [(i, i ^ step) for i in range(sizes[axis])])  6.19 us
    pallas_call x2, Pallas kernels, pack(): pl.pallas_call(functools.partial(pack_kernel, which), in_specs=[hbm] * (3...  3.5 us
    pallas_call x1, Pallas kernels, local(): pl.pallas_call(sweep_kernel, in_specs=[vmem] * 3, out_specs=[vmem] * 3, o...  2.9 us
    ppermute x2, waiting for transfers between devices, alternating(): return lax.ppermute(value, ('sub', 'hor'), pairs)  2.75 us
    ppermute x2, starting transfers between devices, along(): return lax.ppermute(value, axis, pairs)  2.58 us
    pallas_call x1, Pallas kernels, local(): pl.pallas_call(subtract_kernel, in_specs=[vmem] * 3, out_specs=hbm, out_s...  1.07 us
  transfers between devices with their start and end apart: 8, of which 6 were waited for; matrix products, arithmetic and copies ran while one was open for 0% of the time, Pallas kernels for 19%

profile of v8, /device:TPU:0, one launch (start us, length us, event | category | flops | bytes accessed | tf_op | source)
XLA Modules:
  0.0 39.1 jit_solution(10203242174994546290)
XLA Ops:
  0.6 1.8 %pack_a.1.mine_ref = f32[12,16,768]{2,1,0:T(8,128)S(1)} custom-call(f32[1,2,12,16,768]{4,3,2,1,0:T(8,128)} %state_ref.3, f32[1,12,16,768]{3,2,1,0:T(8,128)} %east_ref.5, f32[1,12,16,768]{3,2,1,0:T(8,128)} %north_ref.9, s32[2,2,12]{2,1,0:T(2,128)} %cell_ref.1, s32[4,2,2,12]{3,2,1,0:T(2,128)} %offset_ref.1, f32[4,2,2,12]{3,2,1,0:T(2,128)} %weight_ref.1), custom_call_target="tpu_custom_call" | custom-call | flops 1916928 | bytes 1376256 | tf_op jit(solution)/shard_map/pack_a/pallas_call | solution.py:442
  2.4 0.0 copy-start.1
  2.5 1.4 %collective-permute-start = (f32[12,16,768]{2,1,0:T(8,128)S(1)}, f32[12,16,768]{2,1,0:T(8,128)S(1)}, u32[]{:S(2)}, u32[]{:S(2)}) collective-permute-start(f32[12,16,768]{2,1,0:T(8,128)S(1)} %pack_a.1.mine_ref), channel_id=1, source_target_pairs={{1,0},{2,1},{3,2},{4,5},{5,6},{6,7},{9,8},{10,9},{11,10},{12,13},{... | collective-permute-start | bytes 1769480 | tf_op jit(solution)/shard_map/ppermute | solution.py:32
  3.9 1.7 %pack_b.1.mine_ref = f32[11,16,768]{2,1,0:T(8,128)S(1)} custom-call(f32[1,2,12,16,768]{4,3,2,1,0:T(8,128)} %state_ref.3, f32[1,12,16,768]{3,2,1,0:T(8,128)} %east_ref.5, f32[1,12,16,768]{3,2,1,0:T(8,128)} %north_ref.9), custom_call_target="tpu_custom_call" | custom-call | flops 1916928 | bytes 1376256 | tf_op jit(solution)/shard_map/pack_b/pallas_call | solution.py:442
  5.7 5.7 %collective-permute-start.2 = (f32[11,16,768]{2,1,0:T(8,128)S(1)}, f32[11,16,768]{2,1,0:T(8,128)S(1)}, u32[]{:S(2)}, u32[]{:S(2)}) collective-permute-start(f32[11,16,768]{2,1,0:T(8,128)S(1)} %pack_b.1.mine_ref), channel_id=1, source_target_pairs={{0,1},{1,2},{2,3},{5,4},{6,5},{7,6},{8,9},{9,10},{10,11},{13,12},{... | collective-permute-start | bytes 1622024 | tf_op jit(solution)/shard_map/ppermute | solution.py:32
  11.4 2.9 %sweep.1 = (f32[2,4,16,768]{3,2,1,0:T(8,128)S(1)}, f32[2,8,16,768]{3,2,1,0:T(8,128)S(1)}, f32[2,2,12,16,128]{4,3,2,1,0:T(8,128)S(1)}) custom-call(f32[1,2,12,16,768]{4,3,2,1,0:T(8,128)S(1)} %copy-done.1, f32[1,12,16,768]{3,2,1,0:T(8,128)S(1)} %copy-done.2, f32[1,12,16,768]{3,2,1,0:T(8,128)S(1)} %copy-done), custom_call_target="tpu_custom_call" | custom-call | flops 15335424 | bytes 3538944 | tf_op jit(solution)/shard_map/sweep/pallas_call | solution.py:466
  14.3 0.4 ghost_base.1
  14.7 2.5 %collective-permute-done.other_ref = f32[12,16,768]{2,1,0:T(8,128)S(1)} collective-permute-done((f32[12,16,768]{2,1,0:T(8,128)S(1)}, f32[12,16,768]{2,1,0:T(8,128)S(1)}, u32[]{:S(2)}, u32[]{:S(2)}) %collective-permute-start) | collective-permute-done | bytes 589856 | tf_op jit(solution)/shard_map/ppermute | solution.py:32
  17.2 0.8 %mend_a.1 = (f32[2,8,16,768]{3,2,1,0:T(8,128)S(1)}, f32[2,2,6,16,128]{4,3,2,1,0:T(8,128)S(1)}) custom-call(f32[1,12,16,768]{3,2,1,0:T(8,128)S(1)} %copy-done.2, f32[1,12,16,768]{3,2,1,0:T(8,128)S(1)} %copy-done, f32[11,16,768]{2,1,0:T(8,128)S(1)} %pack_b.1.mine_ref, f32[12,16,768]{2,1,0:T(8,128)S(1)} %collective-permute-done.other_ref, ...), custom_call_target="tpu_custom_call" | custom-call | flops 2555904 | bytes 2654208 | tf_op jit(solution)/shard_map/mend_a/pallas_call | solution.py:497
  18.0 1.3 %collective-permute-start.1 = (f32[2,8,16,768]{3,2,1,0:T(8,128)S(1)}, f32[2,8,16,768]{3,2,1,0:T(8,128)S(1)}, u32[]{:S(2)}, u32[]{:S(2)}) collective-permute-start(f32[2,8,16,768]{3,2,1,0:T(8,128)S(1)} %get-tuple-element.13), channel_id=1, source_target_pairs={{4,0},{8,4},{12,8},{5,1},{9,5},{13,9},{6,2},{10,6},{14,10},{7,3},{... | collective-permute-start | bytes 2359304 | tf_op jit(solution)/shard_map/ppermute | solution.py:23
  19.3 0.3 collective-permute-done.2.other_ref
  19.6 0.8 %mend_b.1 = f32[2,4,16,768]{3,2,1,0:T(8,128)S(1)} custom-call(f32[1,12,16,768]{3,2,1,0:T(8,128)S(1)} %copy-done.2, f32[1,12,16,768]{3,2,1,0:T(8,128)S(1)} %copy-done, f32[12,16,768]{2,1,0:T(8,128)S(1)} %pack_a.1.mine_ref, f32[11,16,768]{2,1,0:T(8,128)S(1)} %collective-permute-done.2.other_ref, f32[2,8,16,768]{3,2,1,0:T(8,128)S(1)} %get-tuple-element.9.ends_ref), custom_call_target="tpu_custom_call" | custom-call | flops 2555904 | bytes 2260992 | tf_op jit(solution)/shard_map/mend_b/pallas_call | solution.py:517
  20.3 1.3 %collective-permute-start.3 = (f32[2,4,16,768]{3,2,1,0:T(8,128)S(1)}, f32[2,4,16,768]{3,2,1,0:T(8,128)S(1)}, u32[]{:S(2)}, u32[]{:S(2)}) collective-permute-start(f32[2,4,16,768]{3,2,1,0:T(8,128)S(1)} %mend_b.1), channel_id=1, source_target_pairs={{4,0},{8,4},{12,8},{5,1},{9,5},{13,9},{6,2},{10,6},{14,10},{7,3},{... | collective-permute-start | bytes 1179656 | tf_op jit(solution)/shard_map/ppermute | solution.py:23
  21.6 0.2 ghost.1
  21.9 2.1 %collective-permute-start.4 = (f32[2,16,32]{2,1,0:T(8,128)S(1)}, f32[2,16,32]{2,1,0:T(8,128)S(1)}, u32[]{:S(2)}, u32[]{:S(2)}) collective-permute-start(f32[2,16,32]{2,1,0:T(8,128)S(1)} %ghost.1), channel_id=1, source_target_pairs={{0,4},{4,0},{8,12},{12,8},{1,5},{5,1},{9,13},{13,9},{2,6},{6,2},{1... | collective-permute-start | bytes 12296 | tf_op jit(solution)/shard_map/ppermute | solution.py:44
  24.0 0.9 %collective-permute-done.4 = f32[2,16,32]{2,1,0:T(8,128)S(1)} collective-permute-done((f32[2,16,32]{2,1,0:T(8,128)S(1)}, f32[2,16,32]{2,1,0:T(8,128)S(1)}, u32[]{:S(2)}, u32[]{:S(2)}) %collective-permute-start.4) | collective-permute-done | bytes 4128 | tf_op jit(solution)/shard_map/ppermute | solution.py:44
  24.9 2.0 %collective-permute-start.5 = (f32[2,16,32]{2,1,0:T(8,128)S(1)}, f32[2,16,32]{2,1,0:T(8,128)S(1)}, u32[]{:S(2)}, u32[]{:S(2)}) collective-permute-start(f32[2,16,32]{2,1,0:T(8,128)S(1)} %add.12), channel_id=1, source_target_pairs={{0,1},{1,0},{2,3},{3,2},{4,5},{5,4},{6,7},{7,6},{8,9},{9,8},{10,11... | collective-permute-start | bytes 12296 | tf_op jit(solution)/shard_map/ppermute | solution.py:44
  26.9 1.7 %collective-permute-done.5 = f32[2,16,32]{2,1,0:T(8,128)S(1)} collective-permute-done((f32[2,16,32]{2,1,0:T(8,128)S(1)}, f32[2,16,32]{2,1,0:T(8,128)S(1)}, u32[]{:S(2)}, u32[]{:S(2)}) %collective-permute-start.5) | collective-permute-done | bytes 4128 | tf_op jit(solution)/shard_map/ppermute | solution.py:44
  28.7 3.0 %collective-permute-start.6 = (f32[2,16,32]{2,1,0:T(8,128)S(1)}, f32[2,16,32]{2,1,0:T(8,128)S(1)}, u32[]{:S(2)}, u32[]{:S(2)}) collective-permute-start(f32[2,16,32]{2,1,0:T(8,128)S(1)} %add.13), channel_id=1, source_target_pairs={{0,2},{1,3},{2,0},{3,1},{4,6},{5,7},{6,4},{7,5},{8,10},{9,11},{10,... | collective-permute-start | bytes 12296 | tf_op jit(solution)/shard_map/ppermute | solution.py:44
  31.7 1.7 %collective-permute-done.6 = f32[2,16,32]{2,1,0:T(8,128)S(1)} collective-permute-done((f32[2,16,32]{2,1,0:T(8,128)S(1)}, f32[2,16,32]{2,1,0:T(8,128)S(1)}, u32[]{:S(2)}, u32[]{:S(2)}) %collective-permute-start.6) | collective-permute-done | bytes 4128 | tf_op jit(solution)/shard_map/ppermute | solution.py:44
  33.4 1.9 %collective-permute-start.7 = (f32[2,16,32]{2,1,0:T(8,128)S(1)}, f32[2,16,32]{2,1,0:T(8,128)S(1)}, u32[]{:S(2)}, u32[]{:S(2)}) collective-permute-start(f32[2,16,32]{2,1,0:T(8,128)S(1)} %add.14), channel_id=1, source_target_pairs={{0,8},{4,12},{8,0},{12,4},{1,9},{5,13},{9,1},{13,5},{2,10},{6,14},... | collective-permute-start | bytes 12296 | tf_op jit(solution)/shard_map/ppermute | solution.py:44
  35.3 1.8 %collective-permute-done.7 = f32[2,16,32]{2,1,0:T(8,128)S(1)} collective-permute-done((f32[2,16,32]{2,1,0:T(8,128)S(1)}, f32[2,16,32]{2,1,0:T(8,128)S(1)}, u32[]{:S(2)}, u32[]{:S(2)}) %collective-permute-start.7) | collective-permute-done | bytes 4128 | tf_op jit(solution)/shard_map/ppermute | solution.py:44
  37.1 0.8 %pick.1 = f32[2,4,8]{2,1,0:T(4,128)} custom-call(f32[2,16,32]{2,1,0:T(8,128)S(1)} %add.15.total_ref, s32[1,32]{1,0:T(1,128)S(1)} %bitcast.1), custom_call_target="tpu_custom_call" | custom-call | tf_op jit(solution)/shard_map/pick/pallas_call | solution.py:529
  38.0 1.1 %subtract.1 = f32[1,2,12,16,768]{4,3,2,1,0:T(8,128)} custom-call(f32[1,2,12,16,768]{4,3,2,1,0:T(8,128)S(1)} %copy-done.1, f32[2,8,16,768]{3,2,1,0:T(8,128)S(1)} %collective-permute-done.1.a_ref, f32[2,4,16,768]{3,2,1,0:T(8,128)S(1)} %collective-permute-done.3.b_ref), custom_call_target="tpu_custom_call" | custom-call | flops 294912 | bytes 3538944 | tf_op jit(solution)/shard_map/subtract/pallas_call | solution.py:538
  (19 shorter events, 0.1 us)
Async XLA Ops:
  2.4 9.0 %copy-start = (f32[1,12,16,768]{3,2,1,0:T(8,128)S(1)}, f32[1,12,16,768]{3,2,1,0:T(8,128)}, u32[]{:S(2)}) copy-start(f32[1,12,16,768]{3,2,1,0:T(8,128)} %north_ref.9) | copy-start | bytes 1769476
  2.4 9.0 %copy-start.1 = (f32[1,2,12,16,768]{4,3,2,1,0:T(8,128)S(1)}, f32[1,2,12,16,768]{4,3,2,1,0:T(8,128)}, u32[]{:S(2)}) copy-start(f32[1,2,12,16,768]{4,3,2,1,0:T(8,128)} %state_ref.3) | copy-start | bytes 3538948
  2.4 9.0 %copy-start.2 = (f32[1,12,16,768]{3,2,1,0:T(8,128)S(1)}, f32[1,12,16,768]{3,2,1,0:T(8,128)}, u32[]{:S(2)}) copy-start(f32[1,12,16,768]{3,2,1,0:T(8,128)} %east_ref.5) | copy-start | bytes 1769476
  2.5 14.7 %collective-permute-start = (f32[12,16,768]{2,1,0:T(8,128)S(1)}, f32[12,16,768]{2,1,0:T(8,128)S(1)}, u32[]{:S(2)}, u32[]{:S(2)}) collective-permute-start(f32[12,16,768]{2,1,0:T(8,128)S(1)} %pack_a.1.mine_ref), channel_id=1, source_target_pairs={{1,0},{2,1},{3,2},{4,5},{5,6},{6,7},{9,8},{10,9},{11,10},{12,13},{... | collective-permute-start | bytes 1769480 | tf_op jit(solution)/shard_map/ppermute | solution.py:32
  5.6 8.7 %copy-start.3 = (s32[4,2,2,12]{3,2,1,0:T(2,128)S(1)}, s32[4,2,2,12]{3,2,1,0:T(2,128)}, u32[]{:S(2)}) copy-start(s32[4,2,2,12]{3,2,1,0:T(2,128)} %offset_ref.1) | copy-start | bytes 2308
  5.6 8.7 %copy-start.4 = (f32[4,2,2,12]{3,2,1,0:T(2,128)S(1)}, f32[4,2,2,12]{3,2,1,0:T(2,128)}, u32[]{:S(2)}) copy-start(f32[4,2,2,12]{3,2,1,0:T(2,128)} %weight_ref.1) | copy-start | bytes 2308
  5.6 8.7 %copy-start.5 = (s32[2,2,12]{2,1,0:T(2,128)S(1)}, s32[2,2,12]{2,1,0:T(2,128)}, u32[]{:S(2)}) copy-start(s32[2,2,12]{2,1,0:T(2,128)} %cell_ref.1) | copy-start | bytes 580
  5.7 13.9 %collective-permute-start.2 = (f32[11,16,768]{2,1,0:T(8,128)S(1)}, f32[11,16,768]{2,1,0:T(8,128)S(1)}, u32[]{:S(2)}, u32[]{:S(2)}) collective-permute-start(f32[11,16,768]{2,1,0:T(8,128)S(1)} %pack_b.1.mine_ref), channel_id=1, source_target_pairs={{0,1},{1,2},{2,3},{5,4},{6,5},{7,6},{8,9},{9,10},{10,11},{13,12},{... | collective-permute-start | bytes 1622024 | tf_op jit(solution)/shard_map/ppermute | solution.py:32
  18.0 20.0 %collective-permute-start.1 = (f32[2,8,16,768]{3,2,1,0:T(8,128)S(1)}, f32[2,8,16,768]{3,2,1,0:T(8,128)S(1)}, u32[]{:S(2)}, u32[]{:S(2)}) collective-permute-start(f32[2,8,16,768]{3,2,1,0:T(8,128)S(1)} %get-tuple-element.13), channel_id=1, source_target_pairs={{4,0},{8,4},{12,8},{5,1},{9,5},{13,9},{6,2},{10,6},{14,10},{7,3},{... | collective-permute-start | bytes 2359304 | tf_op jit(solution)/shard_map/ppermute | solution.py:23
  20.3 16.8 %copy-start.6 = (s32[32]{0:T(128)S(1)}, s32[32]{0:T(128)}, u32[]{:S(2)}) copy-start(s32[32]{0:T(128)} %param.13) | copy-start | bytes 388
  20.3 17.6 %collective-permute-start.3 = (f32[2,4,16,768]{3,2,1,0:T(8,128)S(1)}, f32[2,4,16,768]{3,2,1,0:T(8,128)S(1)}, u32[]{:S(2)}, u32[]{:S(2)}) collective-permute-start(f32[2,4,16,768]{3,2,1,0:T(8,128)S(1)} %mend_b.1), channel_id=1, source_target_pairs={{4,0},{8,4},{12,8},{5,1},{9,5},{13,9},{6,2},{10,6},{14,10},{7,3},{... | collective-permute-start | bytes 1179656 | tf_op jit(solution)/shard_map/ppermute | solution.py:23
  21.9 3.0 %collective-permute-start.4 = (f32[2,16,32]{2,1,0:T(8,128)S(1)}, f32[2,16,32]{2,1,0:T(8,128)S(1)}, u32[]{:S(2)}, u32[]{:S(2)}) collective-permute-start(f32[2,16,32]{2,1,0:T(8,128)S(1)} %ghost.1), channel_id=1, source_target_pairs={{0,4},{4,0},{8,12},{12,8},{1,5},{5,1},{9,13},{13,9},{2,6},{6,2},{1... | collective-permute-start | bytes 12296 | tf_op jit(solution)/shard_map/ppermute | solution.py:44
  24.9 3.7 %collective-permute-start.5 = (f32[2,16,32]{2,1,0:T(8,128)S(1)}, f32[2,16,32]{2,1,0:T(8,128)S(1)}, u32[]{:S(2)}, u32[]{:S(2)}) collective-permute-start(f32[2,16,32]{2,1,0:T(8,128)S(1)} %add.12), channel_id=1, source_target_pairs={{0,1},{1,0},{2,3},{3,2},{4,5},{5,4},{6,7},{7,6},{8,9},{9,8},{10,11... | collective-permute-start | bytes 12296 | tf_op jit(solution)/shard_map/ppermute | solution.py:44
  28.7 4.7 %collective-permute-start.6 = (f32[2,16,32]{2,1,0:T(8,128)S(1)}, f32[2,16,32]{2,1,0:T(8,128)S(1)}, u32[]{:S(2)}, u32[]{:S(2)}) collective-permute-start(f32[2,16,32]{2,1,0:T(8,128)S(1)} %add.13), channel_id=1, source_target_pairs={{0,2},{1,3},{2,0},{3,1},{4,6},{5,7},{6,4},{7,5},{8,10},{9,11},{10,... | collective-permute-start | bytes 12296 | tf_op jit(solution)/shard_map/ppermute | solution.py:44
  33.4 3.7 %collective-permute-start.7 = (f32[2,16,32]{2,1,0:T(8,128)S(1)}, f32[2,16,32]{2,1,0:T(8,128)S(1)}, u32[]{:S(2)}, u32[]{:S(2)}) collective-permute-start(f32[2,16,32]{2,1,0:T(8,128)S(1)} %add.14), channel_id=1, source_target_pairs={{0,8},{4,12},{8,0},{12,4},{1,9},{5,13},{9,1},{13,5},{2,10},{6,14},... | collective-permute-start | bytes 12296 | tf_op jit(solution)/shard_map/ppermute | solution.py:44

commit v9 on v8

--- a/solution.py
+++ b/solution.py
@@ -33,15 +33,19 @@
 
 
 def added_up(value):
-    sizes = {axis: lax.axis_size(axis) for axis in ("sub", "hor")}
+    sizes = {axis: lax.axis_size(axis) for axis in ("hor", "sub")}
     if any(size & (size - 1) for size in sizes.values()):
         return lax.psum(value, ("sub", "hor"))
-    steps = {axis: [1 << n for n in range(size.bit_length() - 1)] for axis, size in sizes.items()}
-    order = [("sub", step) for step in steps["sub"][:1]]
-    order += [("hor", step) for step in steps["hor"]]
-    order += [("sub", step) for step in steps["sub"][1:]]
-    for axis, step in order:
-        value = value + lax.ppermute(value, axis, [(i, i ^ step) for i in range(sizes[axis])])
+    for axis, size in sizes.items():
+        step = 1
+        while step < size:
+            group = min(4, size // step)
+            came = [
+                lax.ppermute(value, axis, [(i, i ^ (step * j)) for i in range(size)])
+                for j in range(1, group)
+            ]
+            value = sum(came, value)
+            step *= group
     return value
 
 
@@ -91,16 +95,19 @@
     if which == 0:
         state_hbm, east_hbm, north_hbm, cell_hbm, offset_hbm, weight_hbm = refs[:6]
         pack_ref, state_ref, east_ref, north_ref, cell_ref, offset_ref, weight_ref, sems, small_sems = refs[6:]
+        parts, rows, levels, width = state_hbm.shape[1:]
     else:
-        state_hbm, east_hbm, north_hbm, pack_ref, state_ref, east_ref, north_ref, sems = refs
-    parts, rows, levels, width = state_hbm.shape[1:]
+        state_ref, east_ref, north_ref, pack_ref = refs
+        parts, rows, levels, width = state_ref.shape[1:]
+        state_ref, east_ref, north_ref = state_ref.at[0], east_ref.at[0], north_ref.at[0]
     flip = parity() if which == 0 else 1 - parity()
     sign = sign_of(flip)
     at_end = pl.ds(flip * (rows - STEPS), STEPS)
-    place = lambda r: r + flip * (STEPS - 1 - 2 * r)
+    before = 0 if which == 0 else flip * (rows - STEPS)
+    place = lambda r: before + r + flip * (STEPS - 1 - 2 * r)
     halves = levels // HALF
-    copies = []
-    for h in range(halves):
+    copies = [[]] * halves
+    for h in range(halves if which == 0 else 0):
         at = pl.ds(h * HALF, HALF)
         sem = sems.at[h]
         batch = [
@@ -109,7 +116,7 @@
         ]
         batch.append(pltpu.make_async_copy(east_hbm.at[0, at_end, at], east_ref.at[:, at], sem.at[parts]))
         batch.append(pltpu.make_async_copy(north_hbm.at[0, at_end, at], north_ref.at[:, at], sem.at[parts + 1]))
-        copies.append(batch)
+        copies[h] = batch
         for copy in batch:
             copy.start()
     if which == 0:
@@ -348,21 +355,17 @@
     level_halves(levels, half)
 
 
-def mend_a_kernel(east_ref, north_ref, mine_ref, other_ref, ends_ref, middle_ref, base_ref, out_ref, column_ref):
-    parts, inner = middle_ref.shape[:2]
+def mend_a_kernel(east_ref, north_ref, mine_ref, other_ref, ends_ref, base_ref, out_ref, column_ref):
     flip = 1 - parity()
     turn = lambda r: r + flip * (STEPS - 1 - 2 * r)
 
     def store(c, r, at, value):
-        out_ref[c, inner + turn(r), at, :] = ends_ref[c, flip * STEPS + turn(r), at, :] + value
+        out_ref[c, turn(r), at, :] = ends_ref[c, flip * STEPS + turn(r), at, :] + value
 
     def store_column(c, s, r, at, value):
         column_ref[c, s, r, at, :] = value
 
     mend_side(flip, east_ref, north_ref, mine_ref, other_ref, store, store_column)
-    for c in range(parts):
-        for i in range(inner):
-            out_ref[c, i] = middle_ref[c, i]
 
 
 def mend_b_kernel(east_ref, north_ref, mine_ref, other_ref, ends_ref, out_ref):
@@ -375,8 +378,25 @@
     mend_side(flip, east_ref, north_ref, mine_ref, other_ref, store, None)
 
 
-def pick_kernel(total_ref, owner_ref, out_ref):
-    parts, share, mine = out_ref.shape
+def finish_kernel(
+    total_ref, owner_ref, state_ref, middle_ref, a_ref, b_ref, out_hbm, gradient_ref, buffer, sems
+):
+    parts, rows = state_ref.shape[1:3]
+    inner = rows - 2 * STEPS
+    a_start = parity() * (rows - STEPS)
+    b_start = (1 - parity()) * (rows - STEPS)
+    copies = []
+    for start, other in ((STEPS, middle_ref), (a_start, a_ref), (b_start, b_ref)):
+        for c in range(parts):
+            count = other.shape[1]
+            for r in range(count):
+                buffer[c, start + r] = state_ref[0, c, start + r] - other[c, r]
+            at = pl.ds(start, count)
+            copy = pltpu.make_async_copy(buffer.at[c, at], out_hbm.at[0, c, at], sems.at[len(copies)])
+            copy.start()
+            copies.append(copy)
+
+    share, mine = gradient_ref.shape[1:]
     slots = owner_ref.shape[-1]
     to_slot = lax.broadcasted_iota(jnp.int32, (slots, mine), 1) + lax.axis_index("hor") * mine
     pick = jnp.where(as_column(owner_ref[...]) == to_slot, 1.0, 0.0)
@@ -385,25 +405,7 @@
         for s in range(total_ref.shape[1] // share):
             block = total_ref[c, s * share:(s + 1) * share, :]
             chosen = jnp.where(lax.axis_index("sub") == s, block, chosen)
-        out_ref[c] = jnp.dot(chosen, pick, precision=lax.Precision.HIGHEST, preferred_element_type=jnp.float32)
-
-
-def subtract_kernel(state_ref, a_ref, b_ref, out_hbm, buffer, sems):
-    parts, rows = state_ref.shape[1:3]
-    inner = rows - 2 * STEPS
-    a_start = parity() * (rows - STEPS)
-    b_start = (1 - parity()) * (rows - STEPS)
-    copies = []
-    for start, other, first, count in (
-        (STEPS, a_ref, 0, inner), (a_start, a_ref, inner, STEPS), (b_start, b_ref, 0, STEPS),
-    ):
-        for c in range(parts):
-            for r in range(count):
-                buffer[c, start + r] = state_ref[0, c, start + r] - other[c, first + r]
-            at = pl.ds(start, count)
-            copy = pltpu.make_async_copy(buffer.at[c, at], out_hbm.at[0, c, at], sems.at[len(copies)])
-            copy.start()
-            copies.append(copy)
+        gradient_ref[c] = jnp.dot(chosen, pick, precision=lax.Precision.HIGHEST, preferred_element_type=jnp.float32)
     for copy in copies:
         copy.wait()
 
@@ -437,29 +439,31 @@
     subs, hors = lax.axis_size("sub"), lax.axis_size("hor")
     small = [parent_cell, stencil_offset, stencil_weight]
 
-    def pack(which):
-        extra = small if which == 0 else []
-        return pl.pallas_call(
-            functools.partial(pack_kernel, which),
-            in_specs=[hbm] * (3 + len(extra)),
-            out_specs=vmem,
-            out_shape=f32(PACK_ROWS + 1 - which, levels, width),
-            scratch_shapes=[
-                pltpu.VMEM((parts, STEPS, levels, width), jnp.float32),
-                pltpu.VMEM((STEPS, levels, width), jnp.float32),
-                pltpu.VMEM((STEPS, levels, width), jnp.float32),
-            ]
-            + [pltpu.VMEM(value.shape, value.dtype) for value in extra]
-            + [pltpu.SemaphoreType.DMA((levels // HALF, parts + 2))]
-            + [pltpu.SemaphoreType.DMA((3,)) for _ in extra[:1]],
-            compiler_params=PARAMS,
-            cost_estimate=cost(12 * levels * width * 13, 28 * row_bytes),
-            name="pack_" + "ab"[which],
-        )(*[in_hbm(value) for value in [adjoint_state, courant_east, courant_north] + extra])
-
-    first_pack = pack(0)
+    packing = dict(
+        out_specs=vmem, compiler_params=PARAMS, cost_estimate=cost(12 * levels * width * 13, 28 * row_bytes)
+    )
+    first_pack = pl.pallas_call(
+        functools.partial(pack_kernel, 0),
+        in_specs=[hbm] * 6,
+        out_shape=f32(PACK_ROWS + 1, levels, width),
+        scratch_shapes=[
+            pltpu.VMEM((parts, STEPS, levels, width), jnp.float32),
+            pltpu.VMEM((STEPS, levels, width), jnp.float32),
+            pltpu.VMEM((STEPS, levels, width), jnp.float32),
+        ]
+        + [pltpu.VMEM(value.shape, value.dtype) for value in small]
+        + [pltpu.SemaphoreType.DMA((levels // HALF, parts + 2)), pltpu.SemaphoreType.DMA((3,))],
+        name="pack_a",
+        **packing,
+    )(*[in_hbm(value) for value in [adjoint_state, courant_east, courant_north] + small])
+    second_pack = pl.pallas_call(
+        functools.partial(pack_kernel, 1),
+        in_specs=[vmem] * 3,
+        out_shape=f32(PACK_ROWS, levels, width),
+        name="pack_b",
+        **packing,
+    )(adjoint_state, courant_east, courant_north)
     first_came = alternating(first_pack, -1)
-    second_pack = pack(1)
     second_came = alternating(second_pack, 1)
 
     state, east, north = adjoint_state, courant_east, courant_north
@@ -482,6 +486,7 @@
         cost_estimate=cost(8 * rows * levels * width * 13, 6 * rows * row_bytes),
         name="sweep",
     )(state, east, north)
+    middle_came = along(middle, "sub", -1)
 
     mixing, base = pl.pallas_call(
         ghost_base_kernel,
@@ -496,13 +501,13 @@
     column_shape = (parts, 2, 2 * (STEPS - 1), levels, LANES)
     side_a, a_columns = pl.pallas_call(
         mend_a_kernel,
-        in_specs=[vmem] * 7,
+        in_specs=[vmem] * 6,
         out_specs=[vmem] * 2,
-        out_shape=[f32(parts, inner + STEPS, levels, width), f32(*column_shape)],
+        out_shape=[f32(parts, STEPS, levels, width), f32(*column_shape)],
         compiler_params=PARAMS,
         cost_estimate=cost(16 * levels * width * 13, 54 * row_bytes),
         name="mend_a",
-    )(east, north, second_pack, first_came, ends, middle, base)
+    )(east, north, second_pack, first_came, ends, base)
     a_came = along(side_a, "sub", -1)
     total = pl.pallas_call(
         ghost_kernel,
@@ -526,28 +531,19 @@
     b_came = along(side_b, "sub", -1)
 
     total = added_up(total)
-    boundary_gradient = pl.pallas_call(
-        pick_kernel,
-        in_specs=[vmem] * 2,
-        out_specs=vmem,
-        out_shape=f32(parts, levels // subs, slots // hors),
-        compiler_params=PARAMS,
-        name="pick",
-    )(total, owner_slot[None])
-
-    adjoint_result = pl.pallas_call(
-        subtract_kernel,
-        in_specs=[vmem] * 3,
-        out_specs=hbm,
-        out_shape=f32(*adjoint_state.shape),
+    adjoint_result, boundary_gradient = pl.pallas_call(
+        finish_kernel,
+        in_specs=[vmem] * 6,
+        out_specs=[hbm, vmem],
+        out_shape=[f32(*adjoint_state.shape), f32(parts, levels // subs, slots // hors)],
         scratch_shapes=[
             pltpu.VMEM((parts, rows, levels, width), jnp.float32),
             pltpu.SemaphoreType.DMA((3 * parts,)),
         ],
         compiler_params=PARAMS,
         cost_estimate=cost(parts * rows * levels * width, 6 * rows * row_bytes),
-        name="subtract",
-    )(state, a_came, b_came)
+        name="finish",
+    )(total, owner_slot[None], state, middle_came, a_came, b_came)
     return (adjoint_result, boundary_gradient)
 
 

time: 39.4 us -> 44.9 us (1.14)
  waiting for transfers between devices: 8.94 us -> 13.1 us
  starting transfers between devices: 18.8 us -> 21.4 us
  Pallas kernels: 10.4 us -> 9.15 us
    ppermute x2, waiting for transfers between devices: 2.75 us -> 4.84 us  [alternating(): return lax.ppermute(value, ('sub', 'hor'), pairs)]
    ppermute x4 -> x6, waiting for transfers between devices: 6.19 us -> 8.26 us  [added_up(): lax.ppermute(value, axis, [(i, i ^ step * j) for i in range(size)])]
    ppermute x2 -> x3, starting transfers between devices: 2.58 us -> 4 us  [along(): return lax.ppermute(value, axis, pairs)]
    ppermute x4 -> x6, starting transfers between devices: 9.05 us -> 10.4 us  [added_up(): lax.ppermute(value, axis, [(i, i ^ step * j) for i in range(size)])]
    pallas_call x5 -> x4, Pallas kernels: 6.19 us -> 4.88 us  [the longest x1 1.93 us: local(): pl.pallas_call(functools.partial(pack_kernel, 0), in_specs=[hbm] * 6, out...]
  transfers between devices with their start and end apart: 8 -> 11, of which waited for: 6 -> 2; matrix products, arithmetic and copies ran while one was open for 0% -> 0% of each run, Pallas kernels for 19% -> 12%
where the time goes in v9:
time: 44.9 us; the launch traced here: 44.6 us
  starting transfers between devices  21.4 us (48%)
  waiting for transfers between devices  13.1 us (29%)
  Pallas kernels  9.15 us (20%)
  between operations  0.89 us (2%)
    ppermute x6, starting transfers between devices, added_up(): lax.ppermute(value, axis, [(i, i ^ step * j) for i in range(size)])  10.4 us
    ppermute x6, waiting for transfers between devices, added_up(): lax.ppermute(value, axis, [(i, i ^ step * j) for i in range(size)])  8.26 us
    ppermute x2, starting transfers between devices, alternating(): return lax.ppermute(value, ('sub', 'hor'), pairs)  7.01 us
    ppermute x2, waiting for transfers between devices, alternating(): return lax.ppermute(value, ('sub', 'hor'), pairs)  4.84 us
    ppermute x3, starting transfers between devices, along(): return lax.ppermute(value, axis, pairs)  4 us
    pallas_call x1, Pallas kernels, local(): pl.pallas_call(sweep_kernel, in_specs=[vmem] * 3, out_specs=[vmem] * 3, o...  2.9 us
    pallas_call x1, Pallas kernels, local(): pl.pallas_call(functools.partial(pack_kernel, 0), in_specs=[hbm] * 6, out...  1.93 us
    pallas_call x1, Pallas kernels, local(): pl.pallas_call(finish_kernel, in_specs=[vmem] * 6, out_specs=[hbm, vmem],...  1.67 us
  transfers between devices with their start and end apart: 11, of which 2 were waited for; matrix products, arithmetic and copies ran while one was open for 0% of the time, Pallas kernels for 12%

profile of v9, /device:TPU:0, one launch (start us, length us, event | category | flops | bytes accessed | tf_op | source)
XLA Modules:
  0.0 44.6 jit_solution(6185118781188145163)
XLA Ops:
  0.7 1.9 %pack_a.1.mine_ref = f32[12,16,768]{2,1,0:T(8,128)S(1)} custom-call(f32[1,2,12,16,768]{4,3,2,1,0:T(8,128)} %state_ref.3, f32[1,12,16,768]{3,2,1,0:T(8,128)} %east_ref.5, f32[1,12,16,768]{3,2,1,0:T(8,128)} %north_ref.9, s32[2,2,12]{2,1,0:T(2,128)} %cell_ref.1, s32[4,2,2,12]{3,2,1,0:T(2,128)} %offset_ref.1, f32[4,2,2,12]{3,2,1,0:T(2,128)} %weight_ref.1), custom_call_target="tpu_custom_call" | custom-call | flops 1916928 | bytes 1376256 | tf_op jit(solution)/shard_map/pack_a/pallas_call | solution.py:445
  2.6 1.3 %collective-permute-start = (f32[12,16,768]{2,1,0:T(8,128)S(1)}, f32[12,16,768]{2,1,0:T(8,128)S(1)}, u32[]{:S(2)}, u32[]{:S(2)}) collective-permute-start(f32[12,16,768]{2,1,0:T(8,128)S(1)} %pack_a.1.mine_ref), channel_id=1, source_target_pairs={{1,0},{2,1},{3,2},{4,5},{5,6},{6,7},{9,8},{10,9},{11,10},{12,13},{... | collective-permute-start | bytes 1769480 | tf_op jit(solution)/shard_map/ppermute | solution.py:32
  3.9 0.5 %pack_b.1.mine_ref = f32[11,16,768]{2,1,0:T(8,128)S(1)} custom-call(f32[1,2,12,16,768]{4,3,2,1,0:T(8,128)S(1)} %copy-done.1, f32[1,12,16,768]{3,2,1,0:T(8,128)S(1)} %copy-done.2, f32[1,12,16,768]{3,2,1,0:T(8,128)S(1)} %copy-done), custom_call_target="tpu_custom_call" | custom-call | flops 1916928 | bytes 1376256 | tf_op jit(solution)/shard_map/pack_b/pallas_call | solution.py:459
  4.5 0.0 copy-start.3
  4.5 0.0 copy-start.4
  4.5 0.0 copy-start.5
  4.5 5.7 %collective-permute-start.9 = (f32[11,16,768]{2,1,0:T(8,128)S(1)}, f32[11,16,768]{2,1,0:T(8,128)S(1)}, u32[]{:S(2)}, u32[]{:S(2)}) collective-permute-start(f32[11,16,768]{2,1,0:T(8,128)S(1)} %pack_b.1.mine_ref), channel_id=1, source_target_pairs={{0,1},{1,2},{2,3},{5,4},{6,5},{7,6},{8,9},{9,10},{10,11},{13,12},{... | collective-permute-start | bytes 1622024 | tf_op jit(solution)/shard_map/ppermute | solution.py:32
  10.2 2.9 %sweep.1 = (f32[2,4,16,768]{3,2,1,0:T(8,128)S(1)}, f32[2,8,16,768]{3,2,1,0:T(8,128)S(1)}, f32[2,2,12,16,128]{4,3,2,1,0:T(8,128)S(1)}) custom-call(f32[1,2,12,16,768]{4,3,2,1,0:T(8,128)S(1)} %copy-done.1, f32[1,12,16,768]{3,2,1,0:T(8,128)S(1)} %copy-done.2, f32[1,12,16,768]{3,2,1,0:T(8,128)S(1)} %copy-done), custom_call_target="tpu_custom_call" | custom-call | flops 15335424 | bytes 3538944 | tf_op jit(solution)/shard_map/sweep/pallas_call | solution.py:470
  13.2 0.4 ghost_base.1
  13.5 4.8 %collective-permute-done.other_ref = f32[12,16,768]{2,1,0:T(8,128)S(1)} collective-permute-done((f32[12,16,768]{2,1,0:T(8,128)S(1)}, f32[12,16,768]{2,1,0:T(8,128)S(1)}, u32[]{:S(2)}, u32[]{:S(2)}) %collective-permute-start) | collective-permute-done | bytes 589856 | tf_op jit(solution)/shard_map/ppermute | solution.py:32
  18.4 0.8 %mend_a.1 = (f32[2,4,16,768]{3,2,1,0:T(8,128)S(1)}, f32[2,2,6,16,128]{4,3,2,1,0:T(8,128)S(1)}) custom-call(f32[1,12,16,768]{3,2,1,0:T(8,128)S(1)} %copy-done.2, f32[1,12,16,768]{3,2,1,0:T(8,128)S(1)} %copy-done, f32[11,16,768]{2,1,0:T(8,128)S(1)} %pack_b.1.mine_ref, f32[12,16,768]{2,1,0:T(8,128)S(1)} %collective-permute-done.other_ref, ...), custom_call_target="tpu_custom_call" | custom-call | flops 2555904 | bytes 2654208 | tf_op jit(solution)/shard_map/mend_a/pallas_call | solution.py:502
  19.1 0.2 ghost.1
  19.4 2.5 %collective-permute-start.1 = (f32[2,16,32]{2,1,0:T(8,128)S(1)}, f32[2,16,32]{2,1,0:T(8,128)S(1)}, u32[]{:S(2)}, u32[]{:S(2)}) collective-permute-start(f32[2,16,32]{2,1,0:T(8,128)S(1)} %ghost.1), channel_id=1, source_target_pairs={{0,1},{1,0},{2,3},{3,2},{4,5},{5,4},{6,7},{7,6},{8,9},{9,8},{10,11... | collective-permute-start | bytes 12296 | tf_op jit(solution)/shard_map/ppermute | solution.py:44
  21.9 1.1 %collective-permute-start.2 = (f32[2,16,32]{2,1,0:T(8,128)S(1)}, f32[2,16,32]{2,1,0:T(8,128)S(1)}, u32[]{:S(2)}, u32[]{:S(2)}) collective-permute-start(f32[2,16,32]{2,1,0:T(8,128)S(1)} %ghost.1), channel_id=1, source_target_pairs={{0,2},{1,3},{2,0},{3,1},{4,6},{5,7},{6,4},{7,5},{8,10},{9,11},{10,... | collective-permute-start | bytes 12296 | tf_op jit(solution)/shard_map/ppermute | solution.py:44
  23.0 1.4 %collective-permute-start.3 = (f32[2,16,32]{2,1,0:T(8,128)S(1)}, f32[2,16,32]{2,1,0:T(8,128)S(1)}, u32[]{:S(2)}, u32[]{:S(2)}) collective-permute-start(f32[2,16,32]{2,1,0:T(8,128)S(1)} %ghost.1), channel_id=1, source_target_pairs={{0,3},{1,2},{2,1},{3,0},{4,7},{5,6},{6,5},{7,4},{8,11},{9,10},{10,... | collective-permute-start | bytes 12296 | tf_op jit(solution)/shard_map/ppermute | solution.py:44
  24.4 1.4 %collective-permute-start.7 = (f32[2,4,16,768]{3,2,1,0:T(8,128)S(1)}, f32[2,4,16,768]{3,2,1,0:T(8,128)S(1)}, u32[]{:S(2)}, u32[]{:S(2)}) collective-permute-start(f32[2,4,16,768]{3,2,1,0:T(8,128)S(1)} %get-tuple-element.14), channel_id=1, source_target_pairs={{4,0},{8,4},{12,8},{5,1},{9,5},{13,9},{6,2},{10,6},{14,10},{7,3},{... | collective-permute-start | bytes 1179656 | tf_op jit(solution)/shard_map/ppermute | solution.py:23
  25.8 0.8 %mend_b.1 = f32[2,4,16,768]{3,2,1,0:T(8,128)S(1)} custom-call(f32[1,12,16,768]{3,2,1,0:T(8,128)S(1)} %copy-done.2, f32[1,12,16,768]{3,2,1,0:T(8,128)S(1)} %copy-done, f32[12,16,768]{2,1,0:T(8,128)S(1)} %pack_a.1.mine_ref, f32[11,16,768]{2,1,0:T(8,128)S(1)} %collective-permute-done.9.other_ref, f32[2,8,16,768]{3,2,1,0:T(8,128)S(1)} %get-tuple-element.9.ends_ref), custom_call_target="tpu_custom_call" | custom-call | flops 2555904 | bytes 2260992 | tf_op jit(solution)/shard_map/mend_b/pallas_call | solution.py:522
  26.6 1.3 %collective-permute-start.10 = (f32[2,4,16,768]{3,2,1,0:T(8,128)S(1)}, f32[2,4,16,768]{3,2,1,0:T(8,128)S(1)}, u32[]{:S(2)}, u32[]{:S(2)}) collective-permute-start(f32[2,4,16,768]{3,2,1,0:T(8,128)S(1)} %mend_b.1), channel_id=1, source_target_pairs={{4,0},{8,4},{12,8},{5,1},{9,5},{13,9},{6,2},{10,6},{14,10},{7,3},{... | collective-permute-start | bytes 1179656 | tf_op jit(solution)/shard_map/ppermute | solution.py:23
  27.9 1.3 %collective-permute-start.8 = (f32[2,4,16,768]{3,2,1,0:T(8,128)S(1)}, f32[2,4,16,768]{3,2,1,0:T(8,128)S(1)}, u32[]{:S(2)}, u32[]{:S(2)}) collective-permute-start(f32[2,4,16,768]{3,2,1,0:T(8,128)S(1)} %get-tuple-element.15), channel_id=1, source_target_pairs={{4,0},{8,4},{12,8},{5,1},{9,5},{13,9},{6,2},{10,6},{14,10},{7,3},{... | collective-permute-start | bytes 1179656 | tf_op jit(solution)/shard_map/ppermute | solution.py:23
  29.2 2.4 %collective-permute-start.4 = (f32[2,16,32]{2,1,0:T(8,128)S(1)}, f32[2,16,32]{2,1,0:T(8,128)S(1)}, u32[]{:S(2)}, u32[]{:S(2)}) collective-permute-start(f32[2,16,32]{2,1,0:T(8,128)S(1)} %add_add_fusion.1), channel_id=1, source_target_pairs={{0,4},{4,0},{8,12},{12,8},{1,5},{5,1},{9,13},{13,9},{2,6},{6,2},{1... | collective-permute-start | bytes 12296 | tf_op jit(solution)/shard_map/ppermute | solution.py:44
  31.7 2.1 %collective-permute-start.5 = (f32[2,16,32]{2,1,0:T(8,128)S(1)}, f32[2,16,32]{2,1,0:T(8,128)S(1)}, u32[]{:S(2)}, u32[]{:S(2)}) collective-permute-start(f32[2,16,32]{2,1,0:T(8,128)S(1)} %add_add_fusion.1), channel_id=1, source_target_pairs={{0,8},{4,12},{8,0},{12,4},{1,9},{5,13},{9,1},{13,5},{2,10},{6,14},... | collective-permute-start | bytes 12296 | tf_op jit(solution)/shard_map/ppermute | solution.py:44
  33.8 0.8 %collective-permute-start.6 = (f32[2,16,32]{2,1,0:T(8,128)S(1)}, f32[2,16,32]{2,1,0:T(8,128)S(1)}, u32[]{:S(2)}, u32[]{:S(2)}) collective-permute-start(f32[2,16,32]{2,1,0:T(8,128)S(1)} %add_add_fusion.1), channel_id=1, source_target_pairs={{0,12},{4,8},{8,4},{12,0},{1,13},{5,9},{9,5},{13,1},{2,14},{6,10},... | collective-permute-start | bytes 12296 | tf_op jit(solution)/shard_map/ppermute | solution.py:44
  34.7 8.2 %collective-permute-done.5 = f32[2,16,32]{2,1,0:T(8,128)S(1)} collective-permute-done((f32[2,16,32]{2,1,0:T(8,128)S(1)}, f32[2,16,32]{2,1,0:T(8,128)S(1)}, u32[]{:S(2)}, u32[]{:S(2)}) %collective-permute-start.5) | collective-permute-done | bytes 4128 | tf_op jit(solution)/shard_map/ppermute | solution.py:44
  43.0 1.7 %finish.1 = (f32[1,2,12,16,768]{4,3,2,1,0:T(8,128)}, f32[2,4,8]{2,1,0:T(4,128)}) custom-call(f32[2,16,32]{2,1,0:T(8,128)S(1)} %add_add_fusion.total_ref, s32[1,32]{1,0:T(1,128)S(1)} %bitcast.1, f32[1,2,12,16,768]{4,3,2,1,0:T(8,128)S(1)} %copy-done.1, f32[2,4,16,768]{3,2,1,0:T(8,128)S(1)} %collective-permute-done.7.middle_ref, ...), custom_call_target="tpu_custom_call" | custom-call | flops 294912 | bytes 3538944 | tf_op jit(solution)/shard_map/finish/pallas_call | solution.py:534
  (22 shorter events, 0.1 us)
Async XLA Ops:
  0.6 3.3 %copy-start.1 = (f32[1,2,12,16,768]{4,3,2,1,0:T(8,128)S(1)}, f32[1,2,12,16,768]{4,3,2,1,0:T(8,128)}, u32[]{:S(2)}) copy-start(f32[1,2,12,16,768]{4,3,2,1,0:T(8,128)} %state_ref.3) | copy-start | bytes 3538948
  0.6 3.3 %copy-start.2 = (f32[1,12,16,768]{3,2,1,0:T(8,128)S(1)}, f32[1,12,16,768]{3,2,1,0:T(8,128)}, u32[]{:S(2)}) copy-start(f32[1,12,16,768]{3,2,1,0:T(8,128)} %east_ref.5) | copy-start | bytes 1769476
  0.6 3.3 %copy-start = (f32[1,12,16,768]{3,2,1,0:T(8,128)S(1)}, f32[1,12,16,768]{3,2,1,0:T(8,128)}, u32[]{:S(2)}) copy-start(f32[1,12,16,768]{3,2,1,0:T(8,128)} %north_ref.9) | copy-start | bytes 1769476
  2.6 15.8 %collective-permute-start = (f32[12,16,768]{2,1,0:T(8,128)S(1)}, f32[12,16,768]{2,1,0:T(8,128)S(1)}, u32[]{:S(2)}, u32[]{:S(2)}) collective-permute-start(f32[12,16,768]{2,1,0:T(8,128)S(1)} %pack_a.1.mine_ref), channel_id=1, source_target_pairs={{1,0},{2,1},{3,2},{4,5},{5,6},{6,7},{9,8},{10,9},{11,10},{12,13},{... | collective-permute-start | bytes 1769480 | tf_op jit(solution)/shard_map/ppermute | solution.py:32
  4.5 8.7 %copy-start.3 = (s32[4,2,2,12]{3,2,1,0:T(2,128)S(1)}, s32[4,2,2,12]{3,2,1,0:T(2,128)}, u32[]{:S(2)}) copy-start(s32[4,2,2,12]{3,2,1,0:T(2,128)} %offset_ref.1) | copy-start | bytes 2308
  4.5 8.7 %copy-start.4 = (f32[4,2,2,12]{3,2,1,0:T(2,128)S(1)}, f32[4,2,2,12]{3,2,1,0:T(2,128)}, u32[]{:S(2)}) copy-start(f32[4,2,2,12]{3,2,1,0:T(2,128)} %weight_ref.1) | copy-start | bytes 2308
  4.5 8.7 %copy-start.5 = (s32[2,2,12]{2,1,0:T(2,128)S(1)}, s32[2,2,12]{2,1,0:T(2,128)}, u32[]{:S(2)}) copy-start(s32[2,2,12]{2,1,0:T(2,128)} %cell_ref.1) | copy-start | bytes 580
  4.5 21.3 %collective-permute-start.9 = (f32[11,16,768]{2,1,0:T(8,128)S(1)}, f32[11,16,768]{2,1,0:T(8,128)S(1)}, u32[]{:S(2)}, u32[]{:S(2)}) collective-permute-start(f32[11,16,768]{2,1,0:T(8,128)S(1)} %pack_b.1.mine_ref), channel_id=1, source_target_pairs={{0,1},{1,2},{2,3},{5,4},{6,5},{7,6},{8,9},{9,10},{10,11},{13,12},{... | collective-permute-start | bytes 1622024 | tf_op jit(solution)/shard_map/ppermute | solution.py:32
  19.4 8.5 %collective-permute-start.1 = (f32[2,16,32]{2,1,0:T(8,128)S(1)}, f32[2,16,32]{2,1,0:T(8,128)S(1)}, u32[]{:S(2)}, u32[]{:S(2)}) collective-permute-start(f32[2,16,32]{2,1,0:T(8,128)S(1)} %ghost.1), channel_id=1, source_target_pairs={{0,1},{1,0},{2,3},{3,2},{4,5},{5,4},{6,7},{7,6},{8,9},{9,8},{10,11... | collective-permute-start | bytes 12296 | tf_op jit(solution)/shard_map/ppermute | solution.py:44
  21.9 7.3 %collective-permute-start.2 = (f32[2,16,32]{2,1,0:T(8,128)S(1)}, f32[2,16,32]{2,1,0:T(8,128)S(1)}, u32[]{:S(2)}, u32[]{:S(2)}) collective-permute-start(f32[2,16,32]{2,1,0:T(8,128)S(1)} %ghost.1), channel_id=1, source_target_pairs={{0,2},{1,3},{2,0},{3,1},{4,6},{5,7},{6,4},{7,5},{8,10},{9,11},{10,... | collective-permute-start | bytes 12296 | tf_op jit(solution)/shard_map/ppermute | solution.py:44
  23.0 6.2 %collective-permute-start.3 = (f32[2,16,32]{2,1,0:T(8,128)S(1)}, f32[2,16,32]{2,1,0:T(8,128)S(1)}, u32[]{:S(2)}, u32[]{:S(2)}) collective-permute-start(f32[2,16,32]{2,1,0:T(8,128)S(1)} %ghost.1), channel_id=1, source_target_pairs={{0,3},{1,2},{2,1},{3,0},{4,7},{5,6},{6,5},{7,4},{8,11},{9,10},{10,... | collective-permute-start | bytes 12296 | tf_op jit(solution)/shard_map/ppermute | solution.py:44
  24.4 18.6 %copy-start.6 = (s32[32]{0:T(128)S(1)}, s32[32]{0:T(128)}, u32[]{:S(2)}) copy-start(s32[32]{0:T(128)} %param.13) | copy-start | bytes 388
  24.4 18.5 %collective-permute-start.7 = (f32[2,4,16,768]{3,2,1,0:T(8,128)S(1)}, f32[2,4,16,768]{3,2,1,0:T(8,128)S(1)}, u32[]{:S(2)}, u32[]{:S(2)}) collective-permute-start(f32[2,4,16,768]{3,2,1,0:T(8,128)S(1)} %get-tuple-element.14), channel_id=1, source_target_pairs={{4,0},{8,4},{12,8},{5,1},{9,5},{13,9},{6,2},{10,6},{14,10},{7,3},{... | collective-permute-start | bytes 1179656 | tf_op jit(solution)/shard_map/ppermute | solution.py:23
  26.6 16.3 %collective-permute-start.10 = (f32[2,4,16,768]{3,2,1,0:T(8,128)S(1)}, f32[2,4,16,768]{3,2,1,0:T(8,128)S(1)}, u32[]{:S(2)}, u32[]{:S(2)}) collective-permute-start(f32[2,4,16,768]{3,2,1,0:T(8,128)S(1)} %mend_b.1), channel_id=1, source_target_pairs={{4,0},{8,4},{12,8},{5,1},{9,5},{13,9},{6,2},{10,6},{14,10},{7,3},{... | collective-permute-start | bytes 1179656 | tf_op jit(solution)/shard_map/ppermute | solution.py:23
  27.9 15.0 %collective-permute-start.8 = (f32[2,4,16,768]{3,2,1,0:T(8,128)S(1)}, f32[2,4,16,768]{3,2,1,0:T(8,128)S(1)}, u32[]{:S(2)}, u32[]{:S(2)}) collective-permute-start(f32[2,4,16,768]{3,2,1,0:T(8,128)S(1)} %get-tuple-element.15), channel_id=1, source_target_pairs={{4,0},{8,4},{12,8},{5,1},{9,5},{13,9},{6,2},{10,6},{14,10},{7,3},{... | collective-permute-start | bytes 1179656 | tf_op jit(solution)/shard_map/ppermute | solution.py:23
  29.2 4.6 %collective-permute-start.4 = (f32[2,16,32]{2,1,0:T(8,128)S(1)}, f32[2,16,32]{2,1,0:T(8,128)S(1)}, u32[]{:S(2)}, u32[]{:S(2)}) collective-permute-start(f32[2,16,32]{2,1,0:T(8,128)S(1)} %add_add_fusion.1), channel_id=1, source_target_pairs={{0,4},{4,0},{8,12},{12,8},{1,5},{5,1},{9,13},{13,9},{2,6},{6,2},{1... | collective-permute-start | bytes 12296 | tf_op jit(solution)/shard_map/ppermute | solution.py:44
  31.7 11.2 %collective-permute-start.5 = (f32[2,16,32]{2,1,0:T(8,128)S(1)}, f32[2,16,32]{2,1,0:T(8,128)S(1)}, u32[]{:S(2)}, u32[]{:S(2)}) collective-permute-start(f32[2,16,32]{2,1,0:T(8,128)S(1)} %add_add_fusion.1), channel_id=1, source_target_pairs={{0,8},{4,12},{8,0},{12,4},{1,9},{5,13},{9,1},{13,5},{2,10},{6,14},... | collective-permute-start | bytes 12296 | tf_op jit(solution)/shard_map/ppermute | solution.py:44
  33.8 9.1 %collective-permute-start.6 = (f32[2,16,32]{2,1,0:T(8,128)S(1)}, f32[2,16,32]{2,1,0:T(8,128)S(1)}, u32[]{:S(2)}, u32[]{:S(2)}) collective-permute-start(f32[2,16,32]{2,1,0:T(8,128)S(1)} %add_add_fusion.1), channel_id=1, source_target_pairs={{0,12},{4,8},{8,4},{12,0},{1,13},{5,9},{9,5},{13,1},{2,14},{6,10},... | collective-permute-start | bytes 12296 | tf_op jit(solution)/shard_map/ppermute | solution.py:44

commit v10 on v9

--- a/solution.py
+++ b/solution.py
@@ -32,21 +32,31 @@
     return lax.ppermute(value, ("sub", "hor"), pairs)
 
 
-def added_up(value):
-    sizes = {axis: lax.axis_size(axis) for axis in ("hor", "sub")}
-    if any(size & (size - 1) for size in sizes.values()):
-        return lax.psum(value, ("sub", "hor"))
-    for axis, size in sizes.items():
-        step = 1
-        while step < size:
-            group = min(4, size // step)
-            came = [
-                lax.ppermute(value, axis, [(i, i ^ (step * j)) for i in range(size)])
-                for j in range(1, group)
-            ]
-            value = sum(came, value)
-            step *= group
-    return value
+def peers_along(axis, step, group):
+    size = lax.axis_size(axis)
+    return [[(i, i ^ (step * j)) for i in range(size)] for j in range(1, group)]
+
+
+def rounds():
+    subs, hors = lax.axis_size("sub"), lax.axis_size("hor")
+    assert not subs & (subs - 1) and not hors & (hors - 1)
+    order = []
+    step = 2
+    while step < subs:
+        order.append(("sub", step, 2))
+        step *= 2
+    if subs > 1:
+        order.append(("sub", 1, 2))
+    step = 1
+    while step < hors:
+        group = min(4, hors // step)
+        order.append(("hor", step, group))
+        step *= group
+    return order
+
+
+def exchange(value, axis, step, group):
+    return [lax.ppermute(value, axis, pairs) for pairs in peers_along(axis, step, group)]
 
 
 def parity():
@@ -91,23 +101,18 @@
     lax.fori_loop(0, levels // HALF, step, 0)
 
 
-def pack_kernel(which, *refs):
-    if which == 0:
-        state_hbm, east_hbm, north_hbm, cell_hbm, offset_hbm, weight_hbm = refs[:6]
-        pack_ref, state_ref, east_ref, north_ref, cell_ref, offset_ref, weight_ref, sems, small_sems = refs[6:]
-        parts, rows, levels, width = state_hbm.shape[1:]
-    else:
-        state_ref, east_ref, north_ref, pack_ref = refs
-        parts, rows, levels, width = state_ref.shape[1:]
-        state_ref, east_ref, north_ref = state_ref.at[0], east_ref.at[0], north_ref.at[0]
-    flip = parity() if which == 0 else 1 - parity()
+def pack_kernel(
+    state_hbm, east_hbm, north_hbm, cell_hbm, offset_hbm, weight_hbm,
+    pack_ref, state_ref, east_ref, north_ref, cell_ref, offset_ref, weight_ref, sems, small_sems,
+):
+    parts, rows, levels, width = state_hbm.shape[1:]
+    flip = parity()
     sign = sign_of(flip)
     at_end = pl.ds(flip * (rows - STEPS), STEPS)
-    before = 0 if which == 0 else flip * (rows - STEPS)
-    place = lambda r: before + r + flip * (STEPS - 1 - 2 * r)
+    place = lambda r: r + flip * (STEPS - 1 - 2 * r)
     halves = levels // HALF
-    copies = [[]] * halves
-    for h in range(halves if which == 0 else 0):
+    copies = []
+    for h in range(halves):
         at = pl.ds(h * HALF, HALF)
         sem = sems.at[h]
         batch = [
@@ -116,29 +121,27 @@
         ]
         batch.append(pltpu.make_async_copy(east_hbm.at[0, at_end, at], east_ref.at[:, at], sem.at[parts]))
         batch.append(pltpu.make_async_copy(north_hbm.at[0, at_end, at], north_ref.at[:, at], sem.at[parts + 1]))
-        copies[h] = batch
+        copies.append(batch)
         for copy in batch:
             copy.start()
-    if which == 0:
-        small = [
-            pltpu.make_async_copy(source, target, small_sems.at[n])
-            for n, (source, target) in enumerate(
-                ((cell_hbm, cell_ref), (offset_hbm, offset_ref), (weight_hbm, weight_ref))
-            )
-        ]
-        for copy in small:
-            copy.start()
+    small = [
+        pltpu.make_async_copy(source, target, small_sems.at[n])
+        for n, (source, target) in enumerate(
+            ((cell_hbm, cell_ref), (offset_hbm, offset_ref), (weight_hbm, weight_ref))
+        )
+    ]
+    for copy in small:
+        copy.start()
 
     def half(at):
         row = [Row(east_ref[place(r), at, :] * sign, north_ref[place(r), at, :]) for r in range(STEPS)]
         pack_ref[FLUX_ROWS, at, :] = east_ref[place(0), at, :]
         pack_ref[FLUX_ROWS + 1, at, :] = north_ref[place(0), at, :]
         pack_ref[FLUX_ROWS + 2, at, :] = east_ref[place(1), at, :]
-        if which == 0:
-            for r in (1, 2):
-                lanes = (2 * r - 2) * LANES
-                pack_ref[EXTRA, at, lanes:lanes + LANES] = north_ref[place(r), at, :LANES]
-                pack_ref[EXTRA, at, lanes + LANES:lanes + 2 * LANES] = north_ref[place(r), at, width - LANES:]
+        for r in (1, 2):
+            lanes = (2 * r - 2) * LANES
+            pack_ref[EXTRA, at, lanes:lanes + LANES] = north_ref[place(r), at, :LANES]
+            pack_ref[EXTRA, at, lanes + LANES:lanes + 2 * LANES] = north_ref[place(r), at, width - LANES:]
         for c in range(parts):
             field = [state_ref[c, place(r), at, :] for r in range(STEPS)]
             for k in range(STEPS):
@@ -156,16 +159,15 @@
             copy.wait()
         half(pl.ds(h * HALF, HALF))
 
-    if which == 0:
-        for copy in small:
-            copy.wait()
-        n = 0
-        for point in range(offset_ref.shape[0]):
-            for c in range(parts):
-                target = (cell_ref[c] + offset_ref[point, c]).astype(jnp.float32)
-                pack_ref[EXTRA, n:n + 2, TARGETS:TARGETS + rows] = target
-                pack_ref[EXTRA, n:n + 2, WEIGHTS:WEIGHTS + rows] = weight_ref[point, c]
-                n += 2
+    for copy in small:
+        copy.wait()
+    n = 0
+    for point in range(offset_ref.shape[0]):
+        for c in range(parts):
+            target = (cell_ref[c] + offset_ref[point, c]).astype(jnp.float32)
+            pack_ref[EXTRA, n:n + 2, TARGETS:TARGETS + rows] = target
+            pack_ref[EXTRA, n:n + 2, WEIGHTS:WEIGHTS + rows] = weight_ref[point, c]
+            n += 2
 
 
 def as_column(row):
@@ -176,17 +178,28 @@
 
 
 def sweep_kernel(
-    state_ref, east_ref, north_ref, middle_ref, ends_ref, column_ref,
+    state_ref, east_ref, north_ref, pack_ref, middle_ref, ends_ref, column_ref,
     field, plus_ref, minus_ref, centre_ref,
 ):
     parts, rows, levels, width = state_ref.shape[1:]
+    flip = 1 - parity()
+    sign = sign_of(flip)
+    end_row = flip * (rows - 1)
+    next_row = end_row + 1 - 2 * flip
 
     def half(at):
+        pack_ref[FLUX_ROWS, at, :] = east_ref[0, end_row, at, :]
+        pack_ref[FLUX_ROWS + 1, at, :] = north_ref[0, end_row, at, :]
+        pack_ref[FLUX_ROWS + 2, at, :] = east_ref[0, next_row, at, :]
+
         for k in range(STEPS):
             if k == 0:
                 read = lambda c, i: state_ref[0, c, i, at, :]
             else:
                 read = lambda c, i, slot=k - 1: field[slot, c, i]
+            leaving = jnp.maximum(east_ref[0, end_row, at, :] * sign, 0.0)
+            for c in range(parts):
+                pack_ref[2 * k + c, at, :] = leaving * read(c, end_row)
             west = [None] * parts
             here = [read(c, 0) for c in range(parts)]
             east_here = east_ref[0, 0, at, :]
@@ -368,7 +381,9 @@
     mend_side(flip, east_ref, north_ref, mine_ref, other_ref, store, store_column)
 
 
-def mend_b_kernel(east_ref, north_ref, mine_ref, other_ref, ends_ref, out_ref):
+def mend_b_kernel(*refs):
+    east_ref, north_ref, mine_ref, other_ref, ends_ref, _ = refs[:6]
+    out_ref, sum_ref = refs[-2:]
     flip = parity()
     turn = lambda r: r + flip * (STEPS - 1 - 2 * r)
 
@@ -376,6 +391,7 @@
         out_ref[c, turn(r), at, :] = ends_ref[c, flip * STEPS + turn(r), at, :] + value
 
     mend_side(flip, east_ref, north_ref, mine_ref, other_ref, store, None)
+    sum_ref[...] = sum((ref[...] for ref in refs[7:-2]), refs[6][...])
 
 
 def finish_kernel(
@@ -385,6 +401,23 @@
     inner = rows - 2 * STEPS
     a_start = parity() * (rows - STEPS)
     b_start = (1 - parity()) * (rows - STEPS)
+    share, mine = gradient_ref.shape[1:]
+    start = lax.axis_index("hor") * mine
+    chosen = []
+    for c in range(parts):
+        block = total_ref[c, :share, :]
+        for s in range(1, total_ref.shape[1] // share):
+            block = jnp.where(lax.axis_index("sub") == s, total_ref[c, s * share:(s + 1) * share, :], block)
+        chosen.append(block)
+    chosen = jnp.concatenate(chosen, 0)
+    column = lax.broadcasted_iota(jnp.int32, (parts * share, mine), 1)
+    picked = jnp.zeros((parts * share, mine), jnp.float32)
+    for q in range(mine):
+        value = jnp.sum(jnp.where(owner_ref[...] == start + q, chosen, 0.0), axis=1, keepdims=True)
+        picked = jnp.where(column == q, value, picked)
+    for c in range(parts):
+        gradient_ref[c] = picked[c * share:(c + 1) * share]
+
     copies = []
     for start, other in ((STEPS, middle_ref), (a_start, a_ref), (b_start, b_ref)):
         for c in range(parts):
@@ -396,24 +429,11 @@
             copy.start()
             copies.append(copy)
 
-    share, mine = gradient_ref.shape[1:]
-    slots = owner_ref.shape[-1]
-    to_slot = lax.broadcasted_iota(jnp.int32, (slots, mine), 1) + lax.axis_index("hor") * mine
-    pick = jnp.where(as_column(owner_ref[...]) == to_slot, 1.0, 0.0)
-    for c in range(parts):
-        chosen = jnp.zeros((share, slots), jnp.float32)
-        for s in range(total_ref.shape[1] // share):
-            block = total_ref[c, s * share:(s + 1) * share, :]
-            chosen = jnp.where(lax.axis_index("sub") == s, block, chosen)
-        gradient_ref[c] = jnp.dot(chosen, pick, precision=lax.Precision.HIGHEST, preferred_element_type=jnp.float32)
     for copy in copies:
         copy.wait()
 
 
-def cost(flops, moved):
-    return pl.CostEstimate(flops=flops, bytes_accessed=moved, transcendentals=0)
-
-
+BRIEF = pl.CostEstimate(flops=1, bytes_accessed=1, transcendentals=0)
 PARAMS = pltpu.CompilerParams(vmem_limit_bytes=24 * 1024 * 1024)
 
 
@@ -439,12 +459,10 @@
     subs, hors = lax.axis_size("sub"), lax.axis_size("hor")
     small = [parent_cell, stencil_offset, stencil_weight]
 
-    packing = dict(
-        out_specs=vmem, compiler_params=PARAMS, cost_estimate=cost(12 * levels * width * 13, 28 * row_bytes)
-    )
     first_pack = pl.pallas_call(
-        functools.partial(pack_kernel, 0),
+        pack_kernel,
         in_specs=[hbm] * 6,
+        out_specs=vmem,
         out_shape=f32(PACK_ROWS + 1, levels, width),
         scratch_shapes=[
             pltpu.VMEM((parts, STEPS, levels, width), jnp.float32),
@@ -453,25 +471,19 @@
         ]
         + [pltpu.VMEM(value.shape, value.dtype) for value in small]
         + [pltpu.SemaphoreType.DMA((levels // HALF, parts + 2)), pltpu.SemaphoreType.DMA((3,))],
-        name="pack_a",
-        **packing,
+        compiler_params=PARAMS,
+        cost_estimate=BRIEF,
+        name="pack",
     )(*[in_hbm(value) for value in [adjoint_state, courant_east, courant_north] + small])
-    second_pack = pl.pallas_call(
-        functools.partial(pack_kernel, 1),
-        in_specs=[vmem] * 3,
-        out_shape=f32(PACK_ROWS, levels, width),
-        name="pack_b",
-        **packing,
-    )(adjoint_state, courant_east, courant_north)
     first_came = alternating(first_pack, -1)
-    second_came = alternating(second_pack, 1)
 
     state, east, north = adjoint_state, courant_east, courant_north
-    middle, ends, columns = pl.pallas_call(
+    second_pack, middle, ends, columns = pl.pallas_call(
         sweep_kernel,
         in_specs=[vmem] * 3,
-        out_specs=[vmem] * 3,
+        out_specs=[vmem] * 4,
         out_shape=[
+            f32(PACK_ROWS, levels, width),
             f32(parts, inner, levels, width),
             f32(parts, 2 * STEPS, levels, width),
             f32(parts, 2, rows, levels, LANES),
@@ -483,9 +495,10 @@
             pltpu.VMEM((rows, HALF, width), jnp.float32),
         ],
         compiler_params=PARAMS,
-        cost_estimate=cost(8 * rows * levels * width * 13, 6 * rows * row_bytes),
+        cost_estimate=BRIEF,
         name="sweep",
     )(state, east, north)
+    second_came = alternating(second_pack, 1)
     middle_came = along(middle, "sub", -1)
 
     mixing, base = pl.pallas_call(
@@ -494,7 +507,7 @@
         out_specs=[vmem] * 2,
         out_shape=[f32(parts, 2, rows, slots), f32(parts, levels, slots)],
         compiler_params=PARAMS,
-        cost_estimate=cost(parts * rows * levels * slots * 8, 4 * rows * levels * LANES * 8),
+        cost_estimate=BRIEF,
         name="ghost_base",
     )(*small, columns, north)
 
@@ -505,7 +518,7 @@
         out_specs=[vmem] * 2,
         out_shape=[f32(parts, STEPS, levels, width), f32(*column_shape)],
         compiler_params=PARAMS,
-        cost_estimate=cost(16 * levels * width * 13, 54 * row_bytes),
+        cost_estimate=BRIEF,
         name="mend_a",
     )(east, north, second_pack, first_came, ends, base)
     a_came = along(side_a, "sub", -1)
@@ -516,21 +529,24 @@
         out_shape=f32(parts, levels, slots),
         scratch_shapes=[pltpu.VMEM((parts, 2, rows, slots), jnp.float32)],
         compiler_params=PARAMS,
-        cost_estimate=cost(parts * levels * slots * 64, 8 * row_bytes),
+        cost_estimate=BRIEF,
         name="ghost",
     )(north, first_came, a_columns, mixing, base)
-    side_b = pl.pallas_call(
+    order = rounds()
+    came = exchange(total, *order[0])
+    side_b, total = pl.pallas_call(
         mend_b_kernel,
-        in_specs=[vmem] * 5,
-        out_specs=vmem,
-        out_shape=f32(parts, STEPS, levels, width),
-        compiler_params=PARAMS,
-        cost_estimate=cost(16 * levels * width * 13, 46 * row_bytes),
+        in_specs=[vmem] * 5 + [pl.BlockSpec(memory_space=pl.ANY)] + [vmem] * (1 + len(came)),
+        out_specs=[vmem] * 2,
+        out_shape=[f32(parts, STEPS, levels, width), f32(parts, levels, slots)],
+        compiler_params=PARAMS,
+        cost_estimate=BRIEF,
         name="mend_b",
-    )(east, north, first_pack, second_came, ends)
+    )(east, north, first_pack, second_came, ends, middle_came, total, *came)
     b_came = along(side_b, "sub", -1)
 
-    total = added_up(total)
+    for each in order[1:]:
+        total = sum(exchange(total, *each), total)
     adjoint_result, boundary_gradient = pl.pallas_call(
         finish_kernel,
         in_specs=[vmem] * 6,
@@ -541,7 +557,7 @@
             pltpu.SemaphoreType.DMA((3 * parts,)),
         ],
         compiler_params=PARAMS,
-        cost_estimate=cost(parts * rows * levels * width, 6 * rows * row_bytes),
+        cost_estimate=BRIEF,
         name="finish",
     )(total, owner_slot[None], state, middle_came, a_came, b_came)
     return (adjoint_result, boundary_gradient)

time: 44.9 us -> 38.1 us (0.85)
  waiting for transfers between devices: 13.1 us -> 9.22 us
  starting transfers between devices: 21.4 us -> 19 us
    ppermute x2, waiting for transfers between devices: 4.84 us -> 1.86 us  [alternating(): return lax.ppermute(value, ('sub', 'hor'), pairs)]
    ppermute x6 -> x5, starting transfers between devices: 10.4 us -> 8.01 us  [exchange(): lax.ppermute(value, axis, pairs)]
    ppermute x6 -> x5, waiting for transfers between devices: 8.26 us -> 7.35 us  [exchange(): lax.ppermute(value, axis, pairs)]
    pallas_call x4 -> x3, Pallas kernels: 6.12 us -> 5.67 us  [the longest x1 2.99 us: local(): pl.pallas_call(sweep_kernel, in_specs=[vmem] * 3, out_specs=[vmem] * 4, o...]
  transfers between devices with their start and end apart: 11 -> 10, of which waited for: 2 -> 5; matrix products, arithmetic and copies ran while one was open for 0% -> 0% of each run, Pallas kernels for 12% -> 14%
where the time goes in v10:
time: 38.1 us; the launch traced here: 37.8 us
  starting transfers between devices  19 us (50%)
  waiting for transfers between devices  9.22 us (24%)
  Pallas kernels  8.71 us (23%)
  between operations  0.84 us (2%)
    ppermute x5, starting transfers between devices, exchange(): lax.ppermute(value, axis, pairs)  8.01 us
    ppermute x5, waiting for transfers between devices, exchange(): lax.ppermute(value, axis, pairs)  7.35 us
    ppermute x2, starting transfers between devices, alternating(): return lax.ppermute(value, ('sub', 'hor'), pairs)  7.01 us
    ppermute x3, starting transfers between devices, along(): return lax.ppermute(value, axis, pairs)  4 us
    pallas_call x1, Pallas kernels, local(): pl.pallas_call(sweep_kernel, in_specs=[vmem] * 3, out_specs=[vmem] * 4, o...  2.99 us
    pallas_call x1, Pallas kernels, local(): pl.pallas_call(pack_kernel, in_specs=[hbm] * 6, out_specs=vmem, out_shape...  1.93 us
    ppermute x2, waiting for transfers between devices, alternating(): return lax.ppermute(value, ('sub', 'hor'), pairs)  1.86 us
    pallas_call x1, Pallas kernels, local(): pl.pallas_call(finish_kernel, in_specs=[vmem] * 6, out_specs=[hbm, vmem],...  1.68 us
  transfers between devices with their start and end apart: 10, of which 5 were waited for; matrix products, arithmetic and copies ran while one was open for 0% of the time, Pallas kernels for 14%

profile of v10, /device:TPU:0, one launch (start us, length us, event | category | flops | bytes accessed | tf_op | source)
XLA Modules:
  0.0 37.8 jit_solution(8067263508131103392)
XLA Ops:
  0.7 1.9 %pack.1.refs_2_ = f32[12,16,768]{2,1,0:T(8,128)S(1)} custom-call(f32[1,2,12,16,768]{4,3,2,1,0:T(8,128)} %state_ref.3, f32[1,12,16,768]{3,2,1,0:T(8,128)} %refs_0_.1, f32[1,12,16,768]{3,2,1,0:T(8,128)} %refs_1_.1, s32[2,2,12]{2,1,0:T(2,128)} %cell_ref.1, s32[4,2,2,12]{3,2,1,0:T(2,128)} %offset_ref.1, f32[4,2,2,12]{3,2,1,0:T(2,128)} %weight_ref.1), custom_call_target="tpu_custom_call" | custom-call | flops 1 | bytes 1 | tf_op jit(solution)/shard_map/pack/pallas_call | solution.py:462
  2.6 0.0 copy-start.3
  2.6 0.0 copy-start.4
  2.6 1.4 %collective-permute-start.2 = (f32[12,16,768]{2,1,0:T(8,128)S(1)}, f32[12,16,768]{2,1,0:T(8,128)S(1)}, u32[]{:S(2)}, u32[]{:S(2)}) collective-permute-start(f32[12,16,768]{2,1,0:T(8,128)S(1)} %pack.1.refs_2_), channel_id=1, source_target_pairs={{1,0},{2,1},{3,2},{4,5},{5,6},{6,7},{9,8},{10,9},{11,10},{12,13},{... | collective-permute-start | bytes 1769480 | tf_op jit(solution)/shard_map/ppermute | solution.py:32
  4.1 3.0 %sweep.1 = (f32[11,16,768]{2,1,0:T(8,128)S(1)}, f32[2,4,16,768]{3,2,1,0:T(8,128)S(1)}, f32[2,8,16,768]{3,2,1,0:T(8,128)S(1)}, f32[2,2,12,16,128]{4,3,2,1,0:T(8,128)S(1)}) custom-call(f32[1,2,12,16,768]{4,3,2,1,0:T(8,128)S(1)} %copy-done.1, f32[1,12,16,768]{3,2,1,0:T(8,128)S(1)} %copy-done.2, f32[1,12,16,768]{3,2,1,0:T(8,128)S(1)} %copy-done), custom_call_target="tpu_custom_call" | custom-call | flops 1 | bytes 1 | tf_op jit(solution)/shard_map/sweep/pallas_call | solution.py:481
  7.1 5.6 %collective-permute-start = (f32[11,16,768]{2,1,0:T(8,128)S(1)}, f32[11,16,768]{2,1,0:T(8,128)S(1)}, u32[]{:S(2)}, u32[]{:S(2)}) collective-permute-start(f32[11,16,768]{2,1,0:T(8,128)S(1)} %get-tuple-element.12.mine_ref), channel_id=1, source_target_pairs={{0,1},{1,2},{2,3},{5,4},{6,5},{7,6},{8,9},{9,10},{10,11},{13,12},{... | collective-permute-start | bytes 1622024 | tf_op jit(solution)/shard_map/ppermute | solution.py:32
  12.7 1.3 %collective-permute-start.1 = (f32[2,4,16,768]{3,2,1,0:T(8,128)S(1)}, f32[2,4,16,768]{3,2,1,0:T(8,128)S(1)}, u32[]{:S(2)}, u32[]{:S(2)}) collective-permute-start(f32[2,4,16,768]{3,2,1,0:T(8,128)S(1)} %get-tuple-element.14), channel_id=1, source_target_pairs={{4,0},{8,4},{12,8},{5,1},{9,5},{13,9},{6,2},{10,6},{14,10},{7,3},{... | collective-permute-start | bytes 1179656 | tf_op jit(solution)/shard_map/ppermute | solution.py:23
  14.0 0.4 ghost_base.1
  14.4 1.9 %collective-permute-done.2.other_ref = f32[12,16,768]{2,1,0:T(8,128)S(1)} collective-permute-done((f32[12,16,768]{2,1,0:T(8,128)S(1)}, f32[12,16,768]{2,1,0:T(8,128)S(1)}, u32[]{:S(2)}, u32[]{:S(2)}) %collective-permute-start.2) | collective-permute-done | bytes 589856 | tf_op jit(solution)/shard_map/ppermute | solution.py:32
  16.2 0.8 %mend_a.1 = (f32[2,4,16,768]{3,2,1,0:T(8,128)S(1)}, f32[2,2,6,16,128]{4,3,2,1,0:T(8,128)S(1)}) custom-call(f32[1,12,16,768]{3,2,1,0:T(8,128)S(1)} %copy-done.2, f32[1,12,16,768]{3,2,1,0:T(8,128)S(1)} %copy-done, f32[11,16,768]{2,1,0:T(8,128)S(1)} %get-tuple-element.12.mine_ref, f32[12,16,768]{2,1,0:T(8,128)S(1)} %collective-permute-done.2.other_ref, ...), custom_call_target="tpu_custom_call" | custom-call | flops 1 | bytes 1 | tf_op jit(solution)/shard_map/mend_a/pallas_call | solution.py:515
  17.0 0.2 ghost.1.refs_6_
  17.2 2.4 %collective-permute-start.3 = (f32[2,16,32]{2,1,0:T(8,128)S(1)}, f32[2,16,32]{2,1,0:T(8,128)S(1)}, u32[]{:S(2)}, u32[]{:S(2)}) collective-permute-start(f32[2,16,32]{2,1,0:T(8,128)S(1)} %ghost.1.refs_6_), channel_id=1, source_target_pairs={{0,8},{4,12},{8,0},{12,4},{1,9},{5,13},{9,1},{13,5},{2,10},{6,14},... | collective-permute-start | bytes 12296 | tf_op jit(solution)/shard_map/ppermute | solution.py:59
  19.7 1.4 %collective-permute-start.8 = (f32[2,4,16,768]{3,2,1,0:T(8,128)S(1)}, f32[2,4,16,768]{3,2,1,0:T(8,128)S(1)}, u32[]{:S(2)}, u32[]{:S(2)}) collective-permute-start(f32[2,4,16,768]{3,2,1,0:T(8,128)S(1)} %get-tuple-element.20), channel_id=1, source_target_pairs={{4,0},{8,4},{12,8},{5,1},{9,5},{13,9},{6,2},{10,6},{14,10},{7,3},{... | collective-permute-start | bytes 1179656 | tf_op jit(solution)/shard_map/ppermute | solution.py:23
  21.1 1.5 %collective-permute-done.3.refs_7_ = f32[2,16,32]{2,1,0:T(8,128)S(1)} collective-permute-done((f32[2,16,32]{2,1,0:T(8,128)S(1)}, f32[2,16,32]{2,1,0:T(8,128)S(1)}, u32[]{:S(2)}, u32[]{:S(2)}) %collective-permute-start.3) | collective-permute-done | bytes 4128 | tf_op jit(solution)/shard_map/ppermute | solution.py:59
  22.6 0.8 %mend_b.1 = (f32[2,4,16,768]{3,2,1,0:T(8,128)S(1)}, f32[2,16,32]{2,1,0:T(8,128)S(1)}) custom-call(f32[1,12,16,768]{3,2,1,0:T(8,128)S(1)} %copy-done.2, f32[1,12,16,768]{3,2,1,0:T(8,128)S(1)} %copy-done, f32[12,16,768]{2,1,0:T(8,128)S(1)} %pack.1.refs_2_, f32[11,16,768]{2,1,0:T(8,128)S(1)} %collective-permute-done.refs_3_, ...), custom_call_target="tpu_custom_call" | custom-call | flops 1 | bytes 1 | tf_op jit(solution)/shard_map/mend_b/pallas_call | solution.py:537
  23.4 1.3 %collective-permute-start.9 = (f32[2,4,16,768]{3,2,1,0:T(8,128)S(1)}, f32[2,4,16,768]{3,2,1,0:T(8,128)S(1)}, u32[]{:S(2)}, u32[]{:S(2)}) collective-permute-start(f32[2,4,16,768]{3,2,1,0:T(8,128)S(1)} %get-tuple-element.21), channel_id=1, source_target_pairs={{4,0},{8,4},{12,8},{5,1},{9,5},{13,9},{6,2},{10,6},{14,10},{7,3},{... | collective-permute-start | bytes 1179656 | tf_op jit(solution)/shard_map/ppermute | solution.py:23
  24.7 1.2 %collective-permute-start.4 = (f32[2,16,32]{2,1,0:T(8,128)S(1)}, f32[2,16,32]{2,1,0:T(8,128)S(1)}, u32[]{:S(2)}, u32[]{:S(2)}) collective-permute-start(f32[2,16,32]{2,1,0:T(8,128)S(1)} %get-tuple-element.19), channel_id=1, source_target_pairs={{0,4},{4,0},{8,12},{12,8},{1,5},{5,1},{9,13},{13,9},{2,6},{6,2},{1... | collective-permute-start | bytes 12296 | tf_op jit(solution)/shard_map/ppermute | solution.py:59
  25.9 1.1 %collective-permute-done.4 = f32[2,16,32]{2,1,0:T(8,128)S(1)} collective-permute-done((f32[2,16,32]{2,1,0:T(8,128)S(1)}, f32[2,16,32]{2,1,0:T(8,128)S(1)}, u32[]{:S(2)}, u32[]{:S(2)}) %collective-permute-start.4) | collective-permute-done | bytes 4128 | tf_op jit(solution)/shard_map/ppermute | solution.py:59
  27.0 1.5 %collective-permute-start.5 = (f32[2,16,32]{2,1,0:T(8,128)S(1)}, f32[2,16,32]{2,1,0:T(8,128)S(1)}, u32[]{:S(2)}, u32[]{:S(2)}) collective-permute-start(f32[2,16,32]{2,1,0:T(8,128)S(1)} %add.12), channel_id=1, source_target_pairs={{0,1},{1,0},{2,3},{3,2},{4,5},{5,4},{6,7},{7,6},{8,9},{9,8},{10,11... | collective-permute-start | bytes 12296 | tf_op jit(solution)/shard_map/ppermute | solution.py:59
  28.6 2.0 %collective-permute-start.6 = (f32[2,16,32]{2,1,0:T(8,128)S(1)}, f32[2,16,32]{2,1,0:T(8,128)S(1)}, u32[]{:S(2)}, u32[]{:S(2)}) collective-permute-start(f32[2,16,32]{2,1,0:T(8,128)S(1)} %add.12), channel_id=1, source_target_pairs={{0,2},{1,3},{2,0},{3,1},{4,6},{5,7},{6,4},{7,5},{8,10},{9,11},{10,... | collective-permute-start | bytes 12296 | tf_op jit(solution)/shard_map/ppermute | solution.py:59
  30.6 0.8 %collective-permute-start.7 = (f32[2,16,32]{2,1,0:T(8,128)S(1)}, f32[2,16,32]{2,1,0:T(8,128)S(1)}, u32[]{:S(2)}, u32[]{:S(2)}) collective-permute-start(f32[2,16,32]{2,1,0:T(8,128)S(1)} %add.12), channel_id=1, source_target_pairs={{0,3},{1,2},{2,1},{3,0},{4,7},{5,6},{6,5},{7,4},{8,11},{9,10},{10,... | collective-permute-start | bytes 12296 | tf_op jit(solution)/shard_map/ppermute | solution.py:59
  31.4 1.9 %collective-permute-done.6 = f32[2,16,32]{2,1,0:T(8,128)S(1)} collective-permute-done((f32[2,16,32]{2,1,0:T(8,128)S(1)}, f32[2,16,32]{2,1,0:T(8,128)S(1)}, u32[]{:S(2)}, u32[]{:S(2)}) %collective-permute-start.6) | collective-permute-done | bytes 4128 | tf_op jit(solution)/shard_map/ppermute | solution.py:59
  33.4 2.8 %collective-permute-done.7 = f32[2,16,32]{2,1,0:T(8,128)S(1)} collective-permute-done((f32[2,16,32]{2,1,0:T(8,128)S(1)}, f32[2,16,32]{2,1,0:T(8,128)S(1)}, u32[]{:S(2)}, u32[]{:S(2)}) %collective-permute-start.7) | collective-permute-done | bytes 4128 | tf_op jit(solution)/shard_map/ppermute | solution.py:59
  36.2 1.7 %finish.1 = (f32[1,2,12,16,768]{4,3,2,1,0:T(8,128)}, f32[2,4,8]{2,1,0:T(4,128)}) custom-call(f32[2,16,32]{2,1,0:T(8,128)S(1)} %add_add_fusion.total_ref, s32[1,32]{1,0:T(1,128)S(1)} %bitcast.1, f32[1,2,12,16,768]{4,3,2,1,0:T(8,128)S(1)} %copy-done.1, f32[2,4,16,768]{3,2,1,0:T(8,128)S(1)} %collective-permute-done.1.refs_5_.middle_ref, ...), custom_call_target="tpu_custom_call" | custom-call | flops 1 | bytes 1 | tf_op jit(solution)/shard_map/finish/pallas_call | solution.py:550
  (19 shorter events, 0.1 us)
Async XLA Ops:
  0.6 3.4 %copy-start.1 = (f32[1,2,12,16,768]{4,3,2,1,0:T(8,128)S(1)}, f32[1,2,12,16,768]{4,3,2,1,0:T(8,128)}, u32[]{:S(2)}) copy-start(f32[1,2,12,16,768]{4,3,2,1,0:T(8,128)} %state_ref.3) | copy-start | bytes 3538948
  0.6 3.4 %copy-start.2 = (f32[1,12,16,768]{3,2,1,0:T(8,128)S(1)}, f32[1,12,16,768]{3,2,1,0:T(8,128)}, u32[]{:S(2)}) copy-start(f32[1,12,16,768]{3,2,1,0:T(8,128)} %refs_0_.1) | copy-start | bytes 1769476
  0.6 3.4 %copy-start = (f32[1,12,16,768]{3,2,1,0:T(8,128)S(1)}, f32[1,12,16,768]{3,2,1,0:T(8,128)}, u32[]{:S(2)}) copy-start(f32[1,12,16,768]{3,2,1,0:T(8,128)} %refs_1_.1) | copy-start | bytes 1769476
  2.6 11.4 %copy-start.3 = (s32[4,2,2,12]{3,2,1,0:T(2,128)S(1)}, s32[4,2,2,12]{3,2,1,0:T(2,128)}, u32[]{:S(2)}) copy-start(s32[4,2,2,12]{3,2,1,0:T(2,128)} %offset_ref.1) | copy-start | bytes 2308
  2.6 11.4 %copy-start.4 = (f32[4,2,2,12]{3,2,1,0:T(2,128)S(1)}, f32[4,2,2,12]{3,2,1,0:T(2,128)}, u32[]{:S(2)}) copy-start(f32[4,2,2,12]{3,2,1,0:T(2,128)} %weight_ref.1) | copy-start | bytes 2308
  2.6 11.4 %copy-start.5 = (s32[2,2,12]{2,1,0:T(2,128)S(1)}, s32[2,2,12]{2,1,0:T(2,128)}, u32[]{:S(2)}) copy-start(s32[2,2,12]{2,1,0:T(2,128)} %cell_ref.1) | copy-start | bytes 580
  2.6 13.6 %collective-permute-start.2 = (f32[12,16,768]{2,1,0:T(8,128)S(1)}, f32[12,16,768]{2,1,0:T(8,128)S(1)}, u32[]{:S(2)}, u32[]{:S(2)}) collective-permute-start(f32[12,16,768]{2,1,0:T(8,128)S(1)} %pack.1.refs_2_), channel_id=1, source_target_pairs={{1,0},{2,1},{3,2},{4,5},{5,6},{6,7},{9,8},{10,9},{11,10},{12,13},{... | collective-permute-start | bytes 1769480 | tf_op jit(solution)/shard_map/ppermute | solution.py:32
  7.1 14.0 %collective-permute-start = (f32[11,16,768]{2,1,0:T(8,128)S(1)}, f32[11,16,768]{2,1,0:T(8,128)S(1)}, u32[]{:S(2)}, u32[]{:S(2)}) collective-permute-start(f32[11,16,768]{2,1,0:T(8,128)S(1)} %get-tuple-element.12.mine_ref), channel_id=1, source_target_pairs={{0,1},{1,2},{2,3},{5,4},{6,5},{7,6},{8,9},{9,10},{10,11},{13,12},{... | collective-permute-start | bytes 1622024 | tf_op jit(solution)/shard_map/ppermute | solution.py:32
  12.7 8.4 %collective-permute-start.1 = (f32[2,4,16,768]{3,2,1,0:T(8,128)S(1)}, f32[2,4,16,768]{3,2,1,0:T(8,128)S(1)}, u32[]{:S(2)}, u32[]{:S(2)}) collective-permute-start(f32[2,4,16,768]{3,2,1,0:T(8,128)S(1)} %get-tuple-element.14), channel_id=1, source_target_pairs={{4,0},{8,4},{12,8},{5,1},{9,5},{13,9},{6,2},{10,6},{14,10},{7,3},{... | collective-permute-start | bytes 1179656 | tf_op jit(solution)/shard_map/ppermute | solution.py:23
  17.2 5.4 %collective-permute-start.3 = (f32[2,16,32]{2,1,0:T(8,128)S(1)}, f32[2,16,32]{2,1,0:T(8,128)S(1)}, u32[]{:S(2)}, u32[]{:S(2)}) collective-permute-start(f32[2,16,32]{2,1,0:T(8,128)S(1)} %ghost.1.refs_6_), channel_id=1, source_target_pairs={{0,8},{4,12},{8,0},{12,4},{1,9},{5,13},{9,1},{13,5},{2,10},{6,14},... | collective-permute-start | bytes 12296 | tf_op jit(solution)/shard_map/ppermute | solution.py:59
  19.7 16.5 %copy-start.6 = (s32[32]{0:T(128)S(1)}, s32[32]{0:T(128)}, u32[]{:S(2)}) copy-start(s32[32]{0:T(128)} %param.13) | copy-start | bytes 388
  19.7 16.5 %collective-permute-start.8 = (f32[2,4,16,768]{3,2,1,0:T(8,128)S(1)}, f32[2,4,16,768]{3,2,1,0:T(8,128)S(1)}, u32[]{:S(2)}, u32[]{:S(2)}) collective-permute-start(f32[2,4,16,768]{3,2,1,0:T(8,128)S(1)} %get-tuple-element.20), channel_id=1, source_target_pairs={{4,0},{8,4},{12,8},{5,1},{9,5},{13,9},{6,2},{10,6},{14,10},{7,3},{... | collective-permute-start | bytes 1179656 | tf_op jit(solution)/shard_map/ppermute | solution.py:23
  23.4 12.8 %collective-permute-start.9 = (f32[2,4,16,768]{3,2,1,0:T(8,128)S(1)}, f32[2,4,16,768]{3,2,1,0:T(8,128)S(1)}, u32[]{:S(2)}, u32[]{:S(2)}) collective-permute-start(f32[2,4,16,768]{3,2,1,0:T(8,128)S(1)} %get-tuple-element.21), channel_id=1, source_target_pairs={{4,0},{8,4},{12,8},{5,1},{9,5},{13,9},{6,2},{10,6},{14,10},{7,3},{... | collective-permute-start | bytes 1179656 | tf_op jit(solution)/shard_map/ppermute | solution.py:23
  24.7 2.3 %collective-permute-start.4 = (f32[2,16,32]{2,1,0:T(8,128)S(1)}, f32[2,16,32]{2,1,0:T(8,128)S(1)}, u32[]{:S(2)}, u32[]{:S(2)}) collective-permute-start(f32[2,16,32]{2,1,0:T(8,128)S(1)} %get-tuple-element.19), channel_id=1, source_target_pairs={{0,4},{4,0},{8,12},{12,8},{1,5},{5,1},{9,13},{13,9},{2,6},{6,2},{1... | collective-permute-start | bytes 12296 | tf_op jit(solution)/shard_map/ppermute | solution.py:59
  27.0 4.4 %collective-permute-start.5 = (f32[2,16,32]{2,1,0:T(8,128)S(1)}, f32[2,16,32]{2,1,0:T(8,128)S(1)}, u32[]{:S(2)}, u32[]{:S(2)}) collective-permute-start(f32[2,16,32]{2,1,0:T(8,128)S(1)} %add.12), channel_id=1, source_target_pairs={{0,1},{1,0},{2,3},{3,2},{4,5},{5,4},{6,7},{7,6},{8,9},{9,8},{10,11... | collective-permute-start | bytes 12296 | tf_op jit(solution)/shard_map/ppermute | solution.py:59
  28.6 4.8 %collective-permute-start.6 = (f32[2,16,32]{2,1,0:T(8,128)S(1)}, f32[2,16,32]{2,1,0:T(8,128)S(1)}, u32[]{:S(2)}, u32[]{:S(2)}) collective-permute-start(f32[2,16,32]{2,1,0:T(8,128)S(1)} %add.12), channel_id=1, source_target_pairs={{0,2},{1,3},{2,0},{3,1},{4,6},{5,7},{6,4},{7,5},{8,10},{9,11},{10,... | collective-permute-start | bytes 12296 | tf_op jit(solution)/shard_map/ppermute | solution.py:59
  30.6 5.5 %collective-permute-start.7 = (f32[2,16,32]{2,1,0:T(8,128)S(1)}, f32[2,16,32]{2,1,0:T(8,128)S(1)}, u32[]{:S(2)}, u32[]{:S(2)}) collective-permute-start(f32[2,16,32]{2,1,0:T(8,128)S(1)} %add.12), channel_id=1, source_target_pairs={{0,3},{1,2},{2,1},{3,0},{4,7},{5,6},{6,5},{7,4},{8,11},{9,10},{10,... | collective-permute-start | bytes 12296 | tf_op jit(solution)/shard_map/ppermute | solution.py:59

commit v11 on v10

--- a/solution.py
+++ b/solution.py
@@ -32,31 +32,15 @@
     return lax.ppermute(value, ("sub", "hor"), pairs)
 
 
-def peers_along(axis, step, group):
-    size = lax.axis_size(axis)
-    return [[(i, i ^ (step * j)) for i in range(size)] for j in range(1, group)]
-
-
 def rounds():
     subs, hors = lax.axis_size("sub"), lax.axis_size("hor")
     assert not subs & (subs - 1) and not hors & (hors - 1)
-    order = []
-    step = 2
-    while step < subs:
-        order.append(("sub", step, 2))
-        step *= 2
-    if subs > 1:
-        order.append(("sub", 1, 2))
-    step = 1
-    while step < hors:
-        group = min(4, hors // step)
-        order.append(("hor", step, group))
-        step *= group
-    return order
-
-
-def exchange(value, axis, step, group):
-    return [lax.ppermute(value, axis, pairs) for pairs in peers_along(axis, step, group)]
+    order = [("sub", 1 << n) for n in reversed(range(subs.bit_length() - 1))]
+    return order + [("hor", 1 << n) for n in range(hors.bit_length() - 1)]
+
+
+def exchanged(value, axis, distance):
+    return lax.ppermute(value, axis, [(i, i ^ distance) for i in range(lax.axis_size(axis))])
 
 
 def parity():
@@ -381,9 +365,7 @@
     mend_side(flip, east_ref, north_ref, mine_ref, other_ref, store, store_column)
 
 
-def mend_b_kernel(*refs):
-    east_ref, north_ref, mine_ref, other_ref, ends_ref, _ = refs[:6]
-    out_ref, sum_ref = refs[-2:]
+def mend_b_kernel(east_ref, north_ref, mine_ref, other_ref, ends_ref, _, __, out_ref):
     flip = parity()
     turn = lambda r: r + flip * (STEPS - 1 - 2 * r)
 
@@ -391,23 +373,43 @@
         out_ref[c, turn(r), at, :] = ends_ref[c, flip * STEPS + turn(r), at, :] + value
 
     mend_side(flip, east_ref, north_ref, mine_ref, other_ref, store, None)
-    sum_ref[...] = sum((ref[...] for ref in refs[7:-2]), refs[6][...])
+
+
+def subtract_rows(state_ref, out_hbm, buffer, sems, jobs):
+    copies = []
+    for start, other in jobs:
+        for c in range(other.shape[0]):
+            count = other.shape[1]
+            for r in range(count):
+                buffer[c, start + r] = state_ref[0, c, start + r] - other[c, r]
+            at = pl.ds(start, count)
+            copy = pltpu.make_async_copy(buffer.at[c, at], out_hbm.at[0, c, at], sems.at[len(copies)])
+            copy.start()
+            copies.append(copy)
+    return copies
+
+
+def begin_kernel(state_ref, middle_ref, a_ref, out_hbm, buffer, sems):
+    start = parity() * (state_ref.shape[2] - STEPS)
+    for copy in subtract_rows(state_ref, out_hbm, buffer, sems, ((STEPS, middle_ref), (start, a_ref))):
+        copy.wait()
 
 
 def finish_kernel(
-    total_ref, owner_ref, state_ref, middle_ref, a_ref, b_ref, out_hbm, gradient_ref, buffer, sems
+    begun_hbm, state_ref, b_ref, owner_ref, total_ref, came_ref, out_hbm, gradient_ref, buffer, sems
 ):
-    parts, rows = state_ref.shape[1:3]
-    inner = rows - 2 * STEPS
-    a_start = parity() * (rows - STEPS)
-    b_start = (1 - parity()) * (rows - STEPS)
+    parts = b_ref.shape[0]
+    start = (1 - parity()) * (state_ref.shape[2] - STEPS)
+    copies = subtract_rows(state_ref, out_hbm, buffer, sems, ((start, b_ref),))
+
     share, mine = gradient_ref.shape[1:]
     start = lax.axis_index("hor") * mine
     chosen = []
     for c in range(parts):
-        block = total_ref[c, :share, :]
-        for s in range(1, total_ref.shape[1] // share):
-            block = jnp.where(lax.axis_index("sub") == s, total_ref[c, s * share:(s + 1) * share, :], block)
+        total = total_ref[c] + came_ref[c]
+        block = total[:share]
+        for s in range(1, total.shape[0] // share):
+            block = jnp.where(lax.axis_index("sub") == s, total[s * share:(s + 1) * share], block)
         chosen.append(block)
     chosen = jnp.concatenate(chosen, 0)
     column = lax.broadcasted_iota(jnp.int32, (parts * share, mine), 1)
@@ -417,18 +419,6 @@
         picked = jnp.where(column == q, value, picked)
     for c in range(parts):
         gradient_ref[c] = picked[c * share:(c + 1) * share]
-
-    copies = []
-    for start, other in ((STEPS, middle_ref), (a_start, a_ref), (b_start, b_ref)):
-        for c in range(parts):
-            count = other.shape[1]
-            for r in range(count):
-                buffer[c, start + r] = state_ref[0, c, start + r] - other[c, r]
-            at = pl.ds(start, count)
-            copy = pltpu.make_async_copy(buffer.at[c, at], out_hbm.at[0, c, at], sems.at[len(copies)])
-            copy.start()
-            copies.append(copy)
-
     for copy in copies:
         copy.wait()
 
@@ -533,33 +523,45 @@
         name="ghost",
     )(north, first_came, a_columns, mixing, base)
     order = rounds()
-    came = exchange(total, *order[0])
-    side_b, total = pl.pallas_call(
+    total = total + exchanged(total, *order[0])
+    side_b = pl.pallas_call(
         mend_b_kernel,
-        in_specs=[vmem] * 5 + [pl.BlockSpec(memory_space=pl.ANY)] + [vmem] * (1 + len(came)),
-        out_specs=[vmem] * 2,
-        out_shape=[f32(parts, STEPS, levels, width), f32(parts, levels, slots)],
+        in_specs=[vmem] * 5 + [pl.BlockSpec(memory_space=pl.ANY)] * 2,
+        out_specs=vmem,
+        out_shape=f32(parts, STEPS, levels, width),
         compiler_params=PARAMS,
         cost_estimate=BRIEF,
         name="mend_b",
-    )(east, north, first_pack, second_came, ends, middle_came, total, *came)
+    )(east, north, first_pack, second_came, ends, middle_came, total)
     b_came = along(side_b, "sub", -1)
 
-    for each in order[1:]:
-        total = sum(exchange(total, *each), total)
+    for each in order[1:-1]:
+        total = total + exchanged(total, *each)
+    came = exchanged(total, *order[-1])
+
+    result = f32(*adjoint_state.shape)
+    buffer = pltpu.VMEM((parts, rows, levels, width), jnp.float32)
+    begun = pl.pallas_call(
+        begin_kernel,
+        in_specs=[vmem] * 3,
+        out_specs=hbm,
+        out_shape=result,
+        scratch_shapes=[buffer, pltpu.SemaphoreType.DMA((2 * parts,))],
+        compiler_params=PARAMS,
+        cost_estimate=BRIEF,
+        name="begin",
+    )(state, middle_came, a_came)
     adjoint_result, boundary_gradient = pl.pallas_call(
         finish_kernel,
-        in_specs=[vmem] * 6,
+        in_specs=[hbm] + [vmem] * 5,
         out_specs=[hbm, vmem],
-        out_shape=[f32(*adjoint_state.shape), f32(parts, levels // subs, slots // hors)],
-        scratch_shapes=[
-            pltpu.VMEM((parts, rows, levels, width), jnp.float32),
-            pltpu.SemaphoreType.DMA((3 * parts,)),
-        ],
+        out_shape=[result, f32(parts, levels // subs, slots // hors)],
+        scratch_shapes=[buffer, pltpu.SemaphoreType.DMA((parts,))],
+        input_output_aliases={0: 0},
         compiler_params=PARAMS,
         cost_estimate=BRIEF,
         name="finish",
-    )(total, owner_slot[None], state, middle_came, a_came, b_came)
+    )(begun, state, b_came, owner_slot[None], total, came)
     return (adjoint_result, boundary_gradient)
 
 

time: 38.1 us -> 37.1 us (0.974)
  waiting for transfers between devices: 9.22 us -> 7.97 us
  Pallas kernels: 8.71 us -> 9.36 us
  starting transfers between devices: 19 us -> 18.6 us
    ppermute x5 -> x4, waiting for transfers between devices: 7.35 us -> 6.1 us  [exchanged(): lax.ppermute(value, axis, [(i, i ^ distance) for i in range(lax.axis_size...]
    pallas_call x1 -> x2, Pallas kernels: 1.68 us -> 2.31 us  [the longest x1 1.38 us: local(): pl.pallas_call(finish_kernel, in_specs=[hbm] + [vmem] * 5, out_specs=[hbm...]
    ppermute x5 -> x4, starting transfers between devices: 8.01 us -> 7.76 us  [exchanged(): lax.ppermute(value, axis, [(i, i ^ distance) for i in range(lax.axis_size...]
  transfers between devices with their start and end apart: 10 -> 9, of which waited for: 5 -> 5; matrix products, arithmetic and copies ran while one was open for 0% -> 0% of each run, Pallas kernels for 14% -> 16%
where the time goes in v11:
time: 37.1 us; the launch traced here: 36.8 us
  starting transfers between devices  18.6 us (50%)
  Pallas kernels  9.36 us (25%)
  waiting for transfers between devices  7.97 us (21%)
  between operations  0.83 us (2%)
    ppermute x4, starting transfers between devices, exchanged(): lax.ppermute(value, axis, [(i, i ^ distance) for i in range(lax.axis_size...  7.76 us
    ppermute x2, starting transfers between devices, alternating(): return lax.ppermute(value, ('sub', 'hor'), pairs)  7.01 us
    ppermute x4, waiting for transfers between devices, exchanged(): lax.ppermute(value, axis, [(i, i ^ distance) for i in range(lax.axis_size...  6.1 us
    ppermute x3, starting transfers between devices, along(): return lax.ppermute(value, axis, pairs)  3.86 us
    pallas_call x1, Pallas kernels, local(): pl.pallas_call(sweep_kernel, in_specs=[vmem] * 3, out_specs=[vmem] * 4, o...  2.99 us
    pallas_call x1, Pallas kernels, local(): pl.pallas_call(pack_kernel, in_specs=[hbm] * 6, out_specs=vmem, out_shape...  1.93 us
    ppermute x2, waiting for transfers between devices, alternating(): return lax.ppermute(value, ('sub', 'hor'), pairs)  1.86 us
    pallas_call x1, Pallas kernels, local(): pl.pallas_call(finish_kernel, in_specs=[hbm] + [vmem] * 5, out_specs=[hbm...  1.38 us
  transfers between devices with their start and end apart: 9, of which 5 were waited for; matrix products, arithmetic and copies ran while one was open for 0% of the time, Pallas kernels for 16%

profile of v11, /device:TPU:0, one launch (start us, length us, event | category | flops | bytes accessed | tf_op | source)
XLA Modules:
  0.0 36.8 jit_solution(14716195325346213908)
XLA Ops:
  0.7 1.9 %pack.1.mine_ref = f32[12,16,768]{2,1,0:T(8,128)S(1)} custom-call(f32[1,2,12,16,768]{4,3,2,1,0:T(8,128)} %state_ref.5, f32[1,12,16,768]{3,2,1,0:T(8,128)} %east_ref.5, f32[1,12,16,768]{3,2,1,0:T(8,128)} %north_ref.9, s32[2,2,12]{2,1,0:T(2,128)} %cell_ref.1, s32[4,2,2,12]{3,2,1,0:T(2,128)} %offset_ref.1, f32[4,2,2,12]{3,2,1,0:T(2,128)} %weight_ref.1), custom_call_target="tpu_custom_call" | custom-call | flops 1 | bytes 1 | tf_op jit(solution)/shard_map/pack/pallas_call | solution.py:452
  2.6 0.0 copy-start.4
  2.6 0.0 copy-start.5
  2.6 1.4 %collective-permute-start.1 = (f32[12,16,768]{2,1,0:T(8,128)S(1)}, f32[12,16,768]{2,1,0:T(8,128)S(1)}, u32[]{:S(2)}, u32[]{:S(2)}) collective-permute-start(f32[12,16,768]{2,1,0:T(8,128)S(1)} %pack.1.mine_ref), channel_id=1, source_target_pairs={{1,0},{2,1},{3,2},{4,5},{5,6},{6,7},{9,8},{10,9},{11,10},{12,13},{... | collective-permute-start | bytes 1769480 | tf_op jit(solution)/shard_map/ppermute | solution.py:32
  4.1 3.0 %sweep.1 = (f32[11,16,768]{2,1,0:T(8,128)S(1)}, f32[2,4,16,768]{3,2,1,0:T(8,128)S(1)}, f32[2,8,16,768]{3,2,1,0:T(8,128)S(1)}, f32[2,2,12,16,128]{4,3,2,1,0:T(8,128)S(1)}) custom-call(f32[1,2,12,16,768]{4,3,2,1,0:T(8,128)S(1)} %copy-done.1, f32[1,12,16,768]{3,2,1,0:T(8,128)S(1)} %copy-done.2, f32[1,12,16,768]{3,2,1,0:T(8,128)S(1)} %copy-done), custom_call_target="tpu_custom_call" | custom-call | flops 1 | bytes 1 | tf_op jit(solution)/shard_map/sweep/pallas_call | solution.py:471
  7.1 5.6 %collective-permute-start.3 = (f32[11,16,768]{2,1,0:T(8,128)S(1)}, f32[11,16,768]{2,1,0:T(8,128)S(1)}, u32[]{:S(2)}, u32[]{:S(2)}) collective-permute-start(f32[11,16,768]{2,1,0:T(8,128)S(1)} %get-tuple-element.11.mine_ref), channel_id=1, source_target_pairs={{0,1},{1,2},{2,3},{5,4},{6,5},{7,6},{8,9},{9,10},{10,11},{13,12},{... | collective-permute-start | bytes 1622024 | tf_op jit(solution)/shard_map/ppermute | solution.py:32
  12.7 1.3 %collective-permute-start = (f32[2,4,16,768]{3,2,1,0:T(8,128)S(1)}, f32[2,4,16,768]{3,2,1,0:T(8,128)S(1)}, u32[]{:S(2)}, u32[]{:S(2)}) collective-permute-start(f32[2,4,16,768]{3,2,1,0:T(8,128)S(1)} %get-tuple-element.10), channel_id=1, source_target_pairs={{4,0},{8,4},{12,8},{5,1},{9,5},{13,9},{6,2},{10,6},{14,10},{7,3},{... | collective-permute-start | bytes 1179656 | tf_op jit(solution)/shard_map/ppermute | solution.py:23
  14.0 0.4 ghost_base.1
  14.4 1.9 %collective-permute-done.1.other_ref = f32[12,16,768]{2,1,0:T(8,128)S(1)} collective-permute-done((f32[12,16,768]{2,1,0:T(8,128)S(1)}, f32[12,16,768]{2,1,0:T(8,128)S(1)}, u32[]{:S(2)}, u32[]{:S(2)}) %collective-permute-start.1) | collective-permute-done | bytes 589856 | tf_op jit(solution)/shard_map/ppermute | solution.py:32
  16.2 0.8 %mend_a.1 = (f32[2,4,16,768]{3,2,1,0:T(8,128)S(1)}, f32[2,2,6,16,128]{4,3,2,1,0:T(8,128)S(1)}) custom-call(f32[1,12,16,768]{3,2,1,0:T(8,128)S(1)} %copy-done.2, f32[1,12,16,768]{3,2,1,0:T(8,128)S(1)} %copy-done, f32[11,16,768]{2,1,0:T(8,128)S(1)} %get-tuple-element.11.mine_ref, f32[12,16,768]{2,1,0:T(8,128)S(1)} %collective-permute-done.1.other_ref, ...), custom_call_target="tpu_custom_call" | custom-call | flops 1 | bytes 1 | tf_op jit(solution)/shard_map/mend_a/pallas_call | solution.py:505
  17.0 0.2 ghost.1
  17.2 2.4 %collective-permute-start.4 = (f32[2,16,32]{2,1,0:T(8,128)S(1)}, f32[2,16,32]{2,1,0:T(8,128)S(1)}, u32[]{:S(2)}, u32[]{:S(2)}) collective-permute-start(f32[2,16,32]{2,1,0:T(8,128)S(1)} %ghost.1), channel_id=1, source_target_pairs={{0,8},{4,12},{8,0},{12,4},{1,9},{5,13},{9,1},{13,5},{2,10},{6,14},... | collective-permute-start | bytes 12296 | tf_op jit(solution)/shard_map/ppermute | solution.py:43
  19.7 1.3 %collective-permute-start.2 = (f32[2,4,16,768]{3,2,1,0:T(8,128)S(1)}, f32[2,4,16,768]{3,2,1,0:T(8,128)S(1)}, u32[]{:S(2)}, u32[]{:S(2)}) collective-permute-start(f32[2,4,16,768]{3,2,1,0:T(8,128)S(1)} %get-tuple-element.15), channel_id=1, source_target_pairs={{4,0},{8,4},{12,8},{5,1},{9,5},{13,9},{6,2},{10,6},{14,10},{7,3},{... | collective-permute-start | bytes 1179656 | tf_op jit(solution)/shard_map/ppermute | solution.py:23
  21.0 1.7 %collective-permute-done.4 = f32[2,16,32]{2,1,0:T(8,128)S(1)} collective-permute-done((f32[2,16,32]{2,1,0:T(8,128)S(1)}, f32[2,16,32]{2,1,0:T(8,128)S(1)}, u32[]{:S(2)}, u32[]{:S(2)}) %collective-permute-start.4) | collective-permute-done | bytes 4128 | tf_op jit(solution)/shard_map/ppermute | solution.py:43
  22.6 0.8 %mend_b.1 = f32[2,4,16,768]{3,2,1,0:T(8,128)S(1)} custom-call(f32[1,12,16,768]{3,2,1,0:T(8,128)S(1)} %copy-done.2, f32[1,12,16,768]{3,2,1,0:T(8,128)S(1)} %copy-done, f32[12,16,768]{2,1,0:T(8,128)S(1)} %pack.1.mine_ref, f32[11,16,768]{2,1,0:T(8,128)S(1)} %collective-permute-done.3.other_ref, f32[2,8,16,768]{3,2,1,0:T(8,128)S(1)} %get-tuple-element.12.ends_ref, ...), custom_call_target="tpu_custom_call" | custom-call | flops 1 | bytes 1 | tf_op jit(solution)/shard_map/mend_b/pallas_call | solution.py:527
  23.4 1.3 %collective-permute-start.5 = (f32[2,4,16,768]{3,2,1,0:T(8,128)S(1)}, f32[2,4,16,768]{3,2,1,0:T(8,128)S(1)}, u32[]{:S(2)}, u32[]{:S(2)}) collective-permute-start(f32[2,4,16,768]{3,2,1,0:T(8,128)S(1)} %mend_b.1), channel_id=1, source_target_pairs={{4,0},{8,4},{12,8},{5,1},{9,5},{13,9},{6,2},{10,6},{14,10},{7,3},{... | collective-permute-start | bytes 1179656 | tf_op jit(solution)/shard_map/ppermute | solution.py:23
  24.7 1.2 %collective-permute-start.6 = (f32[2,16,32]{2,1,0:T(8,128)S(1)}, f32[2,16,32]{2,1,0:T(8,128)S(1)}, u32[]{:S(2)}, u32[]{:S(2)}) collective-permute-start(f32[2,16,32]{2,1,0:T(8,128)S(1)} %add.9.__), channel_id=1, source_target_pairs={{0,4},{4,0},{8,12},{12,8},{1,5},{5,1},{9,13},{13,9},{2,6},{6,2},{1... | collective-permute-start | bytes 12296 | tf_op jit(solution)/shard_map/ppermute | solution.py:43
  25.9 1.1 %collective-permute-done.6 = f32[2,16,32]{2,1,0:T(8,128)S(1)} collective-permute-done((f32[2,16,32]{2,1,0:T(8,128)S(1)}, f32[2,16,32]{2,1,0:T(8,128)S(1)}, u32[]{:S(2)}, u32[]{:S(2)}) %collective-permute-start.6) | collective-permute-done | bytes 4128 | tf_op jit(solution)/shard_map/ppermute | solution.py:43
  27.1 1.5 %collective-permute-start.7 = (f32[2,16,32]{2,1,0:T(8,128)S(1)}, f32[2,16,32]{2,1,0:T(8,128)S(1)}, u32[]{:S(2)}, u32[]{:S(2)}) collective-permute-start(f32[2,16,32]{2,1,0:T(8,128)S(1)} %add.10), channel_id=1, source_target_pairs={{0,1},{1,0},{2,3},{3,2},{4,5},{5,4},{6,7},{7,6},{8,9},{9,8},{10,11... | collective-permute-start | bytes 12296 | tf_op jit(solution)/shard_map/ppermute | solution.py:43
  28.6 2.2 %collective-permute-done.7 = f32[2,16,32]{2,1,0:T(8,128)S(1)} collective-permute-done((f32[2,16,32]{2,1,0:T(8,128)S(1)}, f32[2,16,32]{2,1,0:T(8,128)S(1)}, u32[]{:S(2)}, u32[]{:S(2)}) %collective-permute-start.7) | collective-permute-done | bytes 4128 | tf_op jit(solution)/shard_map/ppermute | solution.py:43
  30.8 2.6 %collective-permute-start.8 = (f32[2,16,32]{2,1,0:T(8,128)S(1)}, f32[2,16,32]{2,1,0:T(8,128)S(1)}, u32[]{:S(2)}, u32[]{:S(2)}) collective-permute-start(f32[2,16,32]{2,1,0:T(8,128)S(1)} %add.11.total_ref), channel_id=1, source_target_pairs={{0,2},{1,3},{2,0},{3,1},{4,6},{5,7},{6,4},{7,5},{8,10},{9,11},{10,... | collective-permute-start | bytes 12296 | tf_op jit(solution)/shard_map/ppermute | solution.py:43
  33.4 0.9 %begin.1.begun_hbm = f32[1,2,12,16,768]{4,3,2,1,0:T(8,128)} custom-call(f32[1,2,12,16,768]{4,3,2,1,0:T(8,128)S(1)} %copy-done.1, f32[2,4,16,768]{3,2,1,0:T(8,128)S(1)} %collective-permute-done.middle_ref._, f32[2,4,16,768]{3,2,1,0:T(8,128)S(1)} %collective-permute-done.2.a_ref), custom_call_target="tpu_custom_call" | custom-call | flops 1 | bytes 1 | tf_op jit(solution)/shard_map/begin/pallas_call | solution.py:544
  34.3 1.1 %collective-permute-done.8.came_ref = f32[2,16,32]{2,1,0:T(8,128)S(1)} collective-permute-done((f32[2,16,32]{2,1,0:T(8,128)S(1)}, f32[2,16,32]{2,1,0:T(8,128)S(1)}, u32[]{:S(2)}, u32[]{:S(2)}) %collective-permute-start.8) | collective-permute-done | bytes 4128 | tf_op jit(solution)/shard_map/ppermute | solution.py:43
  35.5 1.4 %finish.1 = (f32[1,2,12,16,768]{4,3,2,1,0:T(8,128)}, f32[2,4,8]{2,1,0:T(4,128)}) custom-call(f32[1,2,12,16,768]{4,3,2,1,0:T(8,128)} %begin.1.begun_hbm, f32[1,2,12,16,768]{4,3,2,1,0:T(8,128)S(1)} %copy-done.1, f32[2,4,16,768]{3,2,1,0:T(8,128)S(1)} %collective-permute-done.5.b_ref, s32[1,32]{1,0:T(1,128)S(1)} %bitcast.1, ...), custom_call_target="tpu_custom_call", output_to_operand_aliasing={{0}: (0, {})} | custom-call | flops 1 | bytes 1 | tf_op jit(solution)/shard_map/finish/pallas_call | solution.py:554
  (19 shorter events, 0.0 us)
Async XLA Ops:
  0.6 3.4 %copy-start.1 = (f32[1,2,12,16,768]{4,3,2,1,0:T(8,128)S(1)}, f32[1,2,12,16,768]{4,3,2,1,0:T(8,128)}, u32[]{:S(2)}) copy-start(f32[1,2,12,16,768]{4,3,2,1,0:T(8,128)} %state_ref.5) | copy-start | bytes 3538948
  0.6 3.4 %copy-start.2 = (f32[1,12,16,768]{3,2,1,0:T(8,128)S(1)}, f32[1,12,16,768]{3,2,1,0:T(8,128)}, u32[]{:S(2)}) copy-start(f32[1,12,16,768]{3,2,1,0:T(8,128)} %east_ref.5) | copy-start | bytes 1769476
  0.6 3.4 %copy-start = (f32[1,12,16,768]{3,2,1,0:T(8,128)S(1)}, f32[1,12,16,768]{3,2,1,0:T(8,128)}, u32[]{:S(2)}) copy-start(f32[1,12,16,768]{3,2,1,0:T(8,128)} %north_ref.9) | copy-start | bytes 1769476
  2.6 11.4 %copy-start.3 = (s32[4,2,2,12]{3,2,1,0:T(2,128)S(1)}, s32[4,2,2,12]{3,2,1,0:T(2,128)}, u32[]{:S(2)}) copy-start(s32[4,2,2,12]{3,2,1,0:T(2,128)} %offset_ref.1) | copy-start | bytes 2308
  2.6 11.4 %copy-start.4 = (f32[4,2,2,12]{3,2,1,0:T(2,128)S(1)}, f32[4,2,2,12]{3,2,1,0:T(2,128)}, u32[]{:S(2)}) copy-start(f32[4,2,2,12]{3,2,1,0:T(2,128)} %weight_ref.1) | copy-start | bytes 2308
  2.6 11.4 %copy-start.5 = (s32[2,2,12]{2,1,0:T(2,128)S(1)}, s32[2,2,12]{2,1,0:T(2,128)}, u32[]{:S(2)}) copy-start(s32[2,2,12]{2,1,0:T(2,128)} %cell_ref.1) | copy-start | bytes 580
  2.6 13.6 %collective-permute-start.1 = (f32[12,16,768]{2,1,0:T(8,128)S(1)}, f32[12,16,768]{2,1,0:T(8,128)S(1)}, u32[]{:S(2)}, u32[]{:S(2)}) collective-permute-start(f32[12,16,768]{2,1,0:T(8,128)S(1)} %pack.1.mine_ref), channel_id=1, source_target_pairs={{1,0},{2,1},{3,2},{4,5},{5,6},{6,7},{9,8},{10,9},{11,10},{12,13},{... | collective-permute-start | bytes 1769480 | tf_op jit(solution)/shard_map/ppermute | solution.py:32
  7.1 15.5 %collective-permute-start.3 = (f32[11,16,768]{2,1,0:T(8,128)S(1)}, f32[11,16,768]{2,1,0:T(8,128)S(1)}, u32[]{:S(2)}, u32[]{:S(2)}) collective-permute-start(f32[11,16,768]{2,1,0:T(8,128)S(1)} %get-tuple-element.11.mine_ref), channel_id=1, source_target_pairs={{0,1},{1,2},{2,3},{5,4},{6,5},{7,6},{8,9},{9,10},{10,11},{13,12},{... | collective-permute-start | bytes 1622024 | tf_op jit(solution)/shard_map/ppermute | solution.py:32
  12.7 9.9 %collective-permute-start = (f32[2,4,16,768]{3,2,1,0:T(8,128)S(1)}, f32[2,4,16,768]{3,2,1,0:T(8,128)S(1)}, u32[]{:S(2)}, u32[]{:S(2)}) collective-permute-start(f32[2,4,16,768]{3,2,1,0:T(8,128)S(1)} %get-tuple-element.10), channel_id=1, source_target_pairs={{4,0},{8,4},{12,8},{5,1},{9,5},{13,9},{6,2},{10,6},{14,10},{7,3},{... | collective-permute-start | bytes 1179656 | tf_op jit(solution)/shard_map/ppermute | solution.py:23
  17.2 5.4 %collective-permute-start.4 = (f32[2,16,32]{2,1,0:T(8,128)S(1)}, f32[2,16,32]{2,1,0:T(8,128)S(1)}, u32[]{:S(2)}, u32[]{:S(2)}) collective-permute-start(f32[2,16,32]{2,1,0:T(8,128)S(1)} %ghost.1), channel_id=1, source_target_pairs={{0,8},{4,12},{8,0},{12,4},{1,9},{5,13},{9,1},{13,5},{2,10},{6,14},... | collective-permute-start | bytes 12296 | tf_op jit(solution)/shard_map/ppermute | solution.py:43
  19.7 13.7 %collective-permute-start.2 = (f32[2,4,16,768]{3,2,1,0:T(8,128)S(1)}, f32[2,4,16,768]{3,2,1,0:T(8,128)S(1)}, u32[]{:S(2)}, u32[]{:S(2)}) collective-permute-start(f32[2,4,16,768]{3,2,1,0:T(8,128)S(1)} %get-tuple-element.15), channel_id=1, source_target_pairs={{4,0},{8,4},{12,8},{5,1},{9,5},{13,9},{6,2},{10,6},{14,10},{7,3},{... | collective-permute-start | bytes 1179656 | tf_op jit(solution)/shard_map/ppermute | solution.py:23
  23.4 12.0 %collective-permute-start.5 = (f32[2,4,16,768]{3,2,1,0:T(8,128)S(1)}, f32[2,4,16,768]{3,2,1,0:T(8,128)S(1)}, u32[]{:S(2)}, u32[]{:S(2)}) collective-permute-start(f32[2,4,16,768]{3,2,1,0:T(8,128)S(1)} %mend_b.1), channel_id=1, source_target_pairs={{4,0},{8,4},{12,8},{5,1},{9,5},{13,9},{6,2},{10,6},{14,10},{7,3},{... | collective-permute-start | bytes 1179656 | tf_op jit(solution)/shard_map/ppermute | solution.py:23
  24.7 2.3 %collective-permute-start.6 = (f32[2,16,32]{2,1,0:T(8,128)S(1)}, f32[2,16,32]{2,1,0:T(8,128)S(1)}, u32[]{:S(2)}, u32[]{:S(2)}) collective-permute-start(f32[2,16,32]{2,1,0:T(8,128)S(1)} %add.9.__), channel_id=1, source_target_pairs={{0,4},{4,0},{8,12},{12,8},{1,5},{5,1},{9,13},{13,9},{2,6},{6,2},{1... | collective-permute-start | bytes 12296 | tf_op jit(solution)/shard_map/ppermute | solution.py:43
  27.1 3.7 %collective-permute-start.7 = (f32[2,16,32]{2,1,0:T(8,128)S(1)}, f32[2,16,32]{2,1,0:T(8,128)S(1)}, u32[]{:S(2)}, u32[]{:S(2)}) collective-permute-start(f32[2,16,32]{2,1,0:T(8,128)S(1)} %add.10), channel_id=1, source_target_pairs={{0,1},{1,0},{2,3},{3,2},{4,5},{5,4},{6,7},{7,6},{8,9},{9,8},{10,11... | collective-permute-start | bytes 12296 | tf_op jit(solution)/shard_map/ppermute | solution.py:43
  30.8 4.6 %copy-start.6 = (s32[32]{0:T(128)S(1)}, s32[32]{0:T(128)}, u32[]{:S(2)}) copy-start(s32[32]{0:T(128)} %param.13) | copy-start | bytes 388
  30.8 4.6 %collective-permute-start.8 = (f32[2,16,32]{2,1,0:T(8,128)S(1)}, f32[2,16,32]{2,1,0:T(8,128)S(1)}, u32[]{:S(2)}, u32[]{:S(2)}) collective-permute-start(f32[2,16,32]{2,1,0:T(8,128)S(1)} %add.11.total_ref), channel_id=1, source_target_pairs={{0,2},{1,3},{2,0},{3,1},{4,6},{5,7},{6,4},{7,5},{8,10},{9,11},{10,... | collective-permute-start | bytes 12296 | tf_op jit(solution)/shard_map/ppermute | solution.py:43

commit v12 on v11

--- a/solution.py
+++ b/solution.py
@@ -35,12 +35,14 @@
 def rounds():
     subs, hors = lax.axis_size("sub"), lax.axis_size("hor")
     assert not subs & (subs - 1) and not hors & (hors - 1)
-    order = [("sub", 1 << n) for n in reversed(range(subs.bit_length() - 1))]
-    return order + [("hor", 1 << n) for n in range(hors.bit_length() - 1)]
-
-
-def exchanged(value, axis, distance):
-    return lax.ppermute(value, axis, [(i, i ^ distance) for i in range(lax.axis_size(axis))])
+    order = [("sub", range(1, min(subs, 4)))]
+    order += [("sub", [1 << n]) for n in range(2, subs.bit_length() - 1)]
+    return order + [("hor", [1 << n]) for n in range(hors.bit_length() - 1)]
+
+
+def exchanged(value, axis, distances):
+    size = lax.axis_size(axis)
+    return sum(lax.ppermute(value, axis, [(i, i ^ distance) for i in range(size)]) for distance in distances)
 
 
 def parity():

time: 37.1 us -> 35.1 us (0.946)
  waiting for transfers between devices: 7.97 us -> 6.91 us
  starting transfers between devices: 18.6 us -> 17.7 us
    ppermute x4 -> x5, waiting for transfers between devices: 6.1 us -> 5.04 us  [exchanged(): lax.ppermute(value, axis, [(i, i ^ distance) for i in range(size)])]
    ppermute x4 -> x5, starting transfers between devices: 7.76 us -> 6.86 us  [exchanged(): lax.ppermute(value, axis, [(i, i ^ distance) for i in range(size)])]
  transfers between devices with their start and end apart: 9 -> 10, of which waited for: 5 -> 5; matrix products, arithmetic and copies ran while one was open for 0% -> 0% of each run, Pallas kernels for 16% -> 17%
where the time goes in v12:
time: 35.1 us; the launch traced here: 34.9 us
  starting transfers between devices  17.7 us (50%)
  Pallas kernels  9.36 us (27%)
  waiting for transfers between devices  6.91 us (20%)
  between operations  0.84 us (2%)
    ppermute x2, starting transfers between devices, alternating(): return lax.ppermute(value, ('sub', 'hor'), pairs)  7.01 us
    ppermute x5, starting transfers between devices, exchanged(): lax.ppermute(value, axis, [(i, i ^ distance) for i in range(size)])  6.86 us
    ppermute x5, waiting for transfers between devices, exchanged(): lax.ppermute(value, axis, [(i, i ^ distance) for i in range(size)])  5.04 us
    ppermute x3, starting transfers between devices, along(): return lax.ppermute(value, axis, pairs)  3.87 us
    pallas_call x1, Pallas kernels, local(): pl.pallas_call(sweep_kernel, in_specs=[vmem] * 3, out_specs=[vmem] * 4, o...  2.99 us
    pallas_call x1, Pallas kernels, local(): pl.pallas_call(pack_kernel, in_specs=[hbm] * 6, out_specs=vmem, out_shape...  1.93 us
    ppermute x2, waiting for transfers between devices, alternating(): return lax.ppermute(value, ('sub', 'hor'), pairs)  1.86 us
    pallas_call x1, Pallas kernels, local(): pl.pallas_call(finish_kernel, in_specs=[hbm] + [vmem] * 5, out_specs=[hbm...  1.38 us
  transfers between devices with their start and end apart: 10, of which 5 were waited for; matrix products, arithmetic and copies ran while one was open for 0% of the time, Pallas kernels for 17%

profile of v12, /device:TPU:0, one launch (start us, length us, event | category | flops | bytes accessed | tf_op | source)
XLA Modules:
  0.0 34.9 jit_solution(18346980795689078763)
XLA Ops:
  0.7 1.9 %pack.1.mine_ref = f32[12,16,768]{2,1,0:T(8,128)S(1)} custom-call(f32[1,2,12,16,768]{4,3,2,1,0:T(8,128)} %state_ref.5, f32[1,12,16,768]{3,2,1,0:T(8,128)} %east_ref.5, f32[1,12,16,768]{3,2,1,0:T(8,128)} %north_ref.9, s32[2,2,12]{2,1,0:T(2,128)} %cell_ref.1, s32[4,2,2,12]{3,2,1,0:T(2,128)} %offset_ref.1, f32[4,2,2,12]{3,2,1,0:T(2,128)} %weight_ref.1), custom_call_target="tpu_custom_call" | custom-call | flops 1 | bytes 1 | tf_op jit(solution)/shard_map/pack/pallas_call | solution.py:454
  2.6 0.0 copy-start.3
  2.6 1.4 %collective-permute-start.1 = (f32[12,16,768]{2,1,0:T(8,128)S(1)}, f32[12,16,768]{2,1,0:T(8,128)S(1)}, u32[]{:S(2)}, u32[]{:S(2)}) collective-permute-start(f32[12,16,768]{2,1,0:T(8,128)S(1)} %pack.1.mine_ref), channel_id=1, source_target_pairs={{1,0},{2,1},{3,2},{4,5},{5,6},{6,7},{9,8},{10,9},{11,10},{12,13},{... | collective-permute-start | bytes 1769480 | tf_op jit(solution)/shard_map/ppermute | solution.py:32
  4.1 3.0 %sweep.1 = (f32[11,16,768]{2,1,0:T(8,128)S(1)}, f32[2,4,16,768]{3,2,1,0:T(8,128)S(1)}, f32[2,8,16,768]{3,2,1,0:T(8,128)S(1)}, f32[2,2,12,16,128]{4,3,2,1,0:T(8,128)S(1)}) custom-call(f32[1,2,12,16,768]{4,3,2,1,0:T(8,128)S(1)} %copy-done.1, f32[1,12,16,768]{3,2,1,0:T(8,128)S(1)} %copy-done.2, f32[1,12,16,768]{3,2,1,0:T(8,128)S(1)} %copy-done), custom_call_target="tpu_custom_call" | custom-call | flops 1 | bytes 1 | tf_op jit(solution)/shard_map/sweep/pallas_call | solution.py:473
  7.1 5.6 %collective-permute-start.3 = (f32[11,16,768]{2,1,0:T(8,128)S(1)}, f32[11,16,768]{2,1,0:T(8,128)S(1)}, u32[]{:S(2)}, u32[]{:S(2)}) collective-permute-start(f32[11,16,768]{2,1,0:T(8,128)S(1)} %get-tuple-element.11.mine_ref), channel_id=1, source_target_pairs={{0,1},{1,2},{2,3},{5,4},{6,5},{7,6},{8,9},{9,10},{10,11},{13,12},{... | collective-permute-start | bytes 1622024 | tf_op jit(solution)/shard_map/ppermute | solution.py:32
  12.7 1.3 %collective-permute-start = (f32[2,4,16,768]{3,2,1,0:T(8,128)S(1)}, f32[2,4,16,768]{3,2,1,0:T(8,128)S(1)}, u32[]{:S(2)}, u32[]{:S(2)}) collective-permute-start(f32[2,4,16,768]{3,2,1,0:T(8,128)S(1)} %get-tuple-element.10), channel_id=1, source_target_pairs={{4,0},{8,4},{12,8},{5,1},{9,5},{13,9},{6,2},{10,6},{14,10},{7,3},{... | collective-permute-start | bytes 1179656 | tf_op jit(solution)/shard_map/ppermute | solution.py:23
  14.0 0.4 %ghost_base.1 = (f32[2,2,12,32]{3,2,1,0:T(8,128)S(1)}, f32[2,16,32]{2,1,0:T(8,128)S(1)}) custom-call(s32[2,2,12]{2,1,0:T(2,128)S(1)} %copy-done.5, s32[4,2,2,12]{3,2,1,0:T(2,128)S(1)} %copy-done.3, f32[4,2,2,12]{3,2,1,0:T(2,128)S(1)} %copy-done.4, f32[2,2,12,16,128]{4,3,2,1,0:T(8,128)S(1)} %get-tuple-element.13.column_ref, f32[1,12,16,768]{3,2,1,0:T(8,128)S(1)} %copy-done), custom_call_target="tpu_custom_call" | custom-call | flops 1 | bytes 1 | tf_op jit(solution)/shard_map/ghost_base/pallas_call | solution.py:496
  14.4 1.9 %collective-permute-done.1.other_ref = f32[12,16,768]{2,1,0:T(8,128)S(1)} collective-permute-done((f32[12,16,768]{2,1,0:T(8,128)S(1)}, f32[12,16,768]{2,1,0:T(8,128)S(1)}, u32[]{:S(2)}, u32[]{:S(2)}) %collective-permute-start.1) | collective-permute-done | bytes 589856 | tf_op jit(solution)/shard_map/ppermute | solution.py:32
  16.2 0.8 %mend_a.1 = (f32[2,4,16,768]{3,2,1,0:T(8,128)S(1)}, f32[2,2,6,16,128]{4,3,2,1,0:T(8,128)S(1)}) custom-call(f32[1,12,16,768]{3,2,1,0:T(8,128)S(1)} %copy-done.2, f32[1,12,16,768]{3,2,1,0:T(8,128)S(1)} %copy-done, f32[11,16,768]{2,1,0:T(8,128)S(1)} %get-tuple-element.11.mine_ref, f32[12,16,768]{2,1,0:T(8,128)S(1)} %collective-permute-done.1.other_ref, ...), custom_call_target="tpu_custom_call" | custom-call | flops 1 | bytes 1 | tf_op jit(solution)/shard_map/mend_a/pallas_call | solution.py:507
  17.0 0.2 ghost.1
  17.2 0.1 collective-permute-start.4
  17.3 2.4 %collective-permute-start.5 = (f32[2,16,32]{2,1,0:T(8,128)S(1)}, f32[2,16,32]{2,1,0:T(8,128)S(1)}, u32[]{:S(2)}, u32[]{:S(2)}) collective-permute-start(f32[2,16,32]{2,1,0:T(8,128)S(1)} %ghost.1), channel_id=1, source_target_pairs={{0,8},{4,12},{8,0},{12,4},{1,9},{5,13},{9,1},{13,5},{2,10},{6,14},... | collective-permute-start | bytes 12296 | tf_op jit(solution)/shard_map/ppermute | solution.py:45
  19.8 0.1 collective-permute-start.6
  19.8 1.3 %collective-permute-start.2 = (f32[2,4,16,768]{3,2,1,0:T(8,128)S(1)}, f32[2,4,16,768]{3,2,1,0:T(8,128)S(1)}, u32[]{:S(2)}, u32[]{:S(2)}) collective-permute-start(f32[2,4,16,768]{3,2,1,0:T(8,128)S(1)} %get-tuple-element.15), channel_id=1, source_target_pairs={{4,0},{8,4},{12,8},{5,1},{9,5},{13,9},{6,2},{10,6},{14,10},{7,3},{... | collective-permute-start | bytes 1179656 | tf_op jit(solution)/shard_map/ppermute | solution.py:23
  21.1 1.5 %collective-permute-done.5 = f32[2,16,32]{2,1,0:T(8,128)S(1)} collective-permute-done((f32[2,16,32]{2,1,0:T(8,128)S(1)}, f32[2,16,32]{2,1,0:T(8,128)S(1)}, u32[]{:S(2)}, u32[]{:S(2)}) %collective-permute-start.5) | collective-permute-done | bytes 4128 | tf_op jit(solution)/shard_map/ppermute | solution.py:45
  22.6 0.3 collective-permute-done.6
  22.9 0.8 %mend_b.1 = f32[2,4,16,768]{3,2,1,0:T(8,128)S(1)} custom-call(f32[1,12,16,768]{3,2,1,0:T(8,128)S(1)} %copy-done.2, f32[1,12,16,768]{3,2,1,0:T(8,128)S(1)} %copy-done, f32[12,16,768]{2,1,0:T(8,128)S(1)} %pack.1.mine_ref, f32[11,16,768]{2,1,0:T(8,128)S(1)} %collective-permute-done.3.other_ref, f32[2,8,16,768]{3,2,1,0:T(8,128)S(1)} %get-tuple-element.12.ends_ref, ...), custom_call_target="tpu_custom_call" | custom-call | flops 1 | bytes 1 | tf_op jit(solution)/shard_map/mend_b/pallas_call | solution.py:529
  23.7 1.3 %collective-permute-start.7 = (f32[2,4,16,768]{3,2,1,0:T(8,128)S(1)}, f32[2,4,16,768]{3,2,1,0:T(8,128)S(1)}, u32[]{:S(2)}, u32[]{:S(2)}) collective-permute-start(f32[2,4,16,768]{3,2,1,0:T(8,128)S(1)} %mend_b.1), channel_id=1, source_target_pairs={{4,0},{8,4},{12,8},{5,1},{9,5},{13,9},{6,2},{10,6},{14,10},{7,3},{... | collective-permute-start | bytes 1179656 | tf_op jit(solution)/shard_map/ppermute | solution.py:23
  25.0 1.7 %collective-permute-start.8 = (f32[2,16,32]{2,1,0:T(8,128)S(1)}, f32[2,16,32]{2,1,0:T(8,128)S(1)}, u32[]{:S(2)}, u32[]{:S(2)}) collective-permute-start(f32[2,16,32]{2,1,0:T(8,128)S(1)} %add_add_fusion.__), channel_id=1, source_target_pairs={{0,1},{1,0},{2,3},{3,2},{4,5},{5,4},{6,7},{7,6},{8,9},{9,8},{10,11... | collective-permute-start | bytes 12296 | tf_op jit(solution)/shard_map/ppermute | solution.py:45
  26.7 2.2 %collective-permute-done.8 = f32[2,16,32]{2,1,0:T(8,128)S(1)} collective-permute-done((f32[2,16,32]{2,1,0:T(8,128)S(1)}, f32[2,16,32]{2,1,0:T(8,128)S(1)}, u32[]{:S(2)}, u32[]{:S(2)}) %collective-permute-start.8) | collective-permute-done | bytes 4128 | tf_op jit(solution)/shard_map/ppermute | solution.py:45
  28.9 2.6 %collective-permute-start.9 = (f32[2,16,32]{2,1,0:T(8,128)S(1)}, f32[2,16,32]{2,1,0:T(8,128)S(1)}, u32[]{:S(2)}, u32[]{:S(2)}) collective-permute-start(f32[2,16,32]{2,1,0:T(8,128)S(1)} %add.15.total_ref), channel_id=1, source_target_pairs={{0,2},{1,3},{2,0},{3,1},{4,6},{5,7},{6,4},{7,5},{8,10},{9,11},{10,... | collective-permute-start | bytes 12296 | tf_op jit(solution)/shard_map/ppermute | solution.py:45
  31.5 0.9 %begin.1.begun_hbm = f32[1,2,12,16,768]{4,3,2,1,0:T(8,128)} custom-call(f32[1,2,12,16,768]{4,3,2,1,0:T(8,128)S(1)} %copy-done.1, f32[2,4,16,768]{3,2,1,0:T(8,128)S(1)} %collective-permute-done.middle_ref._, f32[2,4,16,768]{3,2,1,0:T(8,128)S(1)} %collective-permute-done.2.a_ref), custom_call_target="tpu_custom_call" | custom-call | flops 1 | bytes 1 | tf_op jit(solution)/shard_map/begin/pallas_call | solution.py:546
  32.4 1.1 %collective-permute-done.9.came_ref = f32[2,16,32]{2,1,0:T(8,128)S(1)} collective-permute-done((f32[2,16,32]{2,1,0:T(8,128)S(1)}, f32[2,16,32]{2,1,0:T(8,128)S(1)}, u32[]{:S(2)}, u32[]{:S(2)}) %collective-permute-start.9) | collective-permute-done | bytes 4128 | tf_op jit(solution)/shard_map/ppermute | solution.py:45
  33.5 1.4 %finish.1 = (f32[1,2,12,16,768]{4,3,2,1,0:T(8,128)}, f32[2,4,8]{2,1,0:T(4,128)}) custom-call(f32[1,2,12,16,768]{4,3,2,1,0:T(8,128)} %begin.1.begun_hbm, f32[1,2,12,16,768]{4,3,2,1,0:T(8,128)S(1)} %copy-done.1, f32[2,4,16,768]{3,2,1,0:T(8,128)S(1)} %collective-permute-done.7.b_ref, s32[1,32]{1,0:T(1,128)S(1)} %bitcast.1, ...), custom_call_target="tpu_custom_call", output_to_operand_aliasing={{0}: (0, {})} | custom-call | flops 1 | bytes 1 | tf_op jit(solution)/shard_map/finish/pallas_call | solution.py:556
  (20 shorter events, 0.1 us)
Async XLA Ops:
  0.6 3.4 %copy-start.1 = (f32[1,2,12,16,768]{4,3,2,1,0:T(8,128)S(1)}, f32[1,2,12,16,768]{4,3,2,1,0:T(8,128)}, u32[]{:S(2)}) copy-start(f32[1,2,12,16,768]{4,3,2,1,0:T(8,128)} %state_ref.5) | copy-start | bytes 3538948
  0.6 3.4 %copy-start.2 = (f32[1,12,16,768]{3,2,1,0:T(8,128)S(1)}, f32[1,12,16,768]{3,2,1,0:T(8,128)}, u32[]{:S(2)}) copy-start(f32[1,12,16,768]{3,2,1,0:T(8,128)} %east_ref.5) | copy-start | bytes 1769476
  0.6 3.4 %copy-start = (f32[1,12,16,768]{3,2,1,0:T(8,128)S(1)}, f32[1,12,16,768]{3,2,1,0:T(8,128)}, u32[]{:S(2)}) copy-start(f32[1,12,16,768]{3,2,1,0:T(8,128)} %north_ref.9) | copy-start | bytes 1769476
  2.6 11.4 %copy-start.3 = (s32[4,2,2,12]{3,2,1,0:T(2,128)S(1)}, s32[4,2,2,12]{3,2,1,0:T(2,128)}, u32[]{:S(2)}) copy-start(s32[4,2,2,12]{3,2,1,0:T(2,128)} %offset_ref.1) | copy-start | bytes 2308
  2.6 11.4 %copy-start.4 = (f32[4,2,2,12]{3,2,1,0:T(2,128)S(1)}, f32[4,2,2,12]{3,2,1,0:T(2,128)}, u32[]{:S(2)}) copy-start(f32[4,2,2,12]{3,2,1,0:T(2,128)} %weight_ref.1) | copy-start | bytes 2308
  2.6 11.4 %copy-start.5 = (s32[2,2,12]{2,1,0:T(2,128)S(1)}, s32[2,2,12]{2,1,0:T(2,128)}, u32[]{:S(2)}) copy-start(s32[2,2,12]{2,1,0:T(2,128)} %cell_ref.1) | copy-start | bytes 580
  2.6 13.6 %collective-permute-start.1 = (f32[12,16,768]{2,1,0:T(8,128)S(1)}, f32[12,16,768]{2,1,0:T(8,128)S(1)}, u32[]{:S(2)}, u32[]{:S(2)}) collective-permute-start(f32[12,16,768]{2,1,0:T(8,128)S(1)} %pack.1.mine_ref), channel_id=1, source_target_pairs={{1,0},{2,1},{3,2},{4,5},{5,6},{6,7},{9,8},{10,9},{11,10},{12,13},{... | collective-permute-start | bytes 1769480 | tf_op jit(solution)/shard_map/ppermute | solution.py:32
  7.1 15.9 %collective-permute-start.3 = (f32[11,16,768]{2,1,0:T(8,128)S(1)}, f32[11,16,768]{2,1,0:T(8,128)S(1)}, u32[]{:S(2)}, u32[]{:S(2)}) collective-permute-start(f32[11,16,768]{2,1,0:T(8,128)S(1)} %get-tuple-element.11.mine_ref), channel_id=1, source_target_pairs={{0,1},{1,2},{2,3},{5,4},{6,5},{7,6},{8,9},{9,10},{10,11},{13,12},{... | collective-permute-start | bytes 1622024 | tf_op jit(solution)/shard_map/ppermute | solution.py:32
  12.7 10.2 %collective-permute-start = (f32[2,4,16,768]{3,2,1,0:T(8,128)S(1)}, f32[2,4,16,768]{3,2,1,0:T(8,128)S(1)}, u32[]{:S(2)}, u32[]{:S(2)}) collective-permute-start(f32[2,4,16,768]{3,2,1,0:T(8,128)S(1)} %get-tuple-element.10), channel_id=1, source_target_pairs={{4,0},{8,4},{12,8},{5,1},{9,5},{13,9},{6,2},{10,6},{14,10},{7,3},{... | collective-permute-start | bytes 1179656 | tf_op jit(solution)/shard_map/ppermute | solution.py:23
  17.2 2.6 %collective-permute-start.4 = (f32[2,16,32]{2,1,0:T(8,128)S(1)}, f32[2,16,32]{2,1,0:T(8,128)S(1)}, u32[]{:S(2)}, u32[]{:S(2)}) collective-permute-start(f32[2,16,32]{2,1,0:T(8,128)S(1)} %ghost.1), channel_id=1, source_target_pairs={{0,4},{4,0},{8,12},{12,8},{1,5},{5,1},{9,13},{13,9},{2,6},{6,2},{1... | collective-permute-start | bytes 12296 | tf_op jit(solution)/shard_map/ppermute | solution.py:45
  17.3 5.3 %collective-permute-start.5 = (f32[2,16,32]{2,1,0:T(8,128)S(1)}, f32[2,16,32]{2,1,0:T(8,128)S(1)}, u32[]{:S(2)}, u32[]{:S(2)}) collective-permute-start(f32[2,16,32]{2,1,0:T(8,128)S(1)} %ghost.1), channel_id=1, source_target_pairs={{0,8},{4,12},{8,0},{12,4},{1,9},{5,13},{9,1},{13,5},{2,10},{6,14},... | collective-permute-start | bytes 12296 | tf_op jit(solution)/shard_map/ppermute | solution.py:45
  19.8 3.2 %collective-permute-start.6 = (f32[2,16,32]{2,1,0:T(8,128)S(1)}, f32[2,16,32]{2,1,0:T(8,128)S(1)}, u32[]{:S(2)}, u32[]{:S(2)}) collective-permute-start(f32[2,16,32]{2,1,0:T(8,128)S(1)} %ghost.1), channel_id=1, source_target_pairs={{0,12},{4,8},{8,4},{12,0},{1,13},{5,9},{9,5},{13,1},{2,14},{6,10},... | collective-permute-start | bytes 12296 | tf_op jit(solution)/shard_map/ppermute | solution.py:45
  19.8 11.6 %collective-permute-start.2 = (f32[2,4,16,768]{3,2,1,0:T(8,128)S(1)}, f32[2,4,16,768]{3,2,1,0:T(8,128)S(1)}, u32[]{:S(2)}, u32[]{:S(2)}) collective-permute-start(f32[2,4,16,768]{3,2,1,0:T(8,128)S(1)} %get-tuple-element.15), channel_id=1, source_target_pairs={{4,0},{8,4},{12,8},{5,1},{9,5},{13,9},{6,2},{10,6},{14,10},{7,3},{... | collective-permute-start | bytes 1179656 | tf_op jit(solution)/shard_map/ppermute | solution.py:23
  23.7 9.8 %collective-permute-start.7 = (f32[2,4,16,768]{3,2,1,0:T(8,128)S(1)}, f32[2,4,16,768]{3,2,1,0:T(8,128)S(1)}, u32[]{:S(2)}, u32[]{:S(2)}) collective-permute-start(f32[2,4,16,768]{3,2,1,0:T(8,128)S(1)} %mend_b.1), channel_id=1, source_target_pairs={{4,0},{8,4},{12,8},{5,1},{9,5},{13,9},{6,2},{10,6},{14,10},{7,3},{... | collective-permute-start | bytes 1179656 | tf_op jit(solution)/shard_map/ppermute | solution.py:23
  25.0 3.8 %collective-permute-start.8 = (f32[2,16,32]{2,1,0:T(8,128)S(1)}, f32[2,16,32]{2,1,0:T(8,128)S(1)}, u32[]{:S(2)}, u32[]{:S(2)}) collective-permute-start(f32[2,16,32]{2,1,0:T(8,128)S(1)} %add_add_fusion.__), channel_id=1, source_target_pairs={{0,1},{1,0},{2,3},{3,2},{4,5},{5,4},{6,7},{7,6},{8,9},{9,8},{10,11... | collective-permute-start | bytes 12296 | tf_op jit(solution)/shard_map/ppermute | solution.py:45
  28.9 4.6 %copy-start.6 = (s32[32]{0:T(128)S(1)}, s32[32]{0:T(128)}, u32[]{:S(2)}) copy-start(s32[32]{0:T(128)} %param.13) | copy-start | bytes 388
  28.9 4.6 %collective-permute-start.9 = (f32[2,16,32]{2,1,0:T(8,128)S(1)}, f32[2,16,32]{2,1,0:T(8,128)S(1)}, u32[]{:S(2)}, u32[]{:S(2)}) collective-permute-start(f32[2,16,32]{2,1,0:T(8,128)S(1)} %add.15.total_ref), channel_id=1, source_target_pairs={{0,2},{1,3},{2,0},{3,1},{4,6},{5,7},{6,4},{7,5},{8,10},{9,11},{10,... | collective-permute-start | bytes 12296 | tf_op jit(solution)/shard_map/ppermute | solution.py:45

commit v13 on v12

--- a/solution.py
+++ b/solution.py
@@ -17,10 +17,9 @@
 WEIGHTS = 5 * LANES
 
 
-def along(value, axis, step_of):
-    peers = lax.axis_size(axis)
-    pairs = [(i, i + step_of) for i in range(peers) if 0 <= i + step_of < peers]
-    return lax.ppermute(value, axis, pairs)
+def to_previous(value):
+    peers = lax.axis_size("sub")
+    return lax.ppermute(value, "sub", [(i, (i - 1) % peers) for i in range(peers)])
 
 
 def alternating(value, sign):
@@ -379,11 +378,12 @@
 
 def subtract_rows(state_ref, out_hbm, buffer, sems, jobs):
     copies = []
+    is_last = lax.axis_index("sub") == lax.axis_size("sub") - 1
     for start, other in jobs:
         for c in range(other.shape[0]):
             count = other.shape[1]
             for r in range(count):
-                buffer[c, start + r] = state_ref[0, c, start + r] - other[c, r]
+                buffer[c, start + r] = state_ref[0, c, start + r] - jnp.where(is_last, 0.0, other[c, r])
             at = pl.ds(start, count)
             copy = pltpu.make_async_copy(buffer.at[c, at], out_hbm.at[0, c, at], sems.at[len(copies)])
             copy.start()
@@ -491,7 +491,7 @@
         name="sweep",
     )(state, east, north)
     second_came = alternating(second_pack, 1)
-    middle_came = along(middle, "sub", -1)
+    middle_came = to_previous(middle)
 
     mixing, base = pl.pallas_call(
         ghost_base_kernel,
@@ -513,7 +513,7 @@
         cost_estimate=BRIEF,
         name="mend_a",
     )(east, north, second_pack, first_came, ends, base)
-    a_came = along(side_a, "sub", -1)
+    a_came = to_previous(side_a)
     total = pl.pallas_call(
         ghost_kernel,
         in_specs=[vmem] * 5,
@@ -535,7 +535,7 @@
         cost_estimate=BRIEF,
         name="mend_b",
     )(east, north, first_pack, second_came, ends, middle_came, total)
-    b_came = along(side_b, "sub", -1)
+    b_came = to_previous(side_b)
 
     for each in order[1:-1]:
         total = total + exchanged(total, *each)

time: 35.1 us -> 34 us (0.969)
  starting transfers between devices: 17.7 us -> 16.2 us
  waiting for transfers between devices: 6.91 us -> 7.46 us
    ppermute x3, starting transfers between devices: 3.87 us -> 2.09 us  [to_previous(): lax.ppermute(value, 'sub', [(i, (i - 1) % peers) for i in range(peers)])]
    ppermute x2, waiting for transfers between devices: 1.86 us -> 3.09 us  [alternating(): return lax.ppermute(value, ('sub', 'hor'), pairs)]
    ppermute x5, waiting for transfers between devices: 5.04 us -> 4.36 us  [exchanged(): lax.ppermute(value, axis, [(i, i ^ distance) for i in range(size)])]
  transfers between devices with their start and end apart: 10 -> 10, of which waited for: 5 -> 4; matrix products, arithmetic and copies ran while one was open for 0% -> 0% of each run, Pallas kernels for 17% -> 18%
where the time goes in v13:
time: 34 us; the launch traced here: 33.9 us
  starting transfers between devices  16.2 us (48%)
  Pallas kernels  9.36 us (28%)
  waiting for transfers between devices  7.46 us (22%)
  between operations  0.81 us (2%)
    ppermute x5, starting transfers between devices, exchanged(): lax.ppermute(value, axis, [(i, i ^ distance) for i in range(size)])  7.07 us
    ppermute x2, starting transfers between devices, alternating(): return lax.ppermute(value, ('sub', 'hor'), pairs)  7.01 us
    ppermute x5, waiting for transfers between devices, exchanged(): lax.ppermute(value, axis, [(i, i ^ distance) for i in range(size)])  4.36 us
    ppermute x2, waiting for transfers between devices, alternating(): return lax.ppermute(value, ('sub', 'hor'), pairs)  3.09 us
    pallas_call x1, Pallas kernels, local(): pl.pallas_call(sweep_kernel, in_specs=[vmem] * 3, out_specs=[vmem] * 4, o...  2.99 us
    ppermute x3, starting transfers between devices, to_previous(): lax.ppermute(value, 'sub', [(i, (i - 1) % peers) for i in range(peers)])  2.09 us
    pallas_call x1, Pallas kernels, local(): pl.pallas_call(pack_kernel, in_specs=[hbm] * 6, out_specs=vmem, out_shape...  1.93 us
    pallas_call x1, Pallas kernels, local(): pl.pallas_call(finish_kernel, in_specs=[hbm] + [vmem] * 5, out_specs=[hbm...  1.39 us
  transfers between devices with their start and end apart: 10, of which 4 were waited for; matrix products, arithmetic and copies ran while one was open for 0% of the time, Pallas kernels for 18%

profile of v13, /device:TPU:0, one launch (start us, length us, event | category | flops | bytes accessed | tf_op | source)
XLA Modules:
  0.0 33.9 jit_solution(17249075106291491335)
XLA Ops:
  0.7 1.9 %pack.1.mine_ref = f32[12,16,768]{2,1,0:T(8,128)S(1)} custom-call(f32[1,2,12,16,768]{4,3,2,1,0:T(8,128)} %state_ref.5, f32[1,12,16,768]{3,2,1,0:T(8,128)} %east_ref.5, f32[1,12,16,768]{3,2,1,0:T(8,128)} %north_ref.9, s32[2,2,12]{2,1,0:T(2,128)} %cell_ref.1, s32[4,2,2,12]{3,2,1,0:T(2,128)} %offset_ref.1, f32[4,2,2,12]{3,2,1,0:T(2,128)} %weight_ref.1), custom_call_target="tpu_custom_call" | custom-call | flops 1 | bytes 1 | tf_op jit(solution)/shard_map/pack/pallas_call | solution.py:454
  2.6 0.0 copy-start.3
  2.6 0.0 copy-start.5
  2.6 1.4 %collective-permute-start.1 = (f32[12,16,768]{2,1,0:T(8,128)S(1)}, f32[12,16,768]{2,1,0:T(8,128)S(1)}, u32[]{:S(2)}, u32[]{:S(2)}) collective-permute-start(f32[12,16,768]{2,1,0:T(8,128)S(1)} %pack.1.mine_ref), channel_id=1, source_target_pairs={{1,0},{2,1},{3,2},{4,5},{5,6},{6,7},{9,8},{10,9},{11,10},{12,13},{... | collective-permute-start | bytes 1769480 | tf_op jit(solution)/shard_map/ppermute | solution.py:31
  4.1 3.0 %sweep.1 = (f32[11,16,768]{2,1,0:T(8,128)S(1)}, f32[2,4,16,768]{3,2,1,0:T(8,128)S(1)}, f32[2,8,16,768]{3,2,1,0:T(8,128)S(1)}, f32[2,2,12,16,128]{4,3,2,1,0:T(8,128)S(1)}) custom-call(f32[1,2,12,16,768]{4,3,2,1,0:T(8,128)S(1)} %copy-done.1, f32[1,12,16,768]{3,2,1,0:T(8,128)S(1)} %copy-done.2, f32[1,12,16,768]{3,2,1,0:T(8,128)S(1)} %copy-done), custom_call_target="tpu_custom_call" | custom-call | flops 1 | bytes 1 | tf_op jit(solution)/shard_map/sweep/pallas_call | solution.py:473
  7.1 5.6 %collective-permute-start.3 = (f32[11,16,768]{2,1,0:T(8,128)S(1)}, f32[11,16,768]{2,1,0:T(8,128)S(1)}, u32[]{:S(2)}, u32[]{:S(2)}) collective-permute-start(f32[11,16,768]{2,1,0:T(8,128)S(1)} %get-tuple-element.11.mine_ref), channel_id=1, source_target_pairs={{0,1},{1,2},{2,3},{5,4},{6,5},{7,6},{8,9},{9,10},{10,11},{13,12},{... | collective-permute-start | bytes 1622024 | tf_op jit(solution)/shard_map/ppermute | solution.py:31
  12.7 0.1 collective-permute-start
  12.8 0.4 %ghost_base.1 = (f32[2,2,12,32]{3,2,1,0:T(8,128)S(1)}, f32[2,16,32]{2,1,0:T(8,128)S(1)}) custom-call(s32[2,2,12]{2,1,0:T(2,128)S(1)} %copy-done.5, s32[4,2,2,12]{3,2,1,0:T(2,128)S(1)} %copy-done.3, f32[4,2,2,12]{3,2,1,0:T(2,128)S(1)} %copy-done.4, f32[2,2,12,16,128]{4,3,2,1,0:T(8,128)S(1)} %get-tuple-element.13.column_ref, f32[1,12,16,768]{3,2,1,0:T(8,128)S(1)} %copy-done), custom_call_target="tpu_custom_call" | custom-call | flops 1 | bytes 1 | tf_op jit(solution)/shard_map/ghost_base/pallas_call | solution.py:496
  13.2 3.1 %collective-permute-done.1.other_ref = f32[12,16,768]{2,1,0:T(8,128)S(1)} collective-permute-done((f32[12,16,768]{2,1,0:T(8,128)S(1)}, f32[12,16,768]{2,1,0:T(8,128)S(1)}, u32[]{:S(2)}, u32[]{:S(2)}) %collective-permute-start.1) | collective-permute-done | bytes 589856 | tf_op jit(solution)/shard_map/ppermute | solution.py:31
  16.2 0.8 %mend_a.1 = (f32[2,4,16,768]{3,2,1,0:T(8,128)S(1)}, f32[2,2,6,16,128]{4,3,2,1,0:T(8,128)S(1)}) custom-call(f32[1,12,16,768]{3,2,1,0:T(8,128)S(1)} %copy-done.2, f32[1,12,16,768]{3,2,1,0:T(8,128)S(1)} %copy-done, f32[11,16,768]{2,1,0:T(8,128)S(1)} %get-tuple-element.11.mine_ref, f32[12,16,768]{2,1,0:T(8,128)S(1)} %collective-permute-done.1.other_ref, ...), custom_call_target="tpu_custom_call" | custom-call | flops 1 | bytes 1 | tf_op jit(solution)/shard_map/mend_a/pallas_call | solution.py:507
  17.0 0.2 ghost.1
  17.2 0.1 collective-permute-start.4
  17.3 2.4 %collective-permute-start.5 = (f32[2,16,32]{2,1,0:T(8,128)S(1)}, f32[2,16,32]{2,1,0:T(8,128)S(1)}, u32[]{:S(2)}, u32[]{:S(2)}) collective-permute-start(f32[2,16,32]{2,1,0:T(8,128)S(1)} %ghost.1), channel_id=1, source_target_pairs={{0,8},{4,12},{8,0},{12,4},{1,9},{5,13},{9,1},{13,5},{2,10},{6,14},... | collective-permute-start | bytes 12296 | tf_op jit(solution)/shard_map/ppermute | solution.py:44
  19.8 0.1 collective-permute-start.6
  19.8 1.7 %collective-permute-start.2 = (f32[2,4,16,768]{3,2,1,0:T(8,128)S(1)}, f32[2,4,16,768]{3,2,1,0:T(8,128)S(1)}, u32[]{:S(2)}, u32[]{:S(2)}) collective-permute-start(f32[2,4,16,768]{3,2,1,0:T(8,128)S(1)} %get-tuple-element.15), channel_id=1, source_target_pairs={{0,12},{4,0},{8,4},{12,8},{1,13},{5,1},{9,5},{13,9},{2,14},{6,2},{... | collective-permute-start | bytes 1179656 | tf_op jit(solution)/shard_map/ppermute | solution.py:22
  21.5 1.4 %collective-permute-done.6 = f32[2,16,32]{2,1,0:T(8,128)S(1)} collective-permute-done((f32[2,16,32]{2,1,0:T(8,128)S(1)}, f32[2,16,32]{2,1,0:T(8,128)S(1)}, u32[]{:S(2)}, u32[]{:S(2)}) %collective-permute-start.6) | collective-permute-done | bytes 4128 | tf_op jit(solution)/shard_map/ppermute | solution.py:44
  22.9 0.8 %mend_b.1 = f32[2,4,16,768]{3,2,1,0:T(8,128)S(1)} custom-call(f32[1,12,16,768]{3,2,1,0:T(8,128)S(1)} %copy-done.2, f32[1,12,16,768]{3,2,1,0:T(8,128)S(1)} %copy-done, f32[12,16,768]{2,1,0:T(8,128)S(1)} %pack.1.mine_ref, f32[11,16,768]{2,1,0:T(8,128)S(1)} %collective-permute-done.3.other_ref, f32[2,8,16,768]{3,2,1,0:T(8,128)S(1)} %get-tuple-element.12.ends_ref, ...), custom_call_target="tpu_custom_call" | custom-call | flops 1 | bytes 1 | tf_op jit(solution)/shard_map/mend_b/pallas_call | solution.py:529
  23.7 0.3 %collective-permute-start.7 = (f32[2,4,16,768]{3,2,1,0:T(8,128)S(1)}, f32[2,4,16,768]{3,2,1,0:T(8,128)S(1)}, u32[]{:S(2)}, u32[]{:S(2)}) collective-permute-start(f32[2,4,16,768]{3,2,1,0:T(8,128)S(1)} %mend_b.1), channel_id=1, source_target_pairs={{0,12},{4,0},{8,4},{12,8},{1,13},{5,1},{9,5},{13,9},{2,14},{6,2},{... | collective-permute-start | bytes 1179656 | tf_op jit(solution)/shard_map/ppermute | solution.py:22
  24.1 1.7 %collective-permute-start.8 = (f32[2,16,32]{2,1,0:T(8,128)S(1)}, f32[2,16,32]{2,1,0:T(8,128)S(1)}, u32[]{:S(2)}, u32[]{:S(2)}) collective-permute-start(f32[2,16,32]{2,1,0:T(8,128)S(1)} %add_add_fusion.__), channel_id=1, source_target_pairs={{0,1},{1,0},{2,3},{3,2},{4,5},{5,4},{6,7},{7,6},{8,9},{9,8},{10,11... | collective-permute-start | bytes 12296 | tf_op jit(solution)/shard_map/ppermute | solution.py:44
  25.8 2.0 %collective-permute-done.8 = f32[2,16,32]{2,1,0:T(8,128)S(1)} collective-permute-done((f32[2,16,32]{2,1,0:T(8,128)S(1)}, f32[2,16,32]{2,1,0:T(8,128)S(1)}, u32[]{:S(2)}, u32[]{:S(2)}) %collective-permute-start.8) | collective-permute-done | bytes 4128 | tf_op jit(solution)/shard_map/ppermute | solution.py:44
  27.8 2.8 %collective-permute-start.9 = (f32[2,16,32]{2,1,0:T(8,128)S(1)}, f32[2,16,32]{2,1,0:T(8,128)S(1)}, u32[]{:S(2)}, u32[]{:S(2)}) collective-permute-start(f32[2,16,32]{2,1,0:T(8,128)S(1)} %add.15.total_ref), channel_id=1, source_target_pairs={{0,2},{1,3},{2,0},{3,1},{4,6},{5,7},{6,4},{7,5},{8,10},{9,11},{10,... | collective-permute-start | bytes 12296 | tf_op jit(solution)/shard_map/ppermute | solution.py:44
  30.6 0.9 %begin.1.begun_hbm = f32[1,2,12,16,768]{4,3,2,1,0:T(8,128)} custom-call(f32[1,2,12,16,768]{4,3,2,1,0:T(8,128)S(1)} %copy-done.1, f32[2,4,16,768]{3,2,1,0:T(8,128)S(1)} %collective-permute-done.middle_ref._, f32[2,4,16,768]{3,2,1,0:T(8,128)S(1)} %collective-permute-done.2.a_ref), custom_call_target="tpu_custom_call" | custom-call | flops 1 | bytes 1 | tf_op jit(solution)/shard_map/begin/pallas_call | solution.py:546
  31.5 0.9 %collective-permute-done.9.came_ref = f32[2,16,32]{2,1,0:T(8,128)S(1)} collective-permute-done((f32[2,16,32]{2,1,0:T(8,128)S(1)}, f32[2,16,32]{2,1,0:T(8,128)S(1)}, u32[]{:S(2)}, u32[]{:S(2)}) %collective-permute-start.9) | collective-permute-done | bytes 4128 | tf_op jit(solution)/shard_map/ppermute | solution.py:44
  32.5 1.4 %finish.1 = (f32[1,2,12,16,768]{4,3,2,1,0:T(8,128)}, f32[2,4,8]{2,1,0:T(4,128)}) custom-call(f32[1,2,12,16,768]{4,3,2,1,0:T(8,128)} %begin.1.begun_hbm, f32[1,2,12,16,768]{4,3,2,1,0:T(8,128)S(1)} %copy-done.1, f32[2,4,16,768]{3,2,1,0:T(8,128)S(1)} %collective-permute-done.7.b_ref, s32[1,32]{1,0:T(1,128)S(1)} %bitcast.1, ...), custom_call_target="tpu_custom_call", output_to_operand_aliasing={{0}: (0, {})} | custom-call | flops 1 | bytes 1 | tf_op jit(solution)/shard_map/finish/pallas_call | solution.py:556
  (20 shorter events, 0.1 us)
Async XLA Ops:
  0.6 3.4 %copy-start.1 = (f32[1,2,12,16,768]{4,3,2,1,0:T(8,128)S(1)}, f32[1,2,12,16,768]{4,3,2,1,0:T(8,128)}, u32[]{:S(2)}) copy-start(f32[1,2,12,16,768]{4,3,2,1,0:T(8,128)} %state_ref.5) | copy-start | bytes 3538948
  0.6 3.4 %copy-start.2 = (f32[1,12,16,768]{3,2,1,0:T(8,128)S(1)}, f32[1,12,16,768]{3,2,1,0:T(8,128)}, u32[]{:S(2)}) copy-start(f32[1,12,16,768]{3,2,1,0:T(8,128)} %east_ref.5) | copy-start | bytes 1769476
  0.6 3.4 %copy-start = (f32[1,12,16,768]{3,2,1,0:T(8,128)S(1)}, f32[1,12,16,768]{3,2,1,0:T(8,128)}, u32[]{:S(2)}) copy-start(f32[1,12,16,768]{3,2,1,0:T(8,128)} %north_ref.9) | copy-start | bytes 1769476
  2.6 10.2 %copy-start.3 = (s32[4,2,2,12]{3,2,1,0:T(2,128)S(1)}, s32[4,2,2,12]{3,2,1,0:T(2,128)}, u32[]{:S(2)}) copy-start(s32[4,2,2,12]{3,2,1,0:T(2,128)} %offset_ref.1) | copy-start | bytes 2308
  2.6 10.2 %copy-start.4 = (f32[4,2,2,12]{3,2,1,0:T(2,128)S(1)}, f32[4,2,2,12]{3,2,1,0:T(2,128)}, u32[]{:S(2)}) copy-start(f32[4,2,2,12]{3,2,1,0:T(2,128)} %weight_ref.1) | copy-start | bytes 2308
  2.6 10.2 %copy-start.5 = (s32[2,2,12]{2,1,0:T(2,128)S(1)}, s32[2,2,12]{2,1,0:T(2,128)}, u32[]{:S(2)}) copy-start(s32[2,2,12]{2,1,0:T(2,128)} %cell_ref.1) | copy-start | bytes 580
  2.6 13.6 %collective-permute-start.1 = (f32[12,16,768]{2,1,0:T(8,128)S(1)}, f32[12,16,768]{2,1,0:T(8,128)S(1)}, u32[]{:S(2)}, u32[]{:S(2)}) collective-permute-start(f32[12,16,768]{2,1,0:T(8,128)S(1)} %pack.1.mine_ref), channel_id=1, source_target_pairs={{1,0},{2,1},{3,2},{4,5},{5,6},{6,7},{9,8},{10,9},{11,10},{12,13},{... | collective-permute-start | bytes 1769480 | tf_op jit(solution)/shard_map/ppermute | solution.py:31
  7.1 15.9 %collective-permute-start.3 = (f32[11,16,768]{2,1,0:T(8,128)S(1)}, f32[11,16,768]{2,1,0:T(8,128)S(1)}, u32[]{:S(2)}, u32[]{:S(2)}) collective-permute-start(f32[11,16,768]{2,1,0:T(8,128)S(1)} %get-tuple-element.11.mine_ref), channel_id=1, source_target_pairs={{0,1},{1,2},{2,3},{5,4},{6,5},{7,6},{8,9},{9,10},{10,11},{13,12},{... | collective-permute-start | bytes 1622024 | tf_op jit(solution)/shard_map/ppermute | solution.py:31
  12.7 10.2 %collective-permute-start = (f32[2,4,16,768]{3,2,1,0:T(8,128)S(1)}, f32[2,4,16,768]{3,2,1,0:T(8,128)S(1)}, u32[]{:S(2)}, u32[]{:S(2)}) collective-permute-start(f32[2,4,16,768]{3,2,1,0:T(8,128)S(1)} %get-tuple-element.10), channel_id=1, source_target_pairs={{0,12},{4,0},{8,4},{12,8},{1,13},{5,1},{9,5},{13,9},{2,14},{6,2},{... | collective-permute-start | bytes 1179656 | tf_op jit(solution)/shard_map/ppermute | solution.py:22
  17.2 2.6 %collective-permute-start.4 = (f32[2,16,32]{2,1,0:T(8,128)S(1)}, f32[2,16,32]{2,1,0:T(8,128)S(1)}, u32[]{:S(2)}, u32[]{:S(2)}) collective-permute-start(f32[2,16,32]{2,1,0:T(8,128)S(1)} %ghost.1), channel_id=1, source_target_pairs={{0,4},{4,0},{8,12},{12,8},{1,5},{5,1},{9,13},{13,9},{2,6},{6,2},{1... | collective-permute-start | bytes 12296 | tf_op jit(solution)/shard_map/ppermute | solution.py:44
  17.3 4.2 %collective-permute-start.5 = (f32[2,16,32]{2,1,0:T(8,128)S(1)}, f32[2,16,32]{2,1,0:T(8,128)S(1)}, u32[]{:S(2)}, u32[]{:S(2)}) collective-permute-start(f32[2,16,32]{2,1,0:T(8,128)S(1)} %ghost.1), channel_id=1, source_target_pairs={{0,8},{4,12},{8,0},{12,4},{1,9},{5,13},{9,1},{13,5},{2,10},{6,14},... | collective-permute-start | bytes 12296 | tf_op jit(solution)/shard_map/ppermute | solution.py:44
  19.8 3.2 %collective-permute-start.6 = (f32[2,16,32]{2,1,0:T(8,128)S(1)}, f32[2,16,32]{2,1,0:T(8,128)S(1)}, u32[]{:S(2)}, u32[]{:S(2)}) collective-permute-start(f32[2,16,32]{2,1,0:T(8,128)S(1)} %ghost.1), channel_id=1, source_target_pairs={{0,12},{4,8},{8,4},{12,0},{1,13},{5,9},{9,5},{13,1},{2,14},{6,10},... | collective-permute-start | bytes 12296 | tf_op jit(solution)/shard_map/ppermute | solution.py:44
  19.8 10.7 %collective-permute-start.2 = (f32[2,4,16,768]{3,2,1,0:T(8,128)S(1)}, f32[2,4,16,768]{3,2,1,0:T(8,128)S(1)}, u32[]{:S(2)}, u32[]{:S(2)}) collective-permute-start(f32[2,4,16,768]{3,2,1,0:T(8,128)S(1)} %get-tuple-element.15), channel_id=1, source_target_pairs={{0,12},{4,0},{8,4},{12,8},{1,13},{5,1},{9,5},{13,9},{2,14},{6,2},{... | collective-permute-start | bytes 1179656 | tf_op jit(solution)/shard_map/ppermute | solution.py:22
  23.7 8.7 %collective-permute-start.7 = (f32[2,4,16,768]{3,2,1,0:T(8,128)S(1)}, f32[2,4,16,768]{3,2,1,0:T(8,128)S(1)}, u32[]{:S(2)}, u32[]{:S(2)}) collective-permute-start(f32[2,4,16,768]{3,2,1,0:T(8,128)S(1)} %mend_b.1), channel_id=1, source_target_pairs={{0,12},{4,0},{8,4},{12,8},{1,13},{5,1},{9,5},{13,9},{2,14},{6,2},{... | collective-permute-start | bytes 1179656 | tf_op jit(solution)/shard_map/ppermute | solution.py:22
  24.1 3.7 %collective-permute-start.8 = (f32[2,16,32]{2,1,0:T(8,128)S(1)}, f32[2,16,32]{2,1,0:T(8,128)S(1)}, u32[]{:S(2)}, u32[]{:S(2)}) collective-permute-start(f32[2,16,32]{2,1,0:T(8,128)S(1)} %add_add_fusion.__), channel_id=1, source_target_pairs={{0,1},{1,0},{2,3},{3,2},{4,5},{5,4},{6,7},{7,6},{8,9},{9,8},{10,11... | collective-permute-start | bytes 12296 | tf_op jit(solution)/shard_map/ppermute | solution.py:44
  27.8 4.6 %copy-start.6 = (s32[32]{0:T(128)S(1)}, s32[32]{0:T(128)}, u32[]{:S(2)}) copy-start(s32[32]{0:T(128)} %param.13) | copy-start | bytes 388
  27.8 4.6 %collective-permute-start.9 = (f32[2,16,32]{2,1,0:T(8,128)S(1)}, f32[2,16,32]{2,1,0:T(8,128)S(1)}, u32[]{:S(2)}, u32[]{:S(2)}) collective-permute-start(f32[2,16,32]{2,1,0:T(8,128)S(1)} %add.15.total_ref), channel_id=1, source_target_pairs={{0,2},{1,3},{2,0},{3,1},{4,6},{5,7},{6,4},{7,5},{8,10},{9,11},{10,... | collective-permute-start | bytes 12296 | tf_op jit(solution)/shard_map/ppermute | solution.py:44

commit v14 on v13

--- a/solution.py
+++ b/solution.py
@@ -24,11 +24,19 @@
 
 def alternating(value, sign):
     subs, hors = lax.axis_size("sub"), lax.axis_size("hor")
+    assert subs % 2 == 0
     pairs = []
     for s in range(subs):
         step = sign if s % 2 == 0 else -sign
-        pairs += [(s * hors + h, s * hors + h + step) for h in range(hors) if 0 <= h + step < hors]
+        for h in range(hors):
+            inside = 0 <= h + step < hors
+            pairs.append((s * hors + h, s * hors + h + step if inside else (s ^ 1) * hors + h))
     return lax.ppermute(value, ("sub", "hor"), pairs)
+
+
+def has_neighbour(flip):
+    hor = lax.axis_index("hor")
+    return jnp.where(flip == 1, hor < lax.axis_size("hor") - 1, hor > 0)
 
 
 def rounds():
@@ -301,7 +309,7 @@
             north = jnp.maximum(-last_rate[:, LANES - 1:], 0.0) * column_ref[c, 1, STEPS - 1 + r, :, LANES - 1:]
             total = total + south * near_mixing[c, 0, pl.ds(i, 1), :]
             total = total + north * near_mixing[c, 1, pl.ds(i, 1), :]
-        sum_ref[c] = total
+        sum_ref[c] = jnp.where(has_neighbour(flip), total, partial_ref[c])
 
 
 def mend_side(flip, east_ref, north_ref, mine_ref, other_ref, store, store_column):
@@ -353,6 +361,12 @@
     level_halves(levels, half)
 
 
+def copy_end(flip, ends_ref, out_ref):
+    for c in range(out_ref.shape[0]):
+        for r in range(STEPS):
+            out_ref[c, r] = ends_ref[c, flip * STEPS + r]
+
+
 def mend_a_kernel(east_ref, north_ref, mine_ref, other_ref, ends_ref, base_ref, out_ref, column_ref):
     flip = 1 - parity()
     turn = lambda r: r + flip * (STEPS - 1 - 2 * r)
@@ -363,7 +377,14 @@
     def store_column(c, s, r, at, value):
         column_ref[c, s, r, at, :] = value
 
-    mend_side(flip, east_ref, north_ref, mine_ref, other_ref, store, store_column)
+    @pl.when(has_neighbour(flip))
+    def _():
+        mend_side(flip, east_ref, north_ref, mine_ref, other_ref, store, store_column)
+
+    @pl.when(jnp.logical_not(has_neighbour(flip)))
+    def _():
+        column_ref[...] = jnp.zeros_like(column_ref)
+        copy_end(flip, ends_ref, out_ref)
 
 
 def mend_b_kernel(east_ref, north_ref, mine_ref, other_ref, ends_ref, _, __, out_ref):
@@ -373,7 +394,13 @@
     def store(c, r, at, value):
         out_ref[c, turn(r), at, :] = ends_ref[c, flip * STEPS + turn(r), at, :] + value
 
-    mend_side(flip, east_ref, north_ref, mine_ref, other_ref, store, None)
+    @pl.when(has_neighbour(flip))
+    def _():
+        mend_side(flip, east_ref, north_ref, mine_ref, other_ref, store, None)
+
+    @pl.when(jnp.logical_not(has_neighbour(flip)))
+    def _():
+        copy_end(flip, ends_ref, out_ref)
 
 
 def subtract_rows(state_ref, out_hbm, buffer, sems, jobs):

time: 34 us -> 34 us (level)
  waiting for transfers between devices: 7.46 us -> 10.8 us
  starting transfers between devices: 16.2 us -> 13.5 us
  Pallas kernels: 9.36 us -> 8.64 us
    ppermute x2, starting transfers between devices: 7.01 us -> 3.1 us  [alternating(): return lax.ppermute(value, ('sub', 'hor'), pairs)]
    ppermute x2, waiting for transfers between devices: 3.09 us -> 6.41 us  [alternating(): return lax.ppermute(value, ('sub', 'hor'), pairs)]
    ppermute x3, starting transfers between devices: 2.09 us -> 3.41 us  [to_previous(): lax.ppermute(value, 'sub', [(i, (i - 1) % peers) for i in range(peers)])]
    pallas_call x1, Pallas kernels: 0.77 us -> 0.05 us  [local(): pl.pallas_call(mend_b_kernel, in_specs=[vmem] * 5 + [pl.BlockSpec(memory_...]
  transfers between devices with their start and end apart: 10 -> 10, of which waited for: 4 -> 4; matrix products, arithmetic and copies ran while one was open for 0% -> 0% of each run, Pallas kernels for 18% -> 16%
where the time goes in v14:
time: 34 us; the launch traced here: 33.8 us
  starting transfers between devices  13.5 us (40%)
  waiting for transfers between devices  10.8 us (32%)
  Pallas kernels  8.64 us (25%)
  between operations  0.76 us (2%)
    ppermute x5, starting transfers between devices, exchanged(): lax.ppermute(value, axis, [(i, i ^ distance) for i in range(size)])  7.02 us
    ppermute x2, waiting for transfers between devices, alternating(): return lax.ppermute(value, ('sub', 'hor'), pairs)  6.41 us
    ppermute x5, waiting for transfers between devices, exchanged(): lax.ppermute(value, axis, [(i, i ^ distance) for i in range(size)])  4.41 us
    ppermute x3, starting transfers between devices, to_previous(): lax.ppermute(value, 'sub', [(i, (i - 1) % peers) for i in range(peers)])  3.41 us
    ppermute x2, starting transfers between devices, alternating(): return lax.ppermute(value, ('sub', 'hor'), pairs)  3.1 us
    pallas_call x1, Pallas kernels, local(): pl.pallas_call(sweep_kernel, in_specs=[vmem] * 3, out_specs=[vmem] * 4, o...  2.98 us
    pallas_call x1, Pallas kernels, local(): pl.pallas_call(pack_kernel, in_specs=[hbm] * 6, out_specs=vmem, out_shape...  1.93 us
    pallas_call x1, Pallas kernels, local(): pl.pallas_call(finish_kernel, in_specs=[hbm] + [vmem] * 5, out_specs=[hbm...  1.39 us
  transfers between devices with their start and end apart: 10, of which 4 were waited for; matrix products, arithmetic and copies ran while one was open for 0% of the time, Pallas kernels for 16%

profile of v14, /device:TPU:0, one launch (start us, length us, event | category | flops | bytes accessed | tf_op | source)
XLA Modules:
  0.0 33.8 jit_solution(16794743773880618954)
XLA Ops:
  0.7 1.9 %pack.1.mine_ref = f32[12,16,768]{2,1,0:T(8,128)S(1)} custom-call(f32[1,2,12,16,768]{4,3,2,1,0:T(8,128)} %state_ref.5, f32[1,12,16,768]{3,2,1,0:T(8,128)} %east_ref.5, f32[1,12,16,768]{3,2,1,0:T(8,128)} %north_ref.9, s32[2,2,12]{2,1,0:T(2,128)} %cell_ref.1, s32[4,2,2,12]{3,2,1,0:T(2,128)} %offset_ref.1, f32[4,2,2,12]{3,2,1,0:T(2,128)} %weight_ref.1), custom_call_target="tpu_custom_call" | custom-call | flops 1 | bytes 1 | tf_op jit(solution)/shard_map/pack/pallas_call | solution.py:481
  2.6 0.0 copy-start.3
  2.6 0.0 copy-start.4
  2.6 0.5 %collective-permute-start.1 = (f32[12,16,768]{2,1,0:T(8,128)S(1)}, f32[12,16,768]{2,1,0:T(8,128)S(1)}, u32[]{:S(2)}, u32[]{:S(2)}) collective-permute-start(f32[12,16,768]{2,1,0:T(8,128)S(1)} %pack.1.mine_ref), channel_id=1, source_target_pairs={{0,4},{1,0},{2,1},{3,2},{4,5},{5,6},{6,7},{7,3},{8,12},{9,8},{10,9... | collective-permute-start | bytes 1769480 | tf_op jit(solution)/shard_map/ppermute | solution.py:34
  3.1 3.0 %sweep.1 = (f32[11,16,768]{2,1,0:T(8,128)S(1)}, f32[2,4,16,768]{3,2,1,0:T(8,128)S(1)}, f32[2,8,16,768]{3,2,1,0:T(8,128)S(1)}, f32[2,2,12,16,128]{4,3,2,1,0:T(8,128)S(1)}) custom-call(f32[1,2,12,16,768]{4,3,2,1,0:T(8,128)S(1)} %copy-done.1, f32[1,12,16,768]{3,2,1,0:T(8,128)S(1)} %copy-done.2, f32[1,12,16,768]{3,2,1,0:T(8,128)S(1)} %copy-done), custom_call_target="tpu_custom_call" | custom-call | flops 1 | bytes 1 | tf_op jit(solution)/shard_map/sweep/pallas_call | solution.py:500
  6.1 2.6 %collective-permute-start.3 = (f32[11,16,768]{2,1,0:T(8,128)S(1)}, f32[11,16,768]{2,1,0:T(8,128)S(1)}, u32[]{:S(2)}, u32[]{:S(2)}) collective-permute-start(f32[11,16,768]{2,1,0:T(8,128)S(1)} %get-tuple-element.11.mine_ref), channel_id=1, source_target_pairs={{0,1},{1,2},{2,3},{3,7},{4,0},{5,4},{6,5},{7,6},{8,9},{9,10},{10,1... | collective-permute-start | bytes 1622024 | tf_op jit(solution)/shard_map/ppermute | solution.py:34
  8.7 0.7 %collective-permute-start = (f32[2,4,16,768]{3,2,1,0:T(8,128)S(1)}, f32[2,4,16,768]{3,2,1,0:T(8,128)S(1)}, u32[]{:S(2)}, u32[]{:S(2)}) collective-permute-start(f32[2,4,16,768]{3,2,1,0:T(8,128)S(1)} %get-tuple-element.10), channel_id=1, source_target_pairs={{0,12},{4,0},{8,4},{12,8},{1,13},{5,1},{9,5},{13,9},{2,14},{6,2},{... | collective-permute-start | bytes 1179656 | tf_op jit(solution)/shard_map/ppermute | solution.py:22
  9.4 0.4 %ghost_base.1 = (f32[2,2,12,32]{3,2,1,0:T(8,128)S(1)}, f32[2,16,32]{2,1,0:T(8,128)S(1)}) custom-call(s32[2,2,12]{2,1,0:T(2,128)S(1)} %copy-done.5, s32[4,2,2,12]{3,2,1,0:T(2,128)S(1)} %copy-done.3, f32[4,2,2,12]{3,2,1,0:T(2,128)S(1)} %copy-done.4, f32[2,2,12,16,128]{4,3,2,1,0:T(8,128)S(1)} %get-tuple-element.13.column_ref, f32[1,12,16,768]{3,2,1,0:T(8,128)S(1)} %copy-done), custom_call_target="tpu_custom_call" | custom-call | flops 1 | bytes 1 | tf_op jit(solution)/shard_map/ghost_base/pallas_call | solution.py:523
  9.8 6.4 %collective-permute-done.1.other_ref = f32[12,16,768]{2,1,0:T(8,128)S(1)} collective-permute-done((f32[12,16,768]{2,1,0:T(8,128)S(1)}, f32[12,16,768]{2,1,0:T(8,128)S(1)}, u32[]{:S(2)}, u32[]{:S(2)}) %collective-permute-start.1) | collective-permute-done | bytes 589856 | tf_op jit(solution)/shard_map/ppermute | solution.py:34
  16.2 0.8 %mend_a.1 = (f32[2,4,16,768]{3,2,1,0:T(8,128)S(1)}, f32[2,2,6,16,128]{4,3,2,1,0:T(8,128)S(1)}) custom-call(f32[1,12,16,768]{3,2,1,0:T(8,128)S(1)} %copy-done.2, f32[1,12,16,768]{3,2,1,0:T(8,128)S(1)} %copy-done, f32[11,16,768]{2,1,0:T(8,128)S(1)} %get-tuple-element.11.mine_ref, f32[12,16,768]{2,1,0:T(8,128)S(1)} %collective-permute-done.1.other_ref, ...), custom_call_target="tpu_custom_call" | custom-call | flops 1 | bytes 1 | tf_op jit(solution)/shard_map/mend_a/pallas_call | solution.py:534
  16.9 0.2 ghost.1
  17.2 0.1 collective-permute-start.4
  17.3 2.4 %collective-permute-start.5 = (f32[2,16,32]{2,1,0:T(8,128)S(1)}, f32[2,16,32]{2,1,0:T(8,128)S(1)}, u32[]{:S(2)}, u32[]{:S(2)}) collective-permute-start(f32[2,16,32]{2,1,0:T(8,128)S(1)} %ghost.1), channel_id=1, source_target_pairs={{0,8},{4,12},{8,0},{12,4},{1,9},{5,13},{9,1},{13,5},{2,10},{6,14},... | collective-permute-start | bytes 12296 | tf_op jit(solution)/shard_map/ppermute | solution.py:52
  19.7 0.1 collective-permute-start.6
  19.8 1.7 %collective-permute-start.2 = (f32[2,4,16,768]{3,2,1,0:T(8,128)S(1)}, f32[2,4,16,768]{3,2,1,0:T(8,128)S(1)}, u32[]{:S(2)}, u32[]{:S(2)}) collective-permute-start(f32[2,4,16,768]{3,2,1,0:T(8,128)S(1)} %get-tuple-element.15), channel_id=1, source_target_pairs={{0,12},{4,0},{8,4},{12,8},{1,13},{5,1},{9,5},{13,9},{2,14},{6,2},{... | collective-permute-start | bytes 1179656 | tf_op jit(solution)/shard_map/ppermute | solution.py:22
  21.5 1.4 %collective-permute-done.6 = f32[2,16,32]{2,1,0:T(8,128)S(1)} collective-permute-done((f32[2,16,32]{2,1,0:T(8,128)S(1)}, f32[2,16,32]{2,1,0:T(8,128)S(1)}, u32[]{:S(2)}, u32[]{:S(2)}) %collective-permute-start.6) | collective-permute-done | bytes 4128 | tf_op jit(solution)/shard_map/ppermute | solution.py:52
  22.9 0.1 mend_b.1
  23.0 1.1 %collective-permute-start.7 = (f32[2,4,16,768]{3,2,1,0:T(8,128)S(1)}, f32[2,4,16,768]{3,2,1,0:T(8,128)S(1)}, u32[]{:S(2)}, u32[]{:S(2)}) collective-permute-start(f32[2,4,16,768]{3,2,1,0:T(8,128)S(1)} %mend_b.1), channel_id=1, source_target_pairs={{0,12},{4,0},{8,4},{12,8},{1,13},{5,1},{9,5},{13,9},{2,14},{6,2},{... | collective-permute-start | bytes 1179656 | tf_op jit(solution)/shard_map/ppermute | solution.py:22
  24.0 1.7 %collective-permute-start.8 = (f32[2,16,32]{2,1,0:T(8,128)S(1)}, f32[2,16,32]{2,1,0:T(8,128)S(1)}, u32[]{:S(2)}, u32[]{:S(2)}) collective-permute-start(f32[2,16,32]{2,1,0:T(8,128)S(1)} %add_add_fusion.__), channel_id=1, source_target_pairs={{0,1},{1,0},{2,3},{3,2},{4,5},{5,4},{6,7},{7,6},{8,9},{9,8},{10,11... | collective-permute-start | bytes 12296 | tf_op jit(solution)/shard_map/ppermute | solution.py:52
  25.7 2.0 %collective-permute-done.8 = f32[2,16,32]{2,1,0:T(8,128)S(1)} collective-permute-done((f32[2,16,32]{2,1,0:T(8,128)S(1)}, f32[2,16,32]{2,1,0:T(8,128)S(1)}, u32[]{:S(2)}, u32[]{:S(2)}) %collective-permute-start.8) | collective-permute-done | bytes 4128 | tf_op jit(solution)/shard_map/ppermute | solution.py:52
  27.8 2.7 %collective-permute-start.9 = (f32[2,16,32]{2,1,0:T(8,128)S(1)}, f32[2,16,32]{2,1,0:T(8,128)S(1)}, u32[]{:S(2)}, u32[]{:S(2)}) collective-permute-start(f32[2,16,32]{2,1,0:T(8,128)S(1)} %add.15.total_ref), channel_id=1, source_target_pairs={{0,2},{1,3},{2,0},{3,1},{4,6},{5,7},{6,4},{7,5},{8,10},{9,11},{10,... | collective-permute-start | bytes 12296 | tf_op jit(solution)/shard_map/ppermute | solution.py:52
  30.5 0.9 %begin.1.begun_hbm = f32[1,2,12,16,768]{4,3,2,1,0:T(8,128)} custom-call(f32[1,2,12,16,768]{4,3,2,1,0:T(8,128)S(1)} %copy-done.1, f32[2,4,16,768]{3,2,1,0:T(8,128)S(1)} %collective-permute-done.middle_ref._, f32[2,4,16,768]{3,2,1,0:T(8,128)S(1)} %collective-permute-done.2.a_ref), custom_call_target="tpu_custom_call" | custom-call | flops 1 | bytes 1 | tf_op jit(solution)/shard_map/begin/pallas_call | solution.py:573
  31.4 1.0 %collective-permute-done.9.came_ref = f32[2,16,32]{2,1,0:T(8,128)S(1)} collective-permute-done((f32[2,16,32]{2,1,0:T(8,128)S(1)}, f32[2,16,32]{2,1,0:T(8,128)S(1)}, u32[]{:S(2)}, u32[]{:S(2)}) %collective-permute-start.9) | collective-permute-done | bytes 4128 | tf_op jit(solution)/shard_map/ppermute | solution.py:52
  32.4 1.4 %finish.1 = (f32[1,2,12,16,768]{4,3,2,1,0:T(8,128)}, f32[2,4,8]{2,1,0:T(4,128)}) custom-call(f32[1,2,12,16,768]{4,3,2,1,0:T(8,128)} %begin.1.begun_hbm, f32[1,2,12,16,768]{4,3,2,1,0:T(8,128)S(1)} %copy-done.1, f32[2,4,16,768]{3,2,1,0:T(8,128)S(1)} %collective-permute-done.7.b_ref, s32[1,32]{1,0:T(1,128)S(1)} %bitcast.1, ...), custom_call_target="tpu_custom_call", output_to_operand_aliasing={{0}: (0, {})} | custom-call | flops 1 | bytes 1 | tf_op jit(solution)/shard_map/finish/pallas_call | solution.py:583
  (20 shorter events, 0.1 us)
Async XLA Ops:
  0.6 2.5 %copy-start.1 = (f32[1,2,12,16,768]{4,3,2,1,0:T(8,128)S(1)}, f32[1,2,12,16,768]{4,3,2,1,0:T(8,128)}, u32[]{:S(2)}) copy-start(f32[1,2,12,16,768]{4,3,2,1,0:T(8,128)} %state_ref.5) | copy-start | bytes 3538948
  0.6 2.5 %copy-start.2 = (f32[1,12,16,768]{3,2,1,0:T(8,128)S(1)}, f32[1,12,16,768]{3,2,1,0:T(8,128)}, u32[]{:S(2)}) copy-start(f32[1,12,16,768]{3,2,1,0:T(8,128)} %east_ref.5) | copy-start | bytes 1769476
  0.6 2.5 %copy-start = (f32[1,12,16,768]{3,2,1,0:T(8,128)S(1)}, f32[1,12,16,768]{3,2,1,0:T(8,128)}, u32[]{:S(2)}) copy-start(f32[1,12,16,768]{3,2,1,0:T(8,128)} %north_ref.9) | copy-start | bytes 1769476
  2.6 6.8 %copy-start.3 = (s32[4,2,2,12]{3,2,1,0:T(2,128)S(1)}, s32[4,2,2,12]{3,2,1,0:T(2,128)}, u32[]{:S(2)}) copy-start(s32[4,2,2,12]{3,2,1,0:T(2,128)} %offset_ref.1) | copy-start | bytes 2308
  2.6 6.8 %copy-start.4 = (f32[4,2,2,12]{3,2,1,0:T(2,128)S(1)}, f32[4,2,2,12]{3,2,1,0:T(2,128)}, u32[]{:S(2)}) copy-start(f32[4,2,2,12]{3,2,1,0:T(2,128)} %weight_ref.1) | copy-start | bytes 2308
  2.6 6.8 %copy-start.5 = (s32[2,2,12]{2,1,0:T(2,128)S(1)}, s32[2,2,12]{2,1,0:T(2,128)}, u32[]{:S(2)}) copy-start(s32[2,2,12]{2,1,0:T(2,128)} %cell_ref.1) | copy-start | bytes 580
  2.6 13.5 %collective-permute-start.1 = (f32[12,16,768]{2,1,0:T(8,128)S(1)}, f32[12,16,768]{2,1,0:T(8,128)S(1)}, u32[]{:S(2)}, u32[]{:S(2)}) collective-permute-start(f32[12,16,768]{2,1,0:T(8,128)S(1)} %pack.1.mine_ref), channel_id=1, source_target_pairs={{0,4},{1,0},{2,1},{3,2},{4,5},{5,6},{6,7},{7,3},{8,12},{9,8},{10,9... | collective-permute-start | bytes 1769480 | tf_op jit(solution)/shard_map/ppermute | solution.py:34
  6.1 16.8 %collective-permute-start.3 = (f32[11,16,768]{2,1,0:T(8,128)S(1)}, f32[11,16,768]{2,1,0:T(8,128)S(1)}, u32[]{:S(2)}, u32[]{:S(2)}) collective-permute-start(f32[11,16,768]{2,1,0:T(8,128)S(1)} %get-tuple-element.11.mine_ref), channel_id=1, source_target_pairs={{0,1},{1,2},{2,3},{3,7},{4,0},{5,4},{6,5},{7,6},{8,9},{9,10},{10,1... | collective-permute-start | bytes 1622024 | tf_op jit(solution)/shard_map/ppermute | solution.py:34
  8.7 14.2 %collective-permute-start = (f32[2,4,16,768]{3,2,1,0:T(8,128)S(1)}, f32[2,4,16,768]{3,2,1,0:T(8,128)S(1)}, u32[]{:S(2)}, u32[]{:S(2)}) collective-permute-start(f32[2,4,16,768]{3,2,1,0:T(8,128)S(1)} %get-tuple-element.10), channel_id=1, source_target_pairs={{0,12},{4,0},{8,4},{12,8},{1,13},{5,1},{9,5},{13,9},{2,14},{6,2},{... | collective-permute-start | bytes 1179656 | tf_op jit(solution)/shard_map/ppermute | solution.py:22
  17.2 2.6 %collective-permute-start.4 = (f32[2,16,32]{2,1,0:T(8,128)S(1)}, f32[2,16,32]{2,1,0:T(8,128)S(1)}, u32[]{:S(2)}, u32[]{:S(2)}) collective-permute-start(f32[2,16,32]{2,1,0:T(8,128)S(1)} %ghost.1), channel_id=1, source_target_pairs={{0,4},{4,0},{8,12},{12,8},{1,5},{5,1},{9,13},{13,9},{2,6},{6,2},{1... | collective-permute-start | bytes 12296 | tf_op jit(solution)/shard_map/ppermute | solution.py:52
  17.3 4.2 %collective-permute-start.5 = (f32[2,16,32]{2,1,0:T(8,128)S(1)}, f32[2,16,32]{2,1,0:T(8,128)S(1)}, u32[]{:S(2)}, u32[]{:S(2)}) collective-permute-start(f32[2,16,32]{2,1,0:T(8,128)S(1)} %ghost.1), channel_id=1, source_target_pairs={{0,8},{4,12},{8,0},{12,4},{1,9},{5,13},{9,1},{13,5},{2,10},{6,14},... | collective-permute-start | bytes 12296 | tf_op jit(solution)/shard_map/ppermute | solution.py:52
  19.7 3.2 %collective-permute-start.6 = (f32[2,16,32]{2,1,0:T(8,128)S(1)}, f32[2,16,32]{2,1,0:T(8,128)S(1)}, u32[]{:S(2)}, u32[]{:S(2)}) collective-permute-start(f32[2,16,32]{2,1,0:T(8,128)S(1)} %ghost.1), channel_id=1, source_target_pairs={{0,12},{4,8},{8,4},{12,0},{1,13},{5,9},{9,5},{13,1},{2,14},{6,10},... | collective-permute-start | bytes 12296 | tf_op jit(solution)/shard_map/ppermute | solution.py:52
  19.8 10.7 %collective-permute-start.2 = (f32[2,4,16,768]{3,2,1,0:T(8,128)S(1)}, f32[2,4,16,768]{3,2,1,0:T(8,128)S(1)}, u32[]{:S(2)}, u32[]{:S(2)}) collective-permute-start(f32[2,4,16,768]{3,2,1,0:T(8,128)S(1)} %get-tuple-element.15), channel_id=1, source_target_pairs={{0,12},{4,0},{8,4},{12,8},{1,13},{5,1},{9,5},{13,9},{2,14},{6,2},{... | collective-permute-start | bytes 1179656 | tf_op jit(solution)/shard_map/ppermute | solution.py:22
  23.0 9.5 %collective-permute-start.7 = (f32[2,4,16,768]{3,2,1,0:T(8,128)S(1)}, f32[2,4,16,768]{3,2,1,0:T(8,128)S(1)}, u32[]{:S(2)}, u32[]{:S(2)}) collective-permute-start(f32[2,4,16,768]{3,2,1,0:T(8,128)S(1)} %mend_b.1), channel_id=1, source_target_pairs={{0,12},{4,0},{8,4},{12,8},{1,13},{5,1},{9,5},{13,9},{2,14},{6,2},{... | collective-permute-start | bytes 1179656 | tf_op jit(solution)/shard_map/ppermute | solution.py:22
  24.0 3.7 %collective-permute-start.8 = (f32[2,16,32]{2,1,0:T(8,128)S(1)}, f32[2,16,32]{2,1,0:T(8,128)S(1)}, u32[]{:S(2)}, u32[]{:S(2)}) collective-permute-start(f32[2,16,32]{2,1,0:T(8,128)S(1)} %add_add_fusion.__), channel_id=1, source_target_pairs={{0,1},{1,0},{2,3},{3,2},{4,5},{5,4},{6,7},{7,6},{8,9},{9,8},{10,11... | collective-permute-start | bytes 12296 | tf_op jit(solution)/shard_map/ppermute | solution.py:52
  27.8 4.6 %copy-start.6 = (s32[32]{0:T(128)S(1)}, s32[32]{0:T(128)}, u32[]{:S(2)}) copy-start(s32[32]{0:T(128)} %param.13) | copy-start | bytes 388
  27.8 4.6 %collective-permute-start.9 = (f32[2,16,32]{2,1,0:T(8,128)S(1)}, f32[2,16,32]{2,1,0:T(8,128)S(1)}, u32[]{:S(2)}, u32[]{:S(2)}) collective-permute-start(f32[2,16,32]{2,1,0:T(8,128)S(1)} %add.15.total_ref), channel_id=1, source_target_pairs={{0,2},{1,3},{2,0},{3,1},{4,6},{5,7},{6,4},{7,5},{8,10},{9,11},{10,... | collective-permute-start | bytes 12296 | tf_op jit(solution)/shard_map/ppermute | solution.py:52

commit v15 on v14

--- a/solution.py
+++ b/solution.py
@@ -12,7 +12,8 @@
 FLUX_ROWS = 2 * STEPS
 PACK_ROWS = FLUX_ROWS + 3
 LANES = 128
-EXTRA = PACK_ROWS
+PIECE_ROWS = STEPS + 2
+EXTRA = STEPS + 1
 TARGETS = 4 * LANES
 WEIGHTS = 5 * LANES
 
@@ -86,6 +87,22 @@
         return self.centre * value + shifted(self.plus * value, self.minus * value)
 
 
+class Pack:
+    def __init__(self, *refs):
+        self.refs = refs
+
+    def flux(self, c, k, at):
+        return self.refs[c][k, at, :] if len(self.refs) == 2 else self.refs[0][2 * k + c, at, :]
+
+    def east(self, r, at):
+        if len(self.refs) == 2:
+            return self.refs[r][STEPS, at, :]
+        return self.refs[0][FLUX_ROWS + 2 * r, at, :]
+
+    def north(self, at):
+        return self.refs[0][STEPS + 1 if len(self.refs) == 2 else FLUX_ROWS + 1, at, :]
+
+
 def level_halves(levels, body):
     def step(h, carry):
         body(pl.ds(pl.multiple_of(h * HALF, HALF), HALF))
@@ -94,9 +111,24 @@
     lax.fori_loop(0, levels // HALF, step, 0)
 
 
+def end_fluxes(parts, sign, state, east, north, store):
+    row = [Row(east(r) * sign, north(r)) for r in range(STEPS)]
+    for c in range(parts):
+        field = [state(c, r) for r in range(STEPS)]
+        for k in range(STEPS):
+            store(c, k, row[0].outward * field[0])
+            after = []
+            for r in range(STEPS - 1 - k):
+                value = row[r].stay(field[r]) + row[r + 1].outward * field[r + 1]
+                if r > 0:
+                    value = value + row[r - 1].inward * field[r - 1]
+                after.append(value)
+            field = after
+
+
 def pack_kernel(
     state_hbm, east_hbm, north_hbm, cell_hbm, offset_hbm, weight_hbm,
-    pack_ref, state_ref, east_ref, north_ref, cell_ref, offset_ref, weight_ref, sems, small_sems,
+    piece_0, piece_1, state_ref, east_ref, north_ref, cell_ref, offset_ref, weight_ref, sems, small_sems,
 ):
     parts, rows, levels, width = state_hbm.shape[1:]
     flip = parity()
@@ -127,25 +159,24 @@
         copy.start()
 
     def half(at):
-        row = [Row(east_ref[place(r), at, :] * sign, north_ref[place(r), at, :]) for r in range(STEPS)]
-        pack_ref[FLUX_ROWS, at, :] = east_ref[place(0), at, :]
-        pack_ref[FLUX_ROWS + 1, at, :] = north_ref[place(0), at, :]
-        pack_ref[FLUX_ROWS + 2, at, :] = east_ref[place(1), at, :]
+        piece_0[STEPS, at, :] = east_ref[place(0), at, :]
+        piece_0[STEPS + 1, at, :] = north_ref[place(0), at, :]
+        piece_1[STEPS, at, :] = east_ref[place(1), at, :]
         for r in (1, 2):
             lanes = (2 * r - 2) * LANES
-            pack_ref[EXTRA, at, lanes:lanes + LANES] = north_ref[place(r), at, :LANES]
-            pack_ref[EXTRA, at, lanes + LANES:lanes + 2 * LANES] = north_ref[place(r), at, width - LANES:]
-        for c in range(parts):
-            field = [state_ref[c, place(r), at, :] for r in range(STEPS)]
-            for k in range(STEPS):
-                pack_ref[2 * k + c, at, :] = row[0].outward * field[0]
-                after = []
-                for r in range(STEPS - 1 - k):
-                    value = row[r].stay(field[r]) + row[r + 1].outward * field[r + 1]
-                    if r > 0:
-                        value = value + row[r - 1].inward * field[r - 1]
-                    after.append(value)
-                field = after
+            piece_1[EXTRA, at, lanes:lanes + LANES] = north_ref[place(r), at, :LANES]
+            piece_1[EXTRA, at, lanes + LANES:lanes + 2 * LANES] = north_ref[place(r), at, width - LANES:]
+
+        def store(c, k, value):
+            (piece_0, piece_1)[c][k, at, :] = value
+
+        end_fluxes(
+            parts, sign,
+            lambda c, r: state_ref[c, place(r), at, :],
+            lambda r: east_ref[place(r), at, :],
+            lambda r: north_ref[place(r), at, :],
+            store,
+        )
 
     for h in range(halves):
         for copy in copies[h]:
@@ -158,9 +189,34 @@
     for point in range(offset_ref.shape[0]):
         for c in range(parts):
             target = (cell_ref[c] + offset_ref[point, c]).astype(jnp.float32)
-            pack_ref[EXTRA, n:n + 2, TARGETS:TARGETS + rows] = target
-            pack_ref[EXTRA, n:n + 2, WEIGHTS:WEIGHTS + rows] = weight_ref[point, c]
+            piece_1[EXTRA, n:n + 2, TARGETS:TARGETS + rows] = target
+            piece_1[EXTRA, n:n + 2, WEIGHTS:WEIGHTS + rows] = weight_ref[point, c]
             n += 2
+
+
+def second_pack_kernel(state_ref, east_ref, north_ref, _, pack_ref):
+    parts, rows, levels = state_ref.shape[1:4]
+    flip = 1 - parity()
+    sign = sign_of(flip)
+    place = lambda r: r + flip * (rows - 1 - 2 * r)
+
+    def half(at):
+        pack_ref[FLUX_ROWS, at, :] = east_ref[0, place(0), at, :]
+        pack_ref[FLUX_ROWS + 1, at, :] = north_ref[0, place(0), at, :]
+        pack_ref[FLUX_ROWS + 2, at, :] = east_ref[0, place(1), at, :]
+
+        def store(c, k, value):
+            pack_ref[2 * k + c, at, :] = value
+
+        end_fluxes(
+            parts, sign,
+            lambda c, r: state_ref[0, c, place(r), at, :],
+            lambda r: east_ref[0, place(r), at, :],
+            lambda r: north_ref[0, place(r), at, :],
+            store,
+        )
+
+    level_halves(levels, half)
 
 
 def as_column(row):
@@ -171,28 +227,17 @@
 
 
 def sweep_kernel(
-    state_ref, east_ref, north_ref, pack_ref, middle_ref, ends_ref, column_ref,
+    state_ref, east_ref, north_ref, _, middle_ref, ends_ref, column_ref,
     field, plus_ref, minus_ref, centre_ref,
 ):
     parts, rows, levels, width = state_ref.shape[1:]
-    flip = 1 - parity()
-    sign = sign_of(flip)
-    end_row = flip * (rows - 1)
-    next_row = end_row + 1 - 2 * flip
 
     def half(at):
-        pack_ref[FLUX_ROWS, at, :] = east_ref[0, end_row, at, :]
-        pack_ref[FLUX_ROWS + 1, at, :] = north_ref[0, end_row, at, :]
-        pack_ref[FLUX_ROWS + 2, at, :] = east_ref[0, next_row, at, :]
-
         for k in range(STEPS):
             if k == 0:
                 read = lambda c, i: state_ref[0, c, i, at, :]
             else:
                 read = lambda c, i, slot=k - 1: field[slot, c, i]
-            leaving = jnp.maximum(east_ref[0, end_row, at, :] * sign, 0.0)
-            for c in range(parts):
-                pack_ref[2 * k + c, at, :] = leaving * read(c, end_row)
             west = [None] * parts
             here = [read(c, 0) for c in range(parts)]
             east_here = east_ref[0, 0, at, :]
@@ -274,7 +319,7 @@
         partial_ref[c] = total
 
 
-def ghost_kernel(north_ref, other_ref, column_ref, mixing_ref, partial_ref, sum_ref, near_mixing):
+def ghost_kernel(north_ref, other_0, other_1, column_ref, mixing_ref, partial_ref, sum_ref, near_mixing):
     parts, levels, slots = partial_ref.shape
     rows = mixing_ref.shape[2]
     width = north_ref.shape[-1]
@@ -285,8 +330,8 @@
         for s in range(2):
             at = [(point * parts + c) * 2 + s for point in range(points)]
             near_mixing[c, s] = mix(
-                [other_ref[EXTRA, n:n + 1, TARGETS:TARGETS + rows] for n in at],
-                [other_ref[EXTRA, n:n + 1, WEIGHTS:WEIGHTS + rows] for n in at],
+                [other_1[EXTRA, n:n + 1, TARGETS:TARGETS + rows] for n in at],
+                [other_1[EXTRA, n:n + 1, WEIGHTS:WEIGHTS + rows] for n in at],
                 cells, jnp.zeros((rows, slots), jnp.float32),
             )
     for c in range(parts):
@@ -299,12 +344,12 @@
             total = total + north * mixing_ref[c, 1, pl.ds(i, 1), :]
             i = r + (1 - flip) * (rows - 1 - 2 * r)
             if r == 0:
-                first_rate = other_ref[FLUX_ROWS + 1, :, :LANES]
-                last_rate = other_ref[FLUX_ROWS + 1, :, width - LANES:]
+                first_rate = other_0[STEPS + 1, :, :LANES]
+                last_rate = other_0[STEPS + 1, :, width - LANES:]
             else:
                 lanes = (2 * r - 2) * LANES
-                first_rate = other_ref[EXTRA, :, lanes:lanes + LANES]
-                last_rate = other_ref[EXTRA, :, lanes + LANES:lanes + 2 * LANES]
+                first_rate = other_1[EXTRA, :, lanes:lanes + LANES]
+                last_rate = other_1[EXTRA, :, lanes + LANES:lanes + 2 * LANES]
             south = jnp.maximum(first_rate[:, :1], 0.0) * column_ref[c, 0, STEPS - 1 + r, :, :1]
             north = jnp.maximum(-last_rate[:, LANES - 1:], 0.0) * column_ref[c, 1, STEPS - 1 + r, :, LANES - 1:]
             total = total + south * near_mixing[c, 0, pl.ds(i, 1), :]
@@ -312,19 +357,20 @@
         sum_ref[c] = jnp.where(has_neighbour(flip), total, partial_ref[c])
 
 
-def mend_side(flip, east_ref, north_ref, mine_ref, other_ref, store, store_column):
-    levels, width = mine_ref.shape[1:]
+def mend_side(flip, east_ref, north_ref, mine_pack, other_pack, store, store_column):
+    levels, width = east_ref.shape[2:]
     rows = east_ref.shape[1]
     sign = sign_of(flip)
     place = lambda r: flip * (rows - STEPS) + r + flip * (STEPS - 1 - 2 * r)
 
     def half(at):
         own = [Row(east_ref[0, place(r), at, :] * sign, north_ref[0, place(r), at, :]) for r in range(STEPS - 1)]
-        near = Row(other_ref[FLUX_ROWS, at, :] * sign, other_ref[FLUX_ROWS + 1, at, :])
-        far = Row(other_ref[FLUX_ROWS + 2, at, :] * sign)
+        near = Row(other_pack.east(0, at) * sign, other_pack.north(at))
+        far_east = other_pack.east(1, at)
+        far = Row(far_east * sign)
         for c in range(FLUX_ROWS // STEPS):
-            mine = lambda k: mine_ref[2 * k + c, at, :]
-            theirs = lambda k: other_ref[2 * k + c, at, :]
+            mine = lambda k: mine_pack.flux(c, k, at)
+            theirs = lambda k: other_pack.flux(c, k, at)
             a0 = theirs(0)
             n1 = mine(0)
             b0 = own[0].stay(a0) + near.inward * n1 + theirs(1)
@@ -345,8 +391,8 @@
                 tiles = (slice(0, LANES), slice(width - LANES, width))
                 for s, lanes in enumerate(tiles):
                     tile = lambda value: value[:, lanes]
-                    rate = other_ref[EXTRA, at, s * LANES:(s + 1) * LANES]
-                    stays = 1.0 - jnp.abs(other_ref[FLUX_ROWS + 2, at, lanes]) - jnp.abs(rate)
+                    rate = other_pack.refs[1][EXTRA, at, s * LANES:(s + 1) * LANES]
+                    stays = 1.0 - jnp.abs(far_east[:, lanes]) - jnp.abs(rate)
                     drift = jnp.maximum(rate if s == 0 else -rate, 0.0) * tile(bn2)
                     cn2 = stays * tile(bn2) + pltpu.roll(drift, LANES - 1 if s == 0 else 1, 1)
                     cn2 = cn2 + tile(near.outward) * tile(bn1)
@@ -367,7 +413,7 @@
             out_ref[c, r] = ends_ref[c, flip * STEPS + r]
 
 
-def mend_a_kernel(east_ref, north_ref, mine_ref, other_ref, ends_ref, base_ref, out_ref, column_ref):
+def mend_a_kernel(east_ref, north_ref, mine_ref, other_0, other_1, ends_ref, base_ref, out_ref, column_ref):
     flip = 1 - parity()
     turn = lambda r: r + flip * (STEPS - 1 - 2 * r)
 
@@ -379,7 +425,7 @@
 
     @pl.when(has_neighbour(flip))
     def _():
-        mend_side(flip, east_ref, north_ref, mine_ref, other_ref, store, store_column)
+        mend_side(flip, east_ref, north_ref, Pack(mine_ref), Pack(other_0, other_1), store, store_column)
 
     @pl.when(jnp.logical_not(has_neighbour(flip)))
     def _():
@@ -387,7 +433,7 @@
         copy_end(flip, ends_ref, out_ref)
 
 
-def mend_b_kernel(east_ref, north_ref, mine_ref, other_ref, ends_ref, _, __, out_ref):
+def mend_b_kernel(east_ref, north_ref, mine_0, mine_1, other_ref, ends_ref, _, __, out_ref):
     flip = parity()
     turn = lambda r: r + flip * (STEPS - 1 - 2 * r)
 
@@ -396,7 +442,7 @@
 
     @pl.when(has_neighbour(flip))
     def _():
-        mend_side(flip, east_ref, north_ref, mine_ref, other_ref, store, None)
+        mend_side(flip, east_ref, north_ref, Pack(mine_0, mine_1), Pack(other_ref), store, None)
 
     @pl.when(jnp.logical_not(has_neighbour(flip)))
     def _():
@@ -453,6 +499,7 @@
 
 
 BRIEF = pl.CostEstimate(flops=1, bytes_accessed=1, transcendentals=0)
+LONG = pl.CostEstimate(flops=1, bytes_accessed=1 << 26, transcendentals=0)
 PARAMS = pltpu.CompilerParams(vmem_limit_bytes=24 * 1024 * 1024)
 
 
@@ -481,8 +528,8 @@
     first_pack = pl.pallas_call(
         pack_kernel,
         in_specs=[hbm] * 6,
-        out_specs=vmem,
-        out_shape=f32(PACK_ROWS + 1, levels, width),
+        out_specs=[vmem] * 2,
+        out_shape=[f32(PIECE_ROWS, levels, width)] * 2,
         scratch_shapes=[
             pltpu.VMEM((parts, STEPS, levels, width), jnp.float32),
             pltpu.VMEM((STEPS, levels, width), jnp.float32),
@@ -494,15 +541,25 @@
         cost_estimate=BRIEF,
         name="pack",
     )(*[in_hbm(value) for value in [adjoint_state, courant_east, courant_north] + small])
-    first_came = alternating(first_pack, -1)
+    first_came = [alternating(piece, -1) for piece in first_pack]
 
     state, east, north = adjoint_state, courant_east, courant_north
-    second_pack, middle, ends, columns = pl.pallas_call(
+    after = pl.BlockSpec(memory_space=pl.ANY)
+    second_pack = pl.pallas_call(
+        second_pack_kernel,
+        in_specs=[vmem] * 3 + [after],
+        out_specs=vmem,
+        out_shape=f32(PACK_ROWS, levels, width),
+        compiler_params=PARAMS,
+        cost_estimate=BRIEF,
+        name="second_pack",
+    )(state, east, north, first_pack[0])
+    second_came = alternating(second_pack, 1)
+    middle, ends, columns = pl.pallas_call(
         sweep_kernel,
-        in_specs=[vmem] * 3,
-        out_specs=[vmem] * 4,
+        in_specs=[vmem] * 3 + [after],
+        out_specs=[vmem] * 3,
         out_shape=[
-            f32(PACK_ROWS, levels, width),
             f32(parts, inner, levels, width),
             f32(parts, 2 * STEPS, levels, width),
             f32(parts, 2, rows, levels, LANES),
@@ -514,10 +571,9 @@
             pltpu.VMEM((rows, HALF, width), jnp.float32),
         ],
         compiler_params=PARAMS,
-        cost_estimate=BRIEF,
+        cost_estimate=LONG,
         name="sweep",
-    )(state, east, north)
-    second_came = alternating(second_pack, 1)
+    )(state, east, north, second_pack)
     middle_came = to_previous(middle)
 
     mixing, base = pl.pallas_call(
@@ -533,35 +589,35 @@
     column_shape = (parts, 2, 2 * (STEPS - 1), levels, LANES)
     side_a, a_columns = pl.pallas_call(
         mend_a_kernel,
-        in_specs=[vmem] * 6,
+        in_specs=[vmem] * 7,
         out_specs=[vmem] * 2,
         out_shape=[f32(parts, STEPS, levels, width), f32(*column_shape)],
         compiler_params=PARAMS,
         cost_estimate=BRIEF,
         name="mend_a",
-    )(east, north, second_pack, first_came, ends, base)
+    )(east, north, second_pack, *first_came, ends, base)
     a_came = to_previous(side_a)
     total = pl.pallas_call(
         ghost_kernel,
-        in_specs=[vmem] * 5,
+        in_specs=[vmem] * 6,
         out_specs=vmem,
         out_shape=f32(parts, levels, slots),
         scratch_shapes=[pltpu.VMEM((parts, 2, rows, slots), jnp.float32)],
         compiler_params=PARAMS,
         cost_estimate=BRIEF,
         name="ghost",
-    )(north, first_came, a_columns, mixing, base)
+    )(north, *first_came, a_columns, mixing, base)
     order = rounds()
     total = total + exchanged(total, *order[0])
     side_b = pl.pallas_call(
         mend_b_kernel,
-        in_specs=[vmem] * 5 + [pl.BlockSpec(memory_space=pl.ANY)] * 2,
+        in_specs=[vmem] * 6 + [pl.BlockSpec(memory_space=pl.ANY)] * 2,
         out_specs=vmem,
         out_shape=f32(parts, STEPS, levels, width),
         compiler_params=PARAMS,
         cost_estimate=BRIEF,
         name="mend_b",
-    )(east, north, first_pack, second_came, ends, middle_came, total)
+    )(east, north, *first_pack, second_came, ends, middle_came, total)
     b_came = to_previous(side_b)
 
     for each in order[1:-1]:

time: 34 us -> 36.2 us (1.065)
  waiting for transfers between devices: 10.8 us -> 11.8 us
  starting transfers between devices: 13.5 us -> 14.2 us
  Pallas kernels: 8.64 us -> 9.2 us
    ppermute x3, starting transfers between devices: 3.41 us -> 4.8 us  [to_previous(): lax.ppermute(value, 'sub', [(i, (i - 1) % peers) for i in range(peers)])]
    ppermute x2 -> x3, waiting for transfers between devices: 6.41 us -> 7.35 us  [alternating(): return lax.ppermute(value, ('sub', 'hor'), pairs)]
    ppermute x5, starting transfers between devices: 7.02 us -> 6.37 us  [exchanged(): lax.ppermute(value, axis, [(i, i ^ distance) for i in range(size)])]
    pallas_call x5 -> x6, Pallas kernels: 5.96 us -> 6.52 us  [the longest x1 2.9 us: local(): pl.pallas_call(sweep_kernel, in_specs=[vmem] * 3 + [after], out_specs=[vm...]
    ppermute x2 -> x3, starting transfers between devices: 3.1 us -> 3.06 us  [alternating(): return lax.ppermute(value, ('sub', 'hor'), pairs)]
  transfers between devices with their start and end apart: 10 -> 11, of which waited for: 4 -> 6; matrix products, arithmetic and copies ran while one was open for 0% -> 0% of each run, Pallas kernels for 16% -> 15%
where the time goes in v15:
time: 36.2 us; the launch traced here: 36 us
  starting transfers between devices  14.2 us (39%)
  waiting for transfers between devices  11.8 us (33%)
  Pallas kernels  9.2 us (25%)
  between operations  0.78 us (2%)
    ppermute x3, waiting for transfers between devices, alternating(): return lax.ppermute(value, ('sub', 'hor'), pairs)  7.35 us
    ppermute x5, starting transfers between devices, exchanged(): lax.ppermute(value, axis, [(i, i ^ distance) for i in range(size)])  6.37 us
    ppermute x3, starting transfers between devices, to_previous(): lax.ppermute(value, 'sub', [(i, (i - 1) % peers) for i in range(peers)])  4.8 us
    ppermute x5, waiting for transfers between devices, exchanged(): lax.ppermute(value, axis, [(i, i ^ distance) for i in range(size)])  4.41 us
    ppermute x3, starting transfers between devices, alternating(): return lax.ppermute(value, ('sub', 'hor'), pairs)  3.06 us
    pallas_call x1, Pallas kernels, local(): pl.pallas_call(sweep_kernel, in_specs=[vmem] * 3 + [after], out_specs=[vm...  2.9 us
    pallas_call x1, Pallas kernels, local(): pl.pallas_call(pack_kernel, in_specs=[hbm] * 6, out_specs=[vmem] * 2, out...  1.93 us
    pallas_call x1, Pallas kernels, local(): pl.pallas_call(finish_kernel, in_specs=[hbm] + [vmem] * 5, out_specs=[hbm...  1.39 us
  transfers between devices with their start and end apart: 11, of which 6 were waited for; matrix products, arithmetic and copies ran while one was open for 0% of the time, Pallas kernels for 15%

profile of v15, /device:TPU:0, one launch (start us, length us, event | category | flops | bytes accessed | tf_op | source)
XLA Modules:
  0.0 36.0 jit_solution(9261204020894947030)
XLA Ops:
  0.7 1.9 %pack.1 = (f32[6,16,768]{2,1,0:T(8,128)S(1)}, f32[6,16,768]{2,1,0:T(8,128)S(1)}) custom-call(f32[1,2,12,16,768]{4,3,2,1,0:T(8,128)} %state_ref.7, f32[1,12,16,768]{3,2,1,0:T(8,128)} %east_ref.7, f32[1,12,16,768]{3,2,1,0:T(8,128)} %north_ref.11, s32[2,2,12]{2,1,0:T(2,128)} %cell_ref.1, s32[4,2,2,12]{3,2,1,0:T(2,128)} %offset_ref.1, f32[4,2,2,12]{3,2,1,0:T(2,128)} %weight_ref.1), custom_call_target="tpu_custom_call" | custom-call | flops 1 | bytes 1 | tf_op jit(solution)/shard_map/pack/pallas_call | solution.py:528
  2.6 0.6 %second_pack.1._.mine_ref = f32[11,16,768]{2,1,0:T(8,128)S(1)} custom-call(f32[1,2,12,16,768]{4,3,2,1,0:T(8,128)S(1)} %copy-done, f32[1,12,16,768]{3,2,1,0:T(8,128)S(1)} %copy-done.2, f32[1,12,16,768]{3,2,1,0:T(8,128)S(1)} %copy-done.1, f32[6,16,768]{2,1,0:T(8,128)S(1)} %get-tuple-element.11._.mine_0), custom_call_target="tpu_custom_call" | custom-call | flops 1 | bytes 1 | tf_op jit(solution)/shard_map/second_pack/pallas_call | solution.py:548
  3.3 3.0 %collective-permute-start.4 = (f32[11,16,768]{2,1,0:T(8,128)S(1)}, f32[11,16,768]{2,1,0:T(8,128)S(1)}, u32[]{:S(2)}, u32[]{:S(2)}) collective-permute-start(f32[11,16,768]{2,1,0:T(8,128)S(1)} %second_pack.1._.mine_ref), channel_id=1, source_target_pairs={{0,1},{1,2},{2,3},{3,7},{4,0},{5,4},{6,5},{7,6},{8,9},{9,10},{10,1... | collective-permute-start | bytes 1622024 | tf_op jit(solution)/shard_map/ppermute | solution.py:35
  6.4 2.9 %sweep.1 = (f32[2,4,16,768]{3,2,1,0:T(8,128)S(1)}, f32[2,8,16,768]{3,2,1,0:T(8,128)S(1)}, f32[2,2,12,16,128]{4,3,2,1,0:T(8,128)S(1)}) custom-call(f32[1,2,12,16,768]{4,3,2,1,0:T(8,128)S(1)} %copy-done, f32[1,12,16,768]{3,2,1,0:T(8,128)S(1)} %copy-done.2, f32[1,12,16,768]{3,2,1,0:T(8,128)S(1)} %copy-done.1, f32[11,16,768]{2,1,0:T(8,128)S(1)} %second_pack.1._.mine_ref), custom_call_target="tpu_custom_call" | custom-call | flops 1 | bytes 67108864 | tf_op jit(solution)/shard_map/sweep/pallas_call | solution.py:558
  9.3 2.1 %collective-permute-start = (f32[2,4,16,768]{3,2,1,0:T(8,128)S(1)}, f32[2,4,16,768]{3,2,1,0:T(8,128)S(1)}, u32[]{:S(2)}, u32[]{:S(2)}) collective-permute-start(f32[2,4,16,768]{3,2,1,0:T(8,128)S(1)} %get-tuple-element.12), channel_id=1, source_target_pairs={{0,12},{4,0},{8,4},{12,8},{1,13},{5,1},{9,5},{13,9},{2,14},{6,2},{... | collective-permute-start | bytes 1179656 | tf_op jit(solution)/shard_map/ppermute | solution.py:23
  11.4 0.4 %ghost_base.1 = (f32[2,2,12,32]{3,2,1,0:T(8,128)S(1)}, f32[2,16,32]{2,1,0:T(8,128)S(1)}) custom-call(s32[2,2,12]{2,1,0:T(2,128)S(1)} %copy-done.5, s32[4,2,2,12]{3,2,1,0:T(2,128)S(1)} %copy-done.3, f32[4,2,2,12]{3,2,1,0:T(2,128)S(1)} %copy-done.4, f32[2,2,12,16,128]{4,3,2,1,0:T(8,128)S(1)} %get-tuple-element.15.column_ref, f32[1,12,16,768]{3,2,1,0:T(8,128)S(1)} %copy-done.1), custom_call_target="tpu_custom_call" | custom-call | flops 1 | bytes 1 | tf_op jit(solution)/shard_map/ghost_base/pallas_call | solution.py:579
  11.8 4.2 %collective-permute-done.1.other_0 = f32[6,16,768]{2,1,0:T(8,128)S(1)} collective-permute-done((f32[6,16,768]{2,1,0:T(8,128)S(1)}, f32[6,16,768]{2,1,0:T(8,128)S(1)}, u32[]{:S(2)}, u32[]{:S(2)}) %collective-permute-start.1) | collective-permute-done | bytes 294944 | tf_op jit(solution)/shard_map/ppermute | solution.py:35
  16.0 3.2 %collective-permute-done.2.other_1 = f32[6,16,768]{2,1,0:T(8,128)S(1)} collective-permute-done((f32[6,16,768]{2,1,0:T(8,128)S(1)}, f32[6,16,768]{2,1,0:T(8,128)S(1)}, u32[]{:S(2)}, u32[]{:S(2)}) %collective-permute-start.2) | collective-permute-done | bytes 294944 | tf_op jit(solution)/shard_map/ppermute | solution.py:35
  19.1 0.8 %mend_a.1 = (f32[2,4,16,768]{3,2,1,0:T(8,128)S(1)}, f32[2,2,6,16,128]{4,3,2,1,0:T(8,128)S(1)}) custom-call(f32[1,12,16,768]{3,2,1,0:T(8,128)S(1)} %copy-done.2, f32[1,12,16,768]{3,2,1,0:T(8,128)S(1)} %copy-done.1, f32[11,16,768]{2,1,0:T(8,128)S(1)} %second_pack.1._.mine_ref, f32[6,16,768]{2,1,0:T(8,128)S(1)} %collective-permute-done.1.other_0, ...), custom_call_target="tpu_custom_call" | custom-call | flops 1 | bytes 1 | tf_op jit(solution)/shard_map/mend_a/pallas_call | solution.py:590
  19.9 0.2 ghost.1
  20.1 0.1 collective-permute-start.5
  20.2 1.7 %collective-permute-start.6 = (f32[2,16,32]{2,1,0:T(8,128)S(1)}, f32[2,16,32]{2,1,0:T(8,128)S(1)}, u32[]{:S(2)}, u32[]{:S(2)}) collective-permute-start(f32[2,16,32]{2,1,0:T(8,128)S(1)} %ghost.1), channel_id=1, source_target_pairs={{0,8},{4,12},{8,0},{12,4},{1,9},{5,13},{9,1},{13,5},{2,10},{6,14},... | collective-permute-start | bytes 12296 | tf_op jit(solution)/shard_map/ppermute | solution.py:53
  21.9 0.1 collective-permute-start.7
  22.1 1.6 %collective-permute-start.3 = (f32[2,4,16,768]{3,2,1,0:T(8,128)S(1)}, f32[2,4,16,768]{3,2,1,0:T(8,128)S(1)}, u32[]{:S(2)}, u32[]{:S(2)}) collective-permute-start(f32[2,4,16,768]{3,2,1,0:T(8,128)S(1)} %get-tuple-element.17), channel_id=1, source_target_pairs={{0,12},{4,0},{8,4},{12,8},{1,13},{5,1},{9,5},{13,9},{2,14},{6,2},{... | collective-permute-start | bytes 1179656 | tf_op jit(solution)/shard_map/ppermute | solution.py:23
  23.7 0.3 collective-permute-done.6
  24.0 1.1 %collective-permute-done.7 = f32[2,16,32]{2,1,0:T(8,128)S(1)} collective-permute-done((f32[2,16,32]{2,1,0:T(8,128)S(1)}, f32[2,16,32]{2,1,0:T(8,128)S(1)}, u32[]{:S(2)}, u32[]{:S(2)}) %collective-permute-start.7) | collective-permute-done | bytes 4128 | tf_op jit(solution)/shard_map/ppermute | solution.py:53
  25.1 0.1 mend_b.1
  25.2 1.1 %collective-permute-start.8 = (f32[2,4,16,768]{3,2,1,0:T(8,128)S(1)}, f32[2,4,16,768]{3,2,1,0:T(8,128)S(1)}, u32[]{:S(2)}, u32[]{:S(2)}) collective-permute-start(f32[2,4,16,768]{3,2,1,0:T(8,128)S(1)} %mend_b.1), channel_id=1, source_target_pairs={{0,12},{4,0},{8,4},{12,8},{1,13},{5,1},{9,5},{13,9},{2,14},{6,2},{... | collective-permute-start | bytes 1179656 | tf_op jit(solution)/shard_map/ppermute | solution.py:23
  26.2 1.7 %collective-permute-start.9 = (f32[2,16,32]{2,1,0:T(8,128)S(1)}, f32[2,16,32]{2,1,0:T(8,128)S(1)}, u32[]{:S(2)}, u32[]{:S(2)}) collective-permute-start(f32[2,16,32]{2,1,0:T(8,128)S(1)} %add_add_fusion.__), channel_id=1, source_target_pairs={{0,1},{1,0},{2,3},{3,2},{4,5},{5,4},{6,7},{7,6},{8,9},{9,8},{10,11... | collective-permute-start | bytes 12296 | tf_op jit(solution)/shard_map/ppermute | solution.py:53
  28.0 2.0 %collective-permute-done.9 = f32[2,16,32]{2,1,0:T(8,128)S(1)} collective-permute-done((f32[2,16,32]{2,1,0:T(8,128)S(1)}, f32[2,16,32]{2,1,0:T(8,128)S(1)}, u32[]{:S(2)}, u32[]{:S(2)}) %collective-permute-start.9) | collective-permute-done | bytes 4128 | tf_op jit(solution)/shard_map/ppermute | solution.py:53
  30.0 2.7 %collective-permute-start.10 = (f32[2,16,32]{2,1,0:T(8,128)S(1)}, f32[2,16,32]{2,1,0:T(8,128)S(1)}, u32[]{:S(2)}, u32[]{:S(2)}) collective-permute-start(f32[2,16,32]{2,1,0:T(8,128)S(1)} %add.15.total_ref), channel_id=1, source_target_pairs={{0,2},{1,3},{2,0},{3,1},{4,6},{5,7},{6,4},{7,5},{8,10},{9,11},{10,... | collective-permute-start | bytes 12296 | tf_op jit(solution)/shard_map/ppermute | solution.py:53
  32.7 0.9 %begin.1.begun_hbm = f32[1,2,12,16,768]{4,3,2,1,0:T(8,128)} custom-call(f32[1,2,12,16,768]{4,3,2,1,0:T(8,128)S(1)} %copy-done, f32[2,4,16,768]{3,2,1,0:T(8,128)S(1)} %collective-permute-done.middle_ref._, f32[2,4,16,768]{3,2,1,0:T(8,128)S(1)} %collective-permute-done.3.a_ref), custom_call_target="tpu_custom_call" | custom-call | flops 1 | bytes 1 | tf_op jit(solution)/shard_map/begin/pallas_call | solution.py:629
  33.7 1.0 %collective-permute-done.10.came_ref = f32[2,16,32]{2,1,0:T(8,128)S(1)} collective-permute-done((f32[2,16,32]{2,1,0:T(8,128)S(1)}, f32[2,16,32]{2,1,0:T(8,128)S(1)}, u32[]{:S(2)}, u32[]{:S(2)}) %collective-permute-start.10) | collective-permute-done | bytes 4128 | tf_op jit(solution)/shard_map/ppermute | solution.py:53
  34.6 1.4 %finish.1 = (f32[1,2,12,16,768]{4,3,2,1,0:T(8,128)}, f32[2,4,8]{2,1,0:T(4,128)}) custom-call(f32[1,2,12,16,768]{4,3,2,1,0:T(8,128)} %begin.1.begun_hbm, f32[1,2,12,16,768]{4,3,2,1,0:T(8,128)S(1)} %copy-done, f32[2,4,16,768]{3,2,1,0:T(8,128)S(1)} %collective-permute-done.8.b_ref, s32[1,32]{1,0:T(1,128)S(1)} %bitcast.1, ...), custom_call_target="tpu_custom_call", output_to_operand_aliasing={{0}: (0, {})} | custom-call | flops 1 | bytes 1 | tf_op jit(solution)/shard_map/finish/pallas_call | solution.py:639
  (23 shorter events, 0.1 us)
Async XLA Ops:
  0.6 2.0 %copy-start = (f32[1,2,12,16,768]{4,3,2,1,0:T(8,128)S(1)}, f32[1,2,12,16,768]{4,3,2,1,0:T(8,128)}, u32[]{:S(2)}) copy-start(f32[1,2,12,16,768]{4,3,2,1,0:T(8,128)} %state_ref.7) | copy-start | bytes 3538948
  0.6 2.0 %copy-start.2 = (f32[1,12,16,768]{3,2,1,0:T(8,128)S(1)}, f32[1,12,16,768]{3,2,1,0:T(8,128)}, u32[]{:S(2)}) copy-start(f32[1,12,16,768]{3,2,1,0:T(8,128)} %east_ref.7) | copy-start | bytes 1769476
  0.6 2.0 %copy-start.1 = (f32[1,12,16,768]{3,2,1,0:T(8,128)S(1)}, f32[1,12,16,768]{3,2,1,0:T(8,128)}, u32[]{:S(2)}) copy-start(f32[1,12,16,768]{3,2,1,0:T(8,128)} %north_ref.11) | copy-start | bytes 1769476
  3.3 21.8 %collective-permute-start.4 = (f32[11,16,768]{2,1,0:T(8,128)S(1)}, f32[11,16,768]{2,1,0:T(8,128)S(1)}, u32[]{:S(2)}, u32[]{:S(2)}) collective-permute-start(f32[11,16,768]{2,1,0:T(8,128)S(1)} %second_pack.1._.mine_ref), channel_id=1, source_target_pairs={{0,1},{1,2},{2,3},{3,7},{4,0},{5,4},{6,5},{7,6},{8,9},{9,10},{10,1... | collective-permute-start | bytes 1622024 | tf_op jit(solution)/shard_map/ppermute | solution.py:35
  6.3 9.6 %collective-permute-start.1 = (f32[6,16,768]{2,1,0:T(8,128)S(1)}, f32[6,16,768]{2,1,0:T(8,128)S(1)}, u32[]{:S(2)}, u32[]{:S(2)}) collective-permute-start(f32[6,16,768]{2,1,0:T(8,128)S(1)} %get-tuple-element.11._.mine_0), channel_id=1, source_target_pairs={{0,4},{1,0},{2,1},{3,2},{4,5},{5,6},{6,7},{7,3},{8,12},{9,8},{10,9... | collective-permute-start | bytes 884744 | tf_op jit(solution)/shard_map/ppermute | solution.py:35
  6.3 5.1 %copy-start.3 = (s32[4,2,2,12]{3,2,1,0:T(2,128)S(1)}, s32[4,2,2,12]{3,2,1,0:T(2,128)}, u32[]{:S(2)}) copy-start(s32[4,2,2,12]{3,2,1,0:T(2,128)} %offset_ref.1) | copy-start | bytes 2308
  6.3 5.1 %copy-start.4 = (f32[4,2,2,12]{3,2,1,0:T(2,128)S(1)}, f32[4,2,2,12]{3,2,1,0:T(2,128)}, u32[]{:S(2)}) copy-start(f32[4,2,2,12]{3,2,1,0:T(2,128)} %weight_ref.1) | copy-start | bytes 2308
  6.3 5.1 %copy-start.5 = (s32[2,2,12]{2,1,0:T(2,128)S(1)}, s32[2,2,12]{2,1,0:T(2,128)}, u32[]{:S(2)}) copy-start(s32[2,2,12]{2,1,0:T(2,128)} %cell_ref.1) | copy-start | bytes 580
  6.3 12.8 %collective-permute-start.2 = (f32[6,16,768]{2,1,0:T(8,128)S(1)}, f32[6,16,768]{2,1,0:T(8,128)S(1)}, u32[]{:S(2)}, u32[]{:S(2)}) collective-permute-start(f32[6,16,768]{2,1,0:T(8,128)S(1)} %get-tuple-element.13.mine_1), channel_id=1, source_target_pairs={{0,4},{1,0},{2,1},{3,2},{4,5},{5,6},{6,7},{7,3},{8,12},{9,8},{10,9... | collective-permute-start | bytes 884744 | tf_op jit(solution)/shard_map/ppermute | solution.py:35
  9.3 15.8 %collective-permute-start = (f32[2,4,16,768]{3,2,1,0:T(8,128)S(1)}, f32[2,4,16,768]{3,2,1,0:T(8,128)S(1)}, u32[]{:S(2)}, u32[]{:S(2)}) collective-permute-start(f32[2,4,16,768]{3,2,1,0:T(8,128)S(1)} %get-tuple-element.12), channel_id=1, source_target_pairs={{0,12},{4,0},{8,4},{12,8},{1,13},{5,1},{9,5},{13,9},{2,14},{6,2},{... | collective-permute-start | bytes 1179656 | tf_op jit(solution)/shard_map/ppermute | solution.py:23
  20.1 1.9 %collective-permute-start.5 = (f32[2,16,32]{2,1,0:T(8,128)S(1)}, f32[2,16,32]{2,1,0:T(8,128)S(1)}, u32[]{:S(2)}, u32[]{:S(2)}) collective-permute-start(f32[2,16,32]{2,1,0:T(8,128)S(1)} %ghost.1), channel_id=1, source_target_pairs={{0,4},{4,0},{8,12},{12,8},{1,5},{5,1},{9,13},{13,9},{2,6},{6,2},{1... | collective-permute-start | bytes 12296 | tf_op jit(solution)/shard_map/ppermute | solution.py:53
  20.2 3.8 %collective-permute-start.6 = (f32[2,16,32]{2,1,0:T(8,128)S(1)}, f32[2,16,32]{2,1,0:T(8,128)S(1)}, u32[]{:S(2)}, u32[]{:S(2)}) collective-permute-start(f32[2,16,32]{2,1,0:T(8,128)S(1)} %ghost.1), channel_id=1, source_target_pairs={{0,8},{4,12},{8,0},{12,4},{1,9},{5,13},{9,1},{13,5},{2,10},{6,14},... | collective-permute-start | bytes 12296 | tf_op jit(solution)/shard_map/ppermute | solution.py:53
  21.9 3.2 %collective-permute-start.7 = (f32[2,16,32]{2,1,0:T(8,128)S(1)}, f32[2,16,32]{2,1,0:T(8,128)S(1)}, u32[]{:S(2)}, u32[]{:S(2)}) collective-permute-start(f32[2,16,32]{2,1,0:T(8,128)S(1)} %ghost.1), channel_id=1, source_target_pairs={{0,12},{4,8},{8,4},{12,0},{1,13},{5,9},{9,5},{13,1},{2,14},{6,10},... | collective-permute-start | bytes 12296 | tf_op jit(solution)/shard_map/ppermute | solution.py:53
  22.1 10.7 %collective-permute-start.3 = (f32[2,4,16,768]{3,2,1,0:T(8,128)S(1)}, f32[2,4,16,768]{3,2,1,0:T(8,128)S(1)}, u32[]{:S(2)}, u32[]{:S(2)}) collective-permute-start(f32[2,4,16,768]{3,2,1,0:T(8,128)S(1)} %get-tuple-element.17), channel_id=1, source_target_pairs={{0,12},{4,0},{8,4},{12,8},{1,13},{5,1},{9,5},{13,9},{2,14},{6,2},{... | collective-permute-start | bytes 1179656 | tf_op jit(solution)/shard_map/ppermute | solution.py:23
  25.2 9.5 %collective-permute-start.8 = (f32[2,4,16,768]{3,2,1,0:T(8,128)S(1)}, f32[2,4,16,768]{3,2,1,0:T(8,128)S(1)}, u32[]{:S(2)}, u32[]{:S(2)}) collective-permute-start(f32[2,4,16,768]{3,2,1,0:T(8,128)S(1)} %mend_b.1), channel_id=1, source_target_pairs={{0,12},{4,0},{8,4},{12,8},{1,13},{5,1},{9,5},{13,9},{2,14},{6,2},{... | collective-permute-start | bytes 1179656 | tf_op jit(solution)/shard_map/ppermute | solution.py:23
  26.2 3.7 %collective-permute-start.9 = (f32[2,16,32]{2,1,0:T(8,128)S(1)}, f32[2,16,32]{2,1,0:T(8,128)S(1)}, u32[]{:S(2)}, u32[]{:S(2)}) collective-permute-start(f32[2,16,32]{2,1,0:T(8,128)S(1)} %add_add_fusion.__), channel_id=1, source_target_pairs={{0,1},{1,0},{2,3},{3,2},{4,5},{5,4},{6,7},{7,6},{8,9},{9,8},{10,11... | collective-permute-start | bytes 12296 | tf_op jit(solution)/shard_map/ppermute | solution.py:53
  30.0 4.6 %copy-start.6 = (s32[32]{0:T(128)S(1)}, s32[32]{0:T(128)}, u32[]{:S(2)}) copy-start(s32[32]{0:T(128)} %param.13) | copy-start | bytes 388
  30.0 4.6 %collective-permute-start.10 = (f32[2,16,32]{2,1,0:T(8,128)S(1)}, f32[2,16,32]{2,1,0:T(8,128)S(1)}, u32[]{:S(2)}, u32[]{:S(2)}) collective-permute-start(f32[2,16,32]{2,1,0:T(8,128)S(1)} %add.15.total_ref), channel_id=1, source_target_pairs={{0,2},{1,3},{2,0},{3,1},{4,6},{5,7},{6,4},{7,5},{8,10},{9,11},{10,... | collective-permute-start | bytes 12296 | tf_op jit(solution)/shard_map/ppermute | solution.py:53

commit v16 on v14

--- a/solution.py
+++ b/solution.py
@@ -367,7 +367,8 @@
             out_ref[c, r] = ends_ref[c, flip * STEPS + r]
 
 
-def mend_a_kernel(east_ref, north_ref, mine_ref, other_ref, ends_ref, base_ref, out_ref, column_ref):
+def mend_a_kernel(east_ref, north_ref, mine_ref, other_ref, ends_ref, base_ref, out_ref, column_ref, passed_ref):
+    passed_ref[...] = mine_ref[...]
     flip = 1 - parity()
     turn = lambda r: r + flip * (STEPS - 1 - 2 * r)
 
@@ -517,7 +518,6 @@
         cost_estimate=BRIEF,
         name="sweep",
     )(state, east, north)
-    second_came = alternating(second_pack, 1)
     middle_came = to_previous(middle)
 
     mixing, base = pl.pallas_call(
@@ -531,15 +531,18 @@
     )(*small, columns, north)
 
     column_shape = (parts, 2, 2 * (STEPS - 1), levels, LANES)
-    side_a, a_columns = pl.pallas_call(
+    side_a, a_columns, second_sent = pl.pallas_call(
         mend_a_kernel,
         in_specs=[vmem] * 6,
-        out_specs=[vmem] * 2,
-        out_shape=[f32(parts, STEPS, levels, width), f32(*column_shape)],
+        out_specs=[vmem] * 3,
+        out_shape=[
+            f32(parts, STEPS, levels, width), f32(*column_shape), f32(PACK_ROWS, levels, width)
+        ],
         compiler_params=PARAMS,
         cost_estimate=BRIEF,
         name="mend_a",
     )(east, north, second_pack, first_came, ends, base)
+    second_came = alternating(second_sent, 1)
     a_came = to_previous(side_a)
     total = pl.pallas_call(
         ghost_kernel,

time: 34 us -> 36.5 us (1.074)
  the two profiles are of different devices: /device:TPU:0 before, /device:TPU:1 now
where the time goes in v16:
time: 36.5 us; the launch traced here: 36.3 us
  starting transfers between devices  13.6 us (37%)
  waiting for transfers between devices  13.2 us (36%)
  Pallas kernels  8.67 us (24%)
  between operations  0.79 us (2%)
    ppermute x5, starting transfers between devices, exchanged(): lax.ppermute(value, axis, [(i, i ^ distance) for i in range(size)])  6.51 us
    ppermute x5, waiting for transfers between devices, exchanged(): lax.ppermute(value, axis, [(i, i ^ distance) for i in range(size)])  5.75 us
    ppermute x2, starting transfers between devices, alternating(): return lax.ppermute(value, ('sub', 'hor'), pairs)  4.88 us
    ppermute x3, waiting for transfers between devices, to_previous(): lax.ppermute(value, 'sub', [(i, (i - 1) % peers) for i in range(peers)])  4.03 us
    ppermute x2, waiting for transfers between devices, alternating(): return lax.ppermute(value, ('sub', 'hor'), pairs)  3.44 us
    pallas_call x1, Pallas kernels, local(): pl.pallas_call(sweep_kernel, in_specs=[vmem] * 3, out_specs=[vmem] * 4, o...  2.97 us
    ppermute x3, starting transfers between devices, to_previous(): lax.ppermute(value, 'sub', [(i, (i - 1) % peers) for i in range(peers)])  2.2 us
    pallas_call x1, Pallas kernels, local(): pl.pallas_call(pack_kernel, in_specs=[hbm] * 6, out_specs=vmem, out_shape...  1.93 us
  transfers between devices with their start and end apart: 10, of which 5 were waited for; matrix products, arithmetic and copies ran while one was open for 0% of the time, Pallas kernels for 15%

profile of v16, /device:TPU:1, one launch (start us, length us, event | category | flops | bytes accessed | tf_op | source)
XLA Modules:
  0.0 36.3 jit_solution(17434110492124739730)
XLA Ops:
  0.7 1.9 %pack.1.mine_ref = f32[12,16,768]{2,1,0:T(8,128)S(1)} custom-call(f32[1,2,12,16,768]{4,3,2,1,0:T(8,128)} %state_ref.5, f32[1,12,16,768]{3,2,1,0:T(8,128)} %east_ref.5, f32[1,12,16,768]{3,2,1,0:T(8,128)} %north_ref.9, s32[2,2,12]{2,1,0:T(2,128)} %cell_ref.1, s32[4,2,2,12]{3,2,1,0:T(2,128)} %offset_ref.1, f32[4,2,2,12]{3,2,1,0:T(2,128)} %weight_ref.1), custom_call_target="tpu_custom_call" | custom-call | flops 1 | bytes 1 | tf_op jit(solution)/shard_map/pack/pallas_call | solution.py:482
  2.6 0.0 copy-start.3
  2.6 0.0 copy-start.4
  2.6 2.1 %collective-permute-start.1 = (f32[12,16,768]{2,1,0:T(8,128)S(1)}, f32[12,16,768]{2,1,0:T(8,128)S(1)}, u32[]{:S(2)}, u32[]{:S(2)}) collective-permute-start(f32[12,16,768]{2,1,0:T(8,128)S(1)} %pack.1.mine_ref), channel_id=1, source_target_pairs={{0,4},{1,0},{2,1},{3,2},{4,5},{5,6},{6,7},{7,3},{8,12},{9,8},{10,9... | collective-permute-start | bytes 1769480 | tf_op jit(solution)/shard_map/ppermute | solution.py:34
  4.8 3.0 %sweep.1 = (f32[11,16,768]{2,1,0:T(8,128)S(1)}, f32[2,4,16,768]{3,2,1,0:T(8,128)S(1)}, f32[2,8,16,768]{3,2,1,0:T(8,128)S(1)}, f32[2,2,12,16,128]{4,3,2,1,0:T(8,128)S(1)}) custom-call(f32[1,2,12,16,768]{4,3,2,1,0:T(8,128)S(1)} %copy-done.1, f32[1,12,16,768]{3,2,1,0:T(8,128)S(1)} %copy-done.2, f32[1,12,16,768]{3,2,1,0:T(8,128)S(1)} %copy-done), custom_call_target="tpu_custom_call" | custom-call | flops 1 | bytes 1 | tf_op jit(solution)/shard_map/sweep/pallas_call | solution.py:501
  7.8 0.4 %ghost_base.1 = (f32[2,2,12,32]{3,2,1,0:T(8,128)S(1)}, f32[2,16,32]{2,1,0:T(8,128)S(1)}) custom-call(s32[2,2,12]{2,1,0:T(2,128)S(1)} %copy-done.5, s32[4,2,2,12]{3,2,1,0:T(2,128)S(1)} %copy-done.3, f32[4,2,2,12]{3,2,1,0:T(2,128)S(1)} %copy-done.4, f32[2,2,12,16,128]{4,3,2,1,0:T(8,128)S(1)} %get-tuple-element.14.column_ref, f32[1,12,16,768]{3,2,1,0:T(8,128)S(1)} %copy-done), custom_call_target="tpu_custom_call" | custom-call | flops 1 | bytes 1 | tf_op jit(solution)/shard_map/ghost_base/pallas_call | solution.py:523
  8.2 3.4 %collective-permute-done.1.other_ref = f32[12,16,768]{2,1,0:T(8,128)S(1)} collective-permute-done((f32[12,16,768]{2,1,0:T(8,128)S(1)}, f32[12,16,768]{2,1,0:T(8,128)S(1)}, u32[]{:S(2)}, u32[]{:S(2)}) %collective-permute-start.1) | collective-permute-done | bytes 589856 | tf_op jit(solution)/shard_map/ppermute | solution.py:34
  11.6 0.1 mend_a.1
  11.7 2.7 %collective-permute-start.3 = (f32[11,16,768]{2,1,0:T(8,128)S(1)}, f32[11,16,768]{2,1,0:T(8,128)S(1)}, u32[]{:S(2)}, u32[]{:S(2)}) collective-permute-start(f32[11,16,768]{2,1,0:T(8,128)S(1)} %get-tuple-element.17), channel_id=1, source_target_pairs={{0,1},{1,2},{2,3},{3,7},{4,0},{5,4},{6,5},{7,6},{8,9},{9,10},{10,1... | collective-permute-start | bytes 1622024 | tf_op jit(solution)/shard_map/ppermute | solution.py:34
  14.4 2.0 %collective-permute-start = (f32[2,4,16,768]{3,2,1,0:T(8,128)S(1)}, f32[2,4,16,768]{3,2,1,0:T(8,128)S(1)}, u32[]{:S(2)}, u32[]{:S(2)}) collective-permute-start(f32[2,4,16,768]{3,2,1,0:T(8,128)S(1)} %get-tuple-element.11), channel_id=1, source_target_pairs={{0,12},{4,0},{8,4},{12,8},{1,13},{5,1},{9,5},{13,9},{2,14},{6,2},{... | collective-permute-start | bytes 1179656 | tf_op jit(solution)/shard_map/ppermute | solution.py:22
  16.4 0.2 ghost.1
  16.7 1.2 %collective-permute-start.6 = (f32[2,16,32]{2,1,0:T(8,128)S(1)}, f32[2,16,32]{2,1,0:T(8,128)S(1)}, u32[]{:S(2)}, u32[]{:S(2)}) collective-permute-start(f32[2,16,32]{2,1,0:T(8,128)S(1)} %ghost.1), channel_id=1, source_target_pairs={{0,12},{4,8},{8,4},{12,0},{1,13},{5,9},{9,5},{13,1},{2,14},{6,10},... | collective-permute-start | bytes 12296 | tf_op jit(solution)/shard_map/ppermute | solution.py:52
  17.8 0.3 collective-permute-start.5
  18.1 0.8 %collective-permute-start.4 = (f32[2,16,32]{2,1,0:T(8,128)S(1)}, f32[2,16,32]{2,1,0:T(8,128)S(1)}, u32[]{:S(2)}, u32[]{:S(2)}) collective-permute-start(f32[2,16,32]{2,1,0:T(8,128)S(1)} %ghost.1), channel_id=1, source_target_pairs={{0,4},{4,0},{8,12},{12,8},{1,5},{5,1},{9,13},{13,9},{2,6},{6,2},{1... | collective-permute-start | bytes 12296 | tf_op jit(solution)/shard_map/ppermute | solution.py:52
  18.9 4.6 %collective-permute-done.6 = f32[2,16,32]{2,1,0:T(8,128)S(1)} collective-permute-done((f32[2,16,32]{2,1,0:T(8,128)S(1)}, f32[2,16,32]{2,1,0:T(8,128)S(1)}, u32[]{:S(2)}, u32[]{:S(2)}) %collective-permute-start.6) | collective-permute-done | bytes 4128 | tf_op jit(solution)/shard_map/ppermute | solution.py:52
  23.6 0.8 %mend_b.1 = f32[2,4,16,768]{3,2,1,0:T(8,128)S(1)} custom-call(f32[1,12,16,768]{3,2,1,0:T(8,128)S(1)} %copy-done.2, f32[1,12,16,768]{3,2,1,0:T(8,128)S(1)} %copy-done, f32[12,16,768]{2,1,0:T(8,128)S(1)} %pack.1.mine_ref, f32[11,16,768]{2,1,0:T(8,128)S(1)} %collective-permute-done.3.other_ref, f32[2,8,16,768]{3,2,1,0:T(8,128)S(1)} %get-tuple-element.13.ends_ref, ...), custom_call_target="tpu_custom_call" | custom-call | flops 1 | bytes 1 | tf_op jit(solution)/shard_map/mend_b/pallas_call | solution.py:559
  24.4 0.2 collective-permute-start.7
  24.5 2.1 %collective-permute-start.8 = (f32[2,16,32]{2,1,0:T(8,128)S(1)}, f32[2,16,32]{2,1,0:T(8,128)S(1)}, u32[]{:S(2)}, u32[]{:S(2)}) collective-permute-start(f32[2,16,32]{2,1,0:T(8,128)S(1)} %add_add_fusion.__), channel_id=1, source_target_pairs={{0,1},{1,0},{2,3},{3,2},{4,5},{5,4},{6,7},{7,6},{8,9},{9,8},{10,11... | collective-permute-start | bytes 12296 | tf_op jit(solution)/shard_map/ppermute | solution.py:52
  26.7 1.1 %collective-permute-done.8 = f32[2,16,32]{2,1,0:T(8,128)S(1)} collective-permute-done((f32[2,16,32]{2,1,0:T(8,128)S(1)}, f32[2,16,32]{2,1,0:T(8,128)S(1)}, u32[]{:S(2)}, u32[]{:S(2)}) %collective-permute-start.8) | collective-permute-done | bytes 4128 | tf_op jit(solution)/shard_map/ppermute | solution.py:52
  27.8 2.2 %collective-permute-start.9 = (f32[2,16,32]{2,1,0:T(8,128)S(1)}, f32[2,16,32]{2,1,0:T(8,128)S(1)}, u32[]{:S(2)}, u32[]{:S(2)}) collective-permute-start(f32[2,16,32]{2,1,0:T(8,128)S(1)} %add.15.total_ref), channel_id=1, source_target_pairs={{0,2},{1,3},{2,0},{3,1},{4,6},{5,7},{6,4},{7,5},{8,10},{9,11},{10,... | collective-permute-start | bytes 12296 | tf_op jit(solution)/shard_map/ppermute | solution.py:52
  30.0 0.8 %collective-permute-done.2.a_ref = f32[2,4,16,768]{3,2,1,0:T(8,128)S(1)} collective-permute-done((f32[2,4,16,768]{3,2,1,0:T(8,128)S(1)}, f32[2,4,16,768]{3,2,1,0:T(8,128)S(1)}, u32[]{:S(2)}, u32[]{:S(2)}) %collective-permute-start.2) | collective-permute-done | bytes 393248 | tf_op jit(solution)/shard_map/ppermute | solution.py:22
  30.7 0.9 %begin.1.begun_hbm = f32[1,2,12,16,768]{4,3,2,1,0:T(8,128)} custom-call(f32[1,2,12,16,768]{4,3,2,1,0:T(8,128)S(1)} %copy-done.1, f32[2,4,16,768]{3,2,1,0:T(8,128)S(1)} %collective-permute-done.middle_ref._, f32[2,4,16,768]{3,2,1,0:T(8,128)S(1)} %collective-permute-done.2.a_ref), custom_call_target="tpu_custom_call" | custom-call | flops 1 | bytes 1 | tf_op jit(solution)/shard_map/begin/pallas_call | solution.py:576
  31.7 3.3 %collective-permute-done.7.b_ref = f32[2,4,16,768]{3,2,1,0:T(8,128)S(1)} collective-permute-done((f32[2,4,16,768]{3,2,1,0:T(8,128)S(1)}, f32[2,4,16,768]{3,2,1,0:T(8,128)S(1)}, u32[]{:S(2)}, u32[]{:S(2)}) %collective-permute-start.7) | collective-permute-done | bytes 393248 | tf_op jit(solution)/shard_map/ppermute | solution.py:22
  34.9 1.4 %finish.1 = (f32[1,2,12,16,768]{4,3,2,1,0:T(8,128)}, f32[2,4,8]{2,1,0:T(4,128)}) custom-call(f32[1,2,12,16,768]{4,3,2,1,0:T(8,128)} %begin.1.begun_hbm, f32[1,2,12,16,768]{4,3,2,1,0:T(8,128)S(1)} %copy-done.1, f32[2,4,16,768]{3,2,1,0:T(8,128)S(1)} %collective-permute-done.7.b_ref, s32[1,32]{1,0:T(1,128)S(1)} %bitcast.1, ...), custom_call_target="tpu_custom_call", output_to_operand_aliasing={{0}: (0, {})} | custom-call | flops 1 | bytes 1 | tf_op jit(solution)/shard_map/finish/pallas_call | solution.py:586
  (20 shorter events, 0.1 us)
Async XLA Ops:
  0.6 4.1 %copy-start = (f32[1,12,16,768]{3,2,1,0:T(8,128)S(1)}, f32[1,12,16,768]{3,2,1,0:T(8,128)}, u32[]{:S(2)}) copy-start(f32[1,12,16,768]{3,2,1,0:T(8,128)} %north_ref.9) | copy-start | bytes 1769476
  0.6 4.1 %copy-start.2 = (f32[1,12,16,768]{3,2,1,0:T(8,128)S(1)}, f32[1,12,16,768]{3,2,1,0:T(8,128)}, u32[]{:S(2)}) copy-start(f32[1,12,16,768]{3,2,1,0:T(8,128)} %east_ref.5) | copy-start | bytes 1769476
  0.6 4.1 %copy-start.1 = (f32[1,2,12,16,768]{4,3,2,1,0:T(8,128)S(1)}, f32[1,2,12,16,768]{4,3,2,1,0:T(8,128)}, u32[]{:S(2)}) copy-start(f32[1,2,12,16,768]{4,3,2,1,0:T(8,128)} %state_ref.5) | copy-start | bytes 3538948
  2.6 5.2 %copy-start.3 = (s32[4,2,2,12]{3,2,1,0:T(2,128)S(1)}, s32[4,2,2,12]{3,2,1,0:T(2,128)}, u32[]{:S(2)}) copy-start(s32[4,2,2,12]{3,2,1,0:T(2,128)} %offset_ref.1) | copy-start | bytes 2308
  2.6 5.2 %copy-start.4 = (f32[4,2,2,12]{3,2,1,0:T(2,128)S(1)}, f32[4,2,2,12]{3,2,1,0:T(2,128)}, u32[]{:S(2)}) copy-start(f32[4,2,2,12]{3,2,1,0:T(2,128)} %weight_ref.1) | copy-start | bytes 2308
  2.6 5.2 %copy-start.5 = (s32[2,2,12]{2,1,0:T(2,128)S(1)}, s32[2,2,12]{2,1,0:T(2,128)}, u32[]{:S(2)}) copy-start(s32[2,2,12]{2,1,0:T(2,128)} %cell_ref.1) | copy-start | bytes 580
  2.6 9.0 %collective-permute-start.1 = (f32[12,16,768]{2,1,0:T(8,128)S(1)}, f32[12,16,768]{2,1,0:T(8,128)S(1)}, u32[]{:S(2)}, u32[]{:S(2)}) collective-permute-start(f32[12,16,768]{2,1,0:T(8,128)S(1)} %pack.1.mine_ref), channel_id=1, source_target_pairs={{0,4},{1,0},{2,1},{3,2},{4,5},{5,6},{6,7},{7,3},{8,12},{9,8},{10,9... | collective-permute-start | bytes 1769480 | tf_op jit(solution)/shard_map/ppermute | solution.py:34
  11.7 11.9 %collective-permute-start.3 = (f32[11,16,768]{2,1,0:T(8,128)S(1)}, f32[11,16,768]{2,1,0:T(8,128)S(1)}, u32[]{:S(2)}, u32[]{:S(2)}) collective-permute-start(f32[11,16,768]{2,1,0:T(8,128)S(1)} %get-tuple-element.17), channel_id=1, source_target_pairs={{0,1},{1,2},{2,3},{3,7},{4,0},{5,4},{6,5},{7,6},{8,9},{9,10},{10,1... | collective-permute-start | bytes 1622024 | tf_op jit(solution)/shard_map/ppermute | solution.py:34
  14.4 9.1 %collective-permute-start = (f32[2,4,16,768]{3,2,1,0:T(8,128)S(1)}, f32[2,4,16,768]{3,2,1,0:T(8,128)S(1)}, u32[]{:S(2)}, u32[]{:S(2)}) collective-permute-start(f32[2,4,16,768]{3,2,1,0:T(8,128)S(1)} %get-tuple-element.11), channel_id=1, source_target_pairs={{0,12},{4,0},{8,4},{12,8},{1,13},{5,1},{9,5},{13,9},{2,14},{6,2},{... | collective-permute-start | bytes 1179656 | tf_op jit(solution)/shard_map/ppermute | solution.py:22
  16.7 6.8 %collective-permute-start.6 = (f32[2,16,32]{2,1,0:T(8,128)S(1)}, f32[2,16,32]{2,1,0:T(8,128)S(1)}, u32[]{:S(2)}, u32[]{:S(2)}) collective-permute-start(f32[2,16,32]{2,1,0:T(8,128)S(1)} %ghost.1), channel_id=1, source_target_pairs={{0,12},{4,8},{8,4},{12,0},{1,13},{5,9},{9,5},{13,1},{2,14},{6,10},... | collective-permute-start | bytes 12296 | tf_op jit(solution)/shard_map/ppermute | solution.py:52
  17.8 5.7 %collective-permute-start.5 = (f32[2,16,32]{2,1,0:T(8,128)S(1)}, f32[2,16,32]{2,1,0:T(8,128)S(1)}, u32[]{:S(2)}, u32[]{:S(2)}) collective-permute-start(f32[2,16,32]{2,1,0:T(8,128)S(1)} %ghost.1), channel_id=1, source_target_pairs={{0,8},{4,12},{8,0},{12,4},{1,9},{5,13},{9,1},{13,5},{2,10},{6,14},... | collective-permute-start | bytes 12296 | tf_op jit(solution)/shard_map/ppermute | solution.py:52
  18.1 5.4 %collective-permute-start.4 = (f32[2,16,32]{2,1,0:T(8,128)S(1)}, f32[2,16,32]{2,1,0:T(8,128)S(1)}, u32[]{:S(2)}, u32[]{:S(2)}) collective-permute-start(f32[2,16,32]{2,1,0:T(8,128)S(1)} %ghost.1), channel_id=1, source_target_pairs={{0,4},{4,0},{8,12},{12,8},{1,5},{5,1},{9,13},{13,9},{2,6},{6,2},{1... | collective-permute-start | bytes 12296 | tf_op jit(solution)/shard_map/ppermute | solution.py:52
  23.5 7.2 %collective-permute-start.2 = (f32[2,4,16,768]{3,2,1,0:T(8,128)S(1)}, f32[2,4,16,768]{3,2,1,0:T(8,128)S(1)}, u32[]{:S(2)}, u32[]{:S(2)}) collective-permute-start(f32[2,4,16,768]{3,2,1,0:T(8,128)S(1)} %get-tuple-element.16), channel_id=1, source_target_pairs={{0,12},{4,0},{8,4},{12,8},{1,13},{5,1},{9,5},{13,9},{2,14},{6,2},{... | collective-permute-start | bytes 1179656 | tf_op jit(solution)/shard_map/ppermute | solution.py:22
  24.4 10.6 %collective-permute-start.7 = (f32[2,4,16,768]{3,2,1,0:T(8,128)S(1)}, f32[2,4,16,768]{3,2,1,0:T(8,128)S(1)}, u32[]{:S(2)}, u32[]{:S(2)}) collective-permute-start(f32[2,4,16,768]{3,2,1,0:T(8,128)S(1)} %mend_b.1), channel_id=1, source_target_pairs={{0,12},{4,0},{8,4},{12,8},{1,13},{5,1},{9,5},{13,9},{2,14},{6,2},{... | collective-permute-start | bytes 1179656 | tf_op jit(solution)/shard_map/ppermute | solution.py:22
  24.5 3.2 %collective-permute-start.8 = (f32[2,16,32]{2,1,0:T(8,128)S(1)}, f32[2,16,32]{2,1,0:T(8,128)S(1)}, u32[]{:S(2)}, u32[]{:S(2)}) collective-permute-start(f32[2,16,32]{2,1,0:T(8,128)S(1)} %add_add_fusion.__), channel_id=1, source_target_pairs={{0,1},{1,0},{2,3},{3,2},{4,5},{5,4},{6,7},{7,6},{8,9},{9,8},{10,11... | collective-permute-start | bytes 12296 | tf_op jit(solution)/shard_map/ppermute | solution.py:52
  27.8 7.2 %copy-start.6 = (s32[32]{0:T(128)S(1)}, s32[32]{0:T(128)}, u32[]{:S(2)}) copy-start(s32[32]{0:T(128)} %param.13) | copy-start | bytes 388
  27.8 3.9 %collective-permute-start.9 = (f32[2,16,32]{2,1,0:T(8,128)S(1)}, f32[2,16,32]{2,1,0:T(8,128)S(1)}, u32[]{:S(2)}, u32[]{:S(2)}) collective-permute-start(f32[2,16,32]{2,1,0:T(8,128)S(1)} %add.15.total_ref), channel_id=1, source_target_pairs={{0,2},{1,3},{2,0},{3,1},{4,6},{5,7},{6,4},{7,5},{8,10},{9,11},{10,... | collective-permute-start | bytes 12296 | tf_op jit(solution)/shard_map/ppermute | solution.py:52

commit v17 on v14

--- a/solution.py
+++ b/solution.py
@@ -387,7 +387,7 @@
         copy_end(flip, ends_ref, out_ref)
 
 
-def mend_b_kernel(east_ref, north_ref, mine_ref, other_ref, ends_ref, _, __, out_ref):
+def mend_b_kernel(east_ref, north_ref, mine_ref, other_ref, ends_ref, _, out_ref):
     flip = parity()
     turn = lambda r: r + flip * (STEPS - 1 - 2 * r)
 
@@ -424,13 +424,14 @@
         copy.wait()
 
 
-def finish_kernel(
-    begun_hbm, state_ref, b_ref, owner_ref, total_ref, came_ref, out_hbm, gradient_ref, buffer, sems
-):
-    parts = b_ref.shape[0]
+def end_kernel(begun_hbm, state_ref, b_ref, out_hbm, buffer, sems):
     start = (1 - parity()) * (state_ref.shape[2] - STEPS)
-    copies = subtract_rows(state_ref, out_hbm, buffer, sems, ((start, b_ref),))
-
+    for copy in subtract_rows(state_ref, out_hbm, buffer, sems, ((start, b_ref),)):
+        copy.wait()
+
+
+def pick_kernel(_, owner_ref, total_ref, came_ref, gradient_ref):
+    parts = gradient_ref.shape[0]
     share, mine = gradient_ref.shape[1:]
     start = lax.axis_index("hor") * mine
     chosen = []
@@ -448,8 +449,6 @@
         picked = jnp.where(column == q, value, picked)
     for c in range(parts):
         gradient_ref[c] = picked[c * share:(c + 1) * share]
-    for copy in copies:
-        copy.wait()
 
 
 BRIEF = pl.CostEstimate(flops=1, bytes_accessed=1, transcendentals=0)
@@ -555,13 +554,13 @@
     total = total + exchanged(total, *order[0])
     side_b = pl.pallas_call(
         mend_b_kernel,
-        in_specs=[vmem] * 5 + [pl.BlockSpec(memory_space=pl.ANY)] * 2,
+        in_specs=[vmem] * 5 + [pl.BlockSpec(memory_space=pl.ANY)],
         out_specs=vmem,
         out_shape=f32(parts, STEPS, levels, width),
         compiler_params=PARAMS,
         cost_estimate=BRIEF,
         name="mend_b",
-    )(east, north, first_pack, second_came, ends, middle_came, total)
+    )(east, north, first_pack, second_came, ends, total)
     b_came = to_previous(side_b)
 
     for each in order[1:-1]:
@@ -580,17 +579,26 @@
         cost_estimate=BRIEF,
         name="begin",
     )(state, middle_came, a_came)
-    adjoint_result, boundary_gradient = pl.pallas_call(
-        finish_kernel,
-        in_specs=[hbm] + [vmem] * 5,
-        out_specs=[hbm, vmem],
-        out_shape=[result, f32(parts, levels // subs, slots // hors)],
+    adjoint_result = pl.pallas_call(
+        end_kernel,
+        in_specs=[hbm] + [vmem] * 2,
+        out_specs=hbm,
+        out_shape=result,
         scratch_shapes=[buffer, pltpu.SemaphoreType.DMA((parts,))],
         input_output_aliases={0: 0},
         compiler_params=PARAMS,
         cost_estimate=BRIEF,
-        name="finish",
-    )(begun, state, b_came, owner_slot[None], total, came)
+        name="end",
+    )(begun, state, b_came)
+    boundary_gradient = pl.pallas_call(
+        pick_kernel,
+        in_specs=[pl.BlockSpec(memory_space=pl.ANY)] + [vmem] * 3,
+        out_specs=vmem,
+        out_shape=f32(parts, levels // subs, slots // hors),
+        compiler_params=PARAMS,
+        cost_estimate=BRIEF,
+        name="pick",
+    )(adjoint_result, owner_slot[None], total, came)
     return (adjoint_result, boundary_gradient)
 
 

time: 34 us -> 38.2 us (1.12)
  waiting for transfers between devices: 10.8 us -> 14.1 us
  local copies, waits for them, and re-layouts: 0.04 us -> 1.3 us
  starting transfers between devices: 13.5 us -> 13 us
    ppermute x3, waiting for transfers between devices: 0.01 us -> 3.74 us  [to_previous(): lax.ppermute(value, 'sub', [(i, (i - 1) % peers) for i in range(peers)])]
    unnamed x14 -> x16, local copies, waits for them, and re-layouts: 0.04 us -> 1.3 us
    ppermute x5, waiting for transfers between devices: 4.41 us -> 3.28 us  [exchanged(): lax.ppermute(value, axis, [(i, i ^ distance) for i in range(size)])]
    ppermute x2, waiting for transfers between devices: 6.41 us -> 7.08 us  [alternating(): return lax.ppermute(value, ('sub', 'hor'), pairs)]
    ppermute x3, starting transfers between devices: 3.41 us -> 2.92 us  [to_previous(): lax.ppermute(value, 'sub', [(i, (i - 1) % peers) for i in range(peers)])]
    pallas_call x1 -> x2, Pallas kernels: 1.39 us -> 1.47 us  [the longest x1 0.78 us: local(): pl.pallas_call(end_kernel, in_specs=[hbm] + [vmem] * 2, out_specs=hbm, ou...]
  transfers between devices with their start and end apart: 10 -> 10, of which waited for: 4 -> 5; matrix products, arithmetic and copies ran while one was open for 0% -> 0% of each run, Pallas kernels for 16% -> 16%
where the time goes in v17:
time: 38.2 us; the launch traced here: 38 us
  waiting for transfers between devices  14.1 us (37%)
  starting transfers between devices  13 us (34%)
  Pallas kernels  8.72 us (23%)
  local copies, waits for them, and re-layouts  1.3 us (3%)
  between operations  0.79 us (2%)
    ppermute x2, waiting for transfers between devices, alternating(): return lax.ppermute(value, ('sub', 'hor'), pairs)  7.08 us
    ppermute x5, starting transfers between devices, exchanged(): lax.ppermute(value, axis, [(i, i ^ distance) for i in range(size)])  7.02 us
    ppermute x3, waiting for transfers between devices, to_previous(): lax.ppermute(value, 'sub', [(i, (i - 1) % peers) for i in range(peers)])  3.74 us
    ppermute x5, waiting for transfers between devices, exchanged(): lax.ppermute(value, axis, [(i, i ^ distance) for i in range(size)])  3.28 us
    ppermute x2, starting transfers between devices, alternating(): return lax.ppermute(value, ('sub', 'hor'), pairs)  3.1 us
    pallas_call x1, Pallas kernels, local(): pl.pallas_call(sweep_kernel, in_specs=[vmem] * 3, out_specs=[vmem] * 4, o...  2.98 us
    ppermute x3, starting transfers between devices, to_previous(): lax.ppermute(value, 'sub', [(i, (i - 1) % peers) for i in range(peers)])  2.92 us
    pallas_call x1, Pallas kernels, local(): pl.pallas_call(pack_kernel, in_specs=[hbm] * 6, out_specs=vmem, out_shape...  1.93 us
  transfers between devices with their start and end apart: 10, of which 5 were waited for; matrix products, arithmetic and copies ran while one was open for 0% of the time, Pallas kernels for 16%

profile of v17, /device:TPU:0, one launch (start us, length us, event | category | flops | bytes accessed | tf_op | source)
XLA Modules:
  0.0 38.0 jit_solution(4027646704023367043)
XLA Ops:
  0.7 1.9 %pack.1.mine_ref = f32[12,16,768]{2,1,0:T(8,128)S(1)} custom-call(f32[1,2,12,16,768]{4,3,2,1,0:T(8,128)} %state_ref.5, f32[1,12,16,768]{3,2,1,0:T(8,128)} %east_ref.5, f32[1,12,16,768]{3,2,1,0:T(8,128)} %north_ref.9, s32[2,2,12]{2,1,0:T(2,128)} %cell_ref.1, s32[4,2,2,12]{3,2,1,0:T(2,128)} %offset_ref.1, f32[4,2,2,12]{3,2,1,0:T(2,128)} %weight_ref.1), custom_call_target="tpu_custom_call" | custom-call | flops 1 | bytes 1 | tf_op jit(solution)/shard_map/pack/pallas_call | solution.py:480
  2.6 0.5 %collective-permute-start.1 = (f32[12,16,768]{2,1,0:T(8,128)S(1)}, f32[12,16,768]{2,1,0:T(8,128)S(1)}, u32[]{:S(2)}, u32[]{:S(2)}) collective-permute-start(f32[12,16,768]{2,1,0:T(8,128)S(1)} %pack.1.mine_ref), channel_id=1, source_target_pairs={{0,4},{1,0},{2,1},{3,2},{4,5},{5,6},{6,7},{7,3},{8,12},{9,8},{10,9... | collective-permute-start | bytes 1769480 | tf_op jit(solution)/shard_map/ppermute | solution.py:34
  3.1 3.0 %sweep.1 = (f32[11,16,768]{2,1,0:T(8,128)S(1)}, f32[2,4,16,768]{3,2,1,0:T(8,128)S(1)}, f32[2,8,16,768]{3,2,1,0:T(8,128)S(1)}, f32[2,2,12,16,128]{4,3,2,1,0:T(8,128)S(1)}) custom-call(f32[1,2,12,16,768]{4,3,2,1,0:T(8,128)S(1)} %copy-done.1, f32[1,12,16,768]{3,2,1,0:T(8,128)S(1)} %copy-done.3, f32[1,12,16,768]{3,2,1,0:T(8,128)S(1)} %copy-done), custom_call_target="tpu_custom_call" | custom-call | flops 1 | bytes 1 | tf_op jit(solution)/shard_map/sweep/pallas_call | solution.py:499
  6.1 2.6 %collective-permute-start.3 = (f32[11,16,768]{2,1,0:T(8,128)S(1)}, f32[11,16,768]{2,1,0:T(8,128)S(1)}, u32[]{:S(2)}, u32[]{:S(2)}) collective-permute-start(f32[11,16,768]{2,1,0:T(8,128)S(1)} %get-tuple-element.11.mine_ref), channel_id=1, source_target_pairs={{0,1},{1,2},{2,3},{3,7},{4,0},{5,4},{6,5},{7,6},{8,9},{9,10},{10,1... | collective-permute-start | bytes 1622024 | tf_op jit(solution)/shard_map/ppermute | solution.py:34
  8.7 0.4 ghost_base.1
  9.1 7.1 %collective-permute-done.1.other_ref = f32[12,16,768]{2,1,0:T(8,128)S(1)} collective-permute-done((f32[12,16,768]{2,1,0:T(8,128)S(1)}, f32[12,16,768]{2,1,0:T(8,128)S(1)}, u32[]{:S(2)}, u32[]{:S(2)}) %collective-permute-start.1) | collective-permute-done | bytes 589856 | tf_op jit(solution)/shard_map/ppermute | solution.py:34
  16.2 0.8 %mend_a.1 = (f32[2,4,16,768]{3,2,1,0:T(8,128)S(1)}, f32[2,2,6,16,128]{4,3,2,1,0:T(8,128)S(1)}) custom-call(f32[1,12,16,768]{3,2,1,0:T(8,128)S(1)} %copy-done.3, f32[1,12,16,768]{3,2,1,0:T(8,128)S(1)} %copy-done, f32[11,16,768]{2,1,0:T(8,128)S(1)} %get-tuple-element.11.mine_ref, f32[12,16,768]{2,1,0:T(8,128)S(1)} %collective-permute-done.1.other_ref, ...), custom_call_target="tpu_custom_call" | custom-call | flops 1 | bytes 1 | tf_op jit(solution)/shard_map/mend_a/pallas_call | solution.py:533
  16.9 0.2 ghost.1
  17.2 0.1 collective-permute-start.4
  17.3 2.4 %collective-permute-start.5 = (f32[2,16,32]{2,1,0:T(8,128)S(1)}, f32[2,16,32]{2,1,0:T(8,128)S(1)}, u32[]{:S(2)}, u32[]{:S(2)}) collective-permute-start(f32[2,16,32]{2,1,0:T(8,128)S(1)} %ghost.1), channel_id=1, source_target_pairs={{0,8},{4,12},{8,0},{12,4},{1,9},{5,13},{9,1},{13,5},{2,10},{6,14},... | collective-permute-start | bytes 12296 | tf_op jit(solution)/shard_map/ppermute | solution.py:52
  19.7 0.1 collective-permute-start.6
  19.8 1.7 %collective-permute-start = (f32[2,4,16,768]{3,2,1,0:T(8,128)S(1)}, f32[2,4,16,768]{3,2,1,0:T(8,128)S(1)}, u32[]{:S(2)}, u32[]{:S(2)}) collective-permute-start(f32[2,4,16,768]{3,2,1,0:T(8,128)S(1)} %get-tuple-element.10), channel_id=1, source_target_pairs={{0,12},{4,0},{8,4},{12,8},{1,13},{5,1},{9,5},{13,9},{2,14},{6,2},{... | collective-permute-start | bytes 1179656 | tf_op jit(solution)/shard_map/ppermute | solution.py:22
  21.5 0.2 collective-permute-start.2
  21.6 1.2 %collective-permute-done.6 = f32[2,16,32]{2,1,0:T(8,128)S(1)} collective-permute-done((f32[2,16,32]{2,1,0:T(8,128)S(1)}, f32[2,16,32]{2,1,0:T(8,128)S(1)}, u32[]{:S(2)}, u32[]{:S(2)}) %collective-permute-start.6) | collective-permute-done | bytes 4128 | tf_op jit(solution)/shard_map/ppermute | solution.py:52
  23.0 1.1 %collective-permute-start.7 = (f32[2,4,16,768]{3,2,1,0:T(8,128)S(1)}, f32[2,4,16,768]{3,2,1,0:T(8,128)S(1)}, u32[]{:S(2)}, u32[]{:S(2)}) collective-permute-start(f32[2,4,16,768]{3,2,1,0:T(8,128)S(1)} %mend_b.1), channel_id=1, source_target_pairs={{0,12},{4,0},{8,4},{12,8},{1,13},{5,1},{9,5},{13,9},{2,14},{6,2},{... | collective-permute-start | bytes 1179656 | tf_op jit(solution)/shard_map/ppermute | solution.py:22
  24.0 1.7 %collective-permute-start.8 = (f32[2,16,32]{2,1,0:T(8,128)S(1)}, f32[2,16,32]{2,1,0:T(8,128)S(1)}, u32[]{:S(2)}, u32[]{:S(2)}) collective-permute-start(f32[2,16,32]{2,1,0:T(8,128)S(1)} %add_add_fusion._), channel_id=1, source_target_pairs={{0,1},{1,0},{2,3},{3,2},{4,5},{5,4},{6,7},{7,6},{8,9},{9,8},{10,11... | collective-permute-start | bytes 12296 | tf_op jit(solution)/shard_map/ppermute | solution.py:52
  25.7 2.0 %collective-permute-done.8 = f32[2,16,32]{2,1,0:T(8,128)S(1)} collective-permute-done((f32[2,16,32]{2,1,0:T(8,128)S(1)}, f32[2,16,32]{2,1,0:T(8,128)S(1)}, u32[]{:S(2)}, u32[]{:S(2)}) %collective-permute-start.8) | collective-permute-done | bytes 4128 | tf_op jit(solution)/shard_map/ppermute | solution.py:52
  27.8 2.7 %collective-permute-start.9 = (f32[2,16,32]{2,1,0:T(8,128)S(1)}, f32[2,16,32]{2,1,0:T(8,128)S(1)}, u32[]{:S(2)}, u32[]{:S(2)}) collective-permute-start(f32[2,16,32]{2,1,0:T(8,128)S(1)} %add.15.total_ref), channel_id=1, source_target_pairs={{0,2},{1,3},{2,0},{3,1},{4,6},{5,7},{6,4},{7,5},{8,10},{9,11},{10,... | collective-permute-start | bytes 12296 | tf_op jit(solution)/shard_map/ppermute | solution.py:52
  30.5 0.5 %collective-permute-done.2.a_ref = f32[2,4,16,768]{3,2,1,0:T(8,128)S(1)} collective-permute-done((f32[2,4,16,768]{3,2,1,0:T(8,128)S(1)}, f32[2,4,16,768]{3,2,1,0:T(8,128)S(1)}, u32[]{:S(2)}, u32[]{:S(2)}) %collective-permute-start.2) | collective-permute-done | bytes 393248 | tf_op jit(solution)/shard_map/ppermute | solution.py:22
  31.0 0.9 %begin.1.begun_hbm = f32[1,2,12,16,768]{4,3,2,1,0:T(8,128)} custom-call(f32[1,2,12,16,768]{4,3,2,1,0:T(8,128)S(1)} %copy-done.1, f32[2,4,16,768]{3,2,1,0:T(8,128)S(1)} %collective-permute-done.middle_ref, f32[2,4,16,768]{3,2,1,0:T(8,128)S(1)} %collective-permute-done.2.a_ref), custom_call_target="tpu_custom_call" | custom-call | flops 1 | bytes 1 | tf_op jit(solution)/shard_map/begin/pallas_call | solution.py:572
  31.9 3.3 %collective-permute-done.7.b_ref = f32[2,4,16,768]{3,2,1,0:T(8,128)S(1)} collective-permute-done((f32[2,4,16,768]{3,2,1,0:T(8,128)S(1)}, f32[2,4,16,768]{3,2,1,0:T(8,128)S(1)}, u32[]{:S(2)}, u32[]{:S(2)}) %collective-permute-start.7) | collective-permute-done | bytes 393248 | tf_op jit(solution)/shard_map/ppermute | solution.py:22
  35.2 0.8 %end.1._ = f32[1,2,12,16,768]{4,3,2,1,0:T(8,128)} custom-call(f32[1,2,12,16,768]{4,3,2,1,0:T(8,128)} %begin.1.begun_hbm, f32[1,2,12,16,768]{4,3,2,1,0:T(8,128)S(1)} %copy-done.1, f32[2,4,16,768]{3,2,1,0:T(8,128)S(1)} %collective-permute-done.7.b_ref), custom_call_target="tpu_custom_call", output_to_operand_aliasing={{}: (0, {})} | custom-call | flops 1 | bytes 1 | tf_op jit(solution)/shard_map/end/pallas_call | solution.py:582
  36.0 1.3 %copy-done.2 = f32[1,2,12,16,768]{4,3,2,1,0:T(8,128)S(1)} copy-done((f32[1,2,12,16,768]{4,3,2,1,0:T(8,128)S(1)}, f32[1,2,12,16,768]{4,3,2,1,0:T(8,128)}, u32[]{:S(2)}) %copy-start.2) | copy-done | bytes 1179672
  37.3 0.7 %pick.1 = f32[2,4,8]{2,1,0:T(4,128)} custom-call(f32[1,2,12,16,768]{4,3,2,1,0:T(8,128)S(1)} %copy-done.2, s32[1,32]{1,0:T(1,128)S(1)} %bitcast.1, f32[2,16,32]{2,1,0:T(8,128)S(1)} %add.15.total_ref, f32[2,16,32]{2,1,0:T(8,128)S(1)} %collective-permute-done.9.came_ref), custom_call_target="tpu_custom_call" | custom-call | flops 1 | bytes 1 | tf_op jit(solution)/shard_map/pick/pallas_call | solution.py:593
  (23 shorter events, 0.1 us)
Async XLA Ops:
  0.6 2.5 %copy-start.1 = (f32[1,2,12,16,768]{4,3,2,1,0:T(8,128)S(1)}, f32[1,2,12,16,768]{4,3,2,1,0:T(8,128)}, u32[]{:S(2)}) copy-start(f32[1,2,12,16,768]{4,3,2,1,0:T(8,128)} %state_ref.5) | copy-start | bytes 3538948
  0.6 2.5 %copy-start.3 = (f32[1,12,16,768]{3,2,1,0:T(8,128)S(1)}, f32[1,12,16,768]{3,2,1,0:T(8,128)}, u32[]{:S(2)}) copy-start(f32[1,12,16,768]{3,2,1,0:T(8,128)} %east_ref.5) | copy-start | bytes 1769476
  0.6 2.5 %copy-start = (f32[1,12,16,768]{3,2,1,0:T(8,128)S(1)}, f32[1,12,16,768]{3,2,1,0:T(8,128)}, u32[]{:S(2)}) copy-start(f32[1,12,16,768]{3,2,1,0:T(8,128)} %north_ref.9) | copy-start | bytes 1769476
  2.6 6.1 %copy-start.4 = (s32[4,2,2,12]{3,2,1,0:T(2,128)S(1)}, s32[4,2,2,12]{3,2,1,0:T(2,128)}, u32[]{:S(2)}) copy-start(s32[4,2,2,12]{3,2,1,0:T(2,128)} %offset_ref.1) | copy-start | bytes 2308
  2.6 6.1 %copy-start.5 = (f32[4,2,2,12]{3,2,1,0:T(2,128)S(1)}, f32[4,2,2,12]{3,2,1,0:T(2,128)}, u32[]{:S(2)}) copy-start(f32[4,2,2,12]{3,2,1,0:T(2,128)} %weight_ref.1) | copy-start | bytes 2308
  2.6 6.1 %copy-start.6 = (s32[2,2,12]{2,1,0:T(2,128)S(1)}, s32[2,2,12]{2,1,0:T(2,128)}, u32[]{:S(2)}) copy-start(s32[2,2,12]{2,1,0:T(2,128)} %cell_ref.1) | copy-start | bytes 580
  2.6 13.5 %collective-permute-start.1 = (f32[12,16,768]{2,1,0:T(8,128)S(1)}, f32[12,16,768]{2,1,0:T(8,128)S(1)}, u32[]{:S(2)}, u32[]{:S(2)}) collective-permute-start(f32[12,16,768]{2,1,0:T(8,128)S(1)} %pack.1.mine_ref), channel_id=1, source_target_pairs={{0,4},{1,0},{2,1},{3,2},{4,5},{5,6},{6,7},{7,3},{8,12},{9,8},{10,9... | collective-permute-start | bytes 1769480 | tf_op jit(solution)/shard_map/ppermute | solution.py:34
  6.1 16.8 %collective-permute-start.3 = (f32[11,16,768]{2,1,0:T(8,128)S(1)}, f32[11,16,768]{2,1,0:T(8,128)S(1)}, u32[]{:S(2)}, u32[]{:S(2)}) collective-permute-start(f32[11,16,768]{2,1,0:T(8,128)S(1)} %get-tuple-element.11.mine_ref), channel_id=1, source_target_pairs={{0,1},{1,2},{2,3},{3,7},{4,0},{5,4},{6,5},{7,6},{8,9},{9,10},{10,1... | collective-permute-start | bytes 1622024 | tf_op jit(solution)/shard_map/ppermute | solution.py:34
  17.2 4.3 %collective-permute-start.4 = (f32[2,16,32]{2,1,0:T(8,128)S(1)}, f32[2,16,32]{2,1,0:T(8,128)S(1)}, u32[]{:S(2)}, u32[]{:S(2)}) collective-permute-start(f32[2,16,32]{2,1,0:T(8,128)S(1)} %ghost.1), channel_id=1, source_target_pairs={{0,4},{4,0},{8,12},{12,8},{1,5},{5,1},{9,13},{13,9},{2,6},{6,2},{1... | collective-permute-start | bytes 12296 | tf_op jit(solution)/shard_map/ppermute | solution.py:52
  17.3 4.4 %collective-permute-start.5 = (f32[2,16,32]{2,1,0:T(8,128)S(1)}, f32[2,16,32]{2,1,0:T(8,128)S(1)}, u32[]{:S(2)}, u32[]{:S(2)}) collective-permute-start(f32[2,16,32]{2,1,0:T(8,128)S(1)} %ghost.1), channel_id=1, source_target_pairs={{0,8},{4,12},{8,0},{12,4},{1,9},{5,13},{9,1},{13,5},{2,10},{6,14},... | collective-permute-start | bytes 12296 | tf_op jit(solution)/shard_map/ppermute | solution.py:52
  19.7 3.2 %collective-permute-start.6 = (f32[2,16,32]{2,1,0:T(8,128)S(1)}, f32[2,16,32]{2,1,0:T(8,128)S(1)}, u32[]{:S(2)}, u32[]{:S(2)}) collective-permute-start(f32[2,16,32]{2,1,0:T(8,128)S(1)} %ghost.1), channel_id=1, source_target_pairs={{0,12},{4,8},{8,4},{12,0},{1,13},{5,9},{9,5},{13,1},{2,14},{6,10},... | collective-permute-start | bytes 12296 | tf_op jit(solution)/shard_map/ppermute | solution.py:52
  19.8 10.7 %collective-permute-start = (f32[2,4,16,768]{3,2,1,0:T(8,128)S(1)}, f32[2,4,16,768]{3,2,1,0:T(8,128)S(1)}, u32[]{:S(2)}, u32[]{:S(2)}) collective-permute-start(f32[2,4,16,768]{3,2,1,0:T(8,128)S(1)} %get-tuple-element.10), channel_id=1, source_target_pairs={{0,12},{4,0},{8,4},{12,8},{1,13},{5,1},{9,5},{13,9},{2,14},{6,2},{... | collective-permute-start | bytes 1179656 | tf_op jit(solution)/shard_map/ppermute | solution.py:22
  21.5 9.5 %collective-permute-start.2 = (f32[2,4,16,768]{3,2,1,0:T(8,128)S(1)}, f32[2,4,16,768]{3,2,1,0:T(8,128)S(1)}, u32[]{:S(2)}, u32[]{:S(2)}) collective-permute-start(f32[2,4,16,768]{3,2,1,0:T(8,128)S(1)} %get-tuple-element.15), channel_id=1, source_target_pairs={{0,12},{4,0},{8,4},{12,8},{1,13},{5,1},{9,5},{13,9},{2,14},{6,2},{... | collective-permute-start | bytes 1179656 | tf_op jit(solution)/shard_map/ppermute | solution.py:22
  23.0 12.2 %collective-permute-start.7 = (f32[2,4,16,768]{3,2,1,0:T(8,128)S(1)}, f32[2,4,16,768]{3,2,1,0:T(8,128)S(1)}, u32[]{:S(2)}, u32[]{:S(2)}) collective-permute-start(f32[2,4,16,768]{3,2,1,0:T(8,128)S(1)} %mend_b.1), channel_id=1, source_target_pairs={{0,12},{4,0},{8,4},{12,8},{1,13},{5,1},{9,5},{13,9},{2,14},{6,2},{... | collective-permute-start | bytes 1179656 | tf_op jit(solution)/shard_map/ppermute | solution.py:22
  24.0 3.7 %collective-permute-start.8 = (f32[2,16,32]{2,1,0:T(8,128)S(1)}, f32[2,16,32]{2,1,0:T(8,128)S(1)}, u32[]{:S(2)}, u32[]{:S(2)}) collective-permute-start(f32[2,16,32]{2,1,0:T(8,128)S(1)} %add_add_fusion._), channel_id=1, source_target_pairs={{0,1},{1,0},{2,3},{3,2},{4,5},{5,4},{6,7},{7,6},{8,9},{9,8},{10,11... | collective-permute-start | bytes 12296 | tf_op jit(solution)/shard_map/ppermute | solution.py:52
  27.8 8.2 %collective-permute-start.9 = (f32[2,16,32]{2,1,0:T(8,128)S(1)}, f32[2,16,32]{2,1,0:T(8,128)S(1)}, u32[]{:S(2)}, u32[]{:S(2)}) collective-permute-start(f32[2,16,32]{2,1,0:T(8,128)S(1)} %add.15.total_ref), channel_id=1, source_target_pairs={{0,2},{1,3},{2,0},{3,1},{4,6},{5,7},{6,4},{7,5},{8,10},{9,11},{10,... | collective-permute-start | bytes 12296 | tf_op jit(solution)/shard_map/ppermute | solution.py:52
  31.9 4.1 %copy-start.7 = (s32[32]{0:T(128)S(1)}, s32[32]{0:T(128)}, u32[]{:S(2)}) copy-start(s32[32]{0:T(128)} %param.13) | copy-start | bytes 388
  36.0 1.3 %copy-start.2 = (f32[1,2,12,16,768]{4,3,2,1,0:T(8,128)S(1)}, f32[1,2,12,16,768]{4,3,2,1,0:T(8,128)}, u32[]{:S(2)}) copy-start(f32[1,2,12,16,768]{4,3,2,1,0:T(8,128)} %end.1._) | copy-start | bytes 3538948

commit v18 on v17

--- a/solution.py
+++ b/solution.py
@@ -42,7 +42,7 @@
 def rounds():
     subs, hors = lax.axis_size("sub"), lax.axis_size("hor")
     assert not subs & (subs - 1) and not hors & (hors - 1)
-    order = [("sub", range(1, min(subs, 4)))]
+    order = [("sub", range(min(subs, 4) - 1, 0, -1))]
     order += [("sub", [1 << n]) for n in range(2, subs.bit_length() - 1)]
     return order + [("hor", [1 << n]) for n in range(hors.bit_length() - 1)]
 
@@ -249,8 +249,11 @@
 
 
 def ghost_base_kernel(
-    cell_ref, offset_ref, weight_ref, column_ref, north_ref, mixing_ref, partial_ref
+    cell_ref, offset_ref, weight_ref, owner_ref, column_ref, north_ref, pack_ref,
+    mixing_ref, partial_ref, owner_out, pack_out,
 ):
+    owner_out[...] = owner_ref[...]
+    pack_out[...] = pack_ref[...]
     parts, _, rows, levels, _ = column_ref.shape
     slots = mixing_ref.shape[-1]
     width = north_ref.shape[-1]
@@ -387,7 +390,7 @@
         copy_end(flip, ends_ref, out_ref)
 
 
-def mend_b_kernel(east_ref, north_ref, mine_ref, other_ref, ends_ref, _, out_ref):
+def mend_b_kernel(east_ref, north_ref, mine_ref, other_ref, ends_ref, _, __, out_ref):
     flip = parity()
     turn = lambda r: r + flip * (STEPS - 1 - 2 * r)
 
@@ -516,18 +519,21 @@
         cost_estimate=BRIEF,
         name="sweep",
     )(state, east, north)
-    second_came = alternating(second_pack, 1)
     middle_came = to_previous(middle)
 
-    mixing, base = pl.pallas_call(
+    mixing, base, owner, second_sent = pl.pallas_call(
         ghost_base_kernel,
-        in_specs=[vmem] * 5,
-        out_specs=[vmem] * 2,
-        out_shape=[f32(parts, 2, rows, slots), f32(parts, levels, slots)],
+        in_specs=[vmem] * 7,
+        out_specs=[vmem] * 4,
+        out_shape=[
+            f32(parts, 2, rows, slots), f32(parts, levels, slots),
+            jax.ShapeDtypeStruct((1, slots), owner_slot.dtype), f32(PACK_ROWS, levels, width),
+        ],
         compiler_params=PARAMS,
         cost_estimate=BRIEF,
         name="ghost_base",
-    )(*small, columns, north)
+    )(*small, owner_slot[None], columns, north, second_pack)
+    second_came = alternating(second_sent, 1)
 
     column_shape = (parts, 2, 2 * (STEPS - 1), levels, LANES)
     side_a, a_columns = pl.pallas_call(
@@ -554,13 +560,13 @@
     total = total + exchanged(total, *order[0])
     side_b = pl.pallas_call(
         mend_b_kernel,
-        in_specs=[vmem] * 5 + [pl.BlockSpec(memory_space=pl.ANY)],
+        in_specs=[vmem] * 5 + [pl.BlockSpec(memory_space=pl.ANY)] * 2,
         out_specs=vmem,
         out_shape=f32(parts, STEPS, levels, width),
         compiler_params=PARAMS,
         cost_estimate=BRIEF,
         name="mend_b",
-    )(east, north, first_pack, second_came, ends, total)
+    )(east, north, first_pack, second_came, ends, middle_came, total)
     b_came = to_previous(side_b)
 
     for each in order[1:-1]:
@@ -598,7 +604,7 @@
         compiler_params=PARAMS,
         cost_estimate=BRIEF,
         name="pick",
-    )(adjoint_result, owner_slot[None], total, came)
+    )(adjoint_result, owner, total, came)
     return (adjoint_result, boundary_gradient)
 
 

time: 38.2 us -> 34.1 us (0.89)
  waiting for transfers between devices: 14.1 us -> 9.56 us
  starting transfers between devices: 13 us -> 13.5 us
    ppermute x3, waiting for transfers between devices: 3.74 us -> 0.01 us  [to_previous(): lax.ppermute(value, 'sub', [(i, (i - 1) % peers) for i in range(peers)])]
    ppermute x2, waiting for transfers between devices: 7.08 us -> 5.96 us  [alternating(): return lax.ppermute(value, ('sub', 'hor'), pairs)]
    ppermute x3, starting transfers between devices: 2.92 us -> 3.41 us  [to_previous(): lax.ppermute(value, 'sub', [(i, (i - 1) % peers) for i in range(peers)])]
  transfers between devices with their start and end apart: 10 -> 10, of which waited for: 5 -> 4; matrix products, arithmetic and copies ran while one was open for 0% -> 0% of each run, Pallas kernels for 16% -> 18%
where the time goes in v18:
time: 34.1 us; the launch traced here: 34 us
  starting transfers between devices  13.5 us (40%)
  waiting for transfers between devices  9.56 us (28%)
  Pallas kernels  8.75 us (26%)
  local copies, waits for them, and re-layouts  1.31 us (4%)
  between operations  0.81 us (2%)
    ppermute x5, starting transfers between devices, exchanged(): lax.ppermute(value, axis, [(i, i ^ distance) for i in range(size)])  7.02 us
    ppermute x2, waiting for transfers between devices, alternating(): return lax.ppermute(value, ('sub', 'hor'), pairs)  5.96 us
    ppermute x5, waiting for transfers between devices, exchanged(): lax.ppermute(value, axis, [(i, i ^ distance) for i in range(size)])  3.59 us
    ppermute x3, starting transfers between devices, to_previous(): lax.ppermute(value, 'sub', [(i, (i - 1) % peers) for i in range(peers)])  3.41 us
    ppermute x2, starting transfers between devices, alternating(): return lax.ppermute(value, ('sub', 'hor'), pairs)  3.1 us
    pallas_call x1, Pallas kernels, local(): pl.pallas_call(sweep_kernel, in_specs=[vmem] * 3, out_specs=[vmem] * 4, o...  2.98 us
    pallas_call x1, Pallas kernels, local(): pl.pallas_call(pack_kernel, in_specs=[hbm] * 6, out_specs=vmem, out_shape...  1.93 us
    unnamed x16, local copies, waits for them, and re-layouts  1.31 us
  transfers between devices with their start and end apart: 10, of which 4 were waited for; matrix products, arithmetic and copies ran while one was open for 0% of the time, Pallas kernels for 18%

profile of v18, /device:TPU:0, one launch (start us, length us, event | category | flops | bytes accessed | tf_op | source)
XLA Modules:
  0.0 34.0 jit_solution(18146491921823474566)
XLA Ops:
  0.7 1.9 %pack.1.mine_ref = f32[12,16,768]{2,1,0:T(8,128)S(1)} custom-call(f32[1,2,12,16,768]{4,3,2,1,0:T(8,128)} %state_ref.5, f32[1,12,16,768]{3,2,1,0:T(8,128)} %east_ref.5, f32[1,12,16,768]{3,2,1,0:T(8,128)} %north_ref.9, s32[2,2,12]{2,1,0:T(2,128)} %cell_ref.1, s32[4,2,2,12]{3,2,1,0:T(2,128)} %offset_ref.1, f32[4,2,2,12]{3,2,1,0:T(2,128)} %weight_ref.1), custom_call_target="tpu_custom_call" | custom-call | flops 1 | bytes 1 | tf_op jit(solution)/shard_map/pack/pallas_call | solution.py:483
  2.6 0.5 %collective-permute-start.1 = (f32[12,16,768]{2,1,0:T(8,128)S(1)}, f32[12,16,768]{2,1,0:T(8,128)S(1)}, u32[]{:S(2)}, u32[]{:S(2)}) collective-permute-start(f32[12,16,768]{2,1,0:T(8,128)S(1)} %pack.1.mine_ref), channel_id=1, source_target_pairs={{0,4},{1,0},{2,1},{3,2},{4,5},{5,6},{6,7},{7,3},{8,12},{9,8},{10,9... | collective-permute-start | bytes 1769480 | tf_op jit(solution)/shard_map/ppermute | solution.py:34
  3.1 3.0 %sweep.1 = (f32[11,16,768]{2,1,0:T(8,128)S(1)}, f32[2,4,16,768]{3,2,1,0:T(8,128)S(1)}, f32[2,8,16,768]{3,2,1,0:T(8,128)S(1)}, f32[2,2,12,16,128]{4,3,2,1,0:T(8,128)S(1)}) custom-call(f32[1,2,12,16,768]{4,3,2,1,0:T(8,128)S(1)} %copy-done.1, f32[1,12,16,768]{3,2,1,0:T(8,128)S(1)} %copy-done.3, f32[1,12,16,768]{3,2,1,0:T(8,128)S(1)} %copy-done), custom_call_target="tpu_custom_call" | custom-call | flops 1 | bytes 1 | tf_op jit(solution)/shard_map/sweep/pallas_call | solution.py:502
  6.2 0.4 %ghost_base.1 = (f32[2,2,12,32]{3,2,1,0:T(8,128)S(1)}, f32[2,16,32]{2,1,0:T(8,128)S(1)}, s32[1,32]{1,0:T(1,128)S(1)}, f32[11,16,768]{2,1,0:T(8,128)S(1)}) custom-call(s32[2,2,12]{2,1,0:T(2,128)S(1)} %copy-done.6, s32[4,2,2,12]{3,2,1,0:T(2,128)S(1)} %copy-done.4, f32[4,2,2,12]{3,2,1,0:T(2,128)S(1)} %copy-done.5, s32[1,32]{1,0:T(1,128)S(1)} %bitcast.1, ...), custom_call_target="tpu_custom_call" | custom-call | flops 1 | bytes 1 | tf_op jit(solution)/shard_map/ghost_base/pallas_call | solution.py:524
  6.5 2.6 %collective-permute-start.3 = (f32[11,16,768]{2,1,0:T(8,128)S(1)}, f32[11,16,768]{2,1,0:T(8,128)S(1)}, u32[]{:S(2)}, u32[]{:S(2)}) collective-permute-start(f32[11,16,768]{2,1,0:T(8,128)S(1)} %get-tuple-element.18), channel_id=1, source_target_pairs={{0,1},{1,2},{2,3},{3,7},{4,0},{5,4},{6,5},{7,6},{8,9},{9,10},{10,1... | collective-permute-start | bytes 1622024 | tf_op jit(solution)/shard_map/ppermute | solution.py:34
  9.2 0.7 %collective-permute-start = (f32[2,4,16,768]{3,2,1,0:T(8,128)S(1)}, f32[2,4,16,768]{3,2,1,0:T(8,128)S(1)}, u32[]{:S(2)}, u32[]{:S(2)}) collective-permute-start(f32[2,4,16,768]{3,2,1,0:T(8,128)S(1)} %get-tuple-element.12), channel_id=1, source_target_pairs={{0,12},{4,0},{8,4},{12,8},{1,13},{5,1},{9,5},{13,9},{2,14},{6,2},{... | collective-permute-start | bytes 1179656 | tf_op jit(solution)/shard_map/ppermute | solution.py:22
  9.8 6.0 %collective-permute-done.1.other_ref = f32[12,16,768]{2,1,0:T(8,128)S(1)} collective-permute-done((f32[12,16,768]{2,1,0:T(8,128)S(1)}, f32[12,16,768]{2,1,0:T(8,128)S(1)}, u32[]{:S(2)}, u32[]{:S(2)}) %collective-permute-start.1) | collective-permute-done | bytes 589856 | tf_op jit(solution)/shard_map/ppermute | solution.py:34
  15.8 0.8 %mend_a.1 = (f32[2,4,16,768]{3,2,1,0:T(8,128)S(1)}, f32[2,2,6,16,128]{4,3,2,1,0:T(8,128)S(1)}) custom-call(f32[1,12,16,768]{3,2,1,0:T(8,128)S(1)} %copy-done.3, f32[1,12,16,768]{3,2,1,0:T(8,128)S(1)} %copy-done, f32[11,16,768]{2,1,0:T(8,128)S(1)} %get-tuple-element.13.pack_ref.mine_ref, f32[12,16,768]{2,1,0:T(8,128)S(1)} %collective-permute-done.1.other_ref, ...), custom_call_target="tpu_custom_call" | custom-call | flops 1 | bytes 1 | tf_op jit(solution)/shard_map/mend_a/pallas_call | solution.py:539
  16.5 0.2 ghost.1
  16.8 0.1 collective-permute-start.6
  16.9 2.4 %collective-permute-start.5 = (f32[2,16,32]{2,1,0:T(8,128)S(1)}, f32[2,16,32]{2,1,0:T(8,128)S(1)}, u32[]{:S(2)}, u32[]{:S(2)}) collective-permute-start(f32[2,16,32]{2,1,0:T(8,128)S(1)} %ghost.1), channel_id=1, source_target_pairs={{0,8},{4,12},{8,0},{12,4},{1,9},{5,13},{9,1},{13,5},{2,10},{6,14},... | collective-permute-start | bytes 12296 | tf_op jit(solution)/shard_map/ppermute | solution.py:52
  19.3 0.1 collective-permute-start.4
  19.4 1.7 %collective-permute-start.2 = (f32[2,4,16,768]{3,2,1,0:T(8,128)S(1)}, f32[2,4,16,768]{3,2,1,0:T(8,128)S(1)}, u32[]{:S(2)}, u32[]{:S(2)}) collective-permute-start(f32[2,4,16,768]{3,2,1,0:T(8,128)S(1)} %get-tuple-element.17), channel_id=1, source_target_pairs={{0,12},{4,0},{8,4},{12,8},{1,13},{5,1},{9,5},{13,9},{2,14},{6,2},{... | collective-permute-start | bytes 1179656 | tf_op jit(solution)/shard_map/ppermute | solution.py:22
  21.1 1.4 %collective-permute-done.4 = f32[2,16,32]{2,1,0:T(8,128)S(1)} collective-permute-done((f32[2,16,32]{2,1,0:T(8,128)S(1)}, f32[2,16,32]{2,1,0:T(8,128)S(1)}, u32[]{:S(2)}, u32[]{:S(2)}) %collective-permute-start.4) | collective-permute-done | bytes 4128 | tf_op jit(solution)/shard_map/ppermute | solution.py:52
  22.5 0.1 mend_b.1
  22.6 1.1 %collective-permute-start.7 = (f32[2,4,16,768]{3,2,1,0:T(8,128)S(1)}, f32[2,4,16,768]{3,2,1,0:T(8,128)S(1)}, u32[]{:S(2)}, u32[]{:S(2)}) collective-permute-start(f32[2,4,16,768]{3,2,1,0:T(8,128)S(1)} %mend_b.1), channel_id=1, source_target_pairs={{0,12},{4,0},{8,4},{12,8},{1,13},{5,1},{9,5},{13,9},{2,14},{6,2},{... | collective-permute-start | bytes 1179656 | tf_op jit(solution)/shard_map/ppermute | solution.py:22
  23.6 1.7 %collective-permute-start.8 = (f32[2,16,32]{2,1,0:T(8,128)S(1)}, f32[2,16,32]{2,1,0:T(8,128)S(1)}, u32[]{:S(2)}, u32[]{:S(2)}) collective-permute-start(f32[2,16,32]{2,1,0:T(8,128)S(1)} %add_add_fusion.__), channel_id=1, source_target_pairs={{0,1},{1,0},{2,3},{3,2},{4,5},{5,4},{6,7},{7,6},{8,9},{9,8},{10,11... | collective-permute-start | bytes 12296 | tf_op jit(solution)/shard_map/ppermute | solution.py:52
  25.3 2.0 %collective-permute-done.8 = f32[2,16,32]{2,1,0:T(8,128)S(1)} collective-permute-done((f32[2,16,32]{2,1,0:T(8,128)S(1)}, f32[2,16,32]{2,1,0:T(8,128)S(1)}, u32[]{:S(2)}, u32[]{:S(2)}) %collective-permute-start.8) | collective-permute-done | bytes 4128 | tf_op jit(solution)/shard_map/ppermute | solution.py:52
  27.4 2.7 %collective-permute-start.9 = (f32[2,16,32]{2,1,0:T(8,128)S(1)}, f32[2,16,32]{2,1,0:T(8,128)S(1)}, u32[]{:S(2)}, u32[]{:S(2)}) collective-permute-start(f32[2,16,32]{2,1,0:T(8,128)S(1)} %add.15.total_ref), channel_id=1, source_target_pairs={{0,2},{1,3},{2,0},{3,1},{4,6},{5,7},{6,4},{7,5},{8,10},{9,11},{10,... | collective-permute-start | bytes 12296 | tf_op jit(solution)/shard_map/ppermute | solution.py:52
  30.1 0.9 %begin.1.begun_hbm = f32[1,2,12,16,768]{4,3,2,1,0:T(8,128)} custom-call(f32[1,2,12,16,768]{4,3,2,1,0:T(8,128)S(1)} %copy-done.1, f32[2,4,16,768]{3,2,1,0:T(8,128)S(1)} %collective-permute-done.middle_ref._, f32[2,4,16,768]{3,2,1,0:T(8,128)S(1)} %collective-permute-done.2.a_ref), custom_call_target="tpu_custom_call" | custom-call | flops 1 | bytes 1 | tf_op jit(solution)/shard_map/begin/pallas_call | solution.py:578
  31.1 0.8 %end.1._ = f32[1,2,12,16,768]{4,3,2,1,0:T(8,128)} custom-call(f32[1,2,12,16,768]{4,3,2,1,0:T(8,128)} %begin.1.begun_hbm, f32[1,2,12,16,768]{4,3,2,1,0:T(8,128)S(1)} %copy-done.1, f32[2,4,16,768]{3,2,1,0:T(8,128)S(1)} %collective-permute-done.7.b_ref), custom_call_target="tpu_custom_call", output_to_operand_aliasing={{}: (0, {})} | custom-call | flops 1 | bytes 1 | tf_op jit(solution)/shard_map/end/pallas_call | solution.py:588
  31.9 0.2 collective-permute-done.9.came_ref
  32.0 1.3 %copy-done.2 = f32[1,2,12,16,768]{4,3,2,1,0:T(8,128)S(1)} copy-done((f32[1,2,12,16,768]{4,3,2,1,0:T(8,128)S(1)}, f32[1,2,12,16,768]{4,3,2,1,0:T(8,128)}, u32[]{:S(2)}) %copy-start.2) | copy-done | bytes 1179672
  33.3 0.7 %pick.1 = f32[2,4,8]{2,1,0:T(4,128)} custom-call(f32[1,2,12,16,768]{4,3,2,1,0:T(8,128)S(1)} %copy-done.2, s32[1,32]{1,0:T(1,128)S(1)} %get-tuple-element.21.owner_ref, f32[2,16,32]{2,1,0:T(8,128)S(1)} %add.15.total_ref, f32[2,16,32]{2,1,0:T(8,128)S(1)} %collective-permute-done.9.came_ref), custom_call_target="tpu_custom_call" | custom-call | flops 1 | bytes 1 | tf_op jit(solution)/shard_map/pick/pallas_call | solution.py:599
  (23 shorter events, 0.1 us)
Async XLA Ops:
  0.6 2.5 %copy-start = (f32[1,12,16,768]{3,2,1,0:T(8,128)S(1)}, f32[1,12,16,768]{3,2,1,0:T(8,128)}, u32[]{:S(2)}) copy-start(f32[1,12,16,768]{3,2,1,0:T(8,128)} %north_ref.9) | copy-start | bytes 1769476
  0.6 2.5 %copy-start.3 = (f32[1,12,16,768]{3,2,1,0:T(8,128)S(1)}, f32[1,12,16,768]{3,2,1,0:T(8,128)}, u32[]{:S(2)}) copy-start(f32[1,12,16,768]{3,2,1,0:T(8,128)} %east_ref.5) | copy-start | bytes 1769476
  0.6 2.5 %copy-start.1 = (f32[1,2,12,16,768]{4,3,2,1,0:T(8,128)S(1)}, f32[1,2,12,16,768]{4,3,2,1,0:T(8,128)}, u32[]{:S(2)}) copy-start(f32[1,2,12,16,768]{4,3,2,1,0:T(8,128)} %state_ref.5) | copy-start | bytes 3538948
  2.6 3.5 %copy-start.4 = (s32[4,2,2,12]{3,2,1,0:T(2,128)S(1)}, s32[4,2,2,12]{3,2,1,0:T(2,128)}, u32[]{:S(2)}) copy-start(s32[4,2,2,12]{3,2,1,0:T(2,128)} %offset_ref.1) | copy-start | bytes 2308
  2.6 3.5 %copy-start.5 = (f32[4,2,2,12]{3,2,1,0:T(2,128)S(1)}, f32[4,2,2,12]{3,2,1,0:T(2,128)}, u32[]{:S(2)}) copy-start(f32[4,2,2,12]{3,2,1,0:T(2,128)} %weight_ref.1) | copy-start | bytes 2308
  2.6 3.5 %copy-start.6 = (s32[2,2,12]{2,1,0:T(2,128)S(1)}, s32[2,2,12]{2,1,0:T(2,128)}, u32[]{:S(2)}) copy-start(s32[2,2,12]{2,1,0:T(2,128)} %cell_ref.1) | copy-start | bytes 580
  2.6 3.5 %copy-start.7 = (s32[32]{0:T(128)S(1)}, s32[32]{0:T(128)}, u32[]{:S(2)}) copy-start(s32[32]{0:T(128)} %param.13) | copy-start | bytes 388
  2.6 13.1 %collective-permute-start.1 = (f32[12,16,768]{2,1,0:T(8,128)S(1)}, f32[12,16,768]{2,1,0:T(8,128)S(1)}, u32[]{:S(2)}, u32[]{:S(2)}) collective-permute-start(f32[12,16,768]{2,1,0:T(8,128)S(1)} %pack.1.mine_ref), channel_id=1, source_target_pairs={{0,4},{1,0},{2,1},{3,2},{4,5},{5,6},{6,7},{7,3},{8,12},{9,8},{10,9... | collective-permute-start | bytes 1769480 | tf_op jit(solution)/shard_map/ppermute | solution.py:34
  6.5 16.0 %collective-permute-start.3 = (f32[11,16,768]{2,1,0:T(8,128)S(1)}, f32[11,16,768]{2,1,0:T(8,128)S(1)}, u32[]{:S(2)}, u32[]{:S(2)}) collective-permute-start(f32[11,16,768]{2,1,0:T(8,128)S(1)} %get-tuple-element.18), channel_id=1, source_target_pairs={{0,1},{1,2},{2,3},{3,7},{4,0},{5,4},{6,5},{7,6},{8,9},{9,10},{10,1... | collective-permute-start | bytes 1622024 | tf_op jit(solution)/shard_map/ppermute | solution.py:34
  9.2 13.3 %collective-permute-start = (f32[2,4,16,768]{3,2,1,0:T(8,128)S(1)}, f32[2,4,16,768]{3,2,1,0:T(8,128)S(1)}, u32[]{:S(2)}, u32[]{:S(2)}) collective-permute-start(f32[2,4,16,768]{3,2,1,0:T(8,128)S(1)} %get-tuple-element.12), channel_id=1, source_target_pairs={{0,12},{4,0},{8,4},{12,8},{1,13},{5,1},{9,5},{13,9},{2,14},{6,2},{... | collective-permute-start | bytes 1179656 | tf_op jit(solution)/shard_map/ppermute | solution.py:22
  16.8 2.6 %collective-permute-start.6 = (f32[2,16,32]{2,1,0:T(8,128)S(1)}, f32[2,16,32]{2,1,0:T(8,128)S(1)}, u32[]{:S(2)}, u32[]{:S(2)}) collective-permute-start(f32[2,16,32]{2,1,0:T(8,128)S(1)} %ghost.1), channel_id=1, source_target_pairs={{0,4},{4,0},{8,12},{12,8},{1,5},{5,1},{9,13},{13,9},{2,6},{6,2},{1... | collective-permute-start | bytes 12296 | tf_op jit(solution)/shard_map/ppermute | solution.py:52
  16.9 4.2 %collective-permute-start.5 = (f32[2,16,32]{2,1,0:T(8,128)S(1)}, f32[2,16,32]{2,1,0:T(8,128)S(1)}, u32[]{:S(2)}, u32[]{:S(2)}) collective-permute-start(f32[2,16,32]{2,1,0:T(8,128)S(1)} %ghost.1), channel_id=1, source_target_pairs={{0,8},{4,12},{8,0},{12,4},{1,9},{5,13},{9,1},{13,5},{2,10},{6,14},... | collective-permute-start | bytes 12296 | tf_op jit(solution)/shard_map/ppermute | solution.py:52
  19.3 3.2 %collective-permute-start.4 = (f32[2,16,32]{2,1,0:T(8,128)S(1)}, f32[2,16,32]{2,1,0:T(8,128)S(1)}, u32[]{:S(2)}, u32[]{:S(2)}) collective-permute-start(f32[2,16,32]{2,1,0:T(8,128)S(1)} %ghost.1), channel_id=1, source_target_pairs={{0,12},{4,8},{8,4},{12,0},{1,13},{5,9},{9,5},{13,1},{2,14},{6,10},... | collective-permute-start | bytes 12296 | tf_op jit(solution)/shard_map/ppermute | solution.py:52
  19.4 10.7 %collective-permute-start.2 = (f32[2,4,16,768]{3,2,1,0:T(8,128)S(1)}, f32[2,4,16,768]{3,2,1,0:T(8,128)S(1)}, u32[]{:S(2)}, u32[]{:S(2)}) collective-permute-start(f32[2,4,16,768]{3,2,1,0:T(8,128)S(1)} %get-tuple-element.17), channel_id=1, source_target_pairs={{0,12},{4,0},{8,4},{12,8},{1,13},{5,1},{9,5},{13,9},{2,14},{6,2},{... | collective-permute-start | bytes 1179656 | tf_op jit(solution)/shard_map/ppermute | solution.py:22
  22.6 8.5 %collective-permute-start.7 = (f32[2,4,16,768]{3,2,1,0:T(8,128)S(1)}, f32[2,4,16,768]{3,2,1,0:T(8,128)S(1)}, u32[]{:S(2)}, u32[]{:S(2)}) collective-permute-start(f32[2,4,16,768]{3,2,1,0:T(8,128)S(1)} %mend_b.1), channel_id=1, source_target_pairs={{0,12},{4,0},{8,4},{12,8},{1,13},{5,1},{9,5},{13,9},{2,14},{6,2},{... | collective-permute-start | bytes 1179656 | tf_op jit(solution)/shard_map/ppermute | solution.py:22
  23.6 3.7 %collective-permute-start.8 = (f32[2,16,32]{2,1,0:T(8,128)S(1)}, f32[2,16,32]{2,1,0:T(8,128)S(1)}, u32[]{:S(2)}, u32[]{:S(2)}) collective-permute-start(f32[2,16,32]{2,1,0:T(8,128)S(1)} %add_add_fusion.__), channel_id=1, source_target_pairs={{0,1},{1,0},{2,3},{3,2},{4,5},{5,4},{6,7},{7,6},{8,9},{9,8},{10,11... | collective-permute-start | bytes 12296 | tf_op jit(solution)/shard_map/ppermute | solution.py:52
  27.4 4.6 %collective-permute-start.9 = (f32[2,16,32]{2,1,0:T(8,128)S(1)}, f32[2,16,32]{2,1,0:T(8,128)S(1)}, u32[]{:S(2)}, u32[]{:S(2)}) collective-permute-start(f32[2,16,32]{2,1,0:T(8,128)S(1)} %add.15.total_ref), channel_id=1, source_target_pairs={{0,2},{1,3},{2,0},{3,1},{4,6},{5,7},{6,4},{7,5},{8,10},{9,11},{10,... | collective-permute-start | bytes 12296 | tf_op jit(solution)/shard_map/ppermute | solution.py:52
  32.0 1.3 %copy-start.2 = (f32[1,2,12,16,768]{4,3,2,1,0:T(8,128)S(1)}, f32[1,2,12,16,768]{4,3,2,1,0:T(8,128)}, u32[]{:S(2)}) copy-start(f32[1,2,12,16,768]{4,3,2,1,0:T(8,128)} %end.1._) | copy-start | bytes 3538948

commit v19 on v18

--- a/solution.py
+++ b/solution.py
@@ -598,13 +598,13 @@
     )(begun, state, b_came)
     boundary_gradient = pl.pallas_call(
         pick_kernel,
-        in_specs=[pl.BlockSpec(memory_space=pl.ANY)] + [vmem] * 3,
+        in_specs=[hbm] + [vmem] * 3,
         out_specs=vmem,
         out_shape=f32(parts, levels // subs, slots // hors),
         compiler_params=PARAMS,
         cost_estimate=BRIEF,
         name="pick",
-    )(adjoint_result, owner, total, came)
+    )(in_hbm(adjoint_result), owner, total, came)
     return (adjoint_result, boundary_gradient)
 
 

time: 34.1 us -> 32.9 us (0.965)
  local copies, waits for them, and re-layouts: 1.31 us -> 0.04 us
    unnamed x16 -> x14, local copies, waits for them, and re-layouts: 1.31 us -> 0.04 us
  transfers between devices with their start and end apart: 10 -> 10, of which waited for: 4 -> 4; matrix products, arithmetic and copies ran while one was open for 0% -> 0% of each run, Pallas kernels for 18% -> 19%
where the time goes in v19:
time: 32.9 us; the launch traced here: 32.7 us
  starting transfers between devices  13.5 us (41%)
  waiting for transfers between devices  9.56 us (29%)
  Pallas kernels  8.75 us (27%)
  between operations  0.81 us (2%)
    ppermute x5, starting transfers between devices, exchanged(): lax.ppermute(value, axis, [(i, i ^ distance) for i in range(size)])  7.02 us
    ppermute x2, waiting for transfers between devices, alternating(): return lax.ppermute(value, ('sub', 'hor'), pairs)  5.96 us
    ppermute x5, waiting for transfers between devices, exchanged(): lax.ppermute(value, axis, [(i, i ^ distance) for i in range(size)])  3.59 us
    ppermute x3, starting transfers between devices, to_previous(): lax.ppermute(value, 'sub', [(i, (i - 1) % peers) for i in range(peers)])  3.41 us
    ppermute x2, starting transfers between devices, alternating(): return lax.ppermute(value, ('sub', 'hor'), pairs)  3.1 us
    pallas_call x1, Pallas kernels, local(): pl.pallas_call(sweep_kernel, in_specs=[vmem] * 3, out_specs=[vmem] * 4, o...  2.98 us
    pallas_call x1, Pallas kernels, local(): pl.pallas_call(pack_kernel, in_specs=[hbm] * 6, out_specs=vmem, out_shape...  1.93 us
    pallas_call x1, Pallas kernels, local(): pl.pallas_call(begin_kernel, in_specs=[vmem] * 3, out_specs=hbm, out_shap...  0.93 us
  transfers between devices with their start and end apart: 10, of which 4 were waited for; matrix products, arithmetic and copies ran while one was open for 0% of the time, Pallas kernels for 19%

profile of v19, /device:TPU:0, one launch (start us, length us, event | category | flops | bytes accessed | tf_op | source)
XLA Modules:
  0.0 32.7 jit_solution(4207365623731317538)
XLA Ops:
  0.7 1.9 %pack.1.mine_ref = f32[12,16,768]{2,1,0:T(8,128)S(1)} custom-call(f32[1,2,12,16,768]{4,3,2,1,0:T(8,128)} %state_ref.5, f32[1,12,16,768]{3,2,1,0:T(8,128)} %east_ref.5, f32[1,12,16,768]{3,2,1,0:T(8,128)} %north_ref.9, s32[2,2,12]{2,1,0:T(2,128)} %cell_ref.1, s32[4,2,2,12]{3,2,1,0:T(2,128)} %offset_ref.1, f32[4,2,2,12]{3,2,1,0:T(2,128)} %weight_ref.1), custom_call_target="tpu_custom_call" | custom-call | flops 1 | bytes 1 | tf_op jit(solution)/shard_map/pack/pallas_call | solution.py:483
  2.6 0.0 copy-start.5
  2.6 0.5 %collective-permute-start.1 = (f32[12,16,768]{2,1,0:T(8,128)S(1)}, f32[12,16,768]{2,1,0:T(8,128)S(1)}, u32[]{:S(2)}, u32[]{:S(2)}) collective-permute-start(f32[12,16,768]{2,1,0:T(8,128)S(1)} %pack.1.mine_ref), channel_id=1, source_target_pairs={{0,4},{1,0},{2,1},{3,2},{4,5},{5,6},{6,7},{7,3},{8,12},{9,8},{10,9... | collective-permute-start | bytes 1769480 | tf_op jit(solution)/shard_map/ppermute | solution.py:34
  3.1 3.0 %sweep.1 = (f32[11,16,768]{2,1,0:T(8,128)S(1)}, f32[2,4,16,768]{3,2,1,0:T(8,128)S(1)}, f32[2,8,16,768]{3,2,1,0:T(8,128)S(1)}, f32[2,2,12,16,128]{4,3,2,1,0:T(8,128)S(1)}) custom-call(f32[1,2,12,16,768]{4,3,2,1,0:T(8,128)S(1)} %copy-done.1, f32[1,12,16,768]{3,2,1,0:T(8,128)S(1)} %copy-done.2, f32[1,12,16,768]{3,2,1,0:T(8,128)S(1)} %copy-done), custom_call_target="tpu_custom_call" | custom-call | flops 1 | bytes 1 | tf_op jit(solution)/shard_map/sweep/pallas_call | solution.py:502
  6.2 0.4 %ghost_base.1 = (f32[2,2,12,32]{3,2,1,0:T(8,128)S(1)}, f32[2,16,32]{2,1,0:T(8,128)S(1)}, s32[1,32]{1,0:T(1,128)S(1)}, f32[11,16,768]{2,1,0:T(8,128)S(1)}) custom-call(s32[2,2,12]{2,1,0:T(2,128)S(1)} %copy-done.5, s32[4,2,2,12]{3,2,1,0:T(2,128)S(1)} %copy-done.3, f32[4,2,2,12]{3,2,1,0:T(2,128)S(1)} %copy-done.4, s32[1,32]{1,0:T(1,128)S(1)} %bitcast.1, ...), custom_call_target="tpu_custom_call" | custom-call | flops 1 | bytes 1 | tf_op jit(solution)/shard_map/ghost_base/pallas_call | solution.py:524
  6.5 2.6 %collective-permute-start.3 = (f32[11,16,768]{2,1,0:T(8,128)S(1)}, f32[11,16,768]{2,1,0:T(8,128)S(1)}, u32[]{:S(2)}, u32[]{:S(2)}) collective-permute-start(f32[11,16,768]{2,1,0:T(8,128)S(1)} %get-tuple-element.18), channel_id=1, source_target_pairs={{0,1},{1,2},{2,3},{3,7},{4,0},{5,4},{6,5},{7,6},{8,9},{9,10},{10,1... | collective-permute-start | bytes 1622024 | tf_op jit(solution)/shard_map/ppermute | solution.py:34
  9.2 0.7 %collective-permute-start = (f32[2,4,16,768]{3,2,1,0:T(8,128)S(1)}, f32[2,4,16,768]{3,2,1,0:T(8,128)S(1)}, u32[]{:S(2)}, u32[]{:S(2)}) collective-permute-start(f32[2,4,16,768]{3,2,1,0:T(8,128)S(1)} %get-tuple-element.12), channel_id=1, source_target_pairs={{0,12},{4,0},{8,4},{12,8},{1,13},{5,1},{9,5},{13,9},{2,14},{6,2},{... | collective-permute-start | bytes 1179656 | tf_op jit(solution)/shard_map/ppermute | solution.py:22
  9.8 6.0 %collective-permute-done.1.other_ref = f32[12,16,768]{2,1,0:T(8,128)S(1)} collective-permute-done((f32[12,16,768]{2,1,0:T(8,128)S(1)}, f32[12,16,768]{2,1,0:T(8,128)S(1)}, u32[]{:S(2)}, u32[]{:S(2)}) %collective-permute-start.1) | collective-permute-done | bytes 589856 | tf_op jit(solution)/shard_map/ppermute | solution.py:34
  15.8 0.8 %mend_a.1 = (f32[2,4,16,768]{3,2,1,0:T(8,128)S(1)}, f32[2,2,6,16,128]{4,3,2,1,0:T(8,128)S(1)}) custom-call(f32[1,12,16,768]{3,2,1,0:T(8,128)S(1)} %copy-done.2, f32[1,12,16,768]{3,2,1,0:T(8,128)S(1)} %copy-done, f32[11,16,768]{2,1,0:T(8,128)S(1)} %get-tuple-element.13.pack_ref.mine_ref, f32[12,16,768]{2,1,0:T(8,128)S(1)} %collective-permute-done.1.other_ref, ...), custom_call_target="tpu_custom_call" | custom-call | flops 1 | bytes 1 | tf_op jit(solution)/shard_map/mend_a/pallas_call | solution.py:539
  16.5 0.2 ghost.1
  16.8 0.1 collective-permute-start.6
  16.9 2.4 %collective-permute-start.5 = (f32[2,16,32]{2,1,0:T(8,128)S(1)}, f32[2,16,32]{2,1,0:T(8,128)S(1)}, u32[]{:S(2)}, u32[]{:S(2)}) collective-permute-start(f32[2,16,32]{2,1,0:T(8,128)S(1)} %ghost.1), channel_id=1, source_target_pairs={{0,8},{4,12},{8,0},{12,4},{1,9},{5,13},{9,1},{13,5},{2,10},{6,14},... | collective-permute-start | bytes 12296 | tf_op jit(solution)/shard_map/ppermute | solution.py:52
  19.3 0.1 collective-permute-start.4
  19.4 1.7 %collective-permute-start.2 = (f32[2,4,16,768]{3,2,1,0:T(8,128)S(1)}, f32[2,4,16,768]{3,2,1,0:T(8,128)S(1)}, u32[]{:S(2)}, u32[]{:S(2)}) collective-permute-start(f32[2,4,16,768]{3,2,1,0:T(8,128)S(1)} %get-tuple-element.17), channel_id=1, source_target_pairs={{0,12},{4,0},{8,4},{12,8},{1,13},{5,1},{9,5},{13,9},{2,14},{6,2},{... | collective-permute-start | bytes 1179656 | tf_op jit(solution)/shard_map/ppermute | solution.py:22
  21.1 1.4 %collective-permute-done.4 = f32[2,16,32]{2,1,0:T(8,128)S(1)} collective-permute-done((f32[2,16,32]{2,1,0:T(8,128)S(1)}, f32[2,16,32]{2,1,0:T(8,128)S(1)}, u32[]{:S(2)}, u32[]{:S(2)}) %collective-permute-start.4) | collective-permute-done | bytes 4128 | tf_op jit(solution)/shard_map/ppermute | solution.py:52
  22.5 0.1 mend_b.1
  22.6 1.1 %collective-permute-start.7 = (f32[2,4,16,768]{3,2,1,0:T(8,128)S(1)}, f32[2,4,16,768]{3,2,1,0:T(8,128)S(1)}, u32[]{:S(2)}, u32[]{:S(2)}) collective-permute-start(f32[2,4,16,768]{3,2,1,0:T(8,128)S(1)} %mend_b.1), channel_id=1, source_target_pairs={{0,12},{4,0},{8,4},{12,8},{1,13},{5,1},{9,5},{13,9},{2,14},{6,2},{... | collective-permute-start | bytes 1179656 | tf_op jit(solution)/shard_map/ppermute | solution.py:22
  23.6 1.7 %collective-permute-start.8 = (f32[2,16,32]{2,1,0:T(8,128)S(1)}, f32[2,16,32]{2,1,0:T(8,128)S(1)}, u32[]{:S(2)}, u32[]{:S(2)}) collective-permute-start(f32[2,16,32]{2,1,0:T(8,128)S(1)} %add_add_fusion.__), channel_id=1, source_target_pairs={{0,1},{1,0},{2,3},{3,2},{4,5},{5,4},{6,7},{7,6},{8,9},{9,8},{10,11... | collective-permute-start | bytes 12296 | tf_op jit(solution)/shard_map/ppermute | solution.py:52
  25.3 2.0 %collective-permute-done.8 = f32[2,16,32]{2,1,0:T(8,128)S(1)} collective-permute-done((f32[2,16,32]{2,1,0:T(8,128)S(1)}, f32[2,16,32]{2,1,0:T(8,128)S(1)}, u32[]{:S(2)}, u32[]{:S(2)}) %collective-permute-start.8) | collective-permute-done | bytes 4128 | tf_op jit(solution)/shard_map/ppermute | solution.py:52
  27.4 2.7 %collective-permute-start.9 = (f32[2,16,32]{2,1,0:T(8,128)S(1)}, f32[2,16,32]{2,1,0:T(8,128)S(1)}, u32[]{:S(2)}, u32[]{:S(2)}) collective-permute-start(f32[2,16,32]{2,1,0:T(8,128)S(1)} %add.15.total_ref), channel_id=1, source_target_pairs={{0,2},{1,3},{2,0},{3,1},{4,6},{5,7},{6,4},{7,5},{8,10},{9,11},{10,... | collective-permute-start | bytes 12296 | tf_op jit(solution)/shard_map/ppermute | solution.py:52
  30.1 0.9 %begin.1.begun_hbm = f32[1,2,12,16,768]{4,3,2,1,0:T(8,128)} custom-call(f32[1,2,12,16,768]{4,3,2,1,0:T(8,128)S(1)} %copy-done.1, f32[2,4,16,768]{3,2,1,0:T(8,128)S(1)} %collective-permute-done.middle_ref._, f32[2,4,16,768]{3,2,1,0:T(8,128)S(1)} %collective-permute-done.2.a_ref), custom_call_target="tpu_custom_call" | custom-call | flops 1 | bytes 1 | tf_op jit(solution)/shard_map/begin/pallas_call | solution.py:578
  31.1 0.8 %end.1._ = f32[1,2,12,16,768]{4,3,2,1,0:T(8,128)} custom-call(f32[1,2,12,16,768]{4,3,2,1,0:T(8,128)} %begin.1.begun_hbm, f32[1,2,12,16,768]{4,3,2,1,0:T(8,128)S(1)} %copy-done.1, f32[2,4,16,768]{3,2,1,0:T(8,128)S(1)} %collective-permute-done.7.b_ref), custom_call_target="tpu_custom_call", output_to_operand_aliasing={{}: (0, {})} | custom-call | flops 1 | bytes 1 | tf_op jit(solution)/shard_map/end/pallas_call | solution.py:588
  31.9 0.2 collective-permute-done.9.came_ref
  32.0 0.7 %pick.1 = f32[2,4,8]{2,1,0:T(4,128)} custom-call(f32[1,2,12,16,768]{4,3,2,1,0:T(8,128)} %end.1._, s32[1,32]{1,0:T(1,128)S(1)} %get-tuple-element.21.owner_ref, f32[2,16,32]{2,1,0:T(8,128)S(1)} %add.15.total_ref, f32[2,16,32]{2,1,0:T(8,128)S(1)} %collective-permute-done.9.came_ref), custom_call_target="tpu_custom_call" | custom-call | flops 1 | bytes 1 | tf_op jit(solution)/shard_map/pick/pallas_call | solution.py:599
  (21 shorter events, 0.1 us)
Async XLA Ops:
  0.6 2.5 %copy-start = (f32[1,12,16,768]{3,2,1,0:T(8,128)S(1)}, f32[1,12,16,768]{3,2,1,0:T(8,128)}, u32[]{:S(2)}) copy-start(f32[1,12,16,768]{3,2,1,0:T(8,128)} %north_ref.9) | copy-start | bytes 1769476
  0.6 2.5 %copy-start.2 = (f32[1,12,16,768]{3,2,1,0:T(8,128)S(1)}, f32[1,12,16,768]{3,2,1,0:T(8,128)}, u32[]{:S(2)}) copy-start(f32[1,12,16,768]{3,2,1,0:T(8,128)} %east_ref.5) | copy-start | bytes 1769476
  0.6 2.5 %copy-start.1 = (f32[1,2,12,16,768]{4,3,2,1,0:T(8,128)S(1)}, f32[1,2,12,16,768]{4,3,2,1,0:T(8,128)}, u32[]{:S(2)}) copy-start(f32[1,2,12,16,768]{4,3,2,1,0:T(8,128)} %state_ref.5) | copy-start | bytes 3538948
  2.6 3.5 %copy-start.3 = (s32[4,2,2,12]{3,2,1,0:T(2,128)S(1)}, s32[4,2,2,12]{3,2,1,0:T(2,128)}, u32[]{:S(2)}) copy-start(s32[4,2,2,12]{3,2,1,0:T(2,128)} %offset_ref.1) | copy-start | bytes 2308
  2.6 3.5 %copy-start.4 = (f32[4,2,2,12]{3,2,1,0:T(2,128)S(1)}, f32[4,2,2,12]{3,2,1,0:T(2,128)}, u32[]{:S(2)}) copy-start(f32[4,2,2,12]{3,2,1,0:T(2,128)} %weight_ref.1) | copy-start | bytes 2308
  2.6 3.5 %copy-start.5 = (s32[2,2,12]{2,1,0:T(2,128)S(1)}, s32[2,2,12]{2,1,0:T(2,128)}, u32[]{:S(2)}) copy-start(s32[2,2,12]{2,1,0:T(2,128)} %cell_ref.1) | copy-start | bytes 580
  2.6 3.5 %copy-start.6 = (s32[32]{0:T(128)S(1)}, s32[32]{0:T(128)}, u32[]{:S(2)}) copy-start(s32[32]{0:T(128)} %param.13) | copy-start | bytes 388
  2.6 13.1 %collective-permute-start.1 = (f32[12,16,768]{2,1,0:T(8,128)S(1)}, f32[12,16,768]{2,1,0:T(8,128)S(1)}, u32[]{:S(2)}, u32[]{:S(2)}) collective-permute-start(f32[12,16,768]{2,1,0:T(8,128)S(1)} %pack.1.mine_ref), channel_id=1, source_target_pairs={{0,4},{1,0},{2,1},{3,2},{4,5},{5,6},{6,7},{7,3},{8,12},{9,8},{10,9... | collective-permute-start | bytes 1769480 | tf_op jit(solution)/shard_map/ppermute | solution.py:34
  6.5 16.0 %collective-permute-start.3 = (f32[11,16,768]{2,1,0:T(8,128)S(1)}, f32[11,16,768]{2,1,0:T(8,128)S(1)}, u32[]{:S(2)}, u32[]{:S(2)}) collective-permute-start(f32[11,16,768]{2,1,0:T(8,128)S(1)} %get-tuple-element.18), channel_id=1, source_target_pairs={{0,1},{1,2},{2,3},{3,7},{4,0},{5,4},{6,5},{7,6},{8,9},{9,10},{10,1... | collective-permute-start | bytes 1622024 | tf_op jit(solution)/shard_map/ppermute | solution.py:34
  9.2 13.3 %collective-permute-start = (f32[2,4,16,768]{3,2,1,0:T(8,128)S(1)}, f32[2,4,16,768]{3,2,1,0:T(8,128)S(1)}, u32[]{:S(2)}, u32[]{:S(2)}) collective-permute-start(f32[2,4,16,768]{3,2,1,0:T(8,128)S(1)} %get-tuple-element.12), channel_id=1, source_target_pairs={{0,12},{4,0},{8,4},{12,8},{1,13},{5,1},{9,5},{13,9},{2,14},{6,2},{... | collective-permute-start | bytes 1179656 | tf_op jit(solution)/shard_map/ppermute | solution.py:22
  16.8 2.6 %collective-permute-start.6 = (f32[2,16,32]{2,1,0:T(8,128)S(1)}, f32[2,16,32]{2,1,0:T(8,128)S(1)}, u32[]{:S(2)}, u32[]{:S(2)}) collective-permute-start(f32[2,16,32]{2,1,0:T(8,128)S(1)} %ghost.1), channel_id=1, source_target_pairs={{0,4},{4,0},{8,12},{12,8},{1,5},{5,1},{9,13},{13,9},{2,6},{6,2},{1... | collective-permute-start | bytes 12296 | tf_op jit(solution)/shard_map/ppermute | solution.py:52
  16.9 4.2 %collective-permute-start.5 = (f32[2,16,32]{2,1,0:T(8,128)S(1)}, f32[2,16,32]{2,1,0:T(8,128)S(1)}, u32[]{:S(2)}, u32[]{:S(2)}) collective-permute-start(f32[2,16,32]{2,1,0:T(8,128)S(1)} %ghost.1), channel_id=1, source_target_pairs={{0,8},{4,12},{8,0},{12,4},{1,9},{5,13},{9,1},{13,5},{2,10},{6,14},... | collective-permute-start | bytes 12296 | tf_op jit(solution)/shard_map/ppermute | solution.py:52
  19.3 3.2 %collective-permute-start.4 = (f32[2,16,32]{2,1,0:T(8,128)S(1)}, f32[2,16,32]{2,1,0:T(8,128)S(1)}, u32[]{:S(2)}, u32[]{:S(2)}) collective-permute-start(f32[2,16,32]{2,1,0:T(8,128)S(1)} %ghost.1), channel_id=1, source_target_pairs={{0,12},{4,8},{8,4},{12,0},{1,13},{5,9},{9,5},{13,1},{2,14},{6,10},... | collective-permute-start | bytes 12296 | tf_op jit(solution)/shard_map/ppermute | solution.py:52
  19.4 10.7 %collective-permute-start.2 = (f32[2,4,16,768]{3,2,1,0:T(8,128)S(1)}, f32[2,4,16,768]{3,2,1,0:T(8,128)S(1)}, u32[]{:S(2)}, u32[]{:S(2)}) collective-permute-start(f32[2,4,16,768]{3,2,1,0:T(8,128)S(1)} %get-tuple-element.17), channel_id=1, source_target_pairs={{0,12},{4,0},{8,4},{12,8},{1,13},{5,1},{9,5},{13,9},{2,14},{6,2},{... | collective-permute-start | bytes 1179656 | tf_op jit(solution)/shard_map/ppermute | solution.py:22
  22.6 8.5 %collective-permute-start.7 = (f32[2,4,16,768]{3,2,1,0:T(8,128)S(1)}, f32[2,4,16,768]{3,2,1,0:T(8,128)S(1)}, u32[]{:S(2)}, u32[]{:S(2)}) collective-permute-start(f32[2,4,16,768]{3,2,1,0:T(8,128)S(1)} %mend_b.1), channel_id=1, source_target_pairs={{0,12},{4,0},{8,4},{12,8},{1,13},{5,1},{9,5},{13,9},{2,14},{6,2},{... | collective-permute-start | bytes 1179656 | tf_op jit(solution)/shard_map/ppermute | solution.py:22
  23.6 3.7 %collective-permute-start.8 = (f32[2,16,32]{2,1,0:T(8,128)S(1)}, f32[2,16,32]{2,1,0:T(8,128)S(1)}, u32[]{:S(2)}, u32[]{:S(2)}) collective-permute-start(f32[2,16,32]{2,1,0:T(8,128)S(1)} %add_add_fusion.__), channel_id=1, source_target_pairs={{0,1},{1,0},{2,3},{3,2},{4,5},{5,4},{6,7},{7,6},{8,9},{9,8},{10,11... | collective-permute-start | bytes 12296 | tf_op jit(solution)/shard_map/ppermute | solution.py:52
  27.4 4.6 %collective-permute-start.9 = (f32[2,16,32]{2,1,0:T(8,128)S(1)}, f32[2,16,32]{2,1,0:T(8,128)S(1)}, u32[]{:S(2)}, u32[]{:S(2)}) collective-permute-start(f32[2,16,32]{2,1,0:T(8,128)S(1)} %add.15.total_ref), channel_id=1, source_target_pairs={{0,2},{1,3},{2,0},{3,1},{4,6},{5,7},{6,4},{7,5},{8,10},{9,11},{10,... | collective-permute-start | bytes 12296 | tf_op jit(solution)/shard_map/ppermute | solution.py:52

commit v20 on v19

--- a/solution.py
+++ b/solution.py
@@ -171,9 +171,21 @@
 
 
 def sweep_kernel(
-    state_ref, east_ref, north_ref, pack_ref, middle_ref, ends_ref, column_ref,
-    field, plus_ref, minus_ref, centre_ref,
+    state_hbm, east_hbm, north_hbm, _,
+    pack_ref, middle_ref, ends_ref, column_ref, state_ref, east_ref, north_ref,
+    field, plus_ref, minus_ref, centre_ref, sems,
 ):
+    copies = [
+        pltpu.make_async_copy(source, target, sems.at[n])
+        for n, (source, target) in enumerate(
+            ((east_hbm, east_ref), (north_hbm, north_ref))
+            + tuple((state_hbm.at[0, c], state_ref.at[0, c]) for c in range(state_hbm.shape[1]))
+        )
+    ]
+    for copy in copies:
+        copy.start()
+    for copy in copies:
+        copy.wait()
     parts, rows, levels, width = state_ref.shape[1:]
     flip = 1 - parity()
     sign = sign_of(flip)
@@ -498,27 +510,28 @@
     )(*[in_hbm(value) for value in [adjoint_state, courant_east, courant_north] + small])
     first_came = alternating(first_pack, -1)
 
-    state, east, north = adjoint_state, courant_east, courant_north
-    second_pack, middle, ends, columns = pl.pallas_call(
+    second_pack, middle, ends, columns, state, east, north = pl.pallas_call(
         sweep_kernel,
-        in_specs=[vmem] * 3,
-        out_specs=[vmem] * 4,
+        in_specs=[hbm] * 3 + [pl.BlockSpec(memory_space=pl.ANY)],
+        out_specs=[vmem] * 7,
         out_shape=[
             f32(PACK_ROWS, levels, width),
             f32(parts, inner, levels, width),
             f32(parts, 2 * STEPS, levels, width),
             f32(parts, 2, rows, levels, LANES),
+            f32(*adjoint_state.shape), f32(*courant_east.shape), f32(*courant_north.shape),
         ],
         scratch_shapes=[
             pltpu.VMEM((STEPS - 1, parts, rows, HALF, width), jnp.float32),
             pltpu.VMEM((rows, HALF, width), jnp.float32),
             pltpu.VMEM((rows, HALF, width), jnp.float32),
             pltpu.VMEM((rows, HALF, width), jnp.float32),
+            pltpu.SemaphoreType.DMA((parts + 2,)),
         ],
         compiler_params=PARAMS,
         cost_estimate=BRIEF,
         name="sweep",
-    )(state, east, north)
+    )(in_hbm(adjoint_state), in_hbm(courant_east), in_hbm(courant_north), first_pack)
     middle_came = to_previous(middle)
 
     mixing, base, owner, second_sent = pl.pallas_call(

time: 32.9 us -> 31.1 us (0.945)
  waiting for transfers between devices: 9.56 us -> 6.34 us
  Pallas kernels: 8.75 us -> 10.2 us
    ppermute x2, waiting for transfers between devices: 5.96 us -> 2.74 us  [alternating(): return lax.ppermute(value, ('sub', 'hor'), pairs)]
    pallas_call x1, Pallas kernels: 2.98 us -> 4.6 us  [local(): pl.pallas_call(sweep_kernel, in_specs=[hbm] * 3 + [pl.BlockSpec(memory_sp...]
  transfers between devices with their start and end apart: 10 -> 10, of which waited for: 4 -> 4; matrix products, arithmetic and copies ran while one was open for 0% -> 0% of each run, Pallas kernels for 19% -> 25%
where the time goes in v20:
time: 31.1 us; the launch traced here: 30.9 us
  starting transfers between devices  13.5 us (43%)
  Pallas kernels  10.2 us (33%)
  waiting for transfers between devices  6.34 us (20%)
  between operations  0.78 us (3%)
    ppermute x5, starting transfers between devices, exchanged(): lax.ppermute(value, axis, [(i, i ^ distance) for i in range(size)])  7.02 us
    pallas_call x1, Pallas kernels, local(): pl.pallas_call(sweep_kernel, in_specs=[hbm] * 3 + [pl.BlockSpec(memory_sp...  4.6 us
    ppermute x5, waiting for transfers between devices, exchanged(): lax.ppermute(value, axis, [(i, i ^ distance) for i in range(size)])  3.59 us
    ppermute x3, starting transfers between devices, to_previous(): lax.ppermute(value, 'sub', [(i, (i - 1) % peers) for i in range(peers)])  3.43 us
    ppermute x2, starting transfers between devices, alternating(): return lax.ppermute(value, ('sub', 'hor'), pairs)  3.08 us
    ppermute x2, waiting for transfers between devices, alternating(): return lax.ppermute(value, ('sub', 'hor'), pairs)  2.74 us
    pallas_call x1, Pallas kernels, local(): pl.pallas_call(pack_kernel, in_specs=[hbm] * 6, out_specs=vmem, out_shape...  1.78 us
    pallas_call x1, Pallas kernels, local(): pl.pallas_call(begin_kernel, in_specs=[vmem] * 3, out_specs=hbm, out_shap...  0.93 us
  transfers between devices with their start and end apart: 10, of which 4 were waited for; matrix products, arithmetic and copies ran while one was open for 0% of the time, Pallas kernels for 25%

profile of v20, /device:TPU:0, one launch (start us, length us, event | category | flops | bytes accessed | tf_op | source)
XLA Modules:
  0.0 30.9 jit_solution(2196022787775772641)
XLA Ops:
  0.6 1.8 %pack.1._.mine_ref = f32[12,16,768]{2,1,0:T(8,128)S(1)} custom-call(f32[1,2,12,16,768]{4,3,2,1,0:T(8,128)} %state_hbm.3, f32[1,12,16,768]{3,2,1,0:T(8,128)} %east_hbm.3, f32[1,12,16,768]{3,2,1,0:T(8,128)} %north_hbm.3, s32[2,2,12]{2,1,0:T(2,128)} %cell_ref.1, s32[4,2,2,12]{3,2,1,0:T(2,128)} %offset_ref.1, f32[4,2,2,12]{3,2,1,0:T(2,128)} %weight_ref.1), custom_call_target="tpu_custom_call" | custom-call | flops 1 | bytes 1 | tf_op jit(solution)/shard_map/pack/pallas_call | solution.py:495
  2.4 0.0 copy-start.1
  2.5 0.5 %collective-permute-start.1 = (f32[12,16,768]{2,1,0:T(8,128)S(1)}, f32[12,16,768]{2,1,0:T(8,128)S(1)}, u32[]{:S(2)}, u32[]{:S(2)}) collective-permute-start(f32[12,16,768]{2,1,0:T(8,128)S(1)} %pack.1._.mine_ref), channel_id=1, source_target_pairs={{0,4},{1,0},{2,1},{3,2},{4,5},{5,6},{6,7},{7,3},{8,12},{9,8},{10,9... | collective-permute-start | bytes 1769480 | tf_op jit(solution)/shard_map/ppermute | solution.py:34
  2.9 4.6 %sweep.1 = (f32[11,16,768]{2,1,0:T(8,128)S(1)}, f32[2,4,16,768]{3,2,1,0:T(8,128)S(1)}, f32[2,8,16,768]{3,2,1,0:T(8,128)S(1)}, f32[2,2,12,16,128]{4,3,2,1,0:T(8,1...) custom-call(f32[1,2,12,16,768]{4,3,2,1,0:T(8,128)} %state_hbm.3, ...), custom_call_target="tpu_custom_call" | custom-call | flops 1 | bytes 1 | tf_op jit(solution)/shard_map/sweep/pallas_call | solution.py:513
  7.6 0.4 %ghost_base.1 = (f32[2,2,12,32]{3,2,1,0:T(8,128)S(1)}, f32[2,16,32]{2,1,0:T(8,128)S(1)}, s32[1,32]{1,0:T(1,128)S(1)}, f32[11,16,768]{2,1,0:T(8,128)S(1)}) custom-call(s32[2,2,12]{2,1,0:T(2,128)S(1)} %copy-done.2, s32[4,2,2,12]{3,2,1,0:T(2,128)S(1)} %copy-done, f32[4,2,2,12]{3,2,1,0:T(2,128)S(1)} %copy-done.1, s32[1,32]{1,0:T(1,128)S(1)} %bitcast.1, ...), custom_call_target="tpu_custom_call" | custom-call | flops 1 | bytes 1 | tf_op jit(solution)/shard_map/ghost_base/pallas_call | solution.py:537
  8.0 2.6 %collective-permute-start.3 = (f32[11,16,768]{2,1,0:T(8,128)S(1)}, f32[11,16,768]{2,1,0:T(8,128)S(1)}, u32[]{:S(2)}, u32[]{:S(2)}) collective-permute-start(f32[11,16,768]{2,1,0:T(8,128)S(1)} %get-tuple-element.24), channel_id=1, source_target_pairs={{0,1},{1,2},{2,3},{3,7},{4,0},{5,4},{6,5},{7,6},{8,9},{9,10},{10,1... | collective-permute-start | bytes 1622024 | tf_op jit(solution)/shard_map/ppermute | solution.py:34
  10.6 0.7 %collective-permute-start = (f32[2,4,16,768]{3,2,1,0:T(8,128)S(1)}, f32[2,4,16,768]{3,2,1,0:T(8,128)S(1)}, u32[]{:S(2)}, u32[]{:S(2)}) collective-permute-start(f32[2,4,16,768]{3,2,1,0:T(8,128)S(1)} %get-tuple-element.16), channel_id=1, source_target_pairs={{0,12},{4,0},{8,4},{12,8},{1,13},{5,1},{9,5},{13,9},{2,14},{6,2},{... | collective-permute-start | bytes 1179656 | tf_op jit(solution)/shard_map/ppermute | solution.py:22
  11.2 2.7 %collective-permute-done.1.other_ref = f32[12,16,768]{2,1,0:T(8,128)S(1)} collective-permute-done((f32[12,16,768]{2,1,0:T(8,128)S(1)}, f32[12,16,768]{2,1,0:T(8,128)S(1)}, u32[]{:S(2)}, u32[]{:S(2)}) %collective-permute-start.1) | collective-permute-done | bytes 589856 | tf_op jit(solution)/shard_map/ppermute | solution.py:34
  14.0 0.8 %mend_a.1 = (f32[2,4,16,768]{3,2,1,0:T(8,128)S(1)}, f32[2,2,6,16,128]{4,3,2,1,0:T(8,128)S(1)}) custom-call(f32[1,12,16,768]{3,2,1,0:T(8,128)S(1)} %get-tuple-element.17.east_ref, f32[1,12,16,768]{3,2,1,0:T(8,128)S(1)} %get-tuple-element.18.north_ref, f32[11,16,768]{2,1,0:T(8,128)S(1)} %get-tuple-element.19.pack_ref.mine_ref, ...), custom_call_target="tpu_custom_call" | custom-call | flops 1 | bytes 1 | tf_op jit(solution)/shard_map/mend_a/pallas_call | solution.py:552
  14.8 0.2 ghost.1
  15.0 0.1 collective-permute-start.6
  15.1 2.4 %collective-permute-start.5 = (f32[2,16,32]{2,1,0:T(8,128)S(1)}, f32[2,16,32]{2,1,0:T(8,128)S(1)}, u32[]{:S(2)}, u32[]{:S(2)}) collective-permute-start(f32[2,16,32]{2,1,0:T(8,128)S(1)} %ghost.1), channel_id=1, source_target_pairs={{0,8},{4,12},{8,0},{12,4},{1,9},{5,13},{9,1},{13,5},{2,10},{6,14},... | collective-permute-start | bytes 12296 | tf_op jit(solution)/shard_map/ppermute | solution.py:52
  17.5 0.1 collective-permute-start.4
  17.6 1.7 %collective-permute-start.2 = (f32[2,4,16,768]{3,2,1,0:T(8,128)S(1)}, f32[2,4,16,768]{3,2,1,0:T(8,128)S(1)}, u32[]{:S(2)}, u32[]{:S(2)}) collective-permute-start(f32[2,4,16,768]{3,2,1,0:T(8,128)S(1)} %get-tuple-element.23), channel_id=1, source_target_pairs={{0,12},{4,0},{8,4},{12,8},{1,13},{5,1},{9,5},{13,9},{2,14},{6,2},{... | collective-permute-start | bytes 1179656 | tf_op jit(solution)/shard_map/ppermute | solution.py:22
  19.3 1.4 %collective-permute-done.4 = f32[2,16,32]{2,1,0:T(8,128)S(1)} collective-permute-done((f32[2,16,32]{2,1,0:T(8,128)S(1)}, f32[2,16,32]{2,1,0:T(8,128)S(1)}, u32[]{:S(2)}, u32[]{:S(2)}) %collective-permute-start.4) | collective-permute-done | bytes 4128 | tf_op jit(solution)/shard_map/ppermute | solution.py:52
  20.7 0.1 mend_b.1
  20.8 1.1 %collective-permute-start.7 = (f32[2,4,16,768]{3,2,1,0:T(8,128)S(1)}, f32[2,4,16,768]{3,2,1,0:T(8,128)S(1)}, u32[]{:S(2)}, u32[]{:S(2)}) collective-permute-start(f32[2,4,16,768]{3,2,1,0:T(8,128)S(1)} %mend_b.1), channel_id=1, source_target_pairs={{0,12},{4,0},{8,4},{12,8},{1,13},{5,1},{9,5},{13,9},{2,14},{6,2},{... | collective-permute-start | bytes 1179656 | tf_op jit(solution)/shard_map/ppermute | solution.py:22
  21.8 1.7 %collective-permute-start.8 = (f32[2,16,32]{2,1,0:T(8,128)S(1)}, f32[2,16,32]{2,1,0:T(8,128)S(1)}, u32[]{:S(2)}, u32[]{:S(2)}) collective-permute-start(f32[2,16,32]{2,1,0:T(8,128)S(1)} %add_add_fusion.__), channel_id=1, source_target_pairs={{0,1},{1,0},{2,3},{3,2},{4,5},{5,4},{6,7},{7,6},{8,9},{9,8},{10,11... | collective-permute-start | bytes 12296 | tf_op jit(solution)/shard_map/ppermute | solution.py:52
  23.6 2.0 %collective-permute-done.8 = f32[2,16,32]{2,1,0:T(8,128)S(1)} collective-permute-done((f32[2,16,32]{2,1,0:T(8,128)S(1)}, f32[2,16,32]{2,1,0:T(8,128)S(1)}, u32[]{:S(2)}, u32[]{:S(2)}) %collective-permute-start.8) | collective-permute-done | bytes 4128 | tf_op jit(solution)/shard_map/ppermute | solution.py:52
  25.6 2.7 %collective-permute-start.9 = (f32[2,16,32]{2,1,0:T(8,128)S(1)}, f32[2,16,32]{2,1,0:T(8,128)S(1)}, u32[]{:S(2)}, u32[]{:S(2)}) collective-permute-start(f32[2,16,32]{2,1,0:T(8,128)S(1)} %add.15.total_ref), channel_id=1, source_target_pairs={{0,2},{1,3},{2,0},{3,1},{4,6},{5,7},{6,4},{7,5},{8,10},{9,11},{10,... | collective-permute-start | bytes 12296 | tf_op jit(solution)/shard_map/ppermute | solution.py:52
  28.3 0.9 %begin.1.begun_hbm = f32[1,2,12,16,768]{4,3,2,1,0:T(8,128)} custom-call(f32[1,2,12,16,768]{4,3,2,1,0:T(8,128)S(1)} %get-tuple-element.15.state_ref, f32[2,4,16,768]{3,2,1,0:T(8,128)S(1)} %collective-permute-done.middle_ref._, f32[2,4,16,768]{3,2,1,0:T(8,128)S(1)} %collective-permute-done.2.a_ref), custom_call_target="tpu_custom_call" | custom-call | flops 1 | bytes 1 | tf_op jit(solution)/shard_map/begin/pallas_call | solution.py:591
  29.3 0.8 %end.1._ = f32[1,2,12,16,768]{4,3,2,1,0:T(8,128)} custom-call(f32[1,2,12,16,768]{4,3,2,1,0:T(8,128)} %begin.1.begun_hbm, f32[1,2,12,16,768]{4,3,2,1,0:T(8,128)S(1)} %get-tuple-element.15.state_ref, f32[2,4,16,768]{3,2,1,0:T(8,128)S(1)} %collective-permute-done.7.b_ref), custom_call_target="tpu_custom_call", output_to_operand_aliasing={{}: (0, {})} | custom-call | flops 1 | bytes 1 | tf_op jit(solution)/shard_map/end/pallas_call | solution.py:601
  30.1 0.2 collective-permute-done.9.came_ref
  30.2 0.7 %pick.1 = f32[2,4,8]{2,1,0:T(4,128)} custom-call(f32[1,2,12,16,768]{4,3,2,1,0:T(8,128)} %end.1._, s32[1,32]{1,0:T(1,128)S(1)} %get-tuple-element.27.owner_ref, f32[2,16,32]{2,1,0:T(8,128)S(1)} %add.15.total_ref, f32[2,16,32]{2,1,0:T(8,128)S(1)} %collective-permute-done.9.came_ref), custom_call_target="tpu_custom_call" | custom-call | flops 1 | bytes 1 | tf_op jit(solution)/shard_map/pick/pallas_call | solution.py:612
  (15 shorter events, 0.0 us)
Async XLA Ops:
  2.4 5.1 %copy-start = (s32[4,2,2,12]{3,2,1,0:T(2,128)S(1)}, s32[4,2,2,12]{3,2,1,0:T(2,128)}, u32[]{:S(2)}) copy-start(s32[4,2,2,12]{3,2,1,0:T(2,128)} %offset_ref.1) | copy-start | bytes 2308
  2.4 5.1 %copy-start.1 = (f32[4,2,2,12]{3,2,1,0:T(2,128)S(1)}, f32[4,2,2,12]{3,2,1,0:T(2,128)}, u32[]{:S(2)}) copy-start(f32[4,2,2,12]{3,2,1,0:T(2,128)} %weight_ref.1) | copy-start | bytes 2308
  2.4 5.1 %copy-start.2 = (s32[2,2,12]{2,1,0:T(2,128)S(1)}, s32[2,2,12]{2,1,0:T(2,128)}, u32[]{:S(2)}) copy-start(s32[2,2,12]{2,1,0:T(2,128)} %cell_ref.1) | copy-start | bytes 580
  2.5 5.1 %copy-start.3 = (s32[32]{0:T(128)S(1)}, s32[32]{0:T(128)}, u32[]{:S(2)}) copy-start(s32[32]{0:T(128)} %param.13) | copy-start | bytes 388
  2.5 11.5 %collective-permute-start.1 = (f32[12,16,768]{2,1,0:T(8,128)S(1)}, f32[12,16,768]{2,1,0:T(8,128)S(1)}, u32[]{:S(2)}, u32[]{:S(2)}) collective-permute-start(f32[12,16,768]{2,1,0:T(8,128)S(1)} %pack.1._.mine_ref), channel_id=1, source_target_pairs={{0,4},{1,0},{2,1},{3,2},{4,5},{5,6},{6,7},{7,3},{8,12},{9,8},{10,9... | collective-permute-start | bytes 1769480 | tf_op jit(solution)/shard_map/ppermute | solution.py:34
  8.0 12.7 %collective-permute-start.3 = (f32[11,16,768]{2,1,0:T(8,128)S(1)}, f32[11,16,768]{2,1,0:T(8,128)S(1)}, u32[]{:S(2)}, u32[]{:S(2)}) collective-permute-start(f32[11,16,768]{2,1,0:T(8,128)S(1)} %get-tuple-element.24), channel_id=1, source_target_pairs={{0,1},{1,2},{2,3},{3,7},{4,0},{5,4},{6,5},{7,6},{8,9},{9,10},{10,1... | collective-permute-start | bytes 1622024 | tf_op jit(solution)/shard_map/ppermute | solution.py:34
  10.6 10.1 %collective-permute-start = (f32[2,4,16,768]{3,2,1,0:T(8,128)S(1)}, f32[2,4,16,768]{3,2,1,0:T(8,128)S(1)}, u32[]{:S(2)}, u32[]{:S(2)}) collective-permute-start(f32[2,4,16,768]{3,2,1,0:T(8,128)S(1)} %get-tuple-element.16), channel_id=1, source_target_pairs={{0,12},{4,0},{8,4},{12,8},{1,13},{5,1},{9,5},{13,9},{2,14},{6,2},{... | collective-permute-start | bytes 1179656 | tf_op jit(solution)/shard_map/ppermute | solution.py:22
  15.0 2.6 %collective-permute-start.6 = (f32[2,16,32]{2,1,0:T(8,128)S(1)}, f32[2,16,32]{2,1,0:T(8,128)S(1)}, u32[]{:S(2)}, u32[]{:S(2)}) collective-permute-start(f32[2,16,32]{2,1,0:T(8,128)S(1)} %ghost.1), channel_id=1, source_target_pairs={{0,4},{4,0},{8,12},{12,8},{1,5},{5,1},{9,13},{13,9},{2,6},{6,2},{1... | collective-permute-start | bytes 12296 | tf_op jit(solution)/shard_map/ppermute | solution.py:52
  15.1 4.2 %collective-permute-start.5 = (f32[2,16,32]{2,1,0:T(8,128)S(1)}, f32[2,16,32]{2,1,0:T(8,128)S(1)}, u32[]{:S(2)}, u32[]{:S(2)}) collective-permute-start(f32[2,16,32]{2,1,0:T(8,128)S(1)} %ghost.1), channel_id=1, source_target_pairs={{0,8},{4,12},{8,0},{12,4},{1,9},{5,13},{9,1},{13,5},{2,10},{6,14},... | collective-permute-start | bytes 12296 | tf_op jit(solution)/shard_map/ppermute | solution.py:52
  17.5 3.2 %collective-permute-start.4 = (f32[2,16,32]{2,1,0:T(8,128)S(1)}, f32[2,16,32]{2,1,0:T(8,128)S(1)}, u32[]{:S(2)}, u32[]{:S(2)}) collective-permute-start(f32[2,16,32]{2,1,0:T(8,128)S(1)} %ghost.1), channel_id=1, source_target_pairs={{0,12},{4,8},{8,4},{12,0},{1,13},{5,9},{9,5},{13,1},{2,14},{6,10},... | collective-permute-start | bytes 12296 | tf_op jit(solution)/shard_map/ppermute | solution.py:52
  17.6 10.7 %collective-permute-start.2 = (f32[2,4,16,768]{3,2,1,0:T(8,128)S(1)}, f32[2,4,16,768]{3,2,1,0:T(8,128)S(1)}, u32[]{:S(2)}, u32[]{:S(2)}) collective-permute-start(f32[2,4,16,768]{3,2,1,0:T(8,128)S(1)} %get-tuple-element.23), channel_id=1, source_target_pairs={{0,12},{4,0},{8,4},{12,8},{1,13},{5,1},{9,5},{13,9},{2,14},{6,2},{... | collective-permute-start | bytes 1179656 | tf_op jit(solution)/shard_map/ppermute | solution.py:22
  20.8 8.5 %collective-permute-start.7 = (f32[2,4,16,768]{3,2,1,0:T(8,128)S(1)}, f32[2,4,16,768]{3,2,1,0:T(8,128)S(1)}, u32[]{:S(2)}, u32[]{:S(2)}) collective-permute-start(f32[2,4,16,768]{3,2,1,0:T(8,128)S(1)} %mend_b.1), channel_id=1, source_target_pairs={{0,12},{4,0},{8,4},{12,8},{1,13},{5,1},{9,5},{13,9},{2,14},{6,2},{... | collective-permute-start | bytes 1179656 | tf_op jit(solution)/shard_map/ppermute | solution.py:22
  21.8 3.7 %collective-permute-start.8 = (f32[2,16,32]{2,1,0:T(8,128)S(1)}, f32[2,16,32]{2,1,0:T(8,128)S(1)}, u32[]{:S(2)}, u32[]{:S(2)}) collective-permute-start(f32[2,16,32]{2,1,0:T(8,128)S(1)} %add_add_fusion.__), channel_id=1, source_target_pairs={{0,1},{1,0},{2,3},{3,2},{4,5},{5,4},{6,7},{7,6},{8,9},{9,8},{10,11... | collective-permute-start | bytes 12296 | tf_op jit(solution)/shard_map/ppermute | solution.py:52
  25.6 4.6 %collective-permute-start.9 = (f32[2,16,32]{2,1,0:T(8,128)S(1)}, f32[2,16,32]{2,1,0:T(8,128)S(1)}, u32[]{:S(2)}, u32[]{:S(2)}) collective-permute-start(f32[2,16,32]{2,1,0:T(8,128)S(1)} %add.15.total_ref), channel_id=1, source_target_pairs={{0,2},{1,3},{2,0},{3,1},{4,6},{5,7},{6,4},{7,5},{8,10},{9,11},{10,... | collective-permute-start | bytes 12296 | tf_op jit(solution)/shard_map/ppermute | solution.py:52

commit v21 on v20

--- a/solution.py
+++ b/solution.py
@@ -433,7 +433,8 @@
     return copies
 
 
-def begin_kernel(state_ref, middle_ref, a_ref, out_hbm, buffer, sems):
+def begin_kernel(state_ref, middle_ref, a_ref, total_ref, out_hbm, total_out, buffer, sems):
+    total_out[...] = total_ref[...]
     start = parity() * (state_ref.shape[2] - STEPS)
     for copy in subtract_rows(state_ref, out_hbm, buffer, sems, ((STEPS, middle_ref), (start, a_ref))):
         copy.wait()
@@ -582,22 +583,23 @@
     )(east, north, first_pack, second_came, ends, middle_came, total)
     b_came = to_previous(side_b)
 
-    for each in order[1:-1]:
-        total = total + exchanged(total, *each)
-    came = exchanged(total, *order[-1])
-
     result = f32(*adjoint_state.shape)
     buffer = pltpu.VMEM((parts, rows, levels, width), jnp.float32)
-    begun = pl.pallas_call(
+    assert len(order) > 2
+    came = exchanged(total, *order[1])
+    begun, total = pl.pallas_call(
         begin_kernel,
-        in_specs=[vmem] * 3,
-        out_specs=hbm,
-        out_shape=result,
+        in_specs=[vmem] * 4,
+        out_specs=[hbm, vmem],
+        out_shape=[result, f32(parts, levels, slots)],
         scratch_shapes=[buffer, pltpu.SemaphoreType.DMA((2 * parts,))],
         compiler_params=PARAMS,
         cost_estimate=BRIEF,
         name="begin",
-    )(state, middle_came, a_came)
+    )(state, middle_came, a_came, total)
+    for each in order[2:]:
+        total = total + came
+        came = exchanged(total, *each)
     adjoint_result = pl.pallas_call(
         end_kernel,
         in_specs=[hbm] + [vmem] * 2,

time: 31.1 us -> 31.2 us (level)
    ppermute x3, waiting for transfers between devices: 0.01 us -> 1.48 us  [to_previous(): lax.ppermute(value, 'sub', [(i, (i - 1) % peers) for i in range(peers)])]
    ppermute x5, waiting for transfers between devices: 3.59 us -> 2.24 us  [exchanged(): lax.ppermute(value, axis, [(i, i ^ distance) for i in range(size)])]
  transfers between devices with their start and end apart: 10 -> 10, of which waited for: 4 -> 6; matrix products, arithmetic and copies ran while one was open for 0% -> 0% of each run, Pallas kernels for 25% -> 25%
where the time goes in v21:
time: 31.2 us; the launch traced here: 31 us
  starting transfers between devices  13.5 us (43%)
  Pallas kernels  10.2 us (33%)
  waiting for transfers between devices  6.46 us (21%)
  between operations  0.78 us (2%)
    ppermute x5, starting transfers between devices, exchanged(): lax.ppermute(value, axis, [(i, i ^ distance) for i in range(size)])  7.02 us
    pallas_call x1, Pallas kernels, local(): pl.pallas_call(sweep_kernel, in_specs=[hbm] * 3 + [pl.BlockSpec(memory_sp...  4.6 us
    ppermute x3, starting transfers between devices, to_previous(): lax.ppermute(value, 'sub', [(i, (i - 1) % peers) for i in range(peers)])  3.43 us
    ppermute x2, starting transfers between devices, alternating(): return lax.ppermute(value, ('sub', 'hor'), pairs)  3.08 us
    ppermute x2, waiting for transfers between devices, alternating(): return lax.ppermute(value, ('sub', 'hor'), pairs)  2.74 us
    ppermute x5, waiting for transfers between devices, exchanged(): lax.ppermute(value, axis, [(i, i ^ distance) for i in range(size)])  2.24 us
    pallas_call x1, Pallas kernels, local(): pl.pallas_call(pack_kernel, in_specs=[hbm] * 6, out_specs=vmem, out_shape...  1.78 us
    ppermute x3, waiting for transfers between devices, to_previous(): lax.ppermute(value, 'sub', [(i, (i - 1) % peers) for i in range(peers)])  1.48 us
  transfers between devices with their start and end apart: 10, of which 6 were waited for; matrix products, arithmetic and copies ran while one was open for 0% of the time, Pallas kernels for 25%

profile of v21, /device:TPU:0, one launch (start us, length us, event | category | flops | bytes accessed | tf_op | source)
XLA Modules:
  0.0 31.0 jit_solution(3759820324410432048)
XLA Ops:
  0.6 1.8 %pack.1._.mine_ref = f32[12,16,768]{2,1,0:T(8,128)S(1)} custom-call(f32[1,2,12,16,768]{4,3,2,1,0:T(8,128)} %state_hbm.3, f32[1,12,16,768]{3,2,1,0:T(8,128)} %east_hbm.3, f32[1,12,16,768]{3,2,1,0:T(8,128)} %north_hbm.3, s32[2,2,12]{2,1,0:T(2,128)} %cell_ref.1, s32[4,2,2,12]{3,2,1,0:T(2,128)} %offset_ref.1, f32[4,2,2,12]{3,2,1,0:T(2,128)} %weight_ref.1), custom_call_target="tpu_custom_call" | custom-call | flops 1 | bytes 1 | tf_op jit(solution)/shard_map/pack/pallas_call | solution.py:496
  2.5 0.5 %collective-permute-start.1 = (f32[12,16,768]{2,1,0:T(8,128)S(1)}, f32[12,16,768]{2,1,0:T(8,128)S(1)}, u32[]{:S(2)}, u32[]{:S(2)}) collective-permute-start(f32[12,16,768]{2,1,0:T(8,128)S(1)} %pack.1._.mine_ref), channel_id=1, source_target_pairs={{0,4},{1,0},{2,1},{3,2},{4,5},{5,6},{6,7},{7,3},{8,12},{9,8},{10,9... | collective-permute-start | bytes 1769480 | tf_op jit(solution)/shard_map/ppermute | solution.py:34
  2.9 4.6 %sweep.1 = (f32[11,16,768]{2,1,0:T(8,128)S(1)}, f32[2,4,16,768]{3,2,1,0:T(8,128)S(1)}, f32[2,8,16,768]{3,2,1,0:T(8,128)S(1)}, f32[2,2,12,16,128]{4,3,2,1,0:T(8,1...) custom-call(f32[1,2,12,16,768]{4,3,2,1,0:T(8,128)} %state_hbm.3, ...), custom_call_target="tpu_custom_call" | custom-call | flops 1 | bytes 1 | tf_op jit(solution)/shard_map/sweep/pallas_call | solution.py:514
  7.6 0.4 %ghost_base.1 = (f32[2,2,12,32]{3,2,1,0:T(8,128)S(1)}, f32[2,16,32]{2,1,0:T(8,128)S(1)}, s32[1,32]{1,0:T(1,128)S(1)}, f32[11,16,768]{2,1,0:T(8,128)S(1)}) custom-call(s32[2,2,12]{2,1,0:T(2,128)S(1)} %copy-done.2, s32[4,2,2,12]{3,2,1,0:T(2,128)S(1)} %copy-done, f32[4,2,2,12]{3,2,1,0:T(2,128)S(1)} %copy-done.1, s32[1,32]{1,0:T(1,128)S(1)} %bitcast.1, ...), custom_call_target="tpu_custom_call" | custom-call | flops 1 | bytes 1 | tf_op jit(solution)/shard_map/ghost_base/pallas_call | solution.py:538
  8.0 2.6 %collective-permute-start.6 = (f32[11,16,768]{2,1,0:T(8,128)S(1)}, f32[11,16,768]{2,1,0:T(8,128)S(1)}, u32[]{:S(2)}, u32[]{:S(2)}) collective-permute-start(f32[11,16,768]{2,1,0:T(8,128)S(1)} %get-tuple-element.29), channel_id=1, source_target_pairs={{0,1},{1,2},{2,3},{3,7},{4,0},{5,4},{6,5},{7,6},{8,9},{9,10},{10,1... | collective-permute-start | bytes 1622024 | tf_op jit(solution)/shard_map/ppermute | solution.py:34
  10.6 0.7 %collective-permute-start = (f32[2,4,16,768]{3,2,1,0:T(8,128)S(1)}, f32[2,4,16,768]{3,2,1,0:T(8,128)S(1)}, u32[]{:S(2)}, u32[]{:S(2)}) collective-permute-start(f32[2,4,16,768]{3,2,1,0:T(8,128)S(1)} %get-tuple-element.18), channel_id=1, source_target_pairs={{0,12},{4,0},{8,4},{12,8},{1,13},{5,1},{9,5},{13,9},{2,14},{6,2},{... | collective-permute-start | bytes 1179656 | tf_op jit(solution)/shard_map/ppermute | solution.py:22
  11.2 2.7 %collective-permute-done.1.other_ref = f32[12,16,768]{2,1,0:T(8,128)S(1)} collective-permute-done((f32[12,16,768]{2,1,0:T(8,128)S(1)}, f32[12,16,768]{2,1,0:T(8,128)S(1)}, u32[]{:S(2)}, u32[]{:S(2)}) %collective-permute-start.1) | collective-permute-done | bytes 589856 | tf_op jit(solution)/shard_map/ppermute | solution.py:34
  14.0 0.8 %mend_a.1 = (f32[2,4,16,768]{3,2,1,0:T(8,128)S(1)}, f32[2,2,6,16,128]{4,3,2,1,0:T(8,128)S(1)}) custom-call(f32[1,12,16,768]{3,2,1,0:T(8,128)S(1)} %get-tuple-element.19.east_ref, f32[1,12,16,768]{3,2,1,0:T(8,128)S(1)} %get-tuple-element.20.north_ref, f32[11,16,768]{2,1,0:T(8,128)S(1)} %get-tuple-element.21.pack_ref.mine_ref, ...), custom_call_target="tpu_custom_call" | custom-call | flops 1 | bytes 1 | tf_op jit(solution)/shard_map/mend_a/pallas_call | solution.py:553
  14.8 0.2 ghost.1
  15.0 0.1 collective-permute-start.5
  15.1 2.4 %collective-permute-start.4 = (f32[2,16,32]{2,1,0:T(8,128)S(1)}, f32[2,16,32]{2,1,0:T(8,128)S(1)}, u32[]{:S(2)}, u32[]{:S(2)}) collective-permute-start(f32[2,16,32]{2,1,0:T(8,128)S(1)} %ghost.1), channel_id=1, source_target_pairs={{0,8},{4,12},{8,0},{12,4},{1,9},{5,13},{9,1},{13,5},{2,10},{6,14},... | collective-permute-start | bytes 12296 | tf_op jit(solution)/shard_map/ppermute | solution.py:52
  17.5 0.1 collective-permute-start.3
  17.6 1.7 %collective-permute-start.2 = (f32[2,4,16,768]{3,2,1,0:T(8,128)S(1)}, f32[2,4,16,768]{3,2,1,0:T(8,128)S(1)}, u32[]{:S(2)}, u32[]{:S(2)}) collective-permute-start(f32[2,4,16,768]{3,2,1,0:T(8,128)S(1)} %get-tuple-element.25), channel_id=1, source_target_pairs={{0,12},{4,0},{8,4},{12,8},{1,13},{5,1},{9,5},{13,9},{2,14},{6,2},{... | collective-permute-start | bytes 1179656 | tf_op jit(solution)/shard_map/ppermute | solution.py:22
  19.3 1.4 %collective-permute-done.3 = f32[2,16,32]{2,1,0:T(8,128)S(1)} collective-permute-done((f32[2,16,32]{2,1,0:T(8,128)S(1)}, f32[2,16,32]{2,1,0:T(8,128)S(1)}, u32[]{:S(2)}, u32[]{:S(2)}) %collective-permute-start.3) | collective-permute-done | bytes 4128 | tf_op jit(solution)/shard_map/ppermute | solution.py:52
  20.8 1.1 %collective-permute-start.7 = (f32[2,4,16,768]{3,2,1,0:T(8,128)S(1)}, f32[2,4,16,768]{3,2,1,0:T(8,128)S(1)}, u32[]{:S(2)}, u32[]{:S(2)}) collective-permute-start(f32[2,4,16,768]{3,2,1,0:T(8,128)S(1)} %mend_b.1), channel_id=1, source_target_pairs={{0,12},{4,0},{8,4},{12,8},{1,13},{5,1},{9,5},{13,9},{2,14},{6,2},{... | collective-permute-start | bytes 1179656 | tf_op jit(solution)/shard_map/ppermute | solution.py:22
  21.8 1.7 %collective-permute-start.8 = (f32[2,16,32]{2,1,0:T(8,128)S(1)}, f32[2,16,32]{2,1,0:T(8,128)S(1)}, u32[]{:S(2)}, u32[]{:S(2)}) collective-permute-start(f32[2,16,32]{2,1,0:T(8,128)S(1)} %add_add_fusion.total_ref.__), channel_id=1, source_target_pairs={{0,1},{1,0},{2,3},{3,2},{4,5},{5,4},{6,7},{7,6},{8,9},{9,8},{10,11... | collective-permute-start | bytes 12296 | tf_op jit(solution)/shard_map/ppermute | solution.py:52
  23.6 1.0 %collective-permute-done.2.a_ref = f32[2,4,16,768]{3,2,1,0:T(8,128)S(1)} collective-permute-done((f32[2,4,16,768]{3,2,1,0:T(8,128)S(1)}, f32[2,4,16,768]{3,2,1,0:T(8,128)S(1)}, u32[]{:S(2)}, u32[]{:S(2)}) %collective-permute-start.2) | collective-permute-done | bytes 393248 | tf_op jit(solution)/shard_map/ppermute | solution.py:22
  24.6 0.9 %begin.1 = (f32[1,2,12,16,768]{4,3,2,1,0:T(8,128)}, f32[2,16,32]{2,1,0:T(8,128)S(1)}) custom-call(f32[1,2,12,16,768]{4,3,2,1,0:T(8,128)S(1)} %get-tuple-element.17.state_ref, f32[2,4,16,768]{3,2,1,0:T(8,128)S(1)} %collective-permute-done.middle_ref._, f32[2,4,16,768]{3,2,1,0:T(8,128)S(1)} %collective-permute-done.2.a_ref, ...), custom_call_target="tpu_custom_call" | custom-call | flops 1 | bytes 1 | tf_op jit(solution)/shard_map/begin/pallas_call | solution.py:590
  25.5 0.1 collective-permute-done.8
  25.6 2.7 %collective-permute-start.9 = (f32[2,16,32]{2,1,0:T(8,128)S(1)}, f32[2,16,32]{2,1,0:T(8,128)S(1)}, u32[]{:S(2)}, u32[]{:S(2)}) collective-permute-start(f32[2,16,32]{2,1,0:T(8,128)S(1)} %add.15.total_ref), channel_id=1, source_target_pairs={{0,2},{1,3},{2,0},{3,1},{4,6},{5,7},{6,4},{7,5},{8,10},{9,11},{10,... | collective-permute-start | bytes 12296 | tf_op jit(solution)/shard_map/ppermute | solution.py:52
  28.3 0.5 %collective-permute-done.7.b_ref = f32[2,4,16,768]{3,2,1,0:T(8,128)S(1)} collective-permute-done((f32[2,4,16,768]{3,2,1,0:T(8,128)S(1)}, f32[2,4,16,768]{3,2,1,0:T(8,128)S(1)}, u32[]{:S(2)}, u32[]{:S(2)}) %collective-permute-start.7) | collective-permute-done | bytes 393248 | tf_op jit(solution)/shard_map/ppermute | solution.py:22
  28.8 0.8 %end.1._ = f32[1,2,12,16,768]{4,3,2,1,0:T(8,128)} custom-call(f32[1,2,12,16,768]{4,3,2,1,0:T(8,128)} %get-tuple-element.28.begun_hbm, f32[1,2,12,16,768]{4,3,2,1,0:T(8,128)S(1)} %get-tuple-element.17.state_ref, f32[2,4,16,768]{3,2,1,0:T(8,128)S(1)} %collective-permute-done.7.b_ref), custom_call_target="tpu_custom_call", output_to_operand_aliasing={{}: (0, {})} | custom-call | flops 1 | bytes 1 | tf_op jit(solution)/shard_map/end/pallas_call | solution.py:603
  29.6 0.7 %collective-permute-done.9.came_ref = f32[2,16,32]{2,1,0:T(8,128)S(1)} collective-permute-done((f32[2,16,32]{2,1,0:T(8,128)S(1)}, f32[2,16,32]{2,1,0:T(8,128)S(1)}, u32[]{:S(2)}, u32[]{:S(2)}) %collective-permute-start.9) | collective-permute-done | bytes 4128 | tf_op jit(solution)/shard_map/ppermute | solution.py:52
  30.3 0.7 %pick.1 = f32[2,4,8]{2,1,0:T(4,128)} custom-call(f32[1,2,12,16,768]{4,3,2,1,0:T(8,128)} %end.1._, s32[1,32]{1,0:T(1,128)S(1)} %get-tuple-element.30.owner_ref, f32[2,16,32]{2,1,0:T(8,128)S(1)} %add.15.total_ref, f32[2,16,32]{2,1,0:T(8,128)S(1)} %collective-permute-done.9.came_ref), custom_call_target="tpu_custom_call" | custom-call | flops 1 | bytes 1 | tf_op jit(solution)/shard_map/pick/pallas_call | solution.py:614
  (15 shorter events, 0.1 us)
Async XLA Ops:
  2.4 5.1 %copy-start = (s32[4,2,2,12]{3,2,1,0:T(2,128)S(1)}, s32[4,2,2,12]{3,2,1,0:T(2,128)}, u32[]{:S(2)}) copy-start(s32[4,2,2,12]{3,2,1,0:T(2,128)} %offset_ref.1) | copy-start | bytes 2308
  2.4 5.1 %copy-start.1 = (f32[4,2,2,12]{3,2,1,0:T(2,128)S(1)}, f32[4,2,2,12]{3,2,1,0:T(2,128)}, u32[]{:S(2)}) copy-start(f32[4,2,2,12]{3,2,1,0:T(2,128)} %weight_ref.1) | copy-start | bytes 2308
  2.4 5.1 %copy-start.2 = (s32[2,2,12]{2,1,0:T(2,128)S(1)}, s32[2,2,12]{2,1,0:T(2,128)}, u32[]{:S(2)}) copy-start(s32[2,2,12]{2,1,0:T(2,128)} %cell_ref.1) | copy-start | bytes 580
  2.5 5.1 %copy-start.3 = (s32[32]{0:T(128)S(1)}, s32[32]{0:T(128)}, u32[]{:S(2)}) copy-start(s32[32]{0:T(128)} %param.13) | copy-start | bytes 388
  2.5 11.5 %collective-permute-start.1 = (f32[12,16,768]{2,1,0:T(8,128)S(1)}, f32[12,16,768]{2,1,0:T(8,128)S(1)}, u32[]{:S(2)}, u32[]{:S(2)}) collective-permute-start(f32[12,16,768]{2,1,0:T(8,128)S(1)} %pack.1._.mine_ref), channel_id=1, source_target_pairs={{0,4},{1,0},{2,1},{3,2},{4,5},{5,6},{6,7},{7,3},{8,12},{9,8},{10,9... | collective-permute-start | bytes 1769480 | tf_op jit(solution)/shard_map/ppermute | solution.py:34
  8.0 12.7 %collective-permute-start.6 = (f32[11,16,768]{2,1,0:T(8,128)S(1)}, f32[11,16,768]{2,1,0:T(8,128)S(1)}, u32[]{:S(2)}, u32[]{:S(2)}) collective-permute-start(f32[11,16,768]{2,1,0:T(8,128)S(1)} %get-tuple-element.29), channel_id=1, source_target_pairs={{0,1},{1,2},{2,3},{3,7},{4,0},{5,4},{6,5},{7,6},{8,9},{9,10},{10,1... | collective-permute-start | bytes 1622024 | tf_op jit(solution)/shard_map/ppermute | solution.py:34
  10.6 10.1 %collective-permute-start = (f32[2,4,16,768]{3,2,1,0:T(8,128)S(1)}, f32[2,4,16,768]{3,2,1,0:T(8,128)S(1)}, u32[]{:S(2)}, u32[]{:S(2)}) collective-permute-start(f32[2,4,16,768]{3,2,1,0:T(8,128)S(1)} %get-tuple-element.18), channel_id=1, source_target_pairs={{0,12},{4,0},{8,4},{12,8},{1,13},{5,1},{9,5},{13,9},{2,14},{6,2},{... | collective-permute-start | bytes 1179656 | tf_op jit(solution)/shard_map/ppermute | solution.py:22
  15.0 2.6 %collective-permute-start.5 = (f32[2,16,32]{2,1,0:T(8,128)S(1)}, f32[2,16,32]{2,1,0:T(8,128)S(1)}, u32[]{:S(2)}, u32[]{:S(2)}) collective-permute-start(f32[2,16,32]{2,1,0:T(8,128)S(1)} %ghost.1), channel_id=1, source_target_pairs={{0,4},{4,0},{8,12},{12,8},{1,5},{5,1},{9,13},{13,9},{2,6},{6,2},{1... | collective-permute-start | bytes 12296 | tf_op jit(solution)/shard_map/ppermute | solution.py:52
  15.1 4.2 %collective-permute-start.4 = (f32[2,16,32]{2,1,0:T(8,128)S(1)}, f32[2,16,32]{2,1,0:T(8,128)S(1)}, u32[]{:S(2)}, u32[]{:S(2)}) collective-permute-start(f32[2,16,32]{2,1,0:T(8,128)S(1)} %ghost.1), channel_id=1, source_target_pairs={{0,8},{4,12},{8,0},{12,4},{1,9},{5,13},{9,1},{13,5},{2,10},{6,14},... | collective-permute-start | bytes 12296 | tf_op jit(solution)/shard_map/ppermute | solution.py:52
  17.5 3.2 %collective-permute-start.3 = (f32[2,16,32]{2,1,0:T(8,128)S(1)}, f32[2,16,32]{2,1,0:T(8,128)S(1)}, u32[]{:S(2)}, u32[]{:S(2)}) collective-permute-start(f32[2,16,32]{2,1,0:T(8,128)S(1)} %ghost.1), channel_id=1, source_target_pairs={{0,12},{4,8},{8,4},{12,0},{1,13},{5,9},{9,5},{13,1},{2,14},{6,10},... | collective-permute-start | bytes 12296 | tf_op jit(solution)/shard_map/ppermute | solution.py:52
  17.6 7.0 %collective-permute-start.2 = (f32[2,4,16,768]{3,2,1,0:T(8,128)S(1)}, f32[2,4,16,768]{3,2,1,0:T(8,128)S(1)}, u32[]{:S(2)}, u32[]{:S(2)}) collective-permute-start(f32[2,4,16,768]{3,2,1,0:T(8,128)S(1)} %get-tuple-element.25), channel_id=1, source_target_pairs={{0,12},{4,0},{8,4},{12,8},{1,13},{5,1},{9,5},{13,9},{2,14},{6,2},{... | collective-permute-start | bytes 1179656 | tf_op jit(solution)/shard_map/ppermute | solution.py:22
  20.8 8.0 %collective-permute-start.7 = (f32[2,4,16,768]{3,2,1,0:T(8,128)S(1)}, f32[2,4,16,768]{3,2,1,0:T(8,128)S(1)}, u32[]{:S(2)}, u32[]{:S(2)}) collective-permute-start(f32[2,4,16,768]{3,2,1,0:T(8,128)S(1)} %mend_b.1), channel_id=1, source_target_pairs={{0,12},{4,0},{8,4},{12,8},{1,13},{5,1},{9,5},{13,9},{2,14},{6,2},{... | collective-permute-start | bytes 1179656 | tf_op jit(solution)/shard_map/ppermute | solution.py:22
  21.8 3.7 %collective-permute-start.8 = (f32[2,16,32]{2,1,0:T(8,128)S(1)}, f32[2,16,32]{2,1,0:T(8,128)S(1)}, u32[]{:S(2)}, u32[]{:S(2)}) collective-permute-start(f32[2,16,32]{2,1,0:T(8,128)S(1)} %add_add_fusion.total_ref.__), channel_id=1, source_target_pairs={{0,1},{1,0},{2,3},{3,2},{4,5},{5,4},{6,7},{7,6},{8,9},{9,8},{10,11... | collective-permute-start | bytes 12296 | tf_op jit(solution)/shard_map/ppermute | solution.py:52
  25.6 4.7 %collective-permute-start.9 = (f32[2,16,32]{2,1,0:T(8,128)S(1)}, f32[2,16,32]{2,1,0:T(8,128)S(1)}, u32[]{:S(2)}, u32[]{:S(2)}) collective-permute-start(f32[2,16,32]{2,1,0:T(8,128)S(1)} %add.15.total_ref), channel_id=1, source_target_pairs={{0,2},{1,3},{2,0},{3,1},{4,6},{5,7},{6,4},{7,5},{8,10},{9,11},{10,... | collective-permute-start | bytes 12296 | tf_op jit(solution)/shard_map/ppermute | solution.py:52

commit v22 on v20

--- a/solution.py
+++ b/solution.py
@@ -289,6 +289,10 @@
         partial_ref[c] = total
 
 
+def hand_on_kernel(pack_ref, pack_out):
+    pack_out[...] = pack_ref[...]
+
+
 def ghost_kernel(north_ref, other_ref, column_ref, mixing_ref, partial_ref, sum_ref, near_mixing):
     parts, levels, slots = partial_ref.shape
     rows = mixing_ref.shape[2]
@@ -546,6 +550,15 @@
         cost_estimate=BRIEF,
         name="ghost_base",
     )(*small, owner_slot[None], columns, north, second_pack)
+    second_sent = pl.pallas_call(
+        hand_on_kernel,
+        in_specs=[vmem],
+        out_specs=vmem,
+        out_shape=f32(PACK_ROWS, levels, width),
+        compiler_params=PARAMS,
+        cost_estimate=BRIEF,
+        name="hand_on",
+    )(second_sent)
     second_came = alternating(second_sent, 1)
 
     column_shape = (parts, 2, 2 * (STEPS - 1), levels, LANES)

time: 31.1 us -> 31.1 us (level)
  no operation moved by 1% of the time
where the time goes in v22:
time: 31.1 us; the launch traced here: 30.9 us
  starting transfers between devices  13.5 us (43%)
  Pallas kernels  10.3 us (33%)
  waiting for transfers between devices  6.26 us (20%)
  between operations  0.79 us (3%)
    ppermute x5, starting transfers between devices, exchanged(): lax.ppermute(value, axis, [(i, i ^ distance) for i in range(size)])  7.02 us
    pallas_call x1, Pallas kernels, local(): pl.pallas_call(sweep_kernel, in_specs=[hbm] * 3 + [pl.BlockSpec(memory_sp...  4.6 us
    ppermute x5, waiting for transfers between devices, exchanged(): lax.ppermute(value, axis, [(i, i ^ distance) for i in range(size)])  3.59 us
    ppermute x3, starting transfers between devices, to_previous(): lax.ppermute(value, 'sub', [(i, (i - 1) % peers) for i in range(peers)])  3.43 us
    ppermute x2, starting transfers between devices, alternating(): return lax.ppermute(value, ('sub', 'hor'), pairs)  3.08 us
    ppermute x2, waiting for transfers between devices, alternating(): return lax.ppermute(value, ('sub', 'hor'), pairs)  2.65 us
    pallas_call x1, Pallas kernels, local(): pl.pallas_call(pack_kernel, in_specs=[hbm] * 6, out_specs=vmem, out_shape...  1.78 us
    pallas_call x1, Pallas kernels, local(): pl.pallas_call(begin_kernel, in_specs=[vmem] * 3, out_specs=hbm, out_shap...  0.93 us
  transfers between devices with their start and end apart: 10, of which 4 were waited for; matrix products, arithmetic and copies ran while one was open for 0% of the time, Pallas kernels for 25%

profile of v22, /device:TPU:0, one launch (start us, length us, event | category | flops | bytes accessed | tf_op | source)
XLA Modules:
  0.0 30.9 jit_solution(13616691544927087940)
XLA Ops:
  0.6 1.8 %pack.1._.mine_ref = f32[12,16,768]{2,1,0:T(8,128)S(1)} custom-call(f32[1,2,12,16,768]{4,3,2,1,0:T(8,128)} %state_hbm.3, f32[1,12,16,768]{3,2,1,0:T(8,128)} %east_hbm.3, f32[1,12,16,768]{3,2,1,0:T(8,128)} %north_hbm.3, s32[2,2,12]{2,1,0:T(2,128)} %cell_ref.1, s32[4,2,2,12]{3,2,1,0:T(2,128)} %offset_ref.1, f32[4,2,2,12]{3,2,1,0:T(2,128)} %weight_ref.1), custom_call_target="tpu_custom_call" | custom-call | flops 1 | bytes 1 | tf_op jit(solution)/shard_map/pack/pallas_call | solution.py:499
  2.4 0.0 copy-start.1
  2.5 0.5 %collective-permute-start.1 = (f32[12,16,768]{2,1,0:T(8,128)S(1)}, f32[12,16,768]{2,1,0:T(8,128)S(1)}, u32[]{:S(2)}, u32[]{:S(2)}) collective-permute-start(f32[12,16,768]{2,1,0:T(8,128)S(1)} %pack.1._.mine_ref), channel_id=1, source_target_pairs={{0,4},{1,0},{2,1},{3,2},{4,5},{5,6},{6,7},{7,3},{8,12},{9,8},{10,9... | collective-permute-start | bytes 1769480 | tf_op jit(solution)/shard_map/ppermute | solution.py:34
  2.9 4.6 %sweep.1 = (f32[11,16,768]{2,1,0:T(8,128)S(1)}, f32[2,4,16,768]{3,2,1,0:T(8,128)S(1)}, f32[2,8,16,768]{3,2,1,0:T(8,128)S(1)}, f32[2,2,12,16,128]{4,3,2,1,0:T(8,1...) custom-call(f32[1,2,12,16,768]{4,3,2,1,0:T(8,128)} %state_hbm.3, ...), custom_call_target="tpu_custom_call" | custom-call | flops 1 | bytes 1 | tf_op jit(solution)/shard_map/sweep/pallas_call | solution.py:517
  7.6 0.4 %ghost_base.1 = (f32[2,2,12,32]{3,2,1,0:T(8,128)S(1)}, f32[2,16,32]{2,1,0:T(8,128)S(1)}, s32[1,32]{1,0:T(1,128)S(1)}, f32[11,16,768]{2,1,0:T(8,128)S(1)}) custom-call(s32[2,2,12]{2,1,0:T(2,128)S(1)} %copy-done.2, s32[4,2,2,12]{3,2,1,0:T(2,128)S(1)} %copy-done, f32[4,2,2,12]{3,2,1,0:T(2,128)S(1)} %copy-done.1, s32[1,32]{1,0:T(1,128)S(1)} %bitcast.1, ...), custom_call_target="tpu_custom_call" | custom-call | flops 1 | bytes 1 | tf_op jit(solution)/shard_map/ghost_base/pallas_call | solution.py:541
  8.0 2.6 %collective-permute-start.3 = (f32[11,16,768]{2,1,0:T(8,128)S(1)}, f32[11,16,768]{2,1,0:T(8,128)S(1)}, u32[]{:S(2)}, u32[]{:S(2)}) collective-permute-start(f32[11,16,768]{2,1,0:T(8,128)S(1)} %hand_on.1), channel_id=1, source_target_pairs={{0,1},{1,2},{2,3},{3,7},{4,0},{5,4},{6,5},{7,6},{8,9},{9,10},{10,1... | collective-permute-start | bytes 1622024 | tf_op jit(solution)/shard_map/ppermute | solution.py:34
  10.6 0.7 %collective-permute-start = (f32[2,4,16,768]{3,2,1,0:T(8,128)S(1)}, f32[2,4,16,768]{3,2,1,0:T(8,128)S(1)}, u32[]{:S(2)}, u32[]{:S(2)}) collective-permute-start(f32[2,4,16,768]{3,2,1,0:T(8,128)S(1)} %get-tuple-element.16), channel_id=1, source_target_pairs={{0,12},{4,0},{8,4},{12,8},{1,13},{5,1},{9,5},{13,9},{2,14},{6,2},{... | collective-permute-start | bytes 1179656 | tf_op jit(solution)/shard_map/ppermute | solution.py:22
  11.3 2.7 %collective-permute-done.1.other_ref = f32[12,16,768]{2,1,0:T(8,128)S(1)} collective-permute-done((f32[12,16,768]{2,1,0:T(8,128)S(1)}, f32[12,16,768]{2,1,0:T(8,128)S(1)}, u32[]{:S(2)}, u32[]{:S(2)}) %collective-permute-start.1) | collective-permute-done | bytes 589856 | tf_op jit(solution)/shard_map/ppermute | solution.py:34
  13.9 0.8 %mend_a.1 = (f32[2,4,16,768]{3,2,1,0:T(8,128)S(1)}, f32[2,2,6,16,128]{4,3,2,1,0:T(8,128)S(1)}) custom-call(f32[1,12,16,768]{3,2,1,0:T(8,128)S(1)} %get-tuple-element.17.east_ref, f32[1,12,16,768]{3,2,1,0:T(8,128)S(1)} %get-tuple-element.18.north_ref, f32[11,16,768]{2,1,0:T(8,128)S(1)} %get-tuple-element.19.pack_ref.mine_ref, ...), custom_call_target="tpu_custom_call" | custom-call | flops 1 | bytes 1 | tf_op jit(solution)/shard_map/mend_a/pallas_call | solution.py:565
  14.7 0.2 ghost.1
  15.0 0.1 collective-permute-start.6
  15.0 2.4 %collective-permute-start.5 = (f32[2,16,32]{2,1,0:T(8,128)S(1)}, f32[2,16,32]{2,1,0:T(8,128)S(1)}, u32[]{:S(2)}, u32[]{:S(2)}) collective-permute-start(f32[2,16,32]{2,1,0:T(8,128)S(1)} %ghost.1), channel_id=1, source_target_pairs={{0,8},{4,12},{8,0},{12,4},{1,9},{5,13},{9,1},{13,5},{2,10},{6,14},... | collective-permute-start | bytes 12296 | tf_op jit(solution)/shard_map/ppermute | solution.py:52
  17.5 0.1 collective-permute-start.4
  17.6 1.7 %collective-permute-start.2 = (f32[2,4,16,768]{3,2,1,0:T(8,128)S(1)}, f32[2,4,16,768]{3,2,1,0:T(8,128)S(1)}, u32[]{:S(2)}, u32[]{:S(2)}) collective-permute-start(f32[2,4,16,768]{3,2,1,0:T(8,128)S(1)} %get-tuple-element.23), channel_id=1, source_target_pairs={{0,12},{4,0},{8,4},{12,8},{1,13},{5,1},{9,5},{13,9},{2,14},{6,2},{... | collective-permute-start | bytes 1179656 | tf_op jit(solution)/shard_map/ppermute | solution.py:22
  19.2 1.4 %collective-permute-done.4 = f32[2,16,32]{2,1,0:T(8,128)S(1)} collective-permute-done((f32[2,16,32]{2,1,0:T(8,128)S(1)}, f32[2,16,32]{2,1,0:T(8,128)S(1)}, u32[]{:S(2)}, u32[]{:S(2)}) %collective-permute-start.4) | collective-permute-done | bytes 4128 | tf_op jit(solution)/shard_map/ppermute | solution.py:52
  20.7 0.1 mend_b.1
  20.7 1.1 %collective-permute-start.7 = (f32[2,4,16,768]{3,2,1,0:T(8,128)S(1)}, f32[2,4,16,768]{3,2,1,0:T(8,128)S(1)}, u32[]{:S(2)}, u32[]{:S(2)}) collective-permute-start(f32[2,4,16,768]{3,2,1,0:T(8,128)S(1)} %mend_b.1), channel_id=1, source_target_pairs={{0,12},{4,0},{8,4},{12,8},{1,13},{5,1},{9,5},{13,9},{2,14},{6,2},{... | collective-permute-start | bytes 1179656 | tf_op jit(solution)/shard_map/ppermute | solution.py:22
  21.8 1.7 %collective-permute-start.8 = (f32[2,16,32]{2,1,0:T(8,128)S(1)}, f32[2,16,32]{2,1,0:T(8,128)S(1)}, u32[]{:S(2)}, u32[]{:S(2)}) collective-permute-start(f32[2,16,32]{2,1,0:T(8,128)S(1)} %add_add_fusion.__), channel_id=1, source_target_pairs={{0,1},{1,0},{2,3},{3,2},{4,5},{5,4},{6,7},{7,6},{8,9},{9,8},{10,11... | collective-permute-start | bytes 12296 | tf_op jit(solution)/shard_map/ppermute | solution.py:52
  23.5 2.0 %collective-permute-done.8 = f32[2,16,32]{2,1,0:T(8,128)S(1)} collective-permute-done((f32[2,16,32]{2,1,0:T(8,128)S(1)}, f32[2,16,32]{2,1,0:T(8,128)S(1)}, u32[]{:S(2)}, u32[]{:S(2)}) %collective-permute-start.8) | collective-permute-done | bytes 4128 | tf_op jit(solution)/shard_map/ppermute | solution.py:52
  25.5 2.7 %collective-permute-start.9 = (f32[2,16,32]{2,1,0:T(8,128)S(1)}, f32[2,16,32]{2,1,0:T(8,128)S(1)}, u32[]{:S(2)}, u32[]{:S(2)}) collective-permute-start(f32[2,16,32]{2,1,0:T(8,128)S(1)} %add.15.total_ref), channel_id=1, source_target_pairs={{0,2},{1,3},{2,0},{3,1},{4,6},{5,7},{6,4},{7,5},{8,10},{9,11},{10,... | collective-permute-start | bytes 12296 | tf_op jit(solution)/shard_map/ppermute | solution.py:52
  28.3 0.9 %begin.1.begun_hbm = f32[1,2,12,16,768]{4,3,2,1,0:T(8,128)} custom-call(f32[1,2,12,16,768]{4,3,2,1,0:T(8,128)S(1)} %get-tuple-element.15.state_ref, f32[2,4,16,768]{3,2,1,0:T(8,128)S(1)} %collective-permute-done.middle_ref._, f32[2,4,16,768]{3,2,1,0:T(8,128)S(1)} %collective-permute-done.2.a_ref), custom_call_target="tpu_custom_call" | custom-call | flops 1 | bytes 1 | tf_op jit(solution)/shard_map/begin/pallas_call | solution.py:604
  29.2 0.8 %end.1._ = f32[1,2,12,16,768]{4,3,2,1,0:T(8,128)} custom-call(f32[1,2,12,16,768]{4,3,2,1,0:T(8,128)} %begin.1.begun_hbm, f32[1,2,12,16,768]{4,3,2,1,0:T(8,128)S(1)} %get-tuple-element.15.state_ref, f32[2,4,16,768]{3,2,1,0:T(8,128)S(1)} %collective-permute-done.7.b_ref), custom_call_target="tpu_custom_call", output_to_operand_aliasing={{}: (0, {})} | custom-call | flops 1 | bytes 1 | tf_op jit(solution)/shard_map/end/pallas_call | solution.py:614
  30.0 0.2 collective-permute-done.9.came_ref
  30.2 0.7 %pick.1 = f32[2,4,8]{2,1,0:T(4,128)} custom-call(f32[1,2,12,16,768]{4,3,2,1,0:T(8,128)} %end.1._, s32[1,32]{1,0:T(1,128)S(1)} %get-tuple-element.27.owner_ref, f32[2,16,32]{2,1,0:T(8,128)S(1)} %add.15.total_ref, f32[2,16,32]{2,1,0:T(8,128)S(1)} %collective-permute-done.9.came_ref), custom_call_target="tpu_custom_call" | custom-call | flops 1 | bytes 1 | tf_op jit(solution)/shard_map/pick/pallas_call | solution.py:625
  (16 shorter events, 0.1 us)
Async XLA Ops:
  2.4 5.1 %copy-start = (s32[4,2,2,12]{3,2,1,0:T(2,128)S(1)}, s32[4,2,2,12]{3,2,1,0:T(2,128)}, u32[]{:S(2)}) copy-start(s32[4,2,2,12]{3,2,1,0:T(2,128)} %offset_ref.1) | copy-start | bytes 2308
  2.4 5.1 %copy-start.1 = (f32[4,2,2,12]{3,2,1,0:T(2,128)S(1)}, f32[4,2,2,12]{3,2,1,0:T(2,128)}, u32[]{:S(2)}) copy-start(f32[4,2,2,12]{3,2,1,0:T(2,128)} %weight_ref.1) | copy-start | bytes 2308
  2.4 5.1 %copy-start.2 = (s32[2,2,12]{2,1,0:T(2,128)S(1)}, s32[2,2,12]{2,1,0:T(2,128)}, u32[]{:S(2)}) copy-start(s32[2,2,12]{2,1,0:T(2,128)} %cell_ref.1) | copy-start | bytes 580
  2.5 5.1 %copy-start.3 = (s32[32]{0:T(128)S(1)}, s32[32]{0:T(128)}, u32[]{:S(2)}) copy-start(s32[32]{0:T(128)} %param.13) | copy-start | bytes 388
  2.5 11.5 %collective-permute-start.1 = (f32[12,16,768]{2,1,0:T(8,128)S(1)}, f32[12,16,768]{2,1,0:T(8,128)S(1)}, u32[]{:S(2)}, u32[]{:S(2)}) collective-permute-start(f32[12,16,768]{2,1,0:T(8,128)S(1)} %pack.1._.mine_ref), channel_id=1, source_target_pairs={{0,4},{1,0},{2,1},{3,2},{4,5},{5,6},{6,7},{7,3},{8,12},{9,8},{10,9... | collective-permute-start | bytes 1769480 | tf_op jit(solution)/shard_map/ppermute | solution.py:34
  8.0 12.7 %collective-permute-start.3 = (f32[11,16,768]{2,1,0:T(8,128)S(1)}, f32[11,16,768]{2,1,0:T(8,128)S(1)}, u32[]{:S(2)}, u32[]{:S(2)}) collective-permute-start(f32[11,16,768]{2,1,0:T(8,128)S(1)} %hand_on.1), channel_id=1, source_target_pairs={{0,1},{1,2},{2,3},{3,7},{4,0},{5,4},{6,5},{7,6},{8,9},{9,10},{10,1... | collective-permute-start | bytes 1622024 | tf_op jit(solution)/shard_map/ppermute | solution.py:34
  10.6 10.0 %collective-permute-start = (f32[2,4,16,768]{3,2,1,0:T(8,128)S(1)}, f32[2,4,16,768]{3,2,1,0:T(8,128)S(1)}, u32[]{:S(2)}, u32[]{:S(2)}) collective-permute-start(f32[2,4,16,768]{3,2,1,0:T(8,128)S(1)} %get-tuple-element.16), channel_id=1, source_target_pairs={{0,12},{4,0},{8,4},{12,8},{1,13},{5,1},{9,5},{13,9},{2,14},{6,2},{... | collective-permute-start | bytes 1179656 | tf_op jit(solution)/shard_map/ppermute | solution.py:22
  15.0 2.6 %collective-permute-start.6 = (f32[2,16,32]{2,1,0:T(8,128)S(1)}, f32[2,16,32]{2,1,0:T(8,128)S(1)}, u32[]{:S(2)}, u32[]{:S(2)}) collective-permute-start(f32[2,16,32]{2,1,0:T(8,128)S(1)} %ghost.1), channel_id=1, source_target_pairs={{0,4},{4,0},{8,12},{12,8},{1,5},{5,1},{9,13},{13,9},{2,6},{6,2},{1... | collective-permute-start | bytes 12296 | tf_op jit(solution)/shard_map/ppermute | solution.py:52
  15.0 4.2 %collective-permute-start.5 = (f32[2,16,32]{2,1,0:T(8,128)S(1)}, f32[2,16,32]{2,1,0:T(8,128)S(1)}, u32[]{:S(2)}, u32[]{:S(2)}) collective-permute-start(f32[2,16,32]{2,1,0:T(8,128)S(1)} %ghost.1), channel_id=1, source_target_pairs={{0,8},{4,12},{8,0},{12,4},{1,9},{5,13},{9,1},{13,5},{2,10},{6,14},... | collective-permute-start | bytes 12296 | tf_op jit(solution)/shard_map/ppermute | solution.py:52
  17.5 3.2 %collective-permute-start.4 = (f32[2,16,32]{2,1,0:T(8,128)S(1)}, f32[2,16,32]{2,1,0:T(8,128)S(1)}, u32[]{:S(2)}, u32[]{:S(2)}) collective-permute-start(f32[2,16,32]{2,1,0:T(8,128)S(1)} %ghost.1), channel_id=1, source_target_pairs={{0,12},{4,8},{8,4},{12,0},{1,13},{5,9},{9,5},{13,1},{2,14},{6,10},... | collective-permute-start | bytes 12296 | tf_op jit(solution)/shard_map/ppermute | solution.py:52
  17.6 10.7 %collective-permute-start.2 = (f32[2,4,16,768]{3,2,1,0:T(8,128)S(1)}, f32[2,4,16,768]{3,2,1,0:T(8,128)S(1)}, u32[]{:S(2)}, u32[]{:S(2)}) collective-permute-start(f32[2,4,16,768]{3,2,1,0:T(8,128)S(1)} %get-tuple-element.23), channel_id=1, source_target_pairs={{0,12},{4,0},{8,4},{12,8},{1,13},{5,1},{9,5},{13,9},{2,14},{6,2},{... | collective-permute-start | bytes 1179656 | tf_op jit(solution)/shard_map/ppermute | solution.py:22
  20.7 8.5 %collective-permute-start.7 = (f32[2,4,16,768]{3,2,1,0:T(8,128)S(1)}, f32[2,4,16,768]{3,2,1,0:T(8,128)S(1)}, u32[]{:S(2)}, u32[]{:S(2)}) collective-permute-start(f32[2,4,16,768]{3,2,1,0:T(8,128)S(1)} %mend_b.1), channel_id=1, source_target_pairs={{0,12},{4,0},{8,4},{12,8},{1,13},{5,1},{9,5},{13,9},{2,14},{6,2},{... | collective-permute-start | bytes 1179656 | tf_op jit(solution)/shard_map/ppermute | solution.py:22
  21.8 3.7 %collective-permute-start.8 = (f32[2,16,32]{2,1,0:T(8,128)S(1)}, f32[2,16,32]{2,1,0:T(8,128)S(1)}, u32[]{:S(2)}, u32[]{:S(2)}) collective-permute-start(f32[2,16,32]{2,1,0:T(8,128)S(1)} %add_add_fusion.__), channel_id=1, source_target_pairs={{0,1},{1,0},{2,3},{3,2},{4,5},{5,4},{6,7},{7,6},{8,9},{9,8},{10,11... | collective-permute-start | bytes 12296 | tf_op jit(solution)/shard_map/ppermute | solution.py:52
  25.5 4.6 %collective-permute-start.9 = (f32[2,16,32]{2,1,0:T(8,128)S(1)}, f32[2,16,32]{2,1,0:T(8,128)S(1)}, u32[]{:S(2)}, u32[]{:S(2)}) collective-permute-start(f32[2,16,32]{2,1,0:T(8,128)S(1)} %add.15.total_ref), channel_id=1, source_target_pairs={{0,2},{1,3},{2,0},{3,1},{4,6},{5,7},{6,4},{7,5},{8,10},{9,11},{10,... | collective-permute-start | bytes 12296 | tf_op jit(solution)/shard_map/ppermute | solution.py:52
